TPU v7x, 32 devices: a whole 2x2x4 slice. The times are simulated.
32 devices in a mesh: dp: 4 (over y, x), ctx: 4 (over z), mp: 2 (over core).
Axes of the slice: x: 2, y: 2, z: 4, core: 2. Of those that a mesh axis runs over, the one named last changes fastest.
Arguments:
- tokens: bfloat16 [2, 4, 2048, 1024], P(None, 'dp', 'ctx'), may hold values from -6 to 6
- cotangent: bfloat16 [2, 4, 2048, 1024], P(None, 'dp', 'ctx'), may hold values from -6 to 6
- routes: int32 [2, 4, 2048, 8], P(None, 'dp', 'ctx'), may hold values from 0 to 15, all different within a row; in each aligned block of 512 rows (0 to 511, 512 to 1023, ..., all dimensions but the last counted through in order) at most 320 rows name the same one
- norm_gain: bfloat16 [1024], P(('dp', 'ctx')), may hold values from 0.5 to 1.5
- w_query: bfloat16 [1024, 1024], P(('dp', 'ctx'), 'mp'), may hold values from -0.1875 to 0.1875
- w_key: bfloat16 [1024, 512], P(('dp', 'ctx'), 'mp'), may hold values from -0.1875 to 0.1875
- w_value: bfloat16 [1024, 512], P(('dp', 'ctx'), 'mp'), may hold values from -0.1875 to 0.1875
- w_output: bfloat16 [1024, 1024], P(('dp', 'ctx'), 'mp'), may hold values from -1.5 to 1.5
- ffn_gain: bfloat16 [1024], P(('dp', 'ctx')), may hold values from 0.5 to 1.5
- w_router: bfloat16 [1024, 16], P(('dp', 'ctx')), may hold values from -0.09375 to 0.09375
- w_gate: bfloat16 [16, 1024, 512], P(None, ('dp', 'ctx'), 'mp'), may hold values from -0.1875 to 0.1875
- w_up: bfloat16 [16, 1024, 512], P(None, ('dp', 'ctx'), 'mp'), may hold values from -0.1875 to 0.1875
- w_down: bfloat16 [16, 1024, 512], P(None, ('dp', 'ctx'), 'mp'), may hold values from -1 to 1
Outputs:
- output: bfloat16 [2, 4, 2048, 1024], P(None, 'dp', 'ctx')
- input_grad: bfloat16 [2, 4, 2048, 1024], P(None, 'dp', 'ctx')
- grad_norm_gain: float32 [1024], P(('dp', 'ctx'))
- grad_w_query: float32 [1024, 1024], P(('dp', 'ctx'), 'mp')
- grad_w_key: float32 [1024, 512], P(('dp', 'ctx'), 'mp')
- grad_w_value: float32 [1024, 512], P(('dp', 'ctx'), 'mp')
- grad_w_output: float32 [1024, 1024], P(('dp', 'ctx'), 'mp')
- grad_ffn_gain: float32 [1024], P(('dp', 'ctx'))
- grad_w_router: float32 [1024, 16], P(('dp', 'ctx'))
- grad_w_gate: float32 [16, 1024, 512], P(None, ('dp', 'ctx'), 'mp')
- grad_w_up: float32 [16, 1024, 512], P(None, ('dp', 'ctx'), 'mp')
- grad_w_down: float32 [16, 1024, 512], P(None, ('dp', 'ctx'), 'mp')
Inputs may be any that keep to these rules, and one draw needn't show every extreme that they name: `routes`: each row names 8 different experts. Within each aligned block of 512 positions of one sequence, no expert is named by more than 320 rows, and in some block an expert is named by exactly 320 rows.
All inputs are finite; a program needn't handle non-finite values.
Results may differ from a plain program's by a relative error of at most 0.023.
Values may be sent and summed in bfloat16 or wider, within the bound.
No kernel may reach another device: no remote copies, remote signals or barrier semaphores. Data moves between devices by JAX's collectives and lax.ppermute only.
A program may use at most 320 MiB of HBM per device.

v0:
```python
import math

import jax
import jax.numpy as jnp
from jax import lax
from jax.sharding import PartitionSpec as P

HD = 64


EPS = 1e-06
THETA = 10000.0
NEG = -1e30
HIGH = lax.Precision.HIGHEST
block_keys = 512


def normalize(values, gain):
    return values * lax.rsqrt(jnp.mean(values * values, axis=-1, keepdims=True) + EPS) * gain


def rotation(positions, head_dim):
    freqs = THETA ** (-(jnp.arange(head_dim // 2, dtype=jnp.float32) * 2.0) / head_dim)
    angles = positions.astype(jnp.float32)[:, None] * freqs[None, :]
    return (jnp.cos(angles), jnp.sin(angles))


def rotate(values, cosine, sine):
    half_dim = values.shape[-1] // 2
    first_half = values[..., :half_dim]
    second_half = values[..., half_dim:]
    return jnp.concatenate(
        [first_half * cosine - second_half * sine, second_half * cosine + first_half * sine],
        axis=-1,
    )


def pick_rows(table, picks):
    return jax.vmap(lambda source, choose: source[choose])(table, picks)


def slot_table(ids_flat, expert_count, capacity):
    route_total = ids_flat.shape[0]
    onehot = (ids_flat[:, None] == jnp.arange(expert_count, dtype=jnp.int32)[None, :]).astype(
        jnp.int32
    )
    route_rank = jnp.sum(
        (jnp.cumsum(onehot, axis=0, dtype=jnp.int32) - 1) * onehot, axis=1, dtype=jnp.int32
    )
    slot_ids = ids_flat * capacity + route_rank
    owners = (
        jnp.full((expert_count * capacity,), route_total, jnp.int32)
        .at[slot_ids]
        .set(jnp.arange(route_total, dtype=jnp.int32))
    )
    return (slot_ids, owners)


def per_device(
    tokens,
    cotangent,
    routes,
    norm_gain,
    w_query,
    w_key,
    w_value,
    w_output,
    ffn_gain,
    w_router,
    w_gate,
    w_up,
    w_down,
):
    micro_count, seq_count, local_len, model_width = tokens.shape
    route_count = routes.shape[3]
    expert_count = w_gate.shape[0]
    capacity = local_len * route_count * 5 // (expert_count * 4)
    row_count = seq_count * local_len
    scale = HD ** (-0.5)
    q_first = lax.axis_index("ctx") * local_len
    q_where = q_first + jnp.arange(local_len, dtype=jnp.int32)
    cosine, sine = rotation(q_where, HD)
    cosine = cosine[None, :, None, :]
    sine = sine[None, :, None, :]
    attn_total = None
    expert_total = None
    results = []
    input_grads = []
    for micro_id in range(micro_count):
        attn_part = (
            lax.all_gather(norm_gain, ("dp", "ctx"), axis=0, tiled=True),
            lax.all_gather(ffn_gain, ("dp", "ctx"), axis=0, tiled=True),
            lax.all_gather(w_router, ("dp", "ctx"), axis=0, tiled=True),
            lax.all_gather(w_query, ("dp", "ctx"), axis=0, tiled=True),
            lax.all_gather(w_key, ("dp", "ctx"), axis=0, tiled=True),
            lax.all_gather(w_value, ("dp", "ctx"), axis=0, tiled=True),
            lax.all_gather(w_output, ("dp", "ctx"), axis=0, tiled=True),
        )
        expert_part = (
            lax.all_gather(w_gate, ("dp", "ctx"), axis=1, tiled=True),
            lax.all_gather(w_up, ("dp", "ctx"), axis=1, tiled=True),
            lax.all_gather(w_down, ("dp", "ctx"), axis=1, tiled=True),
        )
        attn_part, expert_part = (attn_part, expert_part)
        gain_one, gain_two, router_full, query_full, key_full, value_full, output_full = attn_part
        gate_full, up_full, down_full = expert_part
        gain_one = gain_one.astype(jnp.float32)
        gain_two = gain_two.astype(jnp.float32)
        x_rows = tokens[micro_id].reshape(row_count, model_width).astype(jnp.float32)
        normed = normalize(x_rows, gain_one)
        normed_low = normed.astype(jnp.bfloat16)
        q_rows = jnp.dot(normed_low, query_full, preferred_element_type=jnp.float32)
        k_rows = jnp.dot(normed_low, key_full, preferred_element_type=jnp.float32)
        v_rows = jnp.dot(normed_low, value_full, preferred_element_type=jnp.float32)
        local_heads = q_rows.shape[1] // HD
        local_kv = k_rows.shape[1] // HD
        group_size = local_heads // local_kv
        q_rot = rotate(q_rows.reshape(seq_count, local_len, local_heads, HD), cosine, sine).astype(
            jnp.bfloat16
        )
        q_rot = q_rot.reshape(seq_count, local_len, local_kv, group_size, HD)
        k_rot = rotate(k_rows.reshape(seq_count, local_len, local_kv, HD), cosine, sine).astype(
            jnp.bfloat16
        )
        k_send = k_rot.reshape(seq_count, local_len, local_kv * HD)
        v_send = v_rows.astype(jnp.bfloat16).reshape(seq_count, local_len, local_kv * HD)
        accum_start = jnp.zeros((seq_count, local_len, local_kv, group_size, HD), jnp.float32)
        peak_start = jnp.full(accum_start.shape[:-1], NEG, jnp.float32)
        total_start = jnp.zeros(accum_start.shape[:-1], jnp.float32)
        running = (accum_start, peak_start, total_start)
        keys_in = lax.all_gather(k_send, "ctx", axis=1, tiled=True)
        vals_in = lax.all_gather(v_send, "ctx", axis=1, tiled=True)
        absorb_key_span = math.gcd(keys_in.shape[1], block_keys)

        def visit(state_now, block_id):
            k_begin = block_id * absorb_key_span

            def visit_compute(state_in):
                accum, row_peak, row_total = state_in
                keys_blk = lax.dynamic_slice_in_dim(
                    keys_in, block_id * absorb_key_span, absorb_key_span, 1
                ).reshape(seq_count, absorb_key_span, local_kv, HD)
                vals_blk = lax.dynamic_slice_in_dim(
                    vals_in, block_id * absorb_key_span, absorb_key_span, 1
                ).reshape(seq_count, absorb_key_span, local_kv, HD)
                scores = (
                    jnp.einsum(
                        "scngd,sjnd->scngj", q_rot, keys_blk, preferred_element_type=jnp.float32
                    )
                    * scale
                )
                allowed = (k_begin + jnp.arange(absorb_key_span, dtype=jnp.int32))[
                    None, :
                ] <= q_where[:, None]
                allowed = allowed[None, :, None, None, :]
                new_peak = jnp.maximum(row_peak, jnp.max(jnp.where(allowed, scores, NEG), axis=-1))
                weights = jnp.where(allowed, jnp.exp(scores - new_peak[..., None]), 0.0)
                factor = jnp.exp(row_peak - new_peak)
                row_total = row_total * factor + jnp.sum(weights, axis=-1)
                accum = accum * factor[..., None] + jnp.einsum(
                    "scngj,sjnd->scngd",
                    weights.astype(jnp.bfloat16),
                    vals_blk,
                    preferred_element_type=jnp.float32,
                )
                return (accum, new_peak, row_total)

            return (
                lax.cond(
                    k_begin > q_where[-1], lambda unchanged: unchanged, visit_compute, state_now
                ),
                None,
            )

        running, unused = lax.scan(
            visit, running, jnp.arange(keys_in.shape[1] // absorb_key_span, dtype=jnp.int32)
        )
        accum, row_peak, row_total = running
        attn_heads = accum / row_total[..., None]
        log_total = row_peak + jnp.log(row_total)
        attn_rows = attn_heads.reshape(row_count, local_heads * HD)
        attn_low = attn_rows.astype(jnp.bfloat16)
        mixed_part = jnp.einsum(
            "th,dh->td", attn_low, output_full, preferred_element_type=jnp.float32
        )
        mixed = lax.psum(mixed_part.astype(jnp.bfloat16), "mp").astype(jnp.float32)
        hidden = x_rows + mixed
        ffn_in = normalize(hidden, gain_two)
        ffn_low = ffn_in.astype(jnp.bfloat16)
        logits = jnp.dot(ffn_low, router_full, preferred_element_type=jnp.float32)
        id_rows = routes[micro_id].reshape(row_count, route_count)
        onehot = (
            id_rows[:, :, None] == jnp.arange(expert_count, dtype=jnp.int32)[None, None, :]
        ).astype(jnp.float32)
        picked = jnp.sum(onehot * logits[:, None, :], axis=-1)
        gate_weights = jax.nn.softmax(picked, axis=-1)
        slot_ids, owners = jax.vmap(lambda choose: slot_table(choose, expert_count, capacity))(
            routes[micro_id].reshape(seq_count, local_len * route_count)
        )
        padded_in = jnp.concatenate(
            [
                ffn_low.reshape(seq_count, local_len, model_width),
                jnp.zeros((seq_count, 1, model_width), jnp.bfloat16),
            ],
            axis=1,
        )
        dispatched = pick_rows(padded_in, owners // route_count).reshape(
            seq_count, expert_count, capacity, model_width
        )
        gate_hidden = jnp.einsum(
            "secd,edf->secf", dispatched, gate_full, preferred_element_type=jnp.float32
        )
        up_hidden = jnp.einsum(
            "secd,edf->secf", dispatched, up_full, preferred_element_type=jnp.float32
        )
        gate_act = jax.nn.silu(gate_hidden)
        act_low = (gate_act * up_hidden).astype(jnp.bfloat16)
        expert_out = jnp.einsum(
            "secf,edf->secd", act_low, down_full, preferred_element_type=jnp.float32
        )
        route_out = pick_rows(
            expert_out.reshape(seq_count, expert_count * capacity, model_width), slot_ids
        ).reshape(row_count, route_count, model_width)
        moe_part = jnp.sum(gate_weights[..., None] * route_out, axis=1)
        moe_sum = lax.psum(moe_part.astype(jnp.bfloat16), "mp").astype(jnp.float32)
        results.append(
            (hidden + moe_sum).astype(jnp.bfloat16).reshape(seq_count, local_len, model_width)
        )
        attn_part = (
            lax.all_gather(norm_gain, ("dp", "ctx"), axis=0, tiled=True),
            lax.all_gather(ffn_gain, ("dp", "ctx"), axis=0, tiled=True),
            lax.all_gather(w_router, ("dp", "ctx"), axis=0, tiled=True),
            lax.all_gather(w_query, ("dp", "ctx"), axis=0, tiled=True),
            lax.all_gather(w_key, ("dp", "ctx"), axis=0, tiled=True),
            lax.all_gather(w_value, ("dp", "ctx"), axis=0, tiled=True),
            lax.all_gather(w_output, ("dp", "ctx"), axis=0, tiled=True),
        )
        expert_part = (
            lax.all_gather(w_gate, ("dp", "ctx"), axis=1, tiled=True),
            lax.all_gather(w_up, ("dp", "ctx"), axis=1, tiled=True),
            lax.all_gather(w_down, ("dp", "ctx"), axis=1, tiled=True),
        )
        gain_one, gain_two, router_full, query_full, key_full, value_full, output_full = attn_part
        gate_full, up_full, down_full = expert_part
        gain_one = gain_one.astype(jnp.float32)
        gain_two = gain_two.astype(jnp.float32)
        grad_out = cotangent[micro_id].reshape(row_count, model_width).astype(jnp.float32)
        route_grad = (
            (gate_weights[..., None] * grad_out[:, None, :])
            .astype(jnp.bfloat16)
            .reshape(seq_count, local_len * route_count, model_width)
        )
        route_grad = jnp.concatenate(
            [route_grad, jnp.zeros((seq_count, 1, model_width), jnp.bfloat16)], axis=1
        )
        out_grad = pick_rows(route_grad, owners).reshape(
            seq_count, expert_count, capacity, model_width
        )
        act_grad = jnp.einsum(
            "secd,edf->secf", out_grad, down_full, preferred_element_type=jnp.float32
        )
        sigma = jax.nn.sigmoid(gate_hidden)
        gate_grad = (act_grad * up_hidden * sigma * (1.0 + gate_hidden * (1.0 - sigma))).astype(
            jnp.bfloat16
        )
        up_grad = (act_grad * gate_act).astype(jnp.bfloat16)
        grad_gate_w = jnp.einsum(
            "secd,secf->edf", dispatched, gate_grad, preferred_element_type=jnp.float32
        )
        grad_up_w = jnp.einsum(
            "secd,secf->edf", dispatched, up_grad, preferred_element_type=jnp.float32
        )
        grad_down_w = jnp.einsum(
            "secd,secf->edf", out_grad, act_low, preferred_element_type=jnp.float32
        )
        slot_in_grad = jnp.einsum(
            "secf,edf->secd", gate_grad, gate_full, preferred_element_type=jnp.float32
        )
        slot_in_grad = slot_in_grad + jnp.einsum(
            "secf,edf->secd", up_grad, up_full, preferred_element_type=jnp.float32
        )
        in_routes = pick_rows(
            slot_in_grad.reshape(seq_count, expert_count * capacity, model_width), slot_ids
        ).reshape(row_count, route_count, model_width)
        ffn_grad_part = jnp.sum(in_routes, axis=1)
        gate_grad_part = jnp.sum(grad_out[:, None, :] * route_out, axis=-1)
        ffn_grad_moe, gate_sums = (
            lax.psum(ffn_grad_part.astype(jnp.bfloat16), "mp").astype(jnp.float32),
            lax.psum(gate_grad_part.astype(jnp.bfloat16), "mp").astype(jnp.float32),
        )
        picked_grad = gate_weights * (
            gate_sums - jnp.sum(gate_weights * gate_sums, axis=-1, keepdims=True)
        )
        logit_grad = jnp.sum(onehot * picked_grad[..., None], axis=1)
        grad_router = jnp.einsum(
            "td,te->de", ffn_low.astype(jnp.float32), logit_grad, precision=HIGH
        )
        ffn_grad = ffn_grad_moe + jnp.einsum(
            "te,de->td", logit_grad, router_full.astype(jnp.float32), precision=HIGH
        )
        unused, pull_two = jax.vjp(normalize, hidden, gain_two)
        norm_two_grad, grad_gain_two = pull_two(ffn_grad)
        hidden_grad = grad_out + norm_two_grad
        mixed_grad = hidden_grad.astype(jnp.bfloat16)
        attn_grad = jnp.einsum(
            "td,dh->th", mixed_grad, output_full, preferred_element_type=jnp.float32
        ).astype(jnp.bfloat16)
        grad_output_w = jnp.einsum(
            "td,th->dh", mixed_grad, attn_low, preferred_element_type=jnp.float32
        )
        head_grad = attn_grad.reshape(seq_count, local_len, local_kv, group_size, HD)
        row_delta = jnp.sum(head_grad.astype(jnp.float32) * attn_heads, axis=-1)
        keys_all, vals_all = (
            lax.all_gather(k_send, "ctx", axis=1, tiled=True),
            lax.all_gather(v_send, "ctx", axis=1, tiled=True),
        )
        seq_len = keys_all.shape[1]
        key_span = math.gcd(seq_len, block_keys)

        def revisit(running, block_id):
            k_begin = block_id * key_span

            def revisit_compute(state_in):
                q_grad, key_terms, val_terms = state_in
                keys_blk = lax.dynamic_slice_in_dim(keys_all, k_begin, key_span, 1).reshape(
                    seq_count, key_span, local_kv, HD
                )
                vals_blk = lax.dynamic_slice_in_dim(vals_all, k_begin, key_span, 1).reshape(
                    seq_count, key_span, local_kv, HD
                )
                scores = (
                    jnp.einsum(
                        "scngd,sjnd->scngj", q_rot, keys_blk, preferred_element_type=jnp.float32
                    )
                    * scale
                )
                allowed = (k_begin + jnp.arange(key_span, dtype=jnp.int32))[None, :] <= q_where[
                    :, None
                ]
                allowed = allowed[None, :, None, None, :]
                probs = jnp.where(allowed, jnp.exp(scores - log_total[..., None]), 0.0)
                prob_grad = jnp.einsum(
                    "scngd,sjnd->scngj", head_grad, vals_blk, preferred_element_type=jnp.float32
                )
                score_grad = (probs * (prob_grad - row_delta[..., None])).astype(jnp.bfloat16)
                q_grad = (
                    q_grad
                    + jnp.einsum(
                        "scngj,sjnd->scngd",
                        score_grad,
                        keys_blk,
                        preferred_element_type=jnp.float32,
                    )
                    * scale
                )
                key_part = (
                    jnp.einsum(
                        "scngj,scngd->sjnd", score_grad, q_rot, preferred_element_type=jnp.float32
                    )
                    * scale
                )
                val_part = jnp.einsum(
                    "scngj,scngd->sjnd",
                    probs.astype(jnp.bfloat16),
                    head_grad,
                    preferred_element_type=jnp.float32,
                )
                key_terms = lax.dynamic_update_slice_in_dim(
                    key_terms, key_part.reshape(seq_count, key_span, local_kv * HD), k_begin, 1
                )
                val_terms = lax.dynamic_update_slice_in_dim(
                    val_terms, val_part.reshape(seq_count, key_span, local_kv * HD), k_begin, 1
                )
                return (q_grad, key_terms, val_terms)

            return (
                lax.cond(
                    k_begin > q_where[-1], lambda unchanged: unchanged, revisit_compute, running
                ),
                None,
            )

        q_grad_start = jnp.zeros((seq_count, local_len, local_kv, group_size, HD), jnp.float32)
        term_start = jnp.zeros((seq_count, seq_len, local_kv * HD), jnp.float32)
        (q_grad, key_terms, val_terms), unused = lax.scan(
            revisit,
            (q_grad_start, term_start, term_start),
            jnp.arange(seq_len // key_span, dtype=jnp.int32),
        )
        key_sum, val_sum = (
            lax.psum_scatter(
                key_terms.astype(jnp.bfloat16), "ctx", scatter_dimension=1, tiled=True
            ).astype(jnp.float32),
            lax.psum_scatter(
                val_terms.astype(jnp.bfloat16), "ctx", scatter_dimension=1, tiled=True
            ).astype(jnp.float32),
        )
        q_back = (
            rotate(q_grad.reshape(seq_count, local_len, local_heads, HD), cosine, -sine)
            .astype(jnp.bfloat16)
            .reshape(row_count, local_heads * HD)
        )
        k_back = (
            rotate(key_sum.reshape(seq_count, local_len, local_kv, HD), cosine, -sine)
            .astype(jnp.bfloat16)
            .reshape(row_count, local_kv * HD)
        )
        v_back = val_sum.astype(jnp.bfloat16).reshape(row_count, local_kv * HD)
        grad_query_w = jnp.einsum(
            "td,th->dh", normed_low, q_back, preferred_element_type=jnp.float32
        )
        grad_key_w = jnp.einsum("td,th->dh", normed_low, k_back, preferred_element_type=jnp.float32)
        grad_value_w = jnp.einsum(
            "td,th->dh", normed_low, v_back, preferred_element_type=jnp.float32
        )
        normed_part = jnp.einsum(
            "th,dh->td", q_back, query_full, preferred_element_type=jnp.float32
        )
        normed_part = normed_part + jnp.einsum(
            "th,dh->td", k_back, key_full, preferred_element_type=jnp.float32
        )
        normed_part = normed_part + jnp.einsum(
            "th,dh->td", v_back, value_full, preferred_element_type=jnp.float32
        )
        normed_grad = lax.psum(normed_part.astype(jnp.bfloat16), "mp").astype(jnp.float32)
        unused, pull_one = jax.vjp(normalize, x_rows, gain_one)
        x_grad, grad_gain_one = pull_one(normed_grad)
        input_grads.append(
            (hidden_grad + x_grad).astype(jnp.bfloat16).reshape(seq_count, local_len, model_width)
        )
        attn_step = (
            grad_gain_one,
            grad_gain_two,
            grad_router,
            grad_query_w,
            grad_key_w,
            grad_value_w,
            grad_output_w,
        )
        expert_step = (grad_gate_w, grad_up_w, grad_down_w)
        attn_total = (
            attn_step if attn_total is None else jax.tree.map(jnp.add, attn_total, attn_step)
        )
        expert_total = (
            expert_step
            if expert_total is None
            else jax.tree.map(jnp.add, expert_total, expert_step)
        )
    attn_grads = (
        lax.psum_scatter(attn_total[0], ("dp", "ctx"), scatter_dimension=0, tiled=True),
        lax.psum_scatter(attn_total[1], ("dp", "ctx"), scatter_dimension=0, tiled=True),
        lax.psum_scatter(attn_total[2], ("dp", "ctx"), scatter_dimension=0, tiled=True),
        lax.psum_scatter(attn_total[3], ("dp", "ctx"), scatter_dimension=0, tiled=True),
        lax.psum_scatter(attn_total[4], ("dp", "ctx"), scatter_dimension=0, tiled=True),
        lax.psum_scatter(attn_total[5], ("dp", "ctx"), scatter_dimension=0, tiled=True),
        lax.psum_scatter(attn_total[6], ("dp", "ctx"), scatter_dimension=0, tiled=True),
    )
    expert_grads = (
        lax.psum_scatter(expert_total[0], ("dp", "ctx"), scatter_dimension=1, tiled=True),
        lax.psum_scatter(expert_total[1], ("dp", "ctx"), scatter_dimension=1, tiled=True),
        lax.psum_scatter(expert_total[2], ("dp", "ctx"), scatter_dimension=1, tiled=True),
    )
    return (
        jnp.stack(results),
        jnp.stack(input_grads),
        attn_grads[0],
        attn_grads[3],
        attn_grads[4],
        attn_grads[5],
        attn_grads[6],
        attn_grads[1],
        attn_grads[2],
        expert_grads[0],
        expert_grads[1],
        expert_grads[2],
    )


def solution(mesh):
    placed = (
        P(None, "dp", "ctx", None),
        P(None, "dp", "ctx", None),
        P(None, "dp", "ctx", None),
        P(("dp", "ctx")),
        P(("dp", "ctx"), "mp"),
        P(("dp", "ctx"), "mp"),
        P(("dp", "ctx"), "mp"),
        P(("dp", "ctx"), "mp"),
        P(("dp", "ctx")),
        P(("dp", "ctx"), None),
        P(None, ("dp", "ctx"), "mp"),
        P(None, ("dp", "ctx"), "mp"),
        P(None, ("dp", "ctx"), "mp"),
    )
    return jax.shard_map(
        per_device,
        mesh=mesh,
        in_specs=placed,
        out_specs=(
            P(None, "dp", "ctx", None),
            P(None, "dp", "ctx", None),
            P(("dp", "ctx")),
            P(("dp", "ctx"), "mp"),
            P(("dp", "ctx"), "mp"),
            P(("dp", "ctx"), "mp"),
            P(("dp", "ctx"), "mp"),
            P(("dp", "ctx")),
            P(("dp", "ctx"), None),
            P(None, ("dp", "ctx"), "mp"),
            P(None, ("dp", "ctx"), "mp"),
            P(None, ("dp", "ctx"), "mp"),
        ),
        check_vma=False,
    )
```

profile of v0, /device:TPU:0, one launch (start us, length us, event | category | flops | bytes accessed | tf_op | source)
XLA Modules:
  0.0 3186.8 jit_solution(8052074396920666537)
XLA Ops:
  11.1 44.3 %all-reduce.9 = (bf16[1024]{0:T(1024)(128)(2,1)S(1)}, bf16[1024]{0:T(1024)(128)(2,1)}) all-reduce(bf16[1024]{0:T(1024)(128)(2,1)S(1)} %dynamic-update-slice, bf16[1024]{0:T(1024)(128)(2,1)S(1)} %dynamic-update-slice.1), channel_id=1, replica_groups=mesh['dp'=4,'ctx'=4,'mp'=2] {'dp','ctx'}, use_global_device_ids=true, to_apply=%add.4 | all-reduce | flops 2048 | bytes 8192
  57.5 41.6 %all_gather.32 = bf16[1024,256]{1,0:T(8,128)(2,1)S(1)} all-gather(bf16[64,256]{1,0:T(8,128)(2,1)} %param.35), channel_id=1, replica_groups=mesh['dp'=4,'ctx'=4,'mp'=2] {'dp','ctx'}, dimensions={0}, use_global_device_ids=true | all-gather | bytes 557056 | tf_op jit(solution)/shard_map/all_gather | solution.py:96
  102.5 48.6 %all_gather.29 = bf16[1024,256]{1,0:T(8,128)(2,1)S(1)} all-gather(bf16[64,256]{1,0:T(8,128)(2,1)S(1)} %copy-done.98), channel_id=1, replica_groups=mesh['dp'=4,'ctx'=4,'mp'=2] {'dp','ctx'}, dimensions={0}, use_global_device_ids=true | all-gather | bytes 557056 | tf_op jit(solution)/shard_map/all_gather | solution.py:95
  162.4 55.7 %all-gather.15.cloned.1.call-done = bf16[1024,512]{1,0:T(8,128)(2,1)} async-done(((bf16[64,512]{1,0:T(8,128)(2,1)}), bf16[1024,512]{1,0:T(8,128)(2,1)}) %all-gather.15.cloned.1.call-update) | async-done | bytes 1048592 | tf_op jit(solution)/shard_map/all_gather | solution.py:94
  224.6 22.3 all-gather.13.cloned.1.call-done
  248.0 18.4 while.56
  277.5 18.8 while.57
  300.2 33.7 %all-gather.17.cloned.1.call-done = bf16[1024,512]{1,0:T(8,128)(2,1)} async-done(((bf16[64,512]{1,0:T(8,128)(2,1)}), bf16[1024,512]{1,0:T(8,128)(2,1)}) %all-gather.17.cloned.1.call-update) | async-done | bytes 1048592 | tf_op jit(solution)/shard_map/all_gather | solution.py:97
  352.6 46.5 %all-gather.2 = bf16[16,64,16]{1,2,0:T(8,128)(2,1)S(1)} all-gather(bf16[1,64,16]{1,2,0:T(8,128)(2,1)S(1)} %bitcast.964), channel_id=1, replica_groups=mesh['dp'=4,'ctx'=4,'mp'=2] {'dp','ctx'}, dimensions={0}, use_global_device_ids=true | all-gather | bytes 34816 | tf_op jit(solution)/shard_map/all_gather | solution.py:93
  402.6 15.5 scatter_custom_fusion
  418.4 15.5 scatter_custom_fusion.1
  462.7 126.2 %gather_fusion.4 = bf16[5120,1024]{1,0:T(8,128)(2,1)} fusion(bf16[1,4097,1024]{2,1,0:T(8,128)(2,1)} %concatenate.112, s32[5120]{0:T(1024)S(1)} %bitcast.869), kind=kCustom, calls=%fused_computation.4 | custom fusion | bytes 21012480 | tf_op jit(solution)/shard_map/vmap()/gather | solution.py:39
  589.0 68.2 %gather_fusion = bf16[5120,1024]{1,0:T(8,128)(2,1)} fusion(bf16[1,513,1024]{2,1,0:T(8,128)(2,1)S(1)} %concatenate.106, s32[5120]{0:T(1024)S(1)} %bitcast.868), kind=kCustom, calls=%fused_computation | custom fusion | bytes 21012480 | tf_op jit(solution)/shard_map/vmap()/gather | solution.py:39
  669.6 125.7 %gather_fusion.6 = bf16[5120,1024]{1,0:T(8,128)(2,1)} fusion(bf16[1,4097,1024]{2,1,0:T(8,128)(2,1)} %concatenate.115, s32[5120]{0:T(1024)S(1)} %bitcast.867), kind=kCustom, calls=%fused_computation.6 | custom fusion | bytes 21012480 | tf_op jit(solution)/shard_map/vmap()/gather | solution.py:39
  795.4 68.6 %gather_fusion.2 = bf16[5120,1024]{1,0:T(8,128)(2,1)} fusion(bf16[1,513,1024]{2,1,0:T(8,128)(2,1)S(1)} %concatenate.111, s32[5120]{0:T(1024)S(1)} %bitcast.866), kind=kCustom, calls=%fused_computation.2 | custom fusion | bytes 21012480 | tf_op jit(solution)/shard_map/vmap()/gather | solution.py:39
  887.3 16.8 fusion.115
  904.1 15.3 fusion.251
  919.5 77.3 %gather_fusion.1 = f32[4096,1024]{1,0:T(8,128)} fusion(f32[1,5120,1024]{2,1,0:T(8,128)} %bitcast.861, s32[4096]{0:T(1024)S(1)} %bitcast.864), kind=kCustom, calls=%fused_computation.1 | custom fusion | bytes 33587200 | tf_op jit(solution)/shard_map/vmap()/gather | solution.py:39
  1010.8 18.6 convolution_add_fusion.4
  1029.4 76.9 %gather_fusion.5 = f32[4096,1024]{1,0:T(8,128)} fusion(f32[1,5120,1024]{2,1,0:T(8,128)} %bitcast.858, s32[4096]{0:T(1024)S(1)} %bitcast.865), kind=kCustom, calls=%fused_computation.5 | custom fusion | bytes 33587200 | tf_op jit(solution)/shard_map/vmap()/gather | solution.py:39
  1136.2 16.7 fusion.117
  1152.9 15.1 fusion.119
  1167.9 18.6 convolution_add_fusion.3
  1186.5 76.9 %gather_fusion.7 = f32[4096,1024]{1,0:T(8,128)} fusion(f32[1,5120,1024]{2,1,0:T(8,128)} %bitcast.859, s32[4096]{0:T(1024)S(1)} %bitcast.862), kind=kCustom, calls=%fused_computation.7 | custom fusion | bytes 33587200 | tf_op jit(solution)/shard_map/vmap()/gather | solution.py:39
  1272.8 15.9 fusion.255
  1299.5 77.4 %gather_fusion.3 = f32[4096,1024]{1,0:T(8,128)} fusion(f32[1,5120,1024]{2,1,0:T(8,128)} %bitcast.860, s32[4096]{0:T(1024)S(1)} %bitcast.863), kind=kCustom, calls=%fused_computation.3 | custom fusion | bytes 33587200 | tf_op jit(solution)/shard_map/vmap()/gather | solution.py:39
  1406.0 32.9 %while.59 = (s32[]{:T(128)}, f32[1,512,4,2,64]{1,4,3,2,0:T(8,128)S(1)}, bf16[1,2048,256]{1,2,0:T(8,128)(2,1)}, bf16[1,2048,256]{1,2,0:T(8,128)(2,1)}, s32[4]{0:T...) while((s32[]{:T(128)}, ...), condition=%wide.region_63.64_spmd, body=%wide.region_60.63_spmd.sunk | while | flops 1364197888 | bytes 96524720 | solution.py:385
  1408.5 22.9 conditional.11
  1444.3 33.4 %while.58 = (s32[]{:T(128)}, f32[1,512,4,2,64]{1,4,3,2,0:T(8,128)S(1)}, bf16[1,2048,256]{1,2,0:T(8,128)(2,1)}, bf16[1,2048,256]{1,2,0:T(8,128)(2,1)}, s32[4]{0:T...) while((s32[]{:T(128)}, ...), condition=%wide.region_47.48_spmd, body=%wide.region_44.47_spmd.sunk | while | flops 1364197888 | bytes 100719072 | solution.py:385
  1447.2 23.0 conditional.10
  1487.7 41.1 %reduce-scatter.19.cloned.1.call-done = bf16[1,512,256]{1,2,0:T(8,128)(2,1)} async-done(((bf16[1,2048,256]{1,2,0:T(8,128)(2,1)}), bf16[1,512,256]{1,2,0:T(8,128)(2,1)}) %reduce-scatter.19.cloned.1.call-update) | async-done | bytes 262160 | tf_op jit(solution)/shard_map/reduce_scatter | solution.py:391
  1529.9 105.5 %reduce-scatter.15.cloned.1.call-done = bf16[1,512,256]{1,2,0:T(8,128)(2,1)} async-done(((bf16[1,2048,256]{1,2,0:T(8,128)(2,1)}), bf16[1,512,256]{1,2,0:T(8,128)(2,1)}) %reduce-scatter.15.cloned.1.call-update) | async-done | bytes 262160 | tf_op jit(solution)/shard_map/reduce_scatter | solution.py:391
  1640.2 23.7 reduce-scatter.17.cloned.1.call-done
  1667.7 24.3 reduce-scatter.21.cloned.1.call-done
  1709.7 15.3 fusion.262
  1725.0 16.3 convolution_add_fusion
  1741.7 15.4 fusion.121
  1757.1 16.2 convolution_add_fusion.2
  1773.7 18.1 fusion.261
  1791.7 17.3 convolution_add_fusion.1
  1814.7 41.8 %all-reduce.8 = (f32[1024]{0:T(1024)S(1)}, f32[1024]{0:T(1024)S(1)}) all-reduce(f32[1024]{0:T(1024)S(1)} %add.461, f32[1024]{0:T(1024)S(1)} %add.466), channel_id=8, replica_groups=mesh['dp'=4,'ctx'=4,'mp'=2] {'dp','ctx'}, use_global_device_ids=true, to_apply=%region_70.71.clone | all-reduce | flops 2048 | bytes 16384
  1865.4 15.1 reduce-scatter.27.cloned.1.call-done
  1880.5 78.5 %reduce-scatter.25.cloned.1.call-done = f32[64,256]{1,0:T(8,128)} async-done(((f32[1024,256]{1,0:T(8,128)}), f32[64,256]{1,0:T(8,128)}) %reduce-scatter.25.cloned.1.call-update) | async-done | bytes 65552 | tf_op jit(solution)/shard_map/reduce_scatter | solution.py:454
  1959.0 83.5 %reduce-scatter.29.cloned.1.call-done = f32[64,512]{1,0:T(8,128)} async-done(((f32[1024,512]{1,0:T(8,128)}), f32[64,512]{1,0:T(8,128)}) %reduce-scatter.29.cloned.1.call-update) | async-done | bytes 131088 | tf_op jit(solution)/shard_map/reduce_scatter | solution.py:456
  2042.4 83.8 %reduce-scatter.23.cloned.1.call-done = f32[64,512]{1,0:T(8,128)} async-done(((f32[1024,512]{1,0:T(8,128)}), f32[64,512]{1,0:T(8,128)}) %reduce-scatter.23.cloned.1.call-update) | async-done | bytes 131088 | tf_op jit(solution)/shard_map/reduce_scatter | solution.py:453
  2126.2 349.6 %reduce-scatter.35.cloned.1.call-done = f32[16,64,256]{2,1,0:T(8,128)} async-done(((f32[16,1024,256]{2,1,0:T(8,128)}), f32[16,64,256]{2,1,0:T(8,128)}) %reduce-scatter.35.cloned.1.call-update) | async-done | bytes 1048592 | tf_op jit(solution)/shard_map/reduce_scatter | solution.py:461
  2475.8 351.9 %reduce-scatter.31.cloned.1.call-done = f32[16,64,256]{2,1,0:T(8,128)} async-done(((f32[16,1024,256]{2,1,0:T(8,128)}), f32[16,64,256]{2,1,0:T(8,128)}) %reduce-scatter.31.cloned.1.call-update) | async-done | bytes 1048592 | tf_op jit(solution)/shard_map/reduce_scatter | solution.py:459
  2827.7 351.7 %reduce-scatter.33.cloned.1.call-done = f32[16,64,256]{2,1,0:T(8,128)} async-done(((f32[16,1024,256]{2,1,0:T(8,128)}), f32[16,64,256]{2,1,0:T(8,128)}) %reduce-scatter.33.cloned.1.call-update) | async-done | bytes 1048592 | tf_op jit(solution)/shard_map/reduce_scatter | solution.py:460
  (597 shorter events, 374.4 us)
Async XLA Ops:
  7.2 91.9 %copy-start.10 = (bf16[2,1,512,1024]{3,2,1,0:T(8,128)(2,1)S(1)}, bf16[2,1,512,1024]{3,2,1,0:T(8,128)(2,1)}, u32[]{:S(2)}) copy-start(bf16[2,1,512,1024]{3,2,1,0:T(8,128)(2,1)} %param.29) | copy-start | bytes 6291460
  7.2 148.8 %all-gather.27.cloned.1.call-start = ((), (), s32[]{:S(2)}) async-start(), calls=%async_computation.30 | async-start | bytes 1310720 | tf_op jit(solution)/shard_map/all_gather | solution.py:132
  55.4 167.2 %copy-start.82 = (f32[1024]{0:T(1024)}, f32[1024]{0:T(1024)S(1)}, u32[]{:S(2)}) copy-start(f32[1024]{0:T(1024)S(1)} %convert_element_type.553) | copy-start | bytes 12292
  57.4 43.0 %copy-start.110 = (f32[512]{0:T(512)}, f32[512]{0:T(512)S(1)}, u32[]{:S(2)}) copy-start(f32[512]{0:T(512)S(1)} %get-tuple-element.634) | copy-start | bytes 6148
  57.4 44.2 %copy-start.112 = (f32[512]{0:T(512)}, f32[512]{0:T(512)S(1)}, u32[]{:S(2)}) copy-start(f32[512]{0:T(512)S(1)} %get-tuple-element.635) | copy-start | bytes 6148
  57.4 165.1 %copy-start.104 = (f32[512]{0:T(512)}, f32[512]{0:T(512)S(1)}, u32[]{:S(2)}) copy-start(f32[512]{0:T(512)S(1)} %fusion.222) | copy-start | bytes 6148
  100.3 59.8 %all-gather.29.cloned.1.call-start = ((), (), s32[]{:S(2)}) async-start(), calls=%async_computation.31 | async-start | bytes 1310720 | tf_op jit(solution)/shard_map/all_gather | solution.py:132
  100.4 120.0 %copy-start.90 = (f32[512]{0:T(512)}, f32[512]{0:T(512)S(1)}, u32[]{:S(2)}) copy-start(f32[512]{0:T(512)S(1)} %fusion.224) | copy-start | bytes 6148
  101.7 116.5 %all-gather.15.cloned.1.call-start = ((), (), s32[]{:S(2)}) async-start(), calls=%async_computation.13 | async-start | bytes 1114112 | tf_op jit(solution)/shard_map/all_gather | solution.py:94
  102.4 144.5 %all-gather.13.cloned.1.call-start = ((), (), s32[]{:S(2)}) async-start(), calls=%async_computation.12 | async-start | bytes 1310720 | tf_op jit(solution)/shard_map/all_gather | solution.py:131
  152.2 71.2 %copy-start.60 = (f32[512,32]{0,1:T(8,128)}, f32[512,32]{0,1:T(8,128)S(1)}, u32[]{:S(2)}) copy-start(f32[512,32]{0,1:T(8,128)S(1)} %get-tuple-element.808) | copy-start | bytes 196612
  154.4 122.0 %all-gather.25.cloned.1.call-start = ((), (), s32[]{:S(2)}) async-start(), calls=%async_computation.18 | async-start | bytes 1310720 | tf_op jit(solution)/shard_map/all_gather | solution.py:131
  155.1 178.8 %all-gather.17.cloned.1.call-start = ((), (), s32[]{:S(2)}) async-start(), calls=%async_computation.14 | async-start | bytes 1114112 | tf_op jit(solution)/shard_map/all_gather | solution.py:97
  155.7 284.6 %all-reduce.22.cloned.1.call-start = ((), (), s32[]{:S(2)}) async-start(), calls=%async_computation.35 | async-start | bytes 4194304 | tf_op jit(solution)/shard_map/psum | solution.py:186
  296.3 40.7 %copy-start.8 = (bf16[1,512,4,2,64]{1,4,3,2,0:T(8,128)(2,1)}, bf16[1,512,4,2,64]{1,4,3,2,0:T(8,128)(2,1)S(1)}, u32[]{:S(2)}) copy-start(bf16[1,512,4,2,64]{1,4,3,2,0:T(8,128)(2,1)S(1)} %get-tuple-element.1308) | copy-start | bytes 1572868
  296.3 40.7 %copy-start.70 = (s32[512]{0:T(512)}, s32[512]{0:T(512)S(1)}, u32[]{:S(2)}) copy-start(s32[512]{0:T(512)S(1)} %get-tuple-element.1376) | copy-start | bytes 6148
  296.3 143.4 %copy-start.64 = (f32[1,512,4,2]{1,3,2,0:T(2,128)}, f32[1,512,4,2]{1,3,2,0:T(2,128)S(1)}, u32[]{:S(2)}) copy-start(f32[1,512,4,2]{1,3,2,0:T(2,128)S(1)} %get-tuple-element.397) | copy-start | bytes 49156
  297.8 40.9 %copy-start.51 = (bf16[1,512,4,2,64]{1,4,3,2,0:T(8,128)(2,1)}, bf16[1,512,4,2,64]{1,4,3,2,0:T(8,128)(2,1)S(1)}, u32[]{:S(2)}) copy-start(bf16[1,512,4,2,64]{1,4,3,2,0:T(8,128)(2,1)S(1)} %fusion.172) | copy-start | bytes 1572868
  338.8 525.2 %all-gather.19.cloned.1.call-start = ((), (), s32[]{:S(2)}) async-start(), calls=%async_computation.15 | async-start | bytes 8912896 | tf_op jit(solution)/shard_map/all_gather | solution.py:100
  339.6 536.1 %all-gather.21.cloned.1.call-start = ((), (), s32[]{:S(2)}) async-start(), calls=%async_computation.16 | async-start | bytes 8912896 | tf_op jit(solution)/shard_map/all_gather | solution.py:101
  340.3 547.0 %all-gather.23.cloned.1.call-start = ((), (), s32[]{:S(2)}) async-start(), calls=%async_computation.17 | async-start | bytes 8912896 | tf_op jit(solution)/shard_map/all_gather | solution.py:102
  340.9 1050.6 %all-reduce.20.cloned.1.call-start = ((), (), s32[]{:S(2)}) async-start(), calls=%async_computation.34 | async-start | bytes 4194304 | tf_op jit(solution)/shard_map/psum | solution.py:288
  352.6 90.3 %copy-start.96 = (f32[1024]{0:T(1024)}, f32[1024]{0:T(1024)S(1)}, u32[]{:S(2)}) copy-start(f32[1024]{0:T(1024)S(1)} %convert_element_type.564) | copy-start | bytes 12292
  399.3 49.1 %copy-start.77 = (bf16[1024,16]{0,1:T(8,128)(2,1)}, bf16[1024,16]{0,1:T(8,128)(2,1)S(1)}, u32[]{:S(2)}) copy-start(bf16[1024,16]{0,1:T(8,128)(2,1)S(1)} %reshape.1926) | copy-start | bytes 98308
  462.7 126.2 %copy-start.23 = (bf16[512,1024]{1,0:T(8,128)(2,1)S(1)}, bf16[512,1024]{1,0:T(8,128)(2,1)}, u32[]{:S(2)}) copy-start(bf16[512,1024]{1,0:T(8,128)(2,1)} %copy-done.22) | copy-start | bytes 3145732
  589.0 68.2 %copy-start.17 = (f32[512,1024]{1,0:T(8,128)S(1)}, f32[512,1024]{1,0:T(8,128)}, u32[]{:S(2)}) copy-start(f32[512,1024]{1,0:T(8,128)} %get-tuple-element.769) | copy-start | bytes 6291460
  669.6 125.7 %copy-start.21 = (bf16[512,1024]{1,0:T(8,128)(2,1)S(1)}, bf16[512,1024]{1,0:T(8,128)(2,1)}, u32[]{:S(2)}) copy-start(bf16[512,1024]{1,0:T(8,128)(2,1)} %get-tuple-element.765) | copy-start | bytes 3145732
  904.1 106.7 %copy-start.15 = (bf16[16,320,256]{2,1,0:T(8,128)(2,1)}, bf16[16,320,256]{2,1,0:T(8,128)(2,1)S(1)}, u32[]{:S(2)}) copy-start(bf16[16,320,256]{2,1,0:T(8,128)(2,1)S(1)} %get-tuple-element.754) | copy-start | bytes 7864324
  1272.8 256.1 %reduce-scatter.19.cloned.1.call-start = ((), (), s32[]{:S(2)}) async-start(), calls=%async_computation.21 | async-start | bytes 1310720 | tf_op jit(solution)/shard_map/reduce_scatter | solution.py:391
  1299.5 77.4 %copy-start.18 = (f32[512,1024]{1,0:T(8,128)S(1)}, f32[512,1024]{1,0:T(8,128)}, u32[]{:S(2)}) copy-start(f32[512,1024]{1,0:T(8,128)} %get-tuple-element.769) | copy-start | bytes 6291460
  1299.5 77.4 %copy-start.50 = (f32[512,8]{1,0:T(8,128)S(1)}, f32[512,8]{1,0:T(8,128)}, u32[]{:S(2)}) copy-start(f32[512,8]{1,0:T(8,128)} %copy-done.49) | copy-start | bytes 49156
  1406.0 33.0 %copy-start.63 = (f32[1,512,4,2]{1,3,2,0:T(2,128)S(1)}, f32[1,512,4,2]{1,3,2,0:T(2,128)}, u32[]{:S(2)}) copy-start(f32[1,512,4,2]{1,3,2,0:T(2,128)} %copy-done.62) | copy-start | bytes 49156
  1439.0 196.4 %reduce-scatter.15.cloned.1.call-start = ((), (), s32[]{:S(2)}) async-start(), calls=%async_computation.19 | async-start | bytes 1310720 | tf_op jit(solution)/shard_map/reduce_scatter | solution.py:391
  1477.8 186.1 %reduce-scatter.17.cloned.1.call-start = ((), (), s32[]{:S(2)}) async-start(), calls=%async_computation.20 | async-start | bytes 1310720 | tf_op jit(solution)/shard_map/reduce_scatter | solution.py:394
  1478.3 213.6 %reduce-scatter.21.cloned.1.call-start = ((), (), s32[]{:S(2)}) async-start(), calls=%async_computation.22 | async-start | bytes 1310720 | tf_op jit(solution)/shard_map/reduce_scatter | solution.py:394
  1478.9 331.0 %reduce-scatter.37.cloned.1.call-start = ((), (), s32[]{:S(2)}) async-start(), calls=%async_computation.32 | async-start | bytes 557056
  1483.5 327.8 %all-reduce.18.cloned.1.call-start = ((), (), s32[]{:S(2)}) async-start(), calls=%async_computation.33 | async-start | bytes 8388608 | tf_op jit(solution)/shard_map/psum | solution.py:225
  1487.7 148.9 %copy-start.37 = (bf16[1024,256]{1,0:T(8,128)(2,1)S(1)}, bf16[1024,256]{1,0:T(8,128)(2,1)}, u32[]{:S(2)}) copy-start(bf16[1024,256]{1,0:T(8,128)(2,1)} %copy-done.36) | copy-start | bytes 1572868
  1695.2 185.3 %reduce-scatter.27.cloned.1.call-start = ((), (), s32[]{:S(2)}) async-start(), calls=%async_computation.25 | async-start | bytes 1114112 | tf_op jit(solution)/shard_map/reduce_scatter | solution.py:455
  1699.0 259.9 %reduce-scatter.25.cloned.1.call-start = ((), (), s32[]{:S(2)}) async-start(), calls=%async_computation.24 | async-start | bytes 1114112 | tf_op jit(solution)/shard_map/reduce_scatter | solution.py:454
  1701.4 341.0 %reduce-scatter.29.cloned.1.call-start = ((), (), s32[]{:S(2)}) async-start(), calls=%async_computation.26 | async-start | bytes 2228224 | tf_op jit(solution)/shard_map/reduce_scatter | solution.py:456
  1706.2 420.1 %reduce-scatter.23.cloned.1.call-start = ((), (), s32[]{:S(2)}) async-start(), calls=%async_computation.23 | async-start | bytes 2228224 | tf_op jit(solution)/shard_map/reduce_scatter | solution.py:453
  1709.4 766.4 %reduce-scatter.35.cloned.1.call-start = ((), (), s32[]{:S(2)}) async-start(), calls=%async_computation.29 | async-start | bytes 17825792 | tf_op jit(solution)/shard_map/reduce_scatter | solution.py:461
  1741.4 1086.3 %reduce-scatter.31.cloned.1.call-start = ((), (), s32[]{:S(2)}) async-start(), calls=%async_computation.27 | async-start | bytes 17825792 | tf_op jit(solution)/shard_map/reduce_scatter | solution.py:459
  1773.3 1406.1 %reduce-scatter.33.cloned.1.call-start = ((), (), s32[]{:S(2)}) async-start(), calls=%async_computation.28 | async-start | bytes 17825792 | tf_op jit(solution)/shard_map/reduce_scatter | solution.py:460
  1809.1 48.6 %copy-start.111 = (f32[512]{0:T(512)S(1)}, f32[512]{0:T(512)}, u32[]{:S(2)}) copy-start(f32[512]{0:T(512)} %copy-done.110) | copy-start | bytes 6148
  1809.1 48.6 %copy-start.113 = (f32[512]{0:T(512)S(1)}, f32[512]{0:T(512)}, u32[]{:S(2)}) copy-start(f32[512]{0:T(512)} %copy-done.112) | copy-start | bytes 6148
  1809.1 48.6 %copy-start.26 = (bf16[512,1024]{1,0:T(8,128)(2,1)S(1)}, bf16[512,1024]{1,0:T(8,128)(2,1)}, u32[]{:S(2)}) copy-start(bf16[512,1024]{1,0:T(8,128)(2,1)} %get-tuple-element.736) | copy-start | bytes 3145732
  (102 other events, 621.6 us)
Sparse Core Ops, SparseCore 0:
  100.5 30.0 all-gather.26
  132.7 27.3 all-gather.28
  162.9 55.1 all-gather.14
  220.1 26.7 all-gather.12
  248.9 27.4 all-gather.24
  279.0 54.8 all-gather.16
  338.9 27.3 all-reduce.21
  369.6 114.4 all-gather.18
  487.4 111.6 all-gather.20
  602.2 111.6 all-gather.22
  1272.9 17.6 all-reduce.19
  1439.1 89.7 reduce-scatter.18
  1531.8 103.4 reduce-scatter.14
  1638.1 25.7 reduce-scatter.16
  1666.2 25.7 reduce-scatter.20
  1694.1 75.6 reduce-scatter.36
  1772.6 25.0 all-reduce.17
  1800.4 80.0 reduce-scatter.26
  1883.4 75.4 reduce-scatter.24
  1961.7 80.7 reduce-scatter.28
  2045.3 80.8 reduce-scatter.22
  2129.1 346.6 reduce-scatter.34
  2478.7 348.9 reduce-scatter.30
  2830.4 348.9 reduce-scatter.32
where the time goes:
time: 3200 us; the launch traced here: 3190 us
  waiting for transfers between devices  1640 us (51%)
  local copies, waits for them, and re-layouts  816 us (26%)
  matrix products  361 us (11%)
  blocking collectives  226 us (7%)
  other arithmetic  103 us (3%)
    gather x12, local copies, waits for them, and re-layouts, pick_rows(): return jax.vmap(lambda source, choose: source[choose])(table, picks)  697 us
    reduce_scatter x1, waiting for transfers between devices, per_device(): lax.psum_scatter(expert_total[0], ('dp', 'ctx'), scatter_dimension=1, til...  352 us
    reduce_scatter x1, waiting for transfers between devices, per_device(): lax.psum_scatter(expert_total[1], ('dp', 'ctx'), scatter_dimension=1, til...  352 us
    reduce_scatter x1, waiting for transfers between devices, per_device(): lax.psum_scatter(expert_total[2], ('dp', 'ctx'), scatter_dimension=1, til...  350 us
    reduce_scatter x2, waiting for transfers between devices, per_device(): lax.psum_scatter(key_terms.astype(jnp.bfloat16), 'ctx', scatter_dimension...  147 us
    unnamed x2, blocking collectives  86.1 us
    reduce_scatter x1, waiting for transfers between devices, per_device(): lax.psum_scatter(attn_total[3], ('dp', 'ctx'), scatter_dimension=0, tiled...  83.8 us
    reduce_scatter x1, waiting for transfers between devices, per_device(): lax.psum_scatter(attn_total[6], ('dp', 'ctx'), scatter_dimension=0, tiled...  83.5 us
  transfers between devices with their start and end apart: 24, of which 16 were waited for; matrix products, arithmetic and copies ran while one was open for 26% of the time, Pallas kernels for 0%

commit v1 on v0

v1 whole, which is shorter than its diff:
```python
import functools
import math

import jax
import jax.numpy as jnp
from jax import lax
from jax.experimental import pallas as pl
from jax.experimental.pallas import tpu as pltpu
from jax.sharding import PartitionSpec as P

HD = 64
EPS = 1e-06
THETA = 10000.0
NEG = -1e30
VMEM_LIMIT = 60 * 1024 * 1024
BF = jnp.bfloat16
F32 = jnp.float32


def dot(a, b, ca, cb, precision=None):
    return lax.dot_general(
        a, b, (((ca,), (cb,)), ((), ())), preferred_element_type=F32, precision=precision
    )


def params(*semantics):
    return pltpu.CompilerParams(dimension_semantics=semantics, vmem_limit_bytes=VMEM_LIMIT)


def turn(values, cosine, sine):
    width = values.shape[1]
    lane = lax.broadcasted_iota(jnp.int32, values.shape, 1)
    ahead = pltpu.roll(values, width - HD // 2, 1)
    behind = pltpu.roll(values, HD // 2, 1)
    swapped = jnp.where(lane % HD < HD // 2, ahead, behind)
    reps = width // cosine.shape[1]
    return values * jnp.tile(cosine, (1, reps)) + swapped * jnp.tile(sine, (1, reps))


def qkv_kernel(x_ref, gain_ref, w_ref, cos_ref, sin_ref, normed_ref, q_ref, kv_ref):
    x = x_ref[...].astype(F32)
    inv = lax.rsqrt(jnp.mean(x * x, axis=1, keepdims=True) + EPS)
    normed = (x * inv * gain_ref[...]).astype(BF)
    normed_ref[...] = normed
    qw = q_ref.shape[1]
    kw = kv_ref.shape[1] // 2
    raw = dot(normed, w_ref[...], 1, 0)
    cosine = cos_ref[...]
    sine = sin_ref[...]
    q_ref[...] = turn(raw[:, :qw], cosine, sine).astype(BF)
    kv_ref[:, :kw] = turn(raw[:, qw : qw + kw], cosine, sine).astype(BF)
    kv_ref[:, kw:] = raw[:, qw + kw :].astype(BF)


def qkv_call(x, gain, w, cosine, sine, qw, kw):
    rows, d = x.shape
    local = cosine.shape[0]
    tile = min(256, local)
    per = local // tile
    return pl.pallas_call(
        qkv_kernel,
        grid=(rows // tile,),
        in_specs=[
            pl.BlockSpec((tile, d), lambda i: (i, 0)),
            pl.BlockSpec((1, d), lambda i: (0, 0)),
            pl.BlockSpec(w.shape, lambda i: (0, 0)),
            pl.BlockSpec((tile, 128), lambda i: (i % per, 0)),
            pl.BlockSpec((tile, 128), lambda i: (i % per, 0)),
        ],
        out_specs=[
            pl.BlockSpec((tile, d), lambda i: (i, 0)),
            pl.BlockSpec((tile, qw), lambda i: (i, 0)),
            pl.BlockSpec((tile, 2 * kw), lambda i: (i, 0)),
        ],
        out_shape=[
            jax.ShapeDtypeStruct((rows, d), BF),
            jax.ShapeDtypeStruct((rows, qw), BF),
            jax.ShapeDtypeStruct((rows, 2 * kw), BF),
        ],
        compiler_params=params("arbitrary"),
        cost_estimate=pl.CostEstimate(
            flops=2 * rows * d * w.shape[1], bytes_accessed=6 * rows * d, transcendentals=rows
        ),
        name="qkv",
    )(x, gain, w, cosine, sine)


def half_mask(block, which):
    lane = lax.broadcasted_iota(jnp.int32, block.shape, 1)
    keep = (lane < HD) if which == 0 else (lane >= HD)
    return jnp.where(keep, block, jnp.zeros_like(block))


def attn_fwd_kernel(ctx_ref, q_ref, k_ref, v_ref, o_ref, lse_ref):
    length = q_ref.shape[1]
    both = jnp.concatenate([q_ref[0, :, :128], q_ref[0, :, 128:]], axis=0)
    both = (both.astype(F32) * HD**-0.5).astype(BF)
    c = ctx_ref[0]
    cols = 2 * length

    def visit(j, state, diagonal):
        start = pl.multiple_of(j * length, length)
        k = k_ref[0, pl.ds(start, length), :]
        v = v_ref[0, pl.ds(start, length), :]
        new = []
        for i in range(2):
            peak, total, acc = state[i]
            s = dot(half_mask(k, i), both, 1, 1)
            if diagonal:
                key = lax.broadcasted_iota(jnp.int32, s.shape, 0)
                query = lax.broadcasted_iota(jnp.int32, s.shape, 1) % length
                s = jnp.where(key <= query, s, NEG)
            now = jnp.maximum(peak, jnp.max(s, axis=0, keepdims=True))
            p = jnp.exp(s - now)
            factor = jnp.exp(peak - now)
            total = total * factor + jnp.sum(p, axis=0, keepdims=True)
            acc = acc * factor + dot(v, p.astype(BF), 0, 0)
            new.append((now, total, acc))
        return tuple(new)

    one = (
        jnp.full((1, cols), NEG, F32),
        jnp.zeros((1, cols), F32),
        jnp.zeros((128, cols), F32),
    )
    state = lax.fori_loop(0, c, lambda j, st: visit(j, st, False), (one, one))
    state = visit(c, state, True)
    row = lax.broadcasted_iota(jnp.int32, (128, cols), 0)
    (m0, l0, a0), (m1, l1, a1) = state
    out = jnp.where(row < HD, a0 / l0, a1 / l1).T
    o_ref[0, :, :128] = out[:length].astype(BF)
    o_ref[0, :, 128:] = out[length:].astype(BF)
    lse_ref[0, 0] = jnp.concatenate([m0 + jnp.log(l0), m1 + jnp.log(l1)], axis=0)


def attn_fwd(ctx, q, kv):
    seqs, length, qw = q.shape
    total = kv.shape[1]
    pairs = qw // 256
    kb = kv.shape[2] // 256
    return pl.pallas_call(
        attn_fwd_kernel,
        grid=(seqs, pairs),
        in_specs=[
            pl.BlockSpec(memory_space=pltpu.SMEM),
            pl.BlockSpec((1, length, 256), lambda s, p: (s, 0, p)),
            pl.BlockSpec((1, total, 128), lambda s, p: (s, 0, p)),
            pl.BlockSpec((1, total, 128), lambda s, p: (s, 0, kb + p)),
        ],
        out_specs=[
            pl.BlockSpec((1, length, 256), lambda s, p: (s, 0, p)),
            pl.BlockSpec((1, 1, 2, 2 * length), lambda s, p: (s, p, 0, 0)),
        ],
        out_shape=[
            jax.ShapeDtypeStruct((seqs, length, qw), BF),
            jax.ShapeDtypeStruct((seqs, pairs, 2, 2 * length), F32),
        ],
        compiler_params=params("arbitrary", "arbitrary"),
        cost_estimate=pl.CostEstimate(
            flops=16 * seqs * length * total * qw,
            bytes_accessed=4 * seqs * total * qw,
            transcendentals=seqs * length * total * qw // 64,
        ),
        name="attn_fwd",
    )(ctx, q, kv, kv)


def attn_bwd_kernel(
    ctx_ref, q_ref, k_ref, v_ref, do_ref, o_ref, lse_ref, cos_ref, sin_ref, dq_ref, dk_ref, dv_ref
):
    length = q_ref.shape[1]
    total = k_ref.shape[1]

    def stacked(ref):
        return jnp.concatenate([ref[0, :, :128], ref[0, :, 128:]], axis=0)

    both = (stacked(q_ref).astype(F32) * HD**-0.5).astype(BF)
    dboth = stacked(do_ref)
    prod = dboth.astype(F32) * stacked(o_ref).astype(F32)
    pick_row = lax.broadcasted_iota(jnp.int32, (8, 128), 0)
    pick_lane = lax.broadcasted_iota(jnp.int32, (8, 128), 1) // HD
    picks = (pick_row == pick_lane).astype(F32)
    delta = dot(picks, prod, 1, 1, lax.Precision.HIGHEST)
    c = ctx_ref[0]
    cols = 2 * length

    def visit(j, dq, diagonal):
        start = pl.multiple_of(j * length, length)
        k = k_ref[0, pl.ds(start, length), :]
        v = v_ref[0, pl.ds(start, length), :]
        parts = []
        for i in range(2):
            ki = half_mask(k, i)
            s = dot(ki, both, 1, 1)
            p = jnp.exp(s - lse_ref[0, 0, i : i + 1, :])
            if diagonal:
                key = lax.broadcasted_iota(jnp.int32, s.shape, 0)
                query = lax.broadcasted_iota(jnp.int32, s.shape, 1) % length
                p = jnp.where(key <= query, p, 0.0)
            dp = dot(half_mask(v, i), dboth, 1, 1)
            ds = (p * (dp - delta[i : i + 1, :])).astype(BF)
            parts.append((dot(ds, both, 1, 0), dot(p.astype(BF), dboth, 1, 0)))
            dq = dq + dot(ki, ds, 0, 0)
        low = lax.broadcasted_iota(jnp.int32, (length, 128), 1) < HD
        dk_ref[0, pl.ds(start, length), :] = jnp.where(low, parts[0][0], parts[1][0]).astype(BF)
        dv_ref[0, pl.ds(start, length), :] = jnp.where(low, parts[0][1], parts[1][1]).astype(BF)
        return dq

    dq = lax.fori_loop(0, c, lambda j, st: visit(j, st, False), jnp.zeros((128, cols), F32))
    dq = visit(c, dq, True)

    def clear(j, carry):
        start = pl.multiple_of(j * length, length)
        dk_ref[0, pl.ds(start, length), :] = jnp.zeros((length, 128), BF)
        dv_ref[0, pl.ds(start, length), :] = jnp.zeros((length, 128), BF)
        return carry

    lax.fori_loop(c + 1, total // length, clear, 0)
    out = dq.T * HD**-0.5
    cosine = cos_ref[...]
    sine = -sin_ref[...]
    dq_ref[0, :, :128] = turn(out[:length], cosine, sine).astype(BF)
    dq_ref[0, :, 128:] = turn(out[length:], cosine, sine).astype(BF)


def attn_bwd(ctx, q, kv, do, o, lse, cosine, sine):
    seqs, length, qw = q.shape
    total = kv.shape[1]
    pairs = qw // 256
    kb = kv.shape[2] // 256
    blk = pl.BlockSpec((1, length, 256), lambda s, p: (s, 0, p))
    kblk = pl.BlockSpec((1, total, 128), lambda s, p: (s, 0, p))
    vblk = pl.BlockSpec((1, total, 128), lambda s, p: (s, 0, kb + p))
    tab = pl.BlockSpec((length, 128), lambda s, p: (0, 0))
    return pl.pallas_call(
        attn_bwd_kernel,
        grid=(seqs, pairs),
        in_specs=[
            pl.BlockSpec(memory_space=pltpu.SMEM),
            blk,
            kblk,
            vblk,
            blk,
            blk,
            pl.BlockSpec((1, 1, 2, 2 * length), lambda s, p: (s, p, 0, 0)),
            tab,
            tab,
        ],
        out_specs=[blk, kblk, kblk],
        out_shape=[
            jax.ShapeDtypeStruct((seqs, length, qw), BF),
            jax.ShapeDtypeStruct((seqs, total, kv.shape[2] // 2), BF),
            jax.ShapeDtypeStruct((seqs, total, kv.shape[2] // 2), BF),
        ],
        compiler_params=params("arbitrary", "arbitrary"),
        cost_estimate=pl.CostEstimate(
            flops=40 * seqs * length * total * qw,
            bytes_accessed=8 * seqs * total * qw,
            transcendentals=seqs * length * total * qw // 64,
        ),
        name="attn_bwd",
    )(ctx, q, kv, kv, do, o, lse, cosine, sine)


def masked_softmax(logits, named):
    peak = jnp.max(jnp.where(named, logits, NEG), axis=1, keepdims=True)
    grown = jnp.where(named, jnp.exp(jnp.where(named, logits - peak, 0.0)), 0.0)
    return grown / jnp.sum(grown, axis=1, keepdims=True)


def experts_kernel(
    x_ref, dy_ref, bits_ref, router_ref, w_ref, out_ref, dx_ref, dgate_ref, dw_ref, acc_ref
):
    step = pl.program_id(0)
    count = w_ref.shape[1]
    x = x_ref[...]
    dy = dy_ref[...]
    rows = x.shape[0]
    lane = lax.broadcasted_iota(jnp.int32, (rows, 128), 1)
    named = ((bits_ref[...] >> jnp.minimum(lane, 31)) & 1) == 1
    gates = masked_softmax(dot(x, router_ref[...], 1, 0), named)
    xt = x.T
    dyt = dy.T

    @pl.when(step == 0)
    def _():
        acc_ref[...] = jnp.zeros_like(acc_ref)

    dgates = jnp.zeros((rows, 128), F32)
    out = None
    dx = None
    for e in range(count):
        gate = gates[:, e : e + 1]
        wg = w_ref[0, e]
        wu = w_ref[1, e]
        wd = w_ref[2, e]
        g = dot(x, wg, 1, 0)
        u = dot(x, wu, 1, 0)
        z = dot(dy, wd, 1, 0)
        sig = 1.0 / (1.0 + jnp.exp(-g))
        silu = g * sig
        act = silu * u
        dgates = jnp.where(
            lane == e, jnp.sum(act.astype(BF).astype(F32) * z, axis=1, keepdims=True), dgates
        )
        gact = (gate * act).astype(BF)
        da = gate * z
        du = (da * silu).astype(BF)
        dg = (da * u * (sig * (1.0 + g * (1.0 - sig)))).astype(BF)
        o_part = dot(gact, wd, 1, 1)
        d_part = dot(dg, wg, 1, 1) + dot(du, wu, 1, 1)
        out = o_part if out is None else out + o_part
        dx = d_part if dx is None else dx + d_part
        acc_ref[0, e] += dot(xt, dg, 1, 0)
        acc_ref[1, e] += dot(xt, du, 1, 0)
        acc_ref[2, e] += dot(dyt, gact, 1, 0)
    out_ref[...] = out.astype(BF)
    dx_ref[...] = dx.astype(BF)
    dgate_ref[...] = dgates.T[:8]

    @pl.when(step == pl.num_programs(0) - 1)
    def _():
        dw_ref[...] = acc_ref[...].astype(BF)


def experts_call(x, dy, bits, router, w):
    rows, d = x.shape
    tile = min(512, rows)
    row = pl.BlockSpec((tile, d), lambda i: (i, 0))
    return pl.pallas_call(
        experts_kernel,
        grid=(rows // tile,),
        in_specs=[
            row,
            row,
            pl.BlockSpec((tile, 1), lambda i: (i, 0)),
            pl.BlockSpec((d, 128), lambda i: (0, 0)),
            pl.BlockSpec(memory_space=pltpu.VMEM),
        ],
        out_specs=[
            row,
            row,
            pl.BlockSpec((8, tile), lambda i: (0, i)),
            pl.BlockSpec(memory_space=pltpu.VMEM),
        ],
        out_shape=[
            jax.ShapeDtypeStruct((rows, d), BF),
            jax.ShapeDtypeStruct((rows, d), BF),
            jax.ShapeDtypeStruct((8, rows), F32),
            jax.ShapeDtypeStruct(w.shape, BF),
        ],
        scratch_shapes=[pltpu.VMEM(w.shape, F32)],
        compiler_params=params("arbitrary"),
        cost_estimate=pl.CostEstimate(
            flops=6 * rows * w.size, bytes_accessed=8 * rows * d + 4 * w.size, transcendentals=rows * d
        ),
        name="experts",
    )(x, dy, bits, router, w)


def apart(count, step):
    return [(i, i ^ step) for i in range(count)]


def swap(value):
    return lax.ppermute(value, "mp", [(0, 1), (1, 0)])


def head_order(weight):
    rows, width = weight.shape
    return (
        weight.reshape(rows, width // (4 * HD), 2, 2, HD).swapaxes(2, 3).reshape(rows, width)
    )


def per_device(
    tokens,
    cotangent,
    routes,
    norm_gain,
    w_query,
    w_key,
    w_value,
    w_output,
    ffn_gain,
    w_router,
    w_gate,
    w_up,
    w_down,
):
    micro, seq_count, local, width = tokens.shape
    top = routes.shape[3]
    experts = w_gate.shape[0]
    hidden_units = w_gate.shape[2]
    shard = w_gate.shape[1]
    dp = lax.axis_size("dp")
    ctx_size = lax.axis_size("ctx")
    me_dp = lax.axis_index("dp")
    me_ctx = lax.axis_index("ctx")
    me_mp = lax.axis_index("mp")
    mine_count = experts // dp
    seqs = micro * seq_count
    rows = seqs * local
    half = rows // 2
    qw = w_query.shape[1]
    kw = w_key.shape[1]
    ctx_now = me_ctx.astype(jnp.int32).reshape(1)

    def gather_tokens(halves):
        mine = lax.dynamic_index_in_dim(halves, me_mp, 0, keepdims=False)
        other = lax.dynamic_index_in_dim(halves, 1 - me_mp, 0, keepdims=False)
        far = jnp.stack([lax.ppermute(mine, "dp", apart(dp, s)) for s in range(1, dp)])
        near = swap(far)
        return jnp.concatenate([mine[None], far, other[None], near], axis=0)

    def return_tokens(part):
        cut = part.reshape((2, dp, half) + part.shape[1:])
        summed = (cut[0].astype(F32) + swap(cut[1]).astype(F32)).astype(BF)
        total = summed[0].astype(F32)
        for s in range(1, dp):
            total = total + lax.ppermute(summed[s], "dp", apart(dp, s)).astype(F32)
        total = total.astype(BF)
        return in_order(total, swap(total)).reshape((rows,) + part.shape[1:]).astype(F32)

    def in_order(mine, other):
        first = me_mp == 0
        return jnp.stack([jnp.where(first, mine, other), jnp.where(first, other, mine)])

    small = jnp.concatenate([w_router, norm_gain[:, None], ffn_gain[:, None]], axis=1)
    small = jnp.pad(small, ((0, 0), (0, 128 - small.shape[1])))
    packed = jnp.concatenate([head_order(w_query), w_key, w_value, head_order(w_output), small], axis=1)
    full = lax.all_gather(packed, ("dp", "ctx"), axis=0, tiled=True)
    w_qkv = full[:, : qw + 2 * kw]
    w_out = full[:, qw + 2 * kw : 2 * qw + 2 * kw]
    small = full[:, 2 * qw + 2 * kw :]
    router = small[:, :experts]
    gain_one = small[:, experts].astype(F32)[None, :]
    gain_two = small[:, experts + 1].astype(F32)[None, :]

    w3 = jnp.stack([w_gate, w_up, w_down])
    w3 = lax.all_to_all(w3, "dp", split_axis=1, concat_axis=2, tiled=True)
    w3 = lax.all_gather(w3, "ctx", axis=0, tiled=False)
    w3 = (
        w3.reshape(ctx_size, 3, mine_count, dp, shard, hidden_units)
        .transpose(1, 2, 3, 0, 4, 5)
        .reshape(3, mine_count, width, hidden_units)
    )

    ids = routes.reshape(rows, top)
    bits = jnp.sum(jnp.left_shift(1, ids), axis=1)
    bits_all = gather_tokens(bits.reshape(2, half // math.gcd(half, 128), -1))
    bits_all = bits_all.reshape(2 * dp * half, 1)
    turned = me_dp * mine_count
    bits_all = (bits_all >> turned) | ((bits_all << (experts - turned)) & ((1 << experts) - 1))
    router_turned = jnp.pad(
        jnp.roll(router, -turned, axis=1), ((0, 0), (0, 128 - experts))
    )
    dy = cotangent.reshape(rows, width)
    dy_all = gather_tokens(dy.reshape(2, half, width)).reshape(2 * dp * half, width)

    position = me_ctx * local + jnp.arange(local, dtype=jnp.int32)
    freqs = THETA ** (-(jnp.arange(HD // 2, dtype=F32) * 2.0) / HD)
    angles = position.astype(F32)[:, None] * freqs[None, :]
    cosine = jnp.tile(jnp.cos(angles), (1, 4))
    sine = jnp.sin(angles)
    sine = jnp.concatenate([-sine, sine, -sine, sine], axis=1)
    x = tokens.reshape(rows, width)
    normed, q, kv = qkv_call(x, gain_one, w_qkv, cosine, sine, qw, kw)
    q = q.reshape(seqs, local, qw)
    kv_all = lax.all_gather(kv.reshape(seqs, local, 2 * kw), "ctx", axis=1, tiled=True)
    attn, lse = attn_fwd(ctx_now, q, kv_all)
    attn_rows = attn.reshape(rows, qw)
    mixed_part = dot(attn_rows, w_out, 1, 1).astype(BF)
    x32 = x.astype(F32)
    hidden = x32 + (mixed_part.astype(F32) + swap(mixed_part).astype(F32))
    inv_two = lax.rsqrt(jnp.mean(hidden * hidden, axis=1, keepdims=True) + EPS)
    ffn_low = (hidden * inv_two * gain_two).astype(BF)

    x_all = gather_tokens(ffn_low.reshape(2, half, width)).reshape(2 * dp * half, width)
    out_part, dx_part, dgate, dw = experts_call(x_all, dy_all, bits_all, router_turned, w3)
    output = (hidden + return_tokens(out_part)).astype(BF)

    dw = (
        dw.reshape(3, mine_count, dp, ctx_size, shard, hidden_units)
        .transpose(3, 0, 1, 2, 4, 5)
        .reshape(ctx_size, 3, mine_count, dp * shard, hidden_units)
    )
    dw = lax.psum_scatter(dw, "ctx", scatter_dimension=0, tiled=False)
    dw = lax.all_to_all(dw, "dp", split_axis=2, concat_axis=1, tiled=True).astype(F32)

    moe_dx = return_tokens(dx_part)
    cut = dgate.reshape(8, 2, dp, half)[:mine_count]
    cut = cut[:, 0] + swap(cut[:, 1])
    back = [cut[:, 0]] + [lax.ppermute(cut[:, s], "dp", apart(dp, s)) for s in range(1, dp)]
    order = []
    for k in range(dp):
        order.append(
            functools.reduce(
                jnp.add, [jnp.where((me_dp ^ s) == k, back[s], 0.0) for s in range(dp)]
            )
        )
    dgate_mine = jnp.concatenate(order, axis=0)
    dgate_rows = in_order(dgate_mine, swap(dgate_mine)).transpose(0, 2, 1).reshape(rows, experts)
    named = ((bits[:, None] >> jnp.arange(experts, dtype=jnp.int32)[None, :]) & 1) == 1
    gates = masked_softmax(dot(ffn_low, router, 1, 0), named)
    dlogit = gates * (dgate_rows - jnp.sum(gates * dgate_rows, axis=1, keepdims=True))
    grad_router = dot(ffn_low, dlogit.astype(BF), 0, 0)
    d_ffn = moe_dx + dot(dlogit.astype(BF), router, 1, 1)
    n_two = hidden * inv_two
    grad_gain_two = jnp.sum(d_ffn * n_two, axis=0)
    g_two = d_ffn * gain_two
    dh = dy.astype(F32) + inv_two * (
        g_two - n_two * jnp.mean(g_two * n_two, axis=1, keepdims=True)
    )
    dz = dh.astype(BF)

    d_attn = dot(dz, w_out, 1, 0).astype(BF)
    grad_out = dot(dz, attn_rows, 0, 0).astype(BF)
    dq, dk, dv = attn_bwd(
        ctx_now, q, kv_all, d_attn.reshape(seqs, local, qw), attn, lse, cosine, sine
    )
    dkv = lax.psum_scatter(
        jnp.concatenate([dk, dv], axis=2), "ctx", scatter_dimension=1, tiled=True
    ).reshape(rows, 2 * kw)
    dk = dkv[:, :kw].astype(F32).reshape(seqs, local, kw // HD, 2, HD // 2)
    cos_h = jnp.cos(angles)[None, :, None, :]
    sin_h = jnp.sin(angles)[None, :, None, :]
    dk = jnp.concatenate(
        [
            dk[:, :, :, 0] * cos_h + dk[:, :, :, 1] * sin_h,
            dk[:, :, :, 1] * cos_h - dk[:, :, :, 0] * sin_h,
        ],
        axis=-1,
    )
    dk = dk.astype(BF).reshape(rows, kw)
    dqkv = jnp.concatenate([dq.reshape(rows, qw), dk, dkv[:, kw:]], axis=1)
    grad_qkv = dot(normed, dqkv, 0, 0).astype(BF)
    dn_part = dot(dqkv, w_qkv, 1, 1).astype(BF)
    d_normed = dn_part.astype(F32) + swap(dn_part).astype(F32)
    inv_one = lax.rsqrt(jnp.mean(x32 * x32, axis=1, keepdims=True) + EPS)
    n_one = x32 * inv_one
    grad_gain_one = jnp.sum(d_normed * n_one, axis=0)
    g_one = d_normed * gain_one
    input_grad = (
        dh + inv_one * (g_one - n_one * jnp.mean(g_one * n_one, axis=1, keepdims=True))
    ).astype(BF)

    small_grad = jnp.concatenate(
        [grad_router, grad_gain_one[:, None], grad_gain_two[:, None]], axis=1
    ).astype(BF)
    small_grad = jnp.pad(small_grad, ((0, 0), (0, 128 - small_grad.shape[1])))
    sent = jnp.concatenate([grad_qkv, grad_out, small_grad], axis=1)
    owned = lax.psum_scatter(sent, ("dp", "ctx"), scatter_dimension=0, tiled=True).astype(F32)
    small_grad = owned[:, 2 * qw + 2 * kw :]
    shape = tokens.shape
    return (
        output.reshape(shape),
        input_grad.reshape(shape),
        small_grad[:, experts],
        head_order(owned[:, :qw]),
        owned[:, qw : qw + kw],
        owned[:, qw + kw : qw + 2 * kw],
        head_order(owned[:, qw + 2 * kw : 2 * qw + 2 * kw]),
        small_grad[:, experts + 1],
        small_grad[:, :experts],
        dw[0],
        dw[1],
        dw[2],
    )


def solution(mesh):
    rows = P(None, "dp", "ctx", None)
    vector = P(("dp", "ctx"))
    matrix = P(("dp", "ctx"), "mp")
    router = P(("dp", "ctx"), None)
    expert = P(None, ("dp", "ctx"), "mp")
    return jax.shard_map(
        per_device,
        mesh=mesh,
        in_specs=(
            rows,
            rows,
            rows,
            vector,
            matrix,
            matrix,
            matrix,
            matrix,
            vector,
            router,
            expert,
            expert,
            expert,
        ),
        out_specs=(
            rows,
            rows,
            vector,
            matrix,
            matrix,
            matrix,
            matrix,
            vector,
            router,
            expert,
            expert,
            expert,
        ),
        check_vma=False,
    )
```

time: 3200 us -> 960 us (0.30)
  waiting for transfers between devices: 1640 us -> 563 us
  local copies, waits for them, and re-layouts: 816 us -> 97.4 us
  matrix products: 361 us -> 18.9 us
  blocking collectives: 226 us -> 54.6 us
  Pallas kernels: 0 us -> 136 us
  other arithmetic: 103 us -> 44.7 us
    reduce_scatter x11 -> x2, waiting for transfers between devices: 1510 us -> 209 us  [the longest x1 121 us: per_device(): lax.psum_scatter(jnp.concatenate([dk, dv], axis=2), 'ctx', scatter_dimens...]
    gather x12 -> x0, local copies, waits for them, and re-layouts: 697 us -> none  [pick_rows(): return jax.vmap(lambda source, choose: source[choose])(table, picks)]
    dot_general x62 -> x8, matrix products: 361 us -> 18.9 us  [dot(): lax.dot_general(a, b, (((ca,), (cb,)), ((), ())), preferred_element_type=...]
    ppermute x0 -> x29, waiting for transfers between devices: none -> 179 us  [the longest x9 91.6 us: gather_tokens(): lax.ppermute(mine, 'dp', apart(dp, s))]
    all_gather x3 -> x0, blocking collectives: 137 us -> none  [the longest x1 48.6 us: per_device(): lax.all_gather(w_key, ('dp', 'ctx'), axis=0, tiled=True)]
    pallas_call x0 -> x4, Pallas kernels: none -> 136 us  [the longest x1 102 us: experts_call(): pl.pallas_call(experts_kernel, grid=(rows // tile,), in_specs=[row, row,...]
    unnamed x2 -> x0, blocking collectives: 86.1 us -> none
    all_to_all x0 -> x2, blocking collectives: none -> 54.6 us  [the longest x1 33.2 us: per_device(): lax.all_to_all(dw, 'dp', split_axis=2, concat_axis=1, tiled=True)]
  transfers between devices with their start and end apart: 24 -> 35, of which waited for: 16 -> 19; matrix products, arithmetic and copies ran while one was open for 26% -> 11% of each run, Pallas kernels for 0% -> 1%
where the time goes in v1:
time: 960 us; the launch traced here: 955 us
  waiting for transfers between devices  563 us (59%)
  Pallas kernels  136 us (14%)
  local copies, waits for them, and re-layouts  97.4 us (10%)
  blocking collectives  54.6 us (6%)
  other arithmetic  44.7 us (5%)
  starting transfers between devices  24.8 us (3%)
  matrix products  18.9 us (2%)
  between operations  15.2 us (2%)
    reduce_scatter x1, waiting for transfers between devices, per_device(): lax.psum_scatter(jnp.concatenate([dk, dv], axis=2), 'ctx', scatter_dimens...  121 us
    pallas_call x1, Pallas kernels, experts_call(): pl.pallas_call(experts_kernel, grid=(rows // tile,), in_specs=[row, row,...  102 us
    ppermute x9, waiting for transfers between devices, gather_tokens(): lax.ppermute(mine, 'dp', apart(dp, s))  91.6 us
    reduce_scatter x1, waiting for transfers between devices, per_device(): dw = lax.psum_scatter(dw, 'ctx', scatter_dimension=0, tiled=False)  87.8 us
    ppermute x6, waiting for transfers between devices, return_tokens(): total = total + lax.ppermute(summed[s], 'dp', apart(dp, s)).astype(F32)  79.6 us
    all_gather x1, waiting for transfers between devices, per_device(): full = lax.all_gather(packed, ('dp', 'ctx'), axis=0, tiled=True)  70.1 us
    all_gather x1, waiting for transfers between devices, per_device(): lax.all_gather(kv.reshape(seqs, local, 2 * kw), 'ctx', axis=1, tiled=True)  56.2 us
    unnamed x7, waiting for transfers between devices  48.7 us
  transfers between devices with their start and end apart: 35, of which 19 were waited for; matrix products, arithmetic and copies ran while one was open for 11% of the time, Pallas kernels for 1%

profile of v1, /device:TPU:0, one launch (start us, length us, event | category | flops | bytes accessed | tf_op | source)
XLA Modules:
  0.0 954.9 jit_solution(14099389497708645670)
XLA Ops:
  15.8 70.1 %all-gather.4.cloned.1.call-done = bf16[1024,1664]{1,0:T(8,128)(2,1)} async-done(((bf16[64,1664]{1,0:T(8,128)(2,1)}), bf16[1024,1664]{1,0:T(8,128)(2,1)}) %all-gather.4.cloned.1.call-update) | async-done | bytes 3407888 | tf_op jit(solution)/shard_map/all_gather | solution.py:432
  87.9 3.1 slice.174.w_ref
  91.0 7.2 qkv.1
  98.5 21.3 %all_to_all.24 = bf16[3,16,64,256]{3,2,0,1:T(8,128)(2,1)S(1)} all-to-all(bf16[3,16,64,256]{3,2,0,1:T(8,128)(2,1)S(1)} %pad_maximum_fusion.7), channel_id=1, replica_groups=mesh['dp'=4,'ctx'=4,'mp'=2] {'dp'}, dimensions={1} | all-to-all | bytes 3145728 | tf_op jit(solution)/shard_map/all_to_all | solution.py:441
  121.4 56.2 %all-gather.6.cloned.1.call-done.k_ref.v_ref = bf16[2,2048,512]{2,1,0:T(8,128)(2,1)} async-done(((bf16[2,512,512]{2,1,0:T(8,128)(2,1)}), bf16[2,2048,512]{2,1,0:T(8,128)(2,1)}) %all-gather.6.cloned.1.call-update) | async-done | bytes 4194320 | tf_op jit(solution)/shard_map/all_gather | solution.py:470
  177.7 8.7 attn_fwd.1
  186.3 4.5 convolution_convert_fusion.2
  191.0 2.5 collective-permute-start.7
  194.5 23.4 %collective-permute-done.7 = bf16[512,1024]{1,0:T(8,128)(2,1)S(1)} collective-permute-done((bf16[512,1024]{1,0:T(8,128)(2,1)S(1)}, bf16[512,1024]{1,0:T(8,128)(2,1)S(1)}, u32[]{:S(2)}, u32[]{:S(2)}) %collective-permute-start.7) | collective-permute-done | bytes 1048608 | tf_op jit(solution)/shard_map/ppermute | solution.py:412
  217.9 22.0 %collective-permute-done.6 = bf16[512,1024]{1,0:T(8,128)(2,1)S(1)} collective-permute-done((bf16[512,1024]{1,0:T(8,128)(2,1)S(1)}, bf16[512,1024]{1,0:T(8,128)(2,1)S(1)}, u32[]{:S(2)}, u32[]{:S(2)}) %collective-permute-start.6) | collective-permute-done | bytes 1048608 | tf_op jit(solution)/shard_map/ppermute | solution.py:412
  240.1 2.2 pad_maximum_fusion.3
  242.4 3.3 multiply_reduce_fusion.3
  253.6 43.9 %collective-permute-done.11 = s32[4,128]{1,0:T(4,128)S(1)} collective-permute-done((s32[4,128]{1,0:T(4,128)S(1)}, s32[4,128]{1,0:T(4,128)S(1)}, u32[]{:S(2)}, u32[]{:S(2)}) %collective-permute-start.11) | collective-permute-done | bytes 2080 | tf_op jit(solution)/shard_map/ppermute | solution.py:412
  302.6 2.3 bitcast_dynamic-update-slice_fusion.1
  304.9 3.8 pad_maximum_fusion.2
  311.3 2.4 constant_dynamic-update-slice_fusion.12
  313.7 2.3 constant_dynamic-update-slice_fusion.11
  318.1 3.8 constant_dynamic-update-slice_fusion.9
  323.0 6.6 copy.175
  329.6 2.3 constant_dynamic-update-slice_fusion.8
  331.8 2.3 constant_dynamic-update-slice_fusion.7
  334.1 2.3 constant_dynamic-update-slice_fusion.6
  337.4 3.9 constant_dynamic-update-slice_fusion.5
  341.3 102.2 %experts.1 = (bf16[4096,1024]{1,0:T(8,128)(2,1)}, bf16[4096,1024]{1,0:T(8,128)(2,1)}, f32[8,4096]{1,0:T(8,128)}, bf16[3,4,1024,256]{3,2,1,0:T(8,128)(2,1)}) custom-call(bf16[4096,1024]{1,0:T(8,128)(2,1)} %bitcast.264, bf16[4096,1024]{1,0:T(8,128)(2,1)} %bitcast.263, s32[4096,1]{1,0:T(8,128)} %copy.176.bits_ref, bf16[1024,128]{1,0:T(8,128)(2,1)} %pad.13.router_ref, ...), custom_call_target="tpu_custom_call" | custom-call | flops 77309411328 | bytes 46137344 | tf_op jit(solution)/shard_map/experts/pallas_call | solution.py:330
  443.5 12.4 %fusion.48 = (bf16[2048,1024]{1,0:T(8,128)(2,1)}, bf16[2048,1024]{1,0:T(8,128)(2,1)}, bf16[2048,1024]{1,0:T(8,128)(2,1)}, bf16[2048,1024]{1,0:T(8,128)(2,1)}) fusion(bf16[4096,1024]{1,0:T(8,128)(2,1)} %get-tuple-element.28, bf16[4096,1024]{1,0:T(8,128)(2,1)} %get-tuple-element.27), kind=kLoop, calls=%fused_computation.160 | loop fusion | bytes 33554432 | tf_op jit(solution)/shard_map/slice | solution.py:418
  458.2 4.9 collective-permute-done.23
  469.7 5.6 fusion
  479.3 4.3 fusion.1
  484.7 17.1 %collective-permute-done.19 = bf16[512,1024]{1,0:T(8,128)(2,1)S(1)} collective-permute-done((bf16[512,1024]{1,0:T(8,128)(2,1)S(1)}, bf16[512,1024]{1,0:T(8,128)(2,1)S(1)}, u32[]{:S(2)}, u32[]{:S(2)}) %collective-permute-start.19) | collective-permute-done | bytes 1048608 | tf_op jit(solution)/shard_map/ppermute | solution.py:421
  503.2 21.3 %collective-permute-done.21 = bf16[512,1024]{1,0:T(8,128)(2,1)S(1)} collective-permute-done((bf16[512,1024]{1,0:T(8,128)(2,1)S(1)}, bf16[512,1024]{1,0:T(8,128)(2,1)S(1)}, u32[]{:S(2)}, u32[]{:S(2)}) %collective-permute-start.21) | collective-permute-done | bytes 1048608 | tf_op jit(solution)/shard_map/ppermute | solution.py:421
  527.0 19.8 %collective-permute-done.14 = bf16[512,1024]{1,0:T(8,128)(2,1)S(1)} collective-permute-done((bf16[512,1024]{1,0:T(8,128)(2,1)S(1)}, bf16[512,1024]{1,0:T(8,128)(2,1)S(1)}, u32[]{:S(2)}, u32[]{:S(2)}) %collective-permute-start.14) | collective-permute-done | bytes 1048608 | tf_op jit(solution)/shard_map/ppermute | solution.py:421
  546.8 20.1 %collective-permute-done.16 = bf16[512,1024]{1,0:T(8,128)(2,1)S(1)} collective-permute-done((bf16[512,1024]{1,0:T(8,128)(2,1)S(1)}, bf16[512,1024]{1,0:T(8,128)(2,1)S(1)}, u32[]{:S(2)}, u32[]{:S(2)}) %collective-permute-start.16) | collective-permute-done | bytes 1048608 | tf_op jit(solution)/shard_map/ppermute | solution.py:421
  575.9 3.6 convert_add_fusion.4
  581.5 2.2 convolution_convert_fusion.4
  583.7 18.4 %attn_bwd.1 = (bf16[2,512,512]{2,1,0:T(8,128)(2,1)}, bf16[2,2048,256]{2,1,0:T(8,128)(2,1)}, bf16[2,2048,256]{2,1,0:T(8,128)(2,1)}) custom-call(s32[1]{0:T(128)} %bitcast.1.ctx_ref, bf16[2,512,512]{2,1,0:T(8,128)(2,1)} %bitcast.285, bf16[2,2048,512]{2,1,0:T(8,128)(2,1)} %all-gather.6.cloned.1.call-done.k_ref.v_ref, ...), custom_call_target="tpu_custom_call" | custom-call | flops 42949672960 | bytes 16777216 | tf_op jit(solution)/shard_map/attn_bwd/pallas_call | solution.py:235
  602.1 4.6 pad_maximum_fusion
  606.8 6.6 copy.190
  614.4 121.1 %reduce-scatter.6.cloned.1.call-done = bf16[2,512,512]{2,1,0:T(8,128)(2,1)} async-done(((bf16[2,2048,512]{2,1,0:T(8,128)(2,1)}), bf16[2,512,512]{2,1,0:T(8,128)(2,1)}) %reduce-scatter.6.cloned.1.call-update) | async-done | bytes 1048592 | tf_op jit(solution)/shard_map/reduce_scatter | solution.py:522
  739.6 4.4 convolution_convert_fusion.1
  745.1 2.2 copy-done.7
  749.2 2.5 convolution_convert_fusion
  753.4 2.2 pad_maximum_fusion.1
  755.6 5.6 copy.201
  761.2 87.8 %reduce-scatter.8.cloned.1.call-done = bf16[1,3,4,256,256]{4,3,2,1,0:T(8,128)(2,1)} async-done(((bf16[4,3,4,256,256]{4,3,2,1,0:T(8,128)(2,1)}), bf16[1,3,4,256,256]{4,3,2,1,0:T(8,128)(2,1)}) %reduce-scatter.8.cloned.1.call-update) | async-done | bytes 1572880 | tf_op jit(solution)/shard_map/reduce_scatter | solution.py:488
  849.1 2.6 copy.191
  851.7 33.2 %all_to_all.25 = bf16[3,4,256,256]{3,1,0,2:T(4,128)(2,1)S(1)} all-to-all(bf16[3,4,256,256]{3,1,0,2:T(4,128)(2,1)S(1)} %copy.191), channel_id=1, replica_groups=mesh['dp'=4,'ctx'=4,'mp'=2] {'dp'}, dimensions={2} | all-to-all | bytes 3145728 | tf_op jit(solution)/shard_map/all_to_all | solution.py:489
  890.3 2.9 fusion.9
  893.1 48.6 %reduce-scatter.10.cloned.1.call-done = bf16[64,1664]{1,0:T(8,128)(2,1)} async-done(((bf16[1024,1664]{1,0:T(8,128)(2,1)}), bf16[64,1664]{1,0:T(8,128)(2,1)}) %reduce-scatter.10.cloned.1.call-update) | async-done | bytes 213008
  (239 shorter events, 83.3 us)
Async XLA Ops:
  7.2 78.7 %all-gather.4.cloned.1.call-start = ((), (), s32[]{:S(2)}) async-start(), calls=%async_computation.5 | async-start | bytes 3620864 | tf_op jit(solution)/shard_map/all_gather | solution.py:432
  12.8 164.9 %all-gather.6.cloned.1.call-start = ((), (), s32[]{:S(2)}) async-start(), calls=%async_computation.6 | async-start | bytes 5242880 | tf_op jit(solution)/shard_map/all_gather | solution.py:470
  13.9 84.3 %copy-start.20 = (f32[512,32]{1,0:T(8,128)}, f32[512,32]{1,0:T(8,128)S(1)}, u32[]{:S(2)}) copy-start(f32[512,32]{1,0:T(8,128)S(1)} %get-tuple-element.159) | copy-start | bytes 196612
  14.0 84.2 %copy-start.22 = (f32[512,32]{0,1:T(8,128)}, f32[512,32]{0,1:T(8,128)S(1)}, u32[]{:S(2)}) copy-start(f32[512,32]{0,1:T(8,128)S(1)} %copy.171) | copy-start | bytes 196612
  91.0 7.3 copy-start.24
  91.0 7.3 copy-start.25
  91.0 7.3 copy-start.26
  98.2 224.7 %all-gather.8.cloned.1.call-start = ((), (), s32[]{:S(2)}) async-start(), calls=%async_computation.7 | async-start | bytes 7864320 | tf_op jit(solution)/shard_map/all_gather | solution.py:442
  121.1 614.4 %reduce-scatter.6.cloned.1.call-start = ((), (), s32[]{:S(2)}) async-start(), calls=%async_computation.8 | async-start | bytes 5242880 | tf_op jit(solution)/shard_map/reduce_scatter | solution.py:522
  190.9 51.5 %collective-permute-start = (bf16[1024,1024]{1,0:T(8,128)(2,1)}, bf16[1024,1024]{1,0:T(8,128)(2,1)}, u32[]{:S(2)}, u32[]{:S(2)}) collective-permute-start(bf16[1024,1024]{1,0:T(8,128)(2,1)} %convolution_convert_fusion.2), channel_id=1, source_target_pairs={{0,1},{1,0},{2,3},{3,2},{4,5},{5,4},{6,7},{7,6},{8,9},{9,8},{10,11... | collective-permute-start | bytes 6291464 | tf_op jit(solution)/shard_map/ppermute | solution.py:366
  190.9 51.5 %copy-start.2 = (bf16[2,1,512,1024]{3,2,1,0:T(8,128)(2,1)S(1)}, bf16[2,1,512,1024]{3,2,1,0:T(8,128)(2,1)}, u32[]{:S(2)}) copy-start(bf16[2,1,512,1024]{3,2,1,0:T(8,128)(2,1)} %param.13) | copy-start | bytes 6291460
  191.0 27.0 %collective-permute-start.7 = (bf16[512,1024]{1,0:T(8,128)(2,1)S(1)}, bf16[512,1024]{1,0:T(8,128)(2,1)S(1)}, u32[]{:S(2)}, u32[]{:S(2)}) collective-permute-start(bf16[512,1024]{1,0:T(8,128)(2,1)S(1)} %dynamic-slice_bitcast_fusion), channel_id=1, source_target_pairs={{0,24},{8,16},{16,8},{24,0},{1,25},{9,17},{17,9},{25,1},{2,26},{10... | collective-permute-start | bytes 3145736 | tf_op jit(solution)/shard_map/ppermute | solution.py:412
  193.5 46.5 %collective-permute-start.6 = (bf16[512,1024]{1,0:T(8,128)(2,1)S(1)}, bf16[512,1024]{1,0:T(8,128)(2,1)S(1)}, u32[]{:S(2)}, u32[]{:S(2)}) collective-permute-start(bf16[512,1024]{1,0:T(8,128)(2,1)S(1)} %dynamic-slice_bitcast_fusion), channel_id=1, source_target_pairs={{0,16},{8,24},{16,0},{24,8},{1,17},{9,25},{17,1},{25,9},{2,18},{10... | collective-permute-start | bytes 3145736 | tf_op jit(solution)/shard_map/ppermute | solution.py:412
  194.0 46.0 %collective-permute-start.5 = (bf16[512,1024]{1,0:T(8,128)(2,1)S(1)}, bf16[512,1024]{1,0:T(8,128)(2,1)S(1)}, u32[]{:S(2)}, u32[]{:S(2)}) collective-permute-start(bf16[512,1024]{1,0:T(8,128)(2,1)S(1)} %dynamic-slice_bitcast_fusion), channel_id=1, source_target_pairs={{0,8},{8,0},{16,24},{24,16},{1,9},{9,1},{17,25},{25,17},{2,10},{10... | collective-permute-start | bytes 3145736 | tf_op jit(solution)/shard_map/ppermute | solution.py:412
  242.3 75.8 %collective-permute-start.8 = (bf16[3,512,1024]{2,1,0:T(8,128)(2,1)}, bf16[3,512,1024]{2,1,0:T(8,128)(2,1)}, u32[]{:S(2)}, u32[]{:S(2)}) collective-permute-start(bf16[3,512,1024]{2,1,0:T(8,128)(2,1)} %pad_maximum_fusion.3), channel_id=1, source_target_pairs={{0,1},{1,0},{2,3},{3,2},{4,5},{5,4},{6,7},{7,6},{8,9},{9,8},{10,11... | collective-permute-start | bytes 9437192 | tf_op jit(solution)/shard_map/ppermute | solution.py:366
  245.7 6.2 copy-start.29
  246.1 210.5 %copy-start.4 = (bf16[1024,1024]{1,0:T(8,128)(2,1)}, bf16[1024,1024]{1,0:T(8,128)(2,1)S(1)}, u32[]{:S(2)}) copy-start(bf16[1024,1024]{1,0:T(8,128)(2,1)S(1)} %multiply_convert_fusion) | copy-start | bytes 6291460
  248.3 56.6 %collective-permute-start.3 = (bf16[512,1024]{1,0:T(8,128)(2,1)}, bf16[512,1024]{1,0:T(8,128)(2,1)}, u32[]{:S(2)}, u32[]{:S(2)}) collective-permute-start(bf16[512,1024]{1,0:T(8,128)(2,1)} %get-tuple-element.135), channel_id=1, source_target_pairs={{0,24},{8,16},{16,8},{24,0},{1,25},{9,17},{17,9},{25,1},{2,26},{10... | collective-permute-start | bytes 3145736 | tf_op jit(solution)/shard_map/ppermute | solution.py:412
  250.0 54.9 %collective-permute-start.2 = (bf16[512,1024]{1,0:T(8,128)(2,1)}, bf16[512,1024]{1,0:T(8,128)(2,1)}, u32[]{:S(2)}, u32[]{:S(2)}) collective-permute-start(bf16[512,1024]{1,0:T(8,128)(2,1)} %get-tuple-element.135), channel_id=1, source_target_pairs={{0,16},{8,24},{16,0},{24,8},{1,17},{9,25},{17,1},{25,9},{2,18},{10... | collective-permute-start | bytes 3145736 | tf_op jit(solution)/shard_map/ppermute | solution.py:412
  251.3 53.6 %collective-permute-start.1 = (bf16[512,1024]{1,0:T(8,128)(2,1)}, bf16[512,1024]{1,0:T(8,128)(2,1)}, u32[]{:S(2)}, u32[]{:S(2)}) collective-permute-start(bf16[512,1024]{1,0:T(8,128)(2,1)} %get-tuple-element.135), channel_id=1, source_target_pairs={{0,8},{8,0},{16,24},{24,16},{1,9},{9,1},{17,25},{25,17},{2,10},{10... | collective-permute-start | bytes 3145736 | tf_op jit(solution)/shard_map/ppermute | solution.py:412
  251.9 45.6 %collective-permute-start.11 = (s32[4,128]{1,0:T(4,128)S(1)}, s32[4,128]{1,0:T(4,128)S(1)}, u32[]{:S(2)}, u32[]{:S(2)}) collective-permute-start(s32[4,128]{1,0:T(4,128)S(1)} %get-tuple-element.156), channel_id=1, source_target_pairs={{0,24},{8,16},{16,8},{24,0},{1,25},{9,17},{17,9},{25,1},{2,26},{10... | collective-permute-start | bytes 6152 | tf_op jit(solution)/shard_map/ppermute | solution.py:412
  297.5 3.6 collective-permute-start.10
  301.1 3.8 collective-permute-start.9
  304.9 4.4 collective-permute-start.12
  308.8 28.7 %collective-permute-start.4 = (bf16[3,512,1024]{2,1,0:T(8,128)(2,1)}, bf16[3,512,1024]{2,1,0:T(8,128)(2,1)}, u32[]{:S(2)}, u32[]{:S(2)}) collective-permute-start(bf16[3,512,1024]{2,1,0:T(8,128)(2,1)} %pad_maximum_fusion.2), channel_id=1, source_target_pairs={{0,1},{1,0},{2,3},{3,2},{4,5},{5,4},{6,7},{7,6},{8,9},{9,8},{10,11... | collective-permute-start | bytes 9437192 | tf_op jit(solution)/shard_map/ppermute | solution.py:366
  311.3 5.8 copy-start.11
  443.5 12.9 %copy-start.30 = (f32[8,4096]{1,0:T(8,128)S(1)}, f32[8,4096]{1,0:T(8,128)}, u32[]{:S(2)}) copy-start(f32[8,4096]{1,0:T(8,128)} %get-tuple-element.29) | copy-start | bytes 393220
  455.9 13.9 %collective-permute-start.18 = (bf16[4,512,1024]{2,1,0:T(8,128)(2,1)}, bf16[4,512,1024]{2,1,0:T(8,128)(2,1)}, u32[]{:S(2)}, u32[]{:S(2)}) collective-permute-start(bf16[4,512,1024]{2,1,0:T(8,128)(2,1)} %bitcast.51), channel_id=1, source_target_pairs={{0,1},{1,0},{2,3},{3,2},{4,5},{5,4},{6,7},{7,6},{8,9},{9,8},{10,11... | collective-permute-start | bytes 12582920 | tf_op jit(solution)/shard_map/ppermute | solution.py:366
  455.9 23.4 %collective-permute-start.13 = (bf16[4,512,1024]{2,1,0:T(8,128)(2,1)}, bf16[4,512,1024]{2,1,0:T(8,128)(2,1)}, u32[]{:S(2)}, u32[]{:S(2)}) collective-permute-start(bf16[4,512,1024]{2,1,0:T(8,128)(2,1)} %bitcast.39), channel_id=1, source_target_pairs={{0,1},{1,0},{2,3},{3,2},{4,5},{5,4},{6,7},{7,6},{8,9},{9,8},{10,11... | collective-permute-start | bytes 12582920 | tf_op jit(solution)/shard_map/ppermute | solution.py:366
  456.5 6.6 collective-permute-start.23
  463.2 3.7 collective-permute-start.25
  464.5 4.5 collective-permute-start.26
  466.1 3.7 collective-permute-start.24
  475.6 26.2 %collective-permute-start.19 = (bf16[512,1024]{1,0:T(8,128)(2,1)S(1)}, bf16[512,1024]{1,0:T(8,128)(2,1)S(1)}, u32[]{:S(2)}, u32[]{:S(2)}) collective-permute-start(bf16[512,1024]{1,0:T(8,128)(2,1)S(1)} %get-tuple-element.122), channel_id=1, source_target_pairs={{0,8},{8,0},{16,24},{24,16},{1,9},{9,1},{17,25},{25,17},{2,10},{10... | collective-permute-start | bytes 3145736 | tf_op jit(solution)/shard_map/ppermute | solution.py:421
  476.4 48.0 %collective-permute-start.21 = (bf16[512,1024]{1,0:T(8,128)(2,1)S(1)}, bf16[512,1024]{1,0:T(8,128)(2,1)S(1)}, u32[]{:S(2)}, u32[]{:S(2)}) collective-permute-start(bf16[512,1024]{1,0:T(8,128)(2,1)S(1)} %get-tuple-element.123), channel_id=1, source_target_pairs={{0,24},{8,16},{16,8},{24,0},{1,25},{9,17},{17,9},{25,1},{2,26},{10... | collective-permute-start | bytes 3145736 | tf_op jit(solution)/shard_map/ppermute | solution.py:421
  477.9 47.9 %collective-permute-start.20 = (bf16[512,1024]{1,0:T(8,128)(2,1)S(1)}, bf16[512,1024]{1,0:T(8,128)(2,1)S(1)}, u32[]{:S(2)}, u32[]{:S(2)}) collective-permute-start(bf16[512,1024]{1,0:T(8,128)(2,1)S(1)} %get-tuple-element.124), channel_id=1, source_target_pairs={{0,16},{8,24},{16,0},{24,8},{1,17},{9,25},{17,1},{25,9},{2,18},{10... | collective-permute-start | bytes 3145736 | tf_op jit(solution)/shard_map/ppermute | solution.py:421
  479.2 47.6 %collective-permute-start.27 = (f32[16,512]{1,0:T(8,128)S(1)}, f32[16,512]{1,0:T(8,128)S(1)}, u32[]{:S(2)}, u32[]{:S(2)}) collective-permute-start(f32[16,512]{1,0:T(8,128)S(1)} %pad_maximum_fusion.12), channel_id=1, source_target_pairs={{0,1},{1,0},{2,3},{3,2},{4,5},{5,4},{6,7},{7,6},{8,9},{9,8},{10,11... | collective-permute-start | bytes 98312 | tf_op jit(solution)/shard_map/ppermute | solution.py:366
  484.0 62.8 %collective-permute-start.14 = (bf16[512,1024]{1,0:T(8,128)(2,1)S(1)}, bf16[512,1024]{1,0:T(8,128)(2,1)S(1)}, u32[]{:S(2)}, u32[]{:S(2)}) collective-permute-start(bf16[512,1024]{1,0:T(8,128)(2,1)S(1)} %get-tuple-element.125), channel_id=1, source_target_pairs={{0,8},{8,0},{16,24},{24,16},{1,9},{9,1},{17,25},{25,17},{2,10},{10... | collective-permute-start | bytes 3145736 | tf_op jit(solution)/shard_map/ppermute | solution.py:421
  501.8 65.1 %collective-permute-start.16 = (bf16[512,1024]{1,0:T(8,128)(2,1)S(1)}, bf16[512,1024]{1,0:T(8,128)(2,1)S(1)}, u32[]{:S(2)}, u32[]{:S(2)}) collective-permute-start(bf16[512,1024]{1,0:T(8,128)(2,1)S(1)} %get-tuple-element.126), channel_id=1, source_target_pairs={{0,24},{8,16},{16,8},{24,0},{1,25},{9,17},{17,9},{25,1},{2,26},{10... | collective-permute-start | bytes 3145736 | tf_op jit(solution)/shard_map/ppermute | solution.py:421
  524.4 43.8 %collective-permute-start.15 = (bf16[512,1024]{1,0:T(8,128)(2,1)S(1)}, bf16[512,1024]{1,0:T(8,128)(2,1)S(1)}, u32[]{:S(2)}, u32[]{:S(2)}) collective-permute-start(bf16[512,1024]{1,0:T(8,128)(2,1)S(1)} %get-tuple-element.127), channel_id=1, source_target_pairs={{0,16},{8,24},{16,0},{24,8},{1,17},{9,25},{17,1},{25,9},{2,18},{10... | collective-permute-start | bytes 3145736 | tf_op jit(solution)/shard_map/ppermute | solution.py:421
  526.7 42.5 %collective-permute-start.22 = (bf16[512,1024]{1,0:T(8,128)(2,1)S(1)}, bf16[512,1024]{1,0:T(8,128)(2,1)S(1)}, u32[]{:S(2)}, u32[]{:S(2)}) collective-permute-start(bf16[512,1024]{1,0:T(8,128)(2,1)S(1)} %fusion.15), channel_id=1, source_target_pairs={{0,1},{1,0},{2,3},{3,2},{4,5},{5,4},{6,7},{7,6},{8,9},{9,8},{10,11... | collective-permute-start | bytes 3145736 | tf_op jit(solution)/shard_map/ppermute | solution.py:366
  569.1 5.2 collective-permute-start.17
  606.8 242.3 %reduce-scatter.8.cloned.1.call-start = ((), (), s32[]{:S(2)}) async-start(), calls=%async_computation.9 | async-start | bytes 7864320 | tf_op jit(solution)/shard_map/reduce_scatter | solution.py:488
  613.4 124.7 %copy-start.23 = (f32[512,32]{0,1:T(8,128)S(1)}, f32[512,32]{0,1:T(8,128)}, u32[]{:S(2)}) copy-start(f32[512,32]{0,1:T(8,128)} %copy-done.22) | copy-start | bytes 196612
  613.4 328.3 %reduce-scatter.10.cloned.1.call-start = ((), (), s32[]{:S(2)}) async-start(), calls=%async_computation.10 | async-start | bytes 3620864
  739.6 5.5 copy-start.31
  744.0 7.6 copy-start.13
  744.0 7.6 collective-permute-start.28
  (22 other events, 63.4 us)
Sparse Core Ops, SparseCore 0:
  12.9 72.9 all-gather.3
  98.4 79.2 all-gather.5
  179.8 113.8 all-gather.7
  606.9 128.5 reduce-scatter.5
  737.8 111.2 reduce-scatter.7
  851.3 90.3 reduce-scatter.9

commit v2 on v1

v2 whole, which is shorter than its diff:
```python
import functools
import math

import jax
import jax.numpy as jnp
from jax import lax
from jax.experimental import pallas as pl
from jax.experimental.pallas import tpu as pltpu
from jax.sharding import PartitionSpec as P

HD = 64
EPS = 1e-06
THETA = 10000.0
NEG = -1e30
VMEM_LIMIT = 60 * 1024 * 1024
BF = jnp.bfloat16
F32 = jnp.float32


def dot(a, b, ca, cb, precision=None):
    return lax.dot_general(
        a, b, (((ca,), (cb,)), ((), ())), preferred_element_type=F32, precision=precision
    )


def params(*semantics):
    return pltpu.CompilerParams(dimension_semantics=semantics, vmem_limit_bytes=VMEM_LIMIT)


def turn(values, cosine, sine):
    width = values.shape[1]
    lane = lax.broadcasted_iota(jnp.int32, values.shape, 1)
    ahead = pltpu.roll(values, width - HD // 2, 1)
    behind = pltpu.roll(values, HD // 2, 1)
    swapped = jnp.where(lane % HD < HD // 2, ahead, behind)
    reps = width // cosine.shape[1]
    return values * jnp.tile(cosine, (1, reps)) + swapped * jnp.tile(sine, (1, reps))


def kv_kernel(x_ref, gain_ref, w_ref, cos_ref, sin_ref, normed_ref, kv_ref):
    x = x_ref[...].astype(F32)
    inv = lax.rsqrt(jnp.mean(x * x, axis=1, keepdims=True) + EPS)
    normed = (x * inv * gain_ref[...]).astype(BF)
    normed_ref[...] = normed
    kw = kv_ref.shape[1] // 2
    raw = dot(normed, w_ref[...], 1, 0)
    kv_ref[:, :kw] = turn(raw[:, :kw], cos_ref[...], sin_ref[...]).astype(BF)
    kv_ref[:, kw:] = raw[:, kw:].astype(BF)


def q_kernel(normed_ref, w_ref, cos_ref, sin_ref, q_ref):
    raw = dot(normed_ref[...], w_ref[...], 1, 0)
    q_ref[...] = turn(raw, cos_ref[...], sin_ref[...]).astype(BF)


def row_specs(rows, local, d, lanes):
    tile = min(256, local)
    per = local // tile
    return (
        rows // tile,
        pl.BlockSpec((tile, d), lambda i: (i, 0)),
        pl.BlockSpec((d, lanes), lambda i: (0, 0)),
        pl.BlockSpec((tile, 128), lambda i: (i % per, 0)),
        pl.BlockSpec((tile, lanes), lambda i: (i, 0)),
        pl.CostEstimate(
            flops=2 * rows * d * lanes, bytes_accessed=6 * rows * d, transcendentals=rows
        ),
    )


def kv_call(x, gain, w, lanes, cosine, sine):
    rows, d = x.shape
    steps, row, weight, table, out, cost = row_specs(rows, cosine.shape[0], d, lanes)
    return pl.pallas_call(
        kv_kernel,
        grid=(steps,),
        in_specs=[row, pl.BlockSpec((1, d), lambda i: (0, 0)), weight, table, table],
        out_specs=[row, out],
        out_shape=[
            jax.ShapeDtypeStruct((rows, d), BF),
            jax.ShapeDtypeStruct((rows, lanes), BF),
        ],
        compiler_params=params("arbitrary"),
        cost_estimate=cost,
        name="kv",
    )(x, gain, w, cosine, sine)


def q_call(normed, w, lanes, cosine, sine):
    rows, d = normed.shape
    steps, row, weight, table, out, cost = row_specs(rows, cosine.shape[0], d, lanes)
    return pl.pallas_call(
        q_kernel,
        grid=(steps,),
        in_specs=[row, weight, table, table],
        out_specs=out,
        out_shape=jax.ShapeDtypeStruct((rows, lanes), BF),
        compiler_params=params("arbitrary"),
        cost_estimate=cost,
        name="q",
    )(normed, w, cosine, sine)


def half_mask(block, which):
    lane = lax.broadcasted_iota(jnp.int32, block.shape, 1)
    keep = (lane < HD) if which == 0 else (lane >= HD)
    return jnp.where(keep, block, jnp.zeros_like(block))


def stacked(ref):
    return jnp.concatenate([ref[0, :, :128], ref[0, :, 128:]], axis=0)


def causal(shape, length):
    key = lax.broadcasted_iota(jnp.int32, shape, 0)
    query = lax.broadcasted_iota(jnp.int32, shape, 1) % length
    return key <= query


def each_earlier(c, counts, visit, otherwise=None, first=1):
    for piece, count in enumerate(counts):
        if count == 1:

            @pl.when(c >= first)
            def _():
                visit(piece, 0)

            if otherwise is not None:

                @pl.when(c < first)
                def _():
                    otherwise(piece, 0)

        else:
            reach = jnp.clip(c - first + 1, 0, count)

            @pl.loop(0, reach)
            def _(entry):
                visit(piece, entry)

            if otherwise is not None:

                @pl.loop(reach, count)
                def _(entry):
                    otherwise(piece, entry)

        first += count


def attn_part_kernel(counts, start, first, last, ctx_ref, q_ref, *refs):
    refs = list(refs)
    pieces = len(counts) + first
    keys = [refs.pop(0) for _ in range(pieces)]
    vals = [refs.pop(0) for _ in range(pieces)]
    old = None if first else [refs.pop(0) for _ in range(2)]
    if last:
        o_ref, lse_ref, stats_ref, acc_ref = refs
    else:
        stats_ref, acc_ref = (ref.at[0, 0] for ref in refs)
    length = q_ref.shape[1]
    both = (stacked(q_ref).astype(F32) * HD**-0.5).astype(BF)
    c = ctx_ref[0]

    if first:
        k = keys[0][0, 0]
        v = vals[0][0, 0]
        for i in range(2):
            s = dot(half_mask(k, i), both, 1, 1)
            s = jnp.where(causal(s.shape, length), s, NEG)
            peak = jnp.max(s, axis=0, keepdims=True)
            p = jnp.exp(s - peak)
            stats_ref[i : i + 1] = peak
            stats_ref[i + 2 : i + 3] = jnp.sum(p, axis=0, keepdims=True)
            acc_ref[i] = dot(v, p.astype(BF), 0, 0)
    else:
        stats_ref[...] = old[0][0, 0]
        acc_ref[...] = old[1][0, 0]

    def visit(piece, entry):
        k = keys[piece + first][entry, 0]
        v = vals[piece + first][entry, 0]
        for i in range(2):
            s = dot(half_mask(k, i), both, 1, 1)
            peak = stats_ref[i : i + 1]
            now = jnp.maximum(peak, jnp.max(s, axis=0, keepdims=True))
            p = jnp.exp(s - now)
            factor = jnp.exp(peak - now)
            stats_ref[i : i + 1] = now
            stats_ref[i + 2 : i + 3] = stats_ref[i + 2 : i + 3] * factor + jnp.sum(
                p, axis=0, keepdims=True
            )
            acc_ref[i] = acc_ref[i] * factor + dot(v, p.astype(BF), 0, 0)

    each_earlier(c, counts, visit, None, start)
    if last:
        row = lax.broadcasted_iota(jnp.int32, acc_ref.shape[1:], 0)
        stats = stats_ref[...]
        out = jnp.where(row < HD, acc_ref[0] / stats[2:3], acc_ref[1] / stats[3:4]).T
        o_ref[0, :, :128] = out[:length].astype(BF)
        o_ref[0, :, 128:] = out[length:].astype(BF)
        lse_ref[0, 0] = stats[:2] + jnp.log(stats[2:])


def kv_specs(pieces, length, lanes, at=0):
    kb = lanes // 256
    keys = [
        pl.BlockSpec((a.shape[0], 1, length, 128), lambda s, p: (0, s + at, 0, p)) for a in pieces
    ]
    vals = [
        pl.BlockSpec((a.shape[0], 1, length, 128), lambda s, p: (0, s + at, 0, kb + p))
        for a in pieces
    ]
    return keys + vals


def attn_part(ctx, q, own, prev, start, carry, last):
    seqs, length, qw = q.shape
    pairs = qw // 256
    cols = 2 * length
    first = own is not None
    pieces = ([own] if first else []) + prev
    counts = tuple(a.shape[0] for a in prev)
    spans = first + sum(counts)
    state = [
        pl.BlockSpec((1, 1, 4, cols), lambda s, p: (s, p, 0, 0)),
        pl.BlockSpec((1, 1, 2, 128, cols), lambda s, p: (s, p, 0, 0, 0)),
    ]
    if last:
        out_specs = [
            pl.BlockSpec((1, length, 256), lambda s, p: (s, 0, p)),
            pl.BlockSpec((1, 1, 2, cols), lambda s, p: (s, p, 0, 0)),
        ]
        out_shape = [
            jax.ShapeDtypeStruct((seqs, length, qw), BF),
            jax.ShapeDtypeStruct((seqs, pairs, 2, cols), F32),
        ]
        scratch = [pltpu.VMEM((4, cols), F32), pltpu.VMEM((2, 128, cols), F32)]
    else:
        out_specs = state
        out_shape = [
            jax.ShapeDtypeStruct((seqs, pairs, 4, cols), F32),
            jax.ShapeDtypeStruct((seqs, pairs, 2, 128, cols), F32),
        ]
        scratch = []
    return pl.pallas_call(
        functools.partial(attn_part_kernel, counts, start, first, last),
        grid=(seqs, pairs),
        in_specs=[
            pl.BlockSpec(memory_space=pltpu.SMEM),
            pl.BlockSpec((1, length, 256), lambda s, p: (s, 0, p)),
        ]
        + kv_specs(pieces, length, pieces[0].shape[3])
        + ([] if first else state),
        out_specs=out_specs,
        out_shape=out_shape,
        scratch_shapes=scratch,
        compiler_params=params("arbitrary", "arbitrary"),
        cost_estimate=pl.CostEstimate(
            flops=16 * seqs * length * length * spans * qw,
            bytes_accessed=4 * seqs * length * spans * qw,
            transcendentals=seqs * length * length * spans * qw // 64,
        ),
        name="attn_fwd",
    )(ctx, q, *pieces, *pieces, *(carry or []))


def attn_bwd_kernel(counts, ctx_ref, q_ref, do_ref, o_ref, lse_ref, cos_ref, sin_ref, *refs):
    pieces = len(counts)
    keys = refs[: pieces + 1]
    vals = refs[pieces + 1 : 2 * pieces + 2]
    dq_ref = refs[2 * pieces + 2]
    outs = refs[2 * pieces + 3 : 3 * pieces + 4]
    acc_ref = refs[3 * pieces + 4]
    length = q_ref.shape[1]
    lanes = outs[0].shape[3]
    pair = pl.program_id(1)
    both = (stacked(q_ref).astype(F32) * HD**-0.5).astype(BF)
    dboth = stacked(do_ref)
    prod = dboth.astype(F32) * stacked(o_ref).astype(F32)
    pick_row = lax.broadcasted_iota(jnp.int32, (8, 128), 0)
    pick_lane = lax.broadcasted_iota(jnp.int32, (8, 128), 1) // HD
    picks = (pick_row == pick_lane).astype(F32)
    delta = dot(picks, prod, 1, 1, lax.Precision.HIGHEST)
    c = ctx_ref[0]
    k_at = pl.ds(pl.multiple_of(pair * 128, 128), 128)
    v_at = pl.ds(pl.multiple_of(lanes // 2 + pair * 128, 128), 128)

    def block(piece, entry, diagonal):
        k = keys[piece][entry, 0]
        v = vals[piece][entry, 0]
        parts = []
        dq = None
        for i in range(2):
            ki = half_mask(k, i)
            s = dot(ki, both, 1, 1)
            p = jnp.exp(s - lse_ref[0, 0, i : i + 1, :])
            if diagonal:
                p = jnp.where(causal(s.shape, length), p, 0.0)
            dp = dot(half_mask(v, i), dboth, 1, 1)
            ds = (p * (dp - delta[i : i + 1, :])).astype(BF)
            parts.append((dot(ds, both, 1, 0), dot(p.astype(BF), dboth, 1, 0)))
            part = dot(ki, ds, 0, 0)
            dq = part if dq is None else dq + part
        low = lax.broadcasted_iota(jnp.int32, (length, 128), 1) < HD
        outs[piece][entry, 0, :, k_at] = jnp.where(low, parts[0][0], parts[1][0]).astype(BF)
        outs[piece][entry, 0, :, v_at] = jnp.where(low, parts[0][1], parts[1][1]).astype(BF)
        return dq

    acc_ref[...] = block(0, 0, True)

    def visit(piece, entry):
        acc_ref[...] += block(piece + 1, entry, False)

    def clear(piece, entry):
        outs[piece + 1][entry, 0, :, k_at] = jnp.zeros((length, 128), BF)
        outs[piece + 1][entry, 0, :, v_at] = jnp.zeros((length, 128), BF)

    each_earlier(c, counts, visit, clear)
    out = acc_ref[...].T * HD**-0.5
    cosine = cos_ref[...]
    sine = -sin_ref[...]
    dq_ref[0, :, :128] = turn(out[:length], cosine, sine).astype(BF)
    dq_ref[0, :, 128:] = turn(out[length:], cosine, sine).astype(BF)


def attn_bwd(ctx, q, do, o, lse, cosine, sine, own, prev, at):
    seqs, length, qw = do.shape
    pairs = qw // 256
    pieces = [own] + prev
    counts = tuple(a.shape[0] for a in prev)
    spans = 1 + sum(counts)
    blk = pl.BlockSpec((1, length, 256), lambda s, p: (s, 0, p))
    blk_at = pl.BlockSpec((1, length, 256), lambda s, p: (s + at, 0, p))
    tab = pl.BlockSpec((length, 128), lambda s, p: (0, 0))
    return pl.pallas_call(
        functools.partial(attn_bwd_kernel, counts),
        grid=(seqs, pairs),
        in_specs=[
            pl.BlockSpec(memory_space=pltpu.SMEM),
            blk_at,
            blk,
            blk_at,
            pl.BlockSpec((1, 1, 2, 2 * length), lambda s, p: (s + at, p, 0, 0)),
            tab,
            tab,
        ]
        + kv_specs(pieces, length, own.shape[3], at),
        out_specs=[blk]
        + [
            pl.BlockSpec((a.shape[0], 1) + a.shape[2:], lambda s, p: (0, s, 0, 0)) for a in pieces
        ],
        out_shape=[jax.ShapeDtypeStruct((seqs, length, qw), BF)]
        + [jax.ShapeDtypeStruct((a.shape[0], seqs) + a.shape[2:], BF) for a in pieces],
        scratch_shapes=[pltpu.VMEM((128, 2 * length), F32)],
        compiler_params=params("arbitrary", "arbitrary"),
        cost_estimate=pl.CostEstimate(
            flops=40 * seqs * length * length * spans * qw,
            bytes_accessed=8 * seqs * length * spans * qw,
            transcendentals=seqs * length * length * spans * qw // 64,
        ),
        name="attn_bwd",
    )(ctx, q, do, o, lse, cosine, sine, *pieces, *pieces)


def masked_softmax(logits, named):
    peak = jnp.max(jnp.where(named, logits, NEG), axis=1, keepdims=True)
    grown = jnp.where(named, jnp.exp(jnp.where(named, logits - peak, 0.0)), 0.0)
    return grown / jnp.sum(grown, axis=1, keepdims=True)


def experts_kernel(steps, first, count, more, joined, place_ref, router_ref, *refs):
    refs = list(refs)
    n = 1 if joined else refs[-5].shape[1]
    xs = [refs.pop(0) for _ in range(2 * steps)]
    dys = [refs.pop(0) for _ in range(2 * steps)]
    ws = [refs.pop(0) for _ in range(2 * n - 1)]
    before = [refs.pop(0) for _ in range(4)] if more else None
    outs = [refs.pop(0) for _ in range(4)]
    dws = [refs.pop(0) for _ in range(n)]
    acc_ref, w_ref, xbuf, dybuf, sems, wsems = refs
    step = pl.program_id(0)
    base = place_ref[0]
    c = place_ref[1]
    rows, width = xbuf.shape[1:]
    units = w_ref.shape[-1] // (3 * count)
    both = 2 * count * units
    half = rows // 2

    def copies(t, slot):
        return [
            pltpu.make_async_copy(
                src[2 * t + part],
                buf.at[slot, pl.ds(part * half, half)],
                sems.at[slot, 2 * which + part],
            )
            for which, (src, buf) in enumerate(((xs, xbuf), (dys, dybuf)))
            for part in range(2)
        ]

    def fetch(at, slot):
        for t in range(steps):

            @pl.when(at == t)
            def _():
                for copy in copies(t, slot):
                    copy.start()

    def weight_copy(src, d):
        if joined:
            return pltpu.make_async_copy(src, w_ref, wsems.at[0])
        return pltpu.make_async_copy(src, w_ref.at[:, (c + d) % n], wsems.at[d])

    slot = step % 2

    @pl.when(step == 0)
    def _():
        fetch(step, slot)
        weight_copy(ws[0], 0).start()
        for d in range(1, n):

            @pl.when(c + d < n)
            def _():
                weight_copy(ws[n - 1 + d], d).start()

            @pl.when(c + d >= n)
            def _():
                weight_copy(ws[n - d], d).start()

        for d in range(n):
            weight_copy(ws[0], d).wait()

    @pl.when(step + 1 < steps)
    def _():
        fetch(step + 1, 1 - slot)

    for copy in copies(0, slot):
        copy.wait()

    x = xbuf[slot]
    dy = dybuf[slot, :, :width]
    lane = lax.broadcasted_iota(jnp.int32, (rows, 128), 1)
    named = dybuf[slot, :, width:].astype(F32) > 0.5
    gates = masked_softmax(dot(x, router_ref[...], 1, 0), named)
    gates = pltpu.roll(gates, 128 - base, 1)
    w_in = w_ref[..., :both].reshape(width, both)
    w_back = w_ref[..., both:].reshape(width, both // 2)
    gu = dot(x, w_in, 1, 0)
    g = gu[:, : both // 2]
    u = gu[:, both // 2 :]
    z = dot(dy, w_back, 1, 0)
    gate = jnp.concatenate(
        [
            jnp.broadcast_to(gates[:, first + e : first + e + 1], (rows, units))
            for e in range(count)
        ],
        axis=1,
    )
    sig = 1.0 / (1.0 + jnp.exp(-g))
    silu = g * sig
    act = silu * u
    product = act.astype(BF).astype(F32) * z
    dgates = jnp.zeros((rows, 128), F32)
    for e in range(count):
        total = jnp.sum(product[:, e * units : (e + 1) * units], axis=1, keepdims=True)
        dgates = jnp.where(lane == base + first + e, total, dgates)
    gact = (gate * act).astype(BF)
    da = gate * z
    dgu = jnp.concatenate(
        [
            (da * u * (sig * (1.0 + g * (1.0 - sig)))).astype(BF),
            (da * silu).astype(BF),
        ],
        axis=1,
    )
    out = dot(gact, w_back, 1, 1)
    dx = dot(dgu, w_in, 1, 1)
    for part in range(2):
        at = slice(part * half, (part + 1) * half)
        o, d, t = out[at], dx[at], dgates[at]
        if more:
            o = o + before[part][0].astype(F32)
            d = d + before[2 + part][0, :, :width].astype(F32)
            t = t + before[2 + part][0, :, width:].astype(F32)
        outs[part][0] = o.astype(BF)
        outs[2 + part][0, :, :width] = d.astype(BF)
        outs[2 + part][0, :, width:] = t.astype(BF)
    grad_in = dot(x.T, dgu, 1, 0)
    grad_back = dot(dy.T, gact, 1, 0)

    @pl.when(step == 0)
    def _():
        acc_ref[:, :both] = grad_in
        acc_ref[:, both:] = grad_back

    @pl.when(step > 0)
    def _():
        acc_ref[:, :both] += grad_in
        acc_ref[:, both:] += grad_back

    @pl.when(step == pl.num_programs(0) - 1)
    def _():
        if joined:
            dws[0][...] = acc_ref[...].astype(BF)
        else:
            planes, _, shard, _ = w_ref.shape
            for d in range(n):
                for plane in range(planes):
                    row = pl.multiple_of((plane * n + (c + d) % n) * shard, shard)
                    dws[d][plane] = acc_ref[pl.ds(row, shard)].astype(BF)


def experts_call(xs, dys, place, router, weights, first, count, before):
    steps = len(xs) // 2
    half, width = xs[0].shape
    tile = 2 * half
    n = (len(weights) + 1) // 2
    joined = n == 1
    block = weights[0].shape
    whole_shape = block if joined else block[:1] + (n,) + block[1:]
    lanes = block[-1]
    out_block = pl.BlockSpec((1, half, width), lambda i: (i, 0, 0))
    dx_block = pl.BlockSpec((1, half, width + 128), lambda i: (i, 0, 0))
    whole = pl.BlockSpec(memory_space=pltpu.VMEM)
    anywhere = pl.BlockSpec(memory_space=pl.ANY)
    blocks = [out_block, out_block, dx_block, dx_block]
    rows = steps * tile
    return pl.pallas_call(
        functools.partial(experts_kernel, steps, first, count, bool(before), joined),
        grid=(steps,),
        in_specs=[
            pl.BlockSpec(memory_space=pltpu.SMEM),
            pl.BlockSpec((width, 128), lambda i: (0, 0)),
        ]
        + [anywhere] * (4 * steps + len(weights))
        + (blocks if before else []),
        out_specs=blocks + [whole] * n,
        out_shape=[jax.ShapeDtypeStruct((steps, half, width), BF)] * 2
        + [jax.ShapeDtypeStruct((steps, half, width + 128), BF)] * 2
        + [jax.ShapeDtypeStruct(block, BF)] * n,
        scratch_shapes=[
            pltpu.VMEM((width, lanes), F32),
            pltpu.VMEM(whole_shape, BF),
            pltpu.VMEM((2, tile, width), BF),
            pltpu.VMEM((2, tile, width + 128), BF),
            pltpu.SemaphoreType.DMA((2, 4)),
            pltpu.SemaphoreType.DMA((n,)),
        ],
        compiler_params=params("arbitrary"),
        cost_estimate=pl.CostEstimate(
            flops=6 * rows * width * lanes,
            bytes_accessed=8 * rows * width + 4 * width * lanes,
            transcendentals=rows * lanes // 3,
        ),
        name="experts",
    )(place, router, *xs, *dys, *weights, *(before or []))


def back_kernel(dq_ref, cos_ref, sin_ref, wq_ref, wkv_ref, *refs):
    *terms, dkv_ref, part_ref = refs
    total = functools.reduce(jnp.add, [t[...].astype(F32) for t in terms])
    kw = total.shape[1] // 2
    dk = turn(total[:, :kw], cos_ref[...], -sin_ref[...]).astype(BF)
    dkv = jnp.concatenate([dk, total[:, kw:].astype(BF)], axis=1)
    dkv_ref[...] = dkv
    part_ref[...] = (dot(dq_ref[...], wq_ref[...], 1, 1) + dot(dkv, wkv_ref[...], 1, 1)).astype(BF)


def back_call(dq, terms, cosine, sine, w_qo, w_kv):
    rows, qw = dq.shape
    lanes = terms[0].shape[1]
    d = w_qo.shape[0]
    tile = min(256, cosine.shape[0])
    per = cosine.shape[0] // tile
    row = lambda width: pl.BlockSpec((tile, width), lambda i: (i, 0))
    table = pl.BlockSpec((tile, 128), lambda i: (i % per, 0))
    return pl.pallas_call(
        back_kernel,
        grid=(rows // tile,),
        in_specs=[
            row(qw),
            table,
            table,
            pl.BlockSpec((d, qw), lambda i: (0, 0)),
            pl.BlockSpec((d, lanes), lambda i: (0, 0)),
        ]
        + [row(lanes)] * len(terms),
        out_specs=[row(lanes), row(d)],
        out_shape=[
            jax.ShapeDtypeStruct((rows, lanes), BF),
            jax.ShapeDtypeStruct((rows, d), BF),
        ],
        compiler_params=params("arbitrary"),
        cost_estimate=pl.CostEstimate(
            flops=2 * rows * d * (qw + lanes), bytes_accessed=8 * rows * d, transcendentals=0
        ),
        name="back",
    )(dq, cosine, sine, w_qo, w_kv, *terms)


def grads_kernel(pairs, extra, place_ref, *refs):
    refs = list(refs)
    sides = [[(refs.pop(0), refs.pop(0)) for _ in range(count)] for count in pairs]
    more = refs.pop(0) if extra else None
    count = len(refs)
    block = refs[0].shape[0]
    for s in range(count):
        at = pl.ds(pl.multiple_of((place_ref[0] ^ s) * block, block), block)
        column = 0
        for side in sides:
            total = functools.reduce(
                jnp.add, [dot(left[:, at], right[...], 0, 0) for left, right in side]
            )
            refs[s][:, column : column + total.shape[1]] = total.astype(BF)
            column += total.shape[1]
        if extra:
            refs[s][:, column:] = more[at, :]


def grads_call(me, sides, extra, count):
    d = sides[0][0][0].shape[1]
    lanes = sum(side[0][1].shape[1] for side in sides) + (0 if extra is None else extra.shape[1])
    whole = pl.BlockSpec(memory_space=pltpu.VMEM)
    operands = [a for side in sides for pair in side for a in pair]
    operands += [] if extra is None else [extra]
    return pl.pallas_call(
        functools.partial(grads_kernel, [len(side) for side in sides], extra is not None),
        in_specs=[pl.BlockSpec(memory_space=pltpu.SMEM)] + [whole] * len(operands),
        out_specs=[whole] * count,
        out_shape=[jax.ShapeDtypeStruct((d // count, lanes), BF)] * count,
        compiler_params=pltpu.CompilerParams(vmem_limit_bytes=VMEM_LIMIT),
        cost_estimate=pl.CostEstimate(
            flops=2 * d * lanes * 1024, bytes_accessed=4 * d * lanes, transcendentals=0
        ),
        name="grads",
    )(me, *operands)


def line_kernel(count, place_ref, *refs):
    terms, outs, scratch = refs[:-count - 1], refs[-count - 1 : -1], refs[-1]
    scratch[...] = functools.reduce(jnp.add, [t[...].astype(F32) for t in terms])
    shard = outs[0].shape[0]
    for s in range(count):
        row = pl.multiple_of((place_ref[0] ^ s) * shard, shard)
        outs[s][...] = scratch[pl.ds(row, shard)].astype(BF)


def line_call(me, terms, count):
    rows, lanes = terms[0].shape
    whole = pl.BlockSpec(memory_space=pltpu.VMEM)
    return pl.pallas_call(
        functools.partial(line_kernel, count),
        in_specs=[pl.BlockSpec(memory_space=pltpu.SMEM)] + [whole] * len(terms),
        out_specs=[whole] * count,
        out_shape=[jax.ShapeDtypeStruct((rows // count, lanes), BF)] * count,
        scratch_shapes=[pltpu.VMEM((rows, lanes), F32)],
        compiler_params=pltpu.CompilerParams(vmem_limit_bytes=VMEM_LIMIT),
        name="line",
    )(me, *terms)


def reorder_heads(values):
    parts = []
    for at in range(0, values.shape[1], 256):
        a = values[:, at : at + 128]
        b = values[:, at + 128 : at + 256]
        low = lax.broadcasted_iota(jnp.int32, a.shape, 1) < HD
        parts += [
            jnp.where(low, a, pltpu.roll(b, HD, 1)),
            jnp.where(low, pltpu.roll(a, HD, 1), b),
        ]
    return jnp.concatenate(parts, axis=1)


def finish_kernel(count, *refs):
    early = functools.reduce(jnp.add, [r[...].astype(F32) for r in refs[:count]])
    late = functools.reduce(jnp.add, [r[...].astype(F32) for r in refs[count : 2 * count]])
    q_ref, k_ref, v_ref, o_ref, small_ref = refs[2 * count :]
    qw = q_ref.shape[1]
    kw = k_ref.shape[1]
    q_ref[...] = reorder_heads(early[:, :qw])
    o_ref[...] = reorder_heads(early[:, qw:])
    k_ref[...] = late[:, :kw]
    v_ref[...] = late[:, kw : 2 * kw]
    small_ref[...] = late[:, 2 * kw :]


def finish_call(early, late, qw, kw):
    shard = early[0].shape[0]
    whole = pl.BlockSpec(memory_space=pltpu.VMEM)
    return pl.pallas_call(
        functools.partial(finish_kernel, len(early)),
        in_specs=[whole] * (2 * len(early)),
        out_specs=[whole] * 5,
        out_shape=[
            jax.ShapeDtypeStruct((shard, w), F32) for w in (qw, kw, kw, qw, 128)
        ],
        name="finish",
    )(*early, *late)


def expert_rows_kernel(count, place_ref, *refs):
    pieces, outs = refs[:-3], refs[-3:]
    groups = 2
    units = outs[0].shape[2]
    group = outs[0].shape[0] // (count * groups)
    for g in range(groups):
        for s in range(count):
            piece = pieces[g * count + s]
            at = ((place_ref[0] ^ s) * groups + g) * group
            for i in range(3):
                for e in range(group):
                    lanes = (i * group + e) * units
                    outs[i][at + e] = piece[:, lanes : lanes + units].astype(F32)


def expert_rows_call(me, pieces, experts, units):
    shard = pieces[0].shape[0]
    whole = pl.BlockSpec(memory_space=pltpu.VMEM)
    return pl.pallas_call(
        functools.partial(expert_rows_kernel, len(pieces) // 2),
        in_specs=[pl.BlockSpec(memory_space=pltpu.SMEM)] + [whole] * len(pieces),
        out_specs=[whole] * 3,
        out_shape=[jax.ShapeDtypeStruct((experts, shard, units), F32)] * 3,
        compiler_params=pltpu.CompilerParams(vmem_limit_bytes=VMEM_LIMIT),
        name="expert_rows",
    )(me, *pieces)


def apart(count, step):
    return [(i, i ^ step) for i in range(count)]


def swap(value):
    return lax.ppermute(value, "mp", [(0, 1), (1, 0)])


def pin(*values):
    return lax.optimization_barrier(values)


def up_hop(value, n, s):
    return lax.ppermute(value, "ctx", [(c, c + 1) for c in range(s, n - 1)])


def down_hop(value, n, s):
    return lax.ppermute(value, "ctx", [(c, c - 1) for c in range(1, n - s)])


def sum_up_hop(value, n, s):
    return lax.ppermute(value, "ctx", [(c, c + 1) for c in range(s + 1)])


def sum_down_hop(value, n, s):
    return lax.ppermute(value, "ctx", [(c, c - 1) for c in range(n - 1 - s, n)])


def add(*terms):
    return functools.reduce(jnp.add, [t.astype(F32) for t in terms]).astype(BF)


def by_xor(parts, me):
    bit = 1
    while bit < len(parts):
        flip = (me & bit) != 0
        parts = [jnp.where(flip, parts[i ^ bit], parts[i]) for i in range(len(parts))]
        bit *= 2
    return parts


def exchange(parts, axis):
    count = len(parts)
    return [parts[0]] + [
        lax.ppermute(parts[s], axis, apart(count, s)) for s in range(1, count)
    ]


def from_last(values, start, count):
    values = values[::-1]
    return lax.dynamic_slice_in_dim(jnp.concatenate([values, values]), start, count, 0)


def head_order(weight):
    rows, width = weight.shape
    return (
        weight.reshape(rows, width // (4 * HD), 2, 2, HD).swapaxes(2, 3).reshape(rows, width)
    )


def per_device(
    tokens,
    cotangent,
    routes,
    norm_gain,
    w_query,
    w_key,
    w_value,
    w_output,
    ffn_gain,
    w_router,
    w_gate,
    w_up,
    w_down,
):
    micro, seq_count, local, width = tokens.shape
    top = routes.shape[3]
    experts, shard, units = w_gate.shape
    dp = lax.axis_size("dp")
    n = lax.axis_size("ctx")
    hops = n == 4
    me_dp = lax.axis_index("dp")
    me_ctx = lax.axis_index("ctx")
    me_mp = lax.axis_index("mp")
    mine_count = experts // dp
    group = mine_count // 2
    micros = range(micro)
    per = seq_count * local
    half = per // 2
    rows = micro * per
    qw = w_query.shape[1]
    kw = w_key.shape[1]
    ctx_now = me_ctx.astype(jnp.int32).reshape(1)
    dp_now = me_dp.astype(jnp.int32).reshape(1)
    place = jnp.stack([me_dp * mine_count, me_ctx]).astype(jnp.int32)

    def in_order(mine, other):
        first = me_mp == 0
        return jnp.concatenate([jnp.where(first, mine, other), jnp.where(first, other, mine)])

    def halves(full):
        cut = full.reshape(2, half, full.shape[1])
        mine = lax.dynamic_index_in_dim(cut, me_mp, 0, keepdims=False)
        return mine, lax.dynamic_index_in_dim(cut, 1 - me_mp, 0, keepdims=False)

    def far_pieces(mine):
        return [lax.ppermute(mine, "dp", apart(dp, s)) for s in range(1, dp)]

    def paired(mine, far, other, near):
        return [piece for pair in zip([mine] + far, [other] + near) for piece in pair]

    def gather_line(value):
        return jnp.stack(
            [value] + [lax.ppermute(value, "ctx", apart(n, s)) for s in range(1, n)]
        )

    def gather_plane(value):
        return [value] + [lax.ppermute(value, "dp", apart(dp, s)) for s in range(1, dp)]

    def whole_rows(pieces):
        lines = by_xor(pieces, me_dp)
        full = jnp.stack(lines)
        cols = by_xor([full[:, i] for i in range(n)], me_ctx)
        return jnp.stack(cols, axis=1).reshape(dp * n * shard, full.shape[3])

    small = jnp.concatenate([w_router, norm_gain[:, None], ffn_gain[:, None]], axis=1)
    small = jnp.pad(small, ((0, 0), (0, 128 - small.shape[1])))
    kv_shard = jnp.concatenate([w_key, w_value, small], axis=1)
    qo_shard = jnp.concatenate([head_order(w_query), head_order(w_output)], axis=1)
    side = lambda w: w.reshape(dp, 2, group, shard, units)
    w3 = jnp.concatenate(
        [side(w)[:, :, e] for w in (w_gate, w_up, w_down) for e in range(group)], axis=3
    )
    if hops:
        kv_line = gather_line(kv_shard)
        qo_line = gather_line(qo_shard)
    w3_parts = exchange(by_xor([w3[i] for i in range(dp)], me_dp), "dp")
    own3 = by_xor(w3_parts, me_dp)
    own3 = [jnp.stack([o[g] for o in own3]) for g in range(2)]
    ups = [[], []]
    downs = [[], []]

    def weight_hop(g, s):
        if hops:
            ups[g].append(up_hop(ups[g][-1] if s else own3[g], n, s))
            downs[g].append(down_hop(downs[g][-1] if s else own3[g], n, s))

    if hops:
        kv_line, qo_line, own3 = pin(kv_line, qo_line, own3)
        kv_pieces = gather_plane(kv_line)
        weight_hop(0, 0)
        kv_pieces, qo_line, ups, downs, own3 = pin(kv_pieces, qo_line, ups, downs, own3)
        kv_full = whole_rows(kv_pieces)
        qo_pieces = gather_plane(qo_line)
    else:
        kv_full = lax.all_gather(kv_shard, ("dp", "ctx"), axis=0, tiled=True)
        qo_full = lax.all_gather(qo_shard, ("dp", "ctx"), axis=0, tiled=True)
        own3 = [lax.all_gather(o, "ctx", axis=1, tiled=False) for o in own3]
        own3 = [o.reshape(width, o.shape[-1]) for o in own3]
    small = kv_full[:, 2 * kw :]
    router = small[:, :experts]
    router_wide = jnp.pad(router, ((0, 0), (0, 128 - experts)))
    gain_one = small[:, experts].astype(F32)[None, :]
    gain_two = small[:, experts + 1].astype(F32)[None, :]

    position = me_ctx * local + jnp.arange(local, dtype=jnp.int32)
    freqs = THETA ** (-(jnp.arange(HD // 2, dtype=F32) * 2.0) / HD)
    angles = position.astype(F32)[:, None] * freqs[None, :]
    cosine = jnp.tile(jnp.cos(angles), (1, 4))
    sine = jnp.sin(angles)
    sine = jnp.concatenate([-sine, sine, -sine, sine], axis=1)
    x = tokens.reshape(rows, width)
    normed, kv = kv_call(x, gain_one, kv_full, 2 * kw, cosine, sine)
    kv = kv.reshape(1, micro * seq_count, local, 2 * kw)

    ids = routes.reshape(rows, top)
    marks = jnp.sum(
        (ids[:, :, None] == jnp.arange(128, dtype=jnp.int32)[None, None, :]).astype(F32), axis=1
    ).astype(BF)
    dy = cotangent.reshape(rows, width)
    dyx = jnp.concatenate([dy, marks], axis=1).reshape(micro, per, width + 128)
    dy_cut = [halves(dyx[m]) for m in micros]
    dy_far = [None] * micro
    dy_near = [None] * micro

    if hops:
        kv_got = up_hop(kv, n, 0)
        kv_got, qo_pieces, normed, dy_cut = pin(kv_got, qo_pieces, normed, dy_cut)
        kv_prev = [kv_got]
        qo_full = whole_rows(qo_pieces)
    else:
        every = lax.all_gather(kv[0], "ctx", axis=0, tiled=False)
        kv_prev = [from_last(every, n - me_ctx, n - 1)]
    w_out = qo_full[:, qw:]
    q = q_call(normed, qo_full, qw, cosine, sine).reshape(micro * seq_count, local, qw)
    if hops:
        carry = None
        own = kv
        for s in range(1, n):
            last = s == n - 1
            got = None if last else up_hop(kv_prev[-1], n, s)
            if s - 1 < micro:
                dy_far[s - 1] = far_pieces(dy_cut[s - 1][0])
            else:
                weight_hop(0, 1)
            if s >= 2:
                dy_near[s - 2] = [swap(f) for f in dy_far[s - 2]]
            carry = attn_part(ctx_now, q, own, [kv_prev[-1]], s, carry, last)
            if last:
                attn, lse = carry
                mixed = dot(attn.reshape(rows, qw), w_out, 1, 1).astype(BF)
                mixed, dy_near, ups, downs = pin(mixed, dy_near, ups, downs)
            else:
                got, carry, dy_far, dy_near = pin(got, carry, dy_far, dy_near)
                kv_prev.append(got)
            own = None
    else:
        attn, lse = attn_part(ctx_now, q, kv, kv_prev, 1, None, True)
        mixed = dot(attn.reshape(rows, qw), w_out, 1, 1).astype(BF)
    for m in micros:
        if dy_far[m] is None:
            dy_far[m] = far_pieces(dy_cut[m][0])
        if dy_near[m] is None:
            dy_near[m] = [swap(f) for f in dy_far[m]]
    dys = [paired(dy_cut[m][0], dy_far[m], dy_cut[m][1], dy_near[m]) for m in micros]

    mixed_got = swap(mixed)
    hidden = x.astype(F32) + (mixed.astype(F32) + mixed_got.astype(F32))
    inv_two = lax.rsqrt(jnp.mean(hidden * hidden, axis=1, keepdims=True) + EPS)
    ffn_low = (hidden * inv_two * gain_two).astype(BF)
    x_cut = [halves(ffn_low[m * per : (m + 1) * per]) for m in micros]
    x_far = [None] * micro
    x_near = [None] * micro

    x_cut, hidden, inv_two, ffn_low = pin(x_cut, hidden, inv_two, ffn_low)
    x_far[0] = far_pieces(x_cut[0][0])
    weight_hop(0, 2)
    x_far[0], ups, downs, x_cut = pin(x_far[0], ups, downs, x_cut)
    x_near[0] = [swap(f) for f in x_far[0]]
    x_near[0], x_cut = pin(x_near[0], x_cut)
    sums = []
    dws = [[], []]
    xs = []

    def run(g, m, before):
        whole = [own3[g]] + ups[g] + downs[g]
        part = experts_call(
            xs[m], dys[m], place, router_wide, whole, g * group, group, before
        )
        dws[g].append(part[4:])
        return part[:4]

    for m in micros:
        xs.append(paired(x_cut[m][0], x_far[m], x_cut[m][1], x_near[m]))
        sums.append(run(0, m, None))
        if m + 1 < micro:
            x_far[m + 1] = far_pieces(x_cut[m + 1][0])
        weight_hop(1, m)
        sums, dws, x_far, x_cut, ups, downs = pin(sums, dws, x_far, x_cut, ups, downs)
        if m + 1 < micro:
            x_near[m + 1] = [swap(f) for f in x_far[m + 1]]
            x_near, sums, x_cut, ups, downs = pin(x_near, sums, x_cut, ups, downs)
    if hops:
        for s in range(micro, n - 1):
            weight_hop(1, s)

    rising = [None, None]
    falling = [None, None]

    def grad_hop(g, s):
        if hops:
            d = n - 1 - s
            up_terms = [dw[d] for dw in dws[g]] + ([rising[g]] if s else [])
            down_terms = [dw[n - d] for dw in dws[g]] + ([falling[g]] if s else [])
            rising[g] = sum_up_hop(add(*up_terms), n, s)
            falling[g] = sum_down_hop(add(*down_terms), n, s)

    def grad_own(g):
        if hops:
            own = add(*[dw[0] for dw in dws[g]], rising[g], falling[g])
        else:
            whole = add(*[dw[0] for dw in dws[g]]).reshape(dp, n, shard, -1)
            own = lax.psum_scatter(whole, "ctx", scatter_dimension=1, tiled=False)
        return exchange(by_xor([own[i] for i in range(dp)], me_dp), "dp")

    parts = []
    dx_terms = []
    dx_back = []

    def terms_of(mine, got):
        return [add(mine[s], got[s]) for s in range(dp)]

    for m in micros:
        parts.append(run(1, m, sums[m]))
        if m > 0:
            dx_back.append(exchange(dx_terms[m - 1], "dp"))
        grad_hop(0, m)
        parts, dx_back, rising, falling, dws = pin(parts, dx_back, rising, falling, dws)
        if m + 1 < micro:
            dx_terms.append(terms_of(parts[m][2], swap(parts[m][3])))
            dx_terms, parts, dx_back = pin(dx_terms, parts, dx_back)

    cut = lambda whole, m: whole[m * per : (m + 1) * per]
    marked = dyx.reshape(rows, width + 128)[:, width : width + experts].astype(F32) > 0.5
    gates = masked_softmax(dot(ffn_low, router, 1, 0), marked)
    grad_sums = [0.0, 0.0]

    def before_attention(m):
        total = add(*dx_back[m])
        moe = in_order(total, swap(total)).astype(F32)
        dgate = moe[:, width : width + experts]
        gate = cut(gates, m)
        dlogit = gate * (dgate - jnp.sum(gate * dgate, axis=1, keepdims=True))
        dlogit = dlogit.astype(BF)
        grad_sums[0] = grad_sums[0] + dot(cut(ffn_low, m), dlogit, 0, 0)
        d_ffn = moe[:, :width] + dot(dlogit, router, 1, 1)
        unit = cut(hidden, m) * cut(inv_two, m)
        grad_sums[1] = grad_sums[1] + jnp.sum(d_ffn * unit, axis=0)
        g_two = d_ffn * gain_two
        dh = cut(dy, m).astype(F32) + cut(inv_two, m) * (
            g_two - unit * jnp.mean(g_two * unit, axis=1, keepdims=True)
        )
        dz = dh.astype(BF)
        return dh, dz, dot(dz, w_out, 1, 0).astype(BF)

    def attention_back(m, d_attn):
        dq, *dkv = attn_bwd(
            ctx_now,
            q,
            d_attn.reshape(seq_count, local, qw),
            attn,
            lse,
            cosine,
            sine,
            kv,
            kv_prev,
            m * seq_count,
        )
        return dq.reshape(per, qw), dkv

    dkv_sum = [None] * micro

    def dkv_hop(m, s):
        if hops:
            d = n - 1 - s
            term = dkv[m][d] if s == 0 else add(dkv[m][d], dkv_sum[m])
            dkv_sum[m] = sum_down_hop(term, n, s)

    def dkv_own(m):
        if hops:
            both = [dkv[m][0], dkv_sum[m]]
        else:
            every = from_last(jnp.concatenate(dkv[m]), n - 1 - me_ctx, n)
            both = [lax.psum_scatter(every, "ctx", scatter_dimension=0, tiled=True)]
        return [b.reshape(per, 2 * kw) for b in both]

    dh, dz, d_attn, dq, dkv = ([None] * micro for _ in range(5))
    out_terms = [None] * micro
    out_back = [None] * micro
    last = micro - 1
    dh[0], dz[0], d_attn[0] = before_attention(0)
    dx_terms.append(terms_of(parts[last][2], swap(parts[last][3])))
    d_attn, dx_terms, dh, dz = pin(d_attn, dx_terms, dh, dz)
    dx_back.append(exchange(dx_terms[last], "dp"))
    dq[0], dkv[0] = attention_back(0, d_attn[0])
    grad_hop(0, 2)
    dx_back, dq, dkv, rising, falling = pin(dx_back, dq, dkv, rising, falling)
    dkv_hop(0, 0)
    dh[last], dz[last], d_attn[last] = before_attention(last)
    d_attn, dkv_sum, dh, dz, dkv = pin(d_attn, dkv_sum, dh, dz, dkv)
    dkv_hop(0, 1)
    grad_hop(1, 0)
    dq[last], dkv[last] = attention_back(last, d_attn[last])
    dkv_sum, dq, dkv, rising, falling, parts = pin(dkv_sum, dq, dkv, rising, falling, parts)
    dkv_hop(0, 2)
    dkv_hop(last, 0)
    pieces_now = dp_now if hops else jnp.zeros((1,), jnp.int32)
    early = grads_call(
        pieces_now,
        [
            [(cut(normed, m), dq[m]) for m in micros],
            [(dz[m], attn[m * seq_count : (m + 1) * seq_count].reshape(per, qw)) for m in micros],
        ],
        None,
        dp,
    )
    out_got = [swap(parts[m][1]) for m in micros]
    early, out_got, dkv_sum, dkv, parts = pin(early, out_got, dkv_sum, dkv, parts)
    dkv_hop(last, 1)
    grad_hop(1, 1)
    if hops:
        early = exchange(early, "dp")
    owned = [grad_own(0)]
    out_terms = [terms_of(parts[m][0], out_got[m]) for m in micros]
    dkv_own_m, part = [None] * micro, [None] * micro

    def back(m):
        return back_call(dq[m], dkv_own(m), cosine, sine, qo_full, kv_full)

    dkv_own_m[0], part[0] = back(0)
    early, out_terms, dkv_sum, rising, falling, owned, part, dkv, dkv_own_m = pin(
        early, out_terms, dkv_sum, rising, falling, owned, part, dkv, dkv_own_m
    )
    dkv_hop(last, 2)
    if hops:
        early = exchange(line_call(ctx_now, early, n), "ctx")
    out_back[0] = exchange(out_terms[0], "dp")
    early, dkv_sum, out_back, out_terms, part, dkv = pin(
        early, dkv_sum, out_back, out_terms, part, dkv
    )
    grad_hop(1, 2)
    dkv_own_m[last], part[last] = back(last)
    got = [swap(p) for p in part]
    rows_late = [(cut(normed, m), dkv_own_m[m]) for m in micros]
    d_normed = jnp.concatenate([p.astype(F32) + g.astype(F32) for p, g in zip(part, got)])
    out_back[last] = exchange(out_terms[last], "dp")
    got, d_normed, out_back, rising, falling = pin(got, d_normed, out_back, rising, falling)
    x32 = x.astype(F32)
    inv_one = lax.rsqrt(jnp.mean(x32 * x32, axis=1, keepdims=True) + EPS)
    n_one = x32 * inv_one
    grad_gain_one = jnp.sum(d_normed * n_one, axis=0)
    small_grad = jnp.concatenate(
        [grad_sums[0], grad_gain_one[:, None], grad_sums[1][:, None]], axis=1
    )
    small_grad = jnp.pad(small_grad, ((0, 0), (0, 128 - small_grad.shape[1]))).astype(BF)
    late = grads_call(pieces_now, [rows_late], small_grad, dp)
    if hops:
        late = exchange(late, "dp")
        late = exchange(line_call(ctx_now, late, n), "ctx")
    else:
        early, late = (
            [
                lax.psum_scatter(
                    jnp.concatenate(p), ("dp", "ctx"), scatter_dimension=0, tiled=True
                )
            ]
            for p in (early, late)
        )
    owned.append(grad_own(1))
    g_one = d_normed * gain_one
    input_grad = (
        jnp.concatenate(dh)
        + inv_one * (g_one - n_one * jnp.mean(g_one * n_one, axis=1, keepdims=True))
    ).astype(BF)
    totals = [add(*b) for b in out_back]
    moe = jnp.concatenate([in_order(t, swap(t)) for t in totals])
    output = (hidden + moe.astype(F32)).astype(BF)
    grad_q, grad_k, grad_v, grad_o, small_grad = finish_call(early, late, qw, kw)
    dw_gate, dw_up, dw_down = expert_rows_call(dp_now, owned[0] + owned[1], experts, units)
    shape = tokens.shape
    return (
        output.reshape(shape),
        input_grad.reshape(shape),
        small_grad[:, experts],
        grad_q,
        grad_k,
        grad_v,
        grad_o,
        small_grad[:, experts + 1],
        small_grad[:, :experts],
        dw_gate,
        dw_up,
        dw_down,
    )


def solution(mesh):
    rows = P(None, "dp", "ctx", None)
    vector = P(("dp", "ctx"))
    matrix = P(("dp", "ctx"), "mp")
    router = P(("dp", "ctx"), None)
    expert = P(None, ("dp", "ctx"), "mp")
    return jax.shard_map(
        per_device,
        mesh=mesh,
        in_specs=(
            rows,
            rows,
            rows,
            vector,
            matrix,
            matrix,
            matrix,
            matrix,
            vector,
            router,
            expert,
            expert,
            expert,
        ),
        out_specs=(
            rows,
            rows,
            vector,
            matrix,
            matrix,
            matrix,
            matrix,
            vector,
            router,
            expert,
            expert,
            expert,
        ),
        check_vma=False,
    )
```

time: 960 us -> 731 us (0.76)
  waiting for transfers between devices: 563 us -> 180 us
  starting transfers between devices: 24.8 us -> 196 us
  Pallas kernels: 136 us -> 208 us
  local copies, waits for them, and re-layouts: 97.4 us -> 34.6 us
  blocking collectives: 54.6 us -> 0 us
  other arithmetic: 44.7 us -> 89.6 us
  between operations: 15.2 us -> 2.96 us
    reduce_scatter x2 -> x0, waiting for transfers between devices: 209 us -> none  [the longest x1 121 us: per_device(): lax.psum_scatter(jnp.concatenate([dk, dv], axis=2), 'ctx', scatter_dimens...]
    ppermute x18 -> x90, starting transfers between devices: 22.3 us -> 192 us  [the longest x33 61.9 us: exchange(): lax.ppermute(parts[s], axis, apart(count, s))]
    all_gather x3 -> x0, waiting for transfers between devices: 126 us -> none  [the longest x1 70.1 us: per_device(): full = lax.all_gather(packed, ('dp', 'ctx'), axis=0, tiled=True)]
    pallas_call x4 -> x19, Pallas kernels: 136 us -> 208 us  [the longest x4 128 us: experts_call(): pl.pallas_call(functools.partial(experts_kernel, steps, first, count, boo...]
    all_to_all x2 -> x0, blocking collectives: 54.6 us -> none  [the longest x1 33.2 us: per_device(): lax.all_to_all(dw, 'dp', split_axis=2, concat_axis=1, tiled=True)]
    unnamed x7 -> x0, waiting for transfers between devices: 48.7 us -> none
    convert_element_type x8 -> x32, other arithmetic: 15.1 us -> 58 us  [the longest x24 45.5 us: add(): return functools.reduce(jnp.add, [t.astype(F32) for t in terms]).astype(BF)]
    unnamed x96 -> x233, local copies, waits for them, and re-layouts: 38.5 us -> 21.7 us
  transfers between devices with their start and end apart: 35 -> 113, of which waited for: 19 -> 36; matrix products, arithmetic and copies ran while one was open for 11% -> 14% of each run, Pallas kernels for 1% -> 27%
where the time goes in v2:
time: 731 us; the launch traced here: 722 us
  Pallas kernels  208 us (28%)
  starting transfers between devices  196 us (27%)
  waiting for transfers between devices  180 us (25%)
  other arithmetic  89.6 us (12%)
  local copies, waits for them, and re-layouts  34.6 us (5%)
  matrix products  10.2 us (1%)
    pallas_call x4, Pallas kernels, experts_call(): pl.pallas_call(functools.partial(experts_kernel, steps, first, count, boo...  128 us
    ppermute x33, starting transfers between devices, exchange(): lax.ppermute(parts[s], axis, apart(count, s))  61.9 us
    ppermute x33, waiting for transfers between devices, exchange(): lax.ppermute(parts[s], axis, apart(count, s))  58.7 us
    ppermute x6, starting transfers between devices, sum_up_hop(): return lax.ppermute(value, 'ctx', [(c, c + 1) for c in range(s + 1)])  53.6 us
    convert_element_type x24, other arithmetic, add(): return functools.reduce(jnp.add, [t.astype(F32) for t in terms]).astype(BF)  45.5 us
    ppermute x12, waiting for transfers between devices, far_pieces(): return [lax.ppermute(mine, 'dp', apart(dp, s)) for s in range(1, dp)]  40.5 us
    ppermute x6, waiting for transfers between devices, gather_plane(): lax.ppermute(value, 'dp', apart(dp, s))  29.5 us
    ppermute x6, waiting for transfers between devices, down_hop(): return lax.ppermute(value, 'ctx', [(c, c - 1) for c in range(1, n - s)])  26.1 us
  transfers between devices with their start and end apart: 113, of which 36 were waited for; matrix products, arithmetic and copies ran while one was open for 14% of the time, Pallas kernels for 27%

profile of v2, /device:TPU:0, one launch (start us, length us, event | category | flops | bytes accessed | tf_op | source)
XLA Modules:
  0.0 722.1 jit_solution(18040343699365990139)
XLA Ops:
  2.3 5.1 collective-permute-start.2
  20.6 4.3 collective-permute-done
  27.3 4.4 collective-permute-done.4
  36.4 3.5 collective-permute-start.12
  47.7 4.2 collective-permute-done.9
  51.9 7.0 collective-permute-done.10
  63.0 5.7 kv.1
  68.7 4.6 collective-permute-start.14
  73.5 5.8 convert_reduce_fusion
  85.8 8.4 %collective-permute-done.15 = bf16[4,64,1024]{2,1,0:T(8,128)(2,1)S(1)} collective-permute-done((bf16[4,64,1024]{2,1,0:T(8,128)(2,1)S(1)}, bf16[4,64,1024]{2,1,0:T(8,128)(2,1)S(1)}, u32[]{:S(2)}, u32[]{:S(2)}) %collective-permute-start.15) | collective-permute-done | bytes 524320 | tf_op jit(solution)/shard_map/ppermute | solution.py:846
  94.2 10.0 %collective-permute-done.16 = bf16[4,64,1024]{2,1,0:T(8,128)(2,1)S(1)} collective-permute-done((bf16[4,64,1024]{2,1,0:T(8,128)(2,1)S(1)}, bf16[4,64,1024]{2,1,0:T(8,128)(2,1)S(1)}, u32[]{:S(2)}, u32[]{:S(2)}) %collective-permute-start.16) | collective-permute-done | bytes 524320 | tf_op jit(solution)/shard_map/ppermute | solution.py:846
  112.3 5.7 q.1
  120.8 8.0 %attn_fwd.3 = (f32[2,2,4,1024]{3,2,1,0:T(4,128)}, f32[2,2,2,128,1024]{4,3,2,1,0:T(8,128)}) custom-call(s32[1]{0:T(128)} %bitcast.1.ctx_ref.place_ref, bf16[2,512,512]{2,1,0:T(8,128)(2,1)} %bitcast.236, bf16[1,2,512,512]{3,2,1,0:T(8,128)(2,1)} %bitcast.276, bf16[1,2,512,512]{3,2,1,0:T(8,128)(2,1)} %collective-permute-done.14.refs_1_.refs_3_.refs_5_, ...), custom_call_target="tpu_custom_call" | custom-call | flops 8589934592 | bytes 4194304 | tf_op jit(solution)/shard_map/attn_fwd/pallas_call | solution.py:245
  135.4 10.4 %collective-permute-done.23.refs_10_ = bf16[256,1152]{1,0:T(8,128)(2,1)} collective-permute-done((bf16[256,1152]{1,0:T(8,128)(2,1)S(1)}, bf16[256,1152]{1,0:T(8,128)(2,1)}, u32[]{:S(2)}, u32[]{:S(2)}) %collective-permute-start.23) | collective-permute-done | bytes 589856 | tf_op jit(solution)/shard_map/ppermute | solution.py:835
  145.8 9.3 %collective-permute-done.24.refs_12_ = bf16[256,1152]{1,0:T(8,128)(2,1)} collective-permute-done((bf16[256,1152]{1,0:T(8,128)(2,1)S(1)}, bf16[256,1152]{1,0:T(8,128)(2,1)}, u32[]{:S(2)}, u32[]{:S(2)}) %collective-permute-start.24) | collective-permute-done | bytes 589856 | tf_op jit(solution)/shard_map/ppermute | solution.py:835
  158.0 5.5 attn_fwd.4
  164.7 5.0 attn_fwd.5
  172.6 6.2 collective-permute-done.33.refs_21_
  193.0 8.8 %collective-permute-done.39.refs_22_ = bf16[4,64,1536]{2,1,0:T(8,128)(2,1)S(1)} collective-permute-done((bf16[4,64,1536]{2,1,0:T(8,128)(2,1)}, bf16[4,64,1536]{2,1,0:T(8,128)(2,1)S(1)}, u32[]{:S(2)}, u32[]{:S(2)}) %collective-permute-start.39) | collective-permute-done | bytes 786464 | tf_op jit(solution)/shard_map/ppermute | solution.py:746
  204.3 11.6 %collective-permute-done.36.refs_4_ = bf16[256,1024]{1,0:T(8,128)(2,1)} collective-permute-done((bf16[256,1024]{1,0:T(8,128)(2,1)S(1)}, bf16[256,1024]{1,0:T(8,128)(2,1)}, u32[]{:S(2)}, u32[]{:S(2)}) %collective-permute-start.36) | collective-permute-done | bytes 524320 | tf_op jit(solution)/shard_map/ppermute | solution.py:835
  217.2 4.3 collective-permute-start.46
  227.1 31.3 %experts.4 = (bf16[4,256,1024]{2,1,0:T(8,128)(2,1)}, bf16[4,256,1024]{2,1,0:T(8,128)(2,1)}, bf16[4,256,1152]{2,1,0:T(8,128)(2,1)}, bf16[4,256,1152]{2,1,0:T(8,12...) custom-call(s32[2]{0:T(128)} %pad_add_fusion.place_ref, ...), custom_call_target="tpu_custom_call" | custom-call | flops 19327352832 | bytes 23068672 | tf_op jit(solution)/shard_map/experts/pallas_call | solution.py:527
  266.3 31.4 %experts.5 = (bf16[4,256,1024]{2,1,0:T(8,128)(2,1)}, bf16[4,256,1024]{2,1,0:T(8,128)(2,1)}, bf16[4,256,1152]{2,1,0:T(8,128)(2,1)}, bf16[4,256,1152]{2,1,0:T(8,12...) custom-call(s32[2]{0:T(128)} %pad_add_fusion.place_ref, ...), custom_call_target="tpu_custom_call" | custom-call | flops 19327352832 | bytes 23068672 | tf_op jit(solution)/shard_map/experts/pallas_call | solution.py:527
  303.2 10.7 %collective-permute-start.55 = (bf16[4,64,1536]{2,1,0:T(8,128)(2,1)}, bf16[4,64,1536]{2,1,0:T(8,128)(2,1)}, u32[]{:S(2)}, u32[]{:S(2)}) collective-permute-start(bf16[4,64,1536]{2,1,0:T(8,128)(2,1)} %add_convert_fusion.12), channel_id=1, source_target_pairs={{0,2},{1,3},{8,10},{9,11},{16,18},{17,19},{24,26},{25,27}} | collective-permute-start | bytes 2359304 | tf_op jit(solution)/shard_map/ppermute | solution.py:750
  316.7 8.9 %collective-permute-done.54.refs_22_ = bf16[4,64,1536]{2,1,0:T(8,128)(2,1)} collective-permute-done((bf16[4,64,1536]{2,1,0:T(8,128)(2,1)}, bf16[4,64,1536]{2,1,0:T(8,128)(2,1)}, u32[]{:S(2)}, u32[]{:S(2)}) %collective-permute-start.54) | collective-permute-done | bytes 786464 | tf_op jit(solution)/shard_map/ppermute | solution.py:746
  325.6 32.4 %experts.6 = (bf16[4,256,1024]{2,1,0:T(8,128)(2,1)}, bf16[4,256,1024]{2,1,0:T(8,128)(2,1)}, bf16[4,256,1152]{2,1,0:T(8,128)(2,1)}, bf16[4,256,1152]{2,1,0:T(8,12...) custom-call(s32[2]{0:T(128)} %pad_add_fusion.place_ref, ...), custom_call_target="tpu_custom_call" | custom-call | flops 19327352832 | bytes 23068672 | tf_op jit(solution)/shard_map/experts/pallas_call | solution.py:527
  379.6 32.5 %experts.7 = (bf16[4,256,1024]{2,1,0:T(8,128)(2,1)}, bf16[4,256,1024]{2,1,0:T(8,128)(2,1)}, bf16[4,256,1152]{2,1,0:T(8,128)(2,1)}, bf16[4,256,1152]{2,1,0:T(8,12...) custom-call(s32[2]{0:T(128)} %pad_add_fusion.place_ref, ...), custom_call_target="tpu_custom_call" | custom-call | flops 19327352832 | bytes 23068672 | tf_op jit(solution)/shard_map/experts/pallas_call | solution.py:527
  436.7 10.9 %attn_bwd.2 = (bf16[1,512,512]{2,1,0:T(8,128)(2,1)}, bf16[1,1,512,512]{3,2,1,0:T(8,128)(2,1)}, bf16[1,1,512,512]{3,2,1,0:T(8,128)(2,1)}, bf16[1,1,512,512]{3,2,1,0:T(8,128)(2,1)}, bf16[1,1,512,512]{3,2,1,0:T(8,128)(2,1)}) custom-call(s32[1]{0:T(128)} %bitcast.1.ctx_ref.place_ref, bf16[2,512,512]{2,1,0:T(8,128)(2,1)} %bitcast.239, ...), custom_call_target="tpu_custom_call" | custom-call | flops 21474836480 | bytes 8388608 | tf_op jit(solution)/shard_map/attn_bwd/pallas_call | solution.py:335
  449.8 11.7 %collective-permute-done.66 = bf16[256,1152]{1,0:T(8,128)(2,1)} collective-permute-done((bf16[256,1152]{1,0:T(8,128)(2,1)}, bf16[256,1152]{1,0:T(8,128)(2,1)}, u32[]{:S(2)}, u32[]{:S(2)}) %collective-permute-start.66) | collective-permute-done | bytes 589856 | tf_op jit(solution)/shard_map/ppermute | solution.py:773
  464.7 5.2 collective-permute-start.73
  483.3 10.1 %attn_bwd.3 = (bf16[1,512,512]{2,1,0:T(8,128)(2,1)}, bf16[1,1,512,512]{3,2,1,0:T(8,128)(2,1)}, bf16[1,1,512,512]{3,2,1,0:T(8,128)(2,1)}, bf16[1,1,512,512]{3,2,1,0:T(8,128)(2,1)}, bf16[1,1,512,512]{3,2,1,0:T(8,128)(2,1)}) custom-call(s32[1]{0:T(128)} %bitcast.1.ctx_ref.place_ref, bf16[2,512,512]{2,1,0:T(8,128)(2,1)} %bitcast.240, ...), custom_call_target="tpu_custom_call" | custom-call | flops 21474836480 | bytes 8388608 | tf_op jit(solution)/shard_map/attn_bwd/pallas_call | solution.py:335
  501.5 31.1 %collective-permute-start.83 = (bf16[4,64,1536]{2,1,0:T(8,128)(2,1)}, bf16[4,64,1536]{2,1,0:T(8,128)(2,1)}, u32[]{:S(2)}, u32[]{:S(2)}) collective-permute-start(bf16[4,64,1536]{2,1,0:T(8,128)(2,1)} %get-tuple-element.874), channel_id=1, source_target_pairs={{0,2},{2,4},{1,3},{3,5},{8,10},{10,12},{9,11},{11,13},{16,18},{18,... | collective-permute-start | bytes 2359304 | tf_op jit(solution)/shard_map/ppermute | solution.py:750
  534.5 6.0 grads.2
  547.8 4.5 back.2
  557.9 4.2 fusion.30
  562.1 3.5 fusion.34
  567.6 9.3 %collective-permute-done.80.refs_2_ = bf16[256,1024]{1,0:T(8,128)(2,1)} collective-permute-done((bf16[256,1024]{1,0:T(8,128)(2,1)}, bf16[256,1024]{1,0:T(8,128)(2,1)}, u32[]{:S(2)}, u32[]{:S(2)}) %collective-permute-start.80) | collective-permute-done | bytes 524320 | tf_op jit(solution)/shard_map/ppermute | solution.py:773
  579.6 14.1 %collective-permute-start.88 = (bf16[64,1024]{1,0:T(8,128)(2,1)}, bf16[64,1024]{1,0:T(8,128)(2,1)S(1)}, u32[]{:S(2)}, u32[]{:S(2)}) collective-permute-start(bf16[64,1024]{1,0:T(8,128)(2,1)} %get-tuple-element.686), channel_id=1, source_target_pairs={{0,2},{2,0},{4,6},{6,4},{1,3},{3,1},{5,7},{7,5},{8,10},{10,8},{12,... | collective-permute-start | bytes 393224 | tf_op jit(solution)/shard_map/ppermute | solution.py:773
  601.3 9.0 %collective-permute-start.89 = (bf16[64,1024]{1,0:T(8,128)(2,1)S(1)}, bf16[64,1024]{1,0:T(8,128)(2,1)}, u32[]{:S(2)}, u32[]{:S(2)}) collective-permute-start(bf16[64,1024]{1,0:T(8,128)(2,1)S(1)} %copy-done.111), channel_id=1, source_target_pairs={{0,4},{2,6},{4,0},{6,2},{1,5},{3,7},{5,1},{7,3},{8,12},{10,14},{12... | collective-permute-start | bytes 393224 | tf_op jit(solution)/shard_map/ppermute | solution.py:773
  610.3 11.1 %collective-permute-done.89.refs_2_ = bf16[64,1024]{1,0:T(8,128)(2,1)} collective-permute-done((bf16[64,1024]{1,0:T(8,128)(2,1)S(1)}, bf16[64,1024]{1,0:T(8,128)(2,1)}, u32[]{:S(2)}, u32[]{:S(2)}) %collective-permute-start.89) | collective-permute-done | bytes 131104 | tf_op jit(solution)/shard_map/ppermute | solution.py:773
  621.7 6.5 collective-permute-done.90.refs_3_
  629.6 4.6 back.3
  646.0 8.9 %collective-permute-done.100 = bf16[4,64,1536]{2,1,0:T(8,128)(2,1)S(1)} collective-permute-done((bf16[4,64,1536]{2,1,0:T(8,128)(2,1)S(1)}, bf16[4,64,1536]{2,1,0:T(8,128)(2,1)S(1)}, u32[]{:S(2)}, u32[]{:S(2)}) %collective-permute-start.100) | collective-permute-done | bytes 786464 | tf_op jit(solution)/shard_map/ppermute | solution.py:750
  654.9 4.6 collective-permute-done.101
  659.6 6.4 collective-permute-done.98
  668.4 4.3 grads.3
  685.1 5.7 collective-permute-done.105.refs_2_
  702.0 5.9 fusion.7
  (546 shorter events, 257.0 us)
Async XLA Ops:
  36.4 22.5 %collective-permute-start.12 = (bf16[4,64,1536]{2,1,0:T(8,128)(2,1)S(1)}, bf16[4,64,1536]{2,1,0:T(8,128)(2,1)}, u32[]{:S(2)}, u32[]{:S(2)}) collective-permute-start(bf16[4,64,1536]{2,1,0:T(8,128)(2,1)S(1)} %pad_maximum_fusion.6.refs_16_), channel_id=1, source_target_pairs={{0,2},{2,4},{4,6},{1,3},{3,5},{5,7},{8,10},{10,12},{12,14},{9,11},... | collective-permute-start | bytes 2359304 | tf_op jit(solution)/shard_map/ppermute | solution.py:742
  68.7 35.5 %collective-permute-start.14 = (bf16[1,2,512,512]{3,2,1,0:T(8,128)(2,1)}, bf16[1,2,512,512]{3,2,1,0:T(8,128)(2,1)}, u32[]{:S(2)}, u32[]{:S(2)}) collective-permute-start(bf16[1,2,512,512]{3,2,1,0:T(8,128)(2,1)} %bitcast.275), channel_id=1, source_target_pairs={{0,2},{2,4},{4,6},{1,3},{3,5},{5,7},{8,10},{10,12},{12,14},{9,11},... | collective-permute-start | bytes 3145736 | tf_op jit(solution)/shard_map/ppermute | solution.py:742
  80.8 23.3 %collective-permute-start.16 = (bf16[4,64,1024]{2,1,0:T(8,128)(2,1)S(1)}, bf16[4,64,1024]{2,1,0:T(8,128)(2,1)S(1)}, u32[]{:S(2)}, u32[]{:S(2)}) collective-permute-start(bf16[4,64,1024]{2,1,0:T(8,128)(2,1)S(1)} %pad_maximum_fusion.8), channel_id=1, source_target_pairs={{0,16},{8,24},{16,0},{24,8},{1,17},{9,25},{17,1},{25,9},{2,18},{10... | collective-permute-start | bytes 1572872 | tf_op jit(solution)/shard_map/ppermute | solution.py:846
  80.9 23.2 %collective-permute-start.17 = (bf16[4,64,1024]{2,1,0:T(8,128)(2,1)S(1)}, bf16[4,64,1024]{2,1,0:T(8,128)(2,1)S(1)}, u32[]{:S(2)}, u32[]{:S(2)}) collective-permute-start(bf16[4,64,1024]{2,1,0:T(8,128)(2,1)S(1)} %pad_maximum_fusion.8), channel_id=1, source_target_pairs={{0,24},{8,16},{16,8},{24,0},{1,25},{9,17},{17,9},{25,1},{2,26},{10... | collective-permute-start | bytes 1572872 | tf_op jit(solution)/shard_map/ppermute | solution.py:846
  104.7 25.8 %collective-permute-start.20 = (bf16[256,1152]{1,0:T(8,128)(2,1)S(1)}, bf16[256,1152]{1,0:T(8,128)(2,1)}, u32[]{:S(2)}, u32[]{:S(2)}) collective-permute-start(bf16[256,1152]{1,0:T(8,128)(2,1)S(1)} %get-tuple-element.403.refs_8_), channel_id=1, source_target_pairs={{0,16},{8,24},{16,0},{24,8},{1,17},{9,25},{17,1},{25,9},{2,18},{10... | collective-permute-start | bytes 1769480 | tf_op jit(solution)/shard_map/ppermute | solution.py:835
  106.2 26.8 %collective-permute-start.21 = (bf16[256,1152]{1,0:T(8,128)(2,1)S(1)}, bf16[256,1152]{1,0:T(8,128)(2,1)}, u32[]{:S(2)}, u32[]{:S(2)}) collective-permute-start(bf16[256,1152]{1,0:T(8,128)(2,1)S(1)} %get-tuple-element.403.refs_8_), channel_id=1, source_target_pairs={{0,24},{8,16},{16,8},{24,0},{1,25},{9,17},{17,9},{25,1},{2,26},{10... | collective-permute-start | bytes 1769480 | tf_op jit(solution)/shard_map/ppermute | solution.py:835
  107.6 25.4 %collective-permute-start.18 = (bf16[1,2,512,512]{3,2,1,0:T(8,128)(2,1)}, bf16[1,2,512,512]{3,2,1,0:T(8,128)(2,1)}, u32[]{:S(2)}, u32[]{:S(2)}) collective-permute-start(bf16[1,2,512,512]{3,2,1,0:T(8,128)(2,1)} %collective-permute-done.14.refs_1_.refs_3_.refs_5_), channel_id=1, source_target_pairs={{2,4},{4,6},{3,5},{5,7},{10,12},{12,14},{11,13},{13,15},{18,20},{2... | collective-permute-start | bytes 3145736 | tf_op jit(solution)/shard_map/ppermute | solution.py:742
  109.4 36.4 %collective-permute-start.23 = (bf16[256,1152]{1,0:T(8,128)(2,1)S(1)}, bf16[256,1152]{1,0:T(8,128)(2,1)}, u32[]{:S(2)}, u32[]{:S(2)}) collective-permute-start(bf16[256,1152]{1,0:T(8,128)(2,1)S(1)} %get-tuple-element.412.refs_8_), channel_id=1, source_target_pairs={{0,8},{8,0},{16,24},{24,16},{1,9},{9,1},{17,25},{25,17},{2,10},{10... | collective-permute-start | bytes 1769480 | tf_op jit(solution)/shard_map/ppermute | solution.py:835
  120.4 34.7 %collective-permute-start.24 = (bf16[256,1152]{1,0:T(8,128)(2,1)S(1)}, bf16[256,1152]{1,0:T(8,128)(2,1)}, u32[]{:S(2)}, u32[]{:S(2)}) collective-permute-start(bf16[256,1152]{1,0:T(8,128)(2,1)S(1)} %get-tuple-element.412.refs_8_), channel_id=1, source_target_pairs={{0,16},{8,24},{16,0},{24,8},{1,17},{9,25},{17,1},{25,9},{2,18},{10... | collective-permute-start | bytes 1769480 | tf_op jit(solution)/shard_map/ppermute | solution.py:835
  133.0 30.5 %collective-permute-start.22 = (bf16[1,2,512,512]{3,2,1,0:T(8,128)(2,1)}, bf16[1,2,512,512]{3,2,1,0:T(8,128)(2,1)S(1)}, u32[]{:S(2)}, u32[]{:S(2)}) collective-permute-start(bf16[1,2,512,512]{3,2,1,0:T(8,128)(2,1)} %collective-permute-done.18.refs_0_.refs_1_.refs_2_.refs_6_), channel_id=1, source_target_pairs={{4,6},{5,7},{12,14},{13,15},{20,22},{21,23},{28,30},{29,31}} | collective-permute-start | bytes 3145736 | tf_op jit(solution)/shard_map/ppermute | solution.py:742
  190.9 25.0 %collective-permute-start.36 = (bf16[256,1024]{1,0:T(8,128)(2,1)S(1)}, bf16[256,1024]{1,0:T(8,128)(2,1)}, u32[]{:S(2)}, u32[]{:S(2)}) collective-permute-start(bf16[256,1024]{1,0:T(8,128)(2,1)S(1)} %get-tuple-element.443.refs_0_), channel_id=1, source_target_pairs={{0,16},{8,24},{16,0},{24,8},{1,17},{9,25},{17,1},{25,9},{2,18},{10... | collective-permute-start | bytes 1572872 | tf_op jit(solution)/shard_map/ppermute | solution.py:835
  191.4 24.5 %collective-permute-start.37 = (bf16[256,1024]{1,0:T(8,128)(2,1)S(1)}, bf16[256,1024]{1,0:T(8,128)(2,1)}, u32[]{:S(2)}, u32[]{:S(2)}) collective-permute-start(bf16[256,1024]{1,0:T(8,128)(2,1)S(1)} %get-tuple-element.443.refs_0_), channel_id=1, source_target_pairs={{0,24},{8,16},{16,8},{24,0},{1,25},{9,17},{17,9},{25,1},{2,26},{10... | collective-permute-start | bytes 1572872 | tf_op jit(solution)/shard_map/ppermute | solution.py:835
  217.2 41.2 %collective-permute-start.46 = (bf16[4,64,1536]{2,1,0:T(8,128)(2,1)}, bf16[4,64,1536]{2,1,0:T(8,128)(2,1)}, u32[]{:S(2)}, u32[]{:S(2)}) collective-permute-start(bf16[4,64,1536]{2,1,0:T(8,128)(2,1)} %pad_maximum_fusion.7.refs_16_), channel_id=1, source_target_pairs={{0,2},{2,4},{4,6},{1,3},{3,5},{5,7},{8,10},{10,12},{12,14},{9,11},... | collective-permute-start | bytes 2359304 | tf_op jit(solution)/shard_map/ppermute | solution.py:742
  221.5 37.0 %collective-permute-start.47 = (bf16[4,64,1536]{2,1,0:T(8,128)(2,1)}, bf16[4,64,1536]{2,1,0:T(8,128)(2,1)}, u32[]{:S(2)}, u32[]{:S(2)}) collective-permute-start(bf16[4,64,1536]{2,1,0:T(8,128)(2,1)} %pad_maximum_fusion.7.refs_16_), channel_id=1, source_target_pairs={{2,0},{4,2},{6,4},{3,1},{5,3},{7,5},{10,8},{12,10},{14,12},{11,9},... | collective-permute-start | bytes 2359304 | tf_op jit(solution)/shard_map/ppermute | solution.py:746
  223.5 34.9 %collective-permute-start.43 = (bf16[256,1024]{1,0:T(8,128)(2,1)}, bf16[256,1024]{1,0:T(8,128)(2,1)S(1)}, u32[]{:S(2)}, u32[]{:S(2)}) collective-permute-start(bf16[256,1024]{1,0:T(8,128)(2,1)} %get-tuple-element.494.refs_0_), channel_id=1, source_target_pairs={{0,8},{8,0},{16,24},{24,16},{1,9},{9,1},{17,25},{25,17},{2,10},{10... | collective-permute-start | bytes 1572872 | tf_op jit(solution)/shard_map/ppermute | solution.py:835
  223.9 34.6 %collective-permute-start.44 = (bf16[256,1024]{1,0:T(8,128)(2,1)}, bf16[256,1024]{1,0:T(8,128)(2,1)}, u32[]{:S(2)}, u32[]{:S(2)}) collective-permute-start(bf16[256,1024]{1,0:T(8,128)(2,1)} %get-tuple-element.494.refs_0_), channel_id=1, source_target_pairs={{0,16},{8,24},{16,0},{24,8},{1,17},{9,25},{17,1},{25,9},{2,18},{10... | collective-permute-start | bytes 1572872 | tf_op jit(solution)/shard_map/ppermute | solution.py:835
  225.5 32.9 %collective-permute-start.45 = (bf16[256,1024]{1,0:T(8,128)(2,1)}, bf16[256,1024]{1,0:T(8,128)(2,1)}, u32[]{:S(2)}, u32[]{:S(2)}) collective-permute-start(bf16[256,1024]{1,0:T(8,128)(2,1)} %get-tuple-element.494.refs_0_), channel_id=1, source_target_pairs={{0,24},{8,16},{16,8},{24,0},{1,25},{9,17},{17,9},{25,1},{2,26},{10... | collective-permute-start | bytes 1572872 | tf_op jit(solution)/shard_map/ppermute | solution.py:835
  263.0 34.7 %collective-permute-start.51 = (bf16[4,64,1536]{2,1,0:T(8,128)(2,1)}, bf16[4,64,1536]{2,1,0:T(8,128)(2,1)}, u32[]{:S(2)}, u32[]{:S(2)}) collective-permute-start(bf16[4,64,1536]{2,1,0:T(8,128)(2,1)} %collective-permute-done.46.refs_17_), channel_id=1, source_target_pairs={{2,4},{4,6},{3,5},{5,7},{10,12},{12,14},{11,13},{13,15},{18,20},{2... | collective-permute-start | bytes 2359304 | tf_op jit(solution)/shard_map/ppermute | solution.py:742
  264.5 33.2 %collective-permute-start.52 = (bf16[4,64,1536]{2,1,0:T(8,128)(2,1)}, bf16[4,64,1536]{2,1,0:T(8,128)(2,1)}, u32[]{:S(2)}, u32[]{:S(2)}) collective-permute-start(bf16[4,64,1536]{2,1,0:T(8,128)(2,1)} %collective-permute-done.47.refs_20_), channel_id=1, source_target_pairs={{2,0},{4,2},{3,1},{5,3},{10,8},{12,10},{11,9},{13,11},{18,16},{20,... | collective-permute-start | bytes 2359304 | tf_op jit(solution)/shard_map/ppermute | solution.py:746
  299.4 26.2 %collective-permute-start.54 = (bf16[4,64,1536]{2,1,0:T(8,128)(2,1)}, bf16[4,64,1536]{2,1,0:T(8,128)(2,1)}, u32[]{:S(2)}, u32[]{:S(2)}) collective-permute-start(bf16[4,64,1536]{2,1,0:T(8,128)(2,1)} %collective-permute-done.52.refs_21_), channel_id=1, source_target_pairs={{2,0},{3,1},{10,8},{11,9},{18,16},{19,17},{26,24},{27,25}} | collective-permute-start | bytes 2359304 | tf_op jit(solution)/shard_map/ppermute | solution.py:746
  303.2 54.9 %collective-permute-start.55 = (bf16[4,64,1536]{2,1,0:T(8,128)(2,1)}, bf16[4,64,1536]{2,1,0:T(8,128)(2,1)}, u32[]{:S(2)}, u32[]{:S(2)}) collective-permute-start(bf16[4,64,1536]{2,1,0:T(8,128)(2,1)} %add_convert_fusion.12), channel_id=1, source_target_pairs={{0,2},{1,3},{8,10},{9,11},{16,18},{17,19},{24,26},{25,27}} | collective-permute-start | bytes 2359304 | tf_op jit(solution)/shard_map/ppermute | solution.py:750
  315.0 43.1 %collective-permute-start.56 = (bf16[4,64,1536]{2,1,0:T(8,128)(2,1)}, bf16[4,64,1536]{2,1,0:T(8,128)(2,1)}, u32[]{:S(2)}, u32[]{:S(2)}) collective-permute-start(bf16[4,64,1536]{2,1,0:T(8,128)(2,1)} %add_convert_fusion.11), channel_id=1, source_target_pairs={{6,4},{7,5},{14,12},{15,13},{22,20},{23,21},{30,28},{31,29}} | collective-permute-start | bytes 2359304 | tf_op jit(solution)/shard_map/ppermute | solution.py:754
  368.5 43.5 %collective-permute-start.61 = (bf16[4,64,1536]{2,1,0:T(8,128)(2,1)}, bf16[4,64,1536]{2,1,0:T(8,128)(2,1)}, u32[]{:S(2)}, u32[]{:S(2)}) collective-permute-start(bf16[4,64,1536]{2,1,0:T(8,128)(2,1)} %get-tuple-element.876), channel_id=1, source_target_pairs={{0,2},{2,4},{1,3},{3,5},{8,10},{10,12},{9,11},{11,13},{16,18},{18,... | collective-permute-start | bytes 2359304 | tf_op jit(solution)/shard_map/ppermute | solution.py:750
  370.9 41.2 %collective-permute-start.62 = (bf16[4,64,1536]{2,1,0:T(8,128)(2,1)}, bf16[4,64,1536]{2,1,0:T(8,128)(2,1)}, u32[]{:S(2)}, u32[]{:S(2)}) collective-permute-start(bf16[4,64,1536]{2,1,0:T(8,128)(2,1)} %get-tuple-element.875), channel_id=1, source_target_pairs={{4,2},{6,4},{5,3},{7,5},{12,10},{14,12},{13,11},{15,13},{20,18},{2... | collective-permute-start | bytes 2359304 | tf_op jit(solution)/shard_map/ppermute | solution.py:754
  376.1 36.0 %collective-permute-start.58 = (bf16[256,1152]{1,0:T(8,128)(2,1)}, bf16[256,1152]{1,0:T(8,128)(2,1)}, u32[]{:S(2)}, u32[]{:S(2)}) collective-permute-start(bf16[256,1152]{1,0:T(8,128)(2,1)} %get-tuple-element.562), channel_id=1, source_target_pairs={{0,8},{8,0},{16,24},{24,16},{1,9},{9,1},{17,25},{25,17},{2,10},{10... | collective-permute-start | bytes 1769480 | tf_op jit(solution)/shard_map/ppermute | solution.py:773
  376.6 35.5 %collective-permute-start.59 = (bf16[256,1152]{1,0:T(8,128)(2,1)}, bf16[256,1152]{1,0:T(8,128)(2,1)}, u32[]{:S(2)}, u32[]{:S(2)}) collective-permute-start(bf16[256,1152]{1,0:T(8,128)(2,1)} %get-tuple-element.563), channel_id=1, source_target_pairs={{0,16},{8,24},{16,0},{24,8},{1,17},{9,25},{17,1},{25,9},{2,18},{10... | collective-permute-start | bytes 1769480 | tf_op jit(solution)/shard_map/ppermute | solution.py:773
  378.0 34.1 %collective-permute-start.60 = (bf16[256,1152]{1,0:T(8,128)(2,1)}, bf16[256,1152]{1,0:T(8,128)(2,1)}, u32[]{:S(2)}, u32[]{:S(2)}) collective-permute-start(bf16[256,1152]{1,0:T(8,128)(2,1)} %get-tuple-element.564), channel_id=1, source_target_pairs={{0,24},{8,16},{16,8},{24,0},{1,25},{9,17},{17,9},{25,1},{2,26},{10... | collective-permute-start | bytes 1769480 | tf_op jit(solution)/shard_map/ppermute | solution.py:773
  417.0 30.6 %collective-permute-start.68 = (bf16[4,64,1536]{2,1,0:T(8,128)(2,1)}, bf16[4,64,1536]{2,1,0:T(8,128)(2,1)}, u32[]{:S(2)}, u32[]{:S(2)}) collective-permute-start(bf16[4,64,1536]{2,1,0:T(8,128)(2,1)} %add_convert_fusion.8), channel_id=1, source_target_pairs={{0,2},{2,4},{4,6},{1,3},{3,5},{5,7},{8,10},{10,12},{12,14},{9,11},... | collective-permute-start | bytes 2359304 | tf_op jit(solution)/shard_map/ppermute | solution.py:750
  422.1 25.5 %collective-permute-start.69 = (bf16[4,64,1536]{2,1,0:T(8,128)(2,1)}, bf16[4,64,1536]{2,1,0:T(8,128)(2,1)}, u32[]{:S(2)}, u32[]{:S(2)}) collective-permute-start(bf16[4,64,1536]{2,1,0:T(8,128)(2,1)} %add_convert_fusion.7), channel_id=1, source_target_pairs={{2,0},{4,2},{6,4},{3,1},{5,3},{7,5},{10,8},{12,10},{14,12},{11,9},... | collective-permute-start | bytes 2359304 | tf_op jit(solution)/shard_map/ppermute | solution.py:754
  433.8 27.7 %collective-permute-start.66 = (bf16[256,1152]{1,0:T(8,128)(2,1)}, bf16[256,1152]{1,0:T(8,128)(2,1)}, u32[]{:S(2)}, u32[]{:S(2)}) collective-permute-start(bf16[256,1152]{1,0:T(8,128)(2,1)} %get-tuple-element.593), channel_id=1, source_target_pairs={{0,16},{8,24},{16,0},{24,8},{1,17},{9,25},{17,1},{25,9},{2,18},{10... | collective-permute-start | bytes 1769480 | tf_op jit(solution)/shard_map/ppermute | solution.py:773
  435.1 26.3 %collective-permute-start.67 = (bf16[256,1152]{1,0:T(8,128)(2,1)}, bf16[256,1152]{1,0:T(8,128)(2,1)}, u32[]{:S(2)}, u32[]{:S(2)}) collective-permute-start(bf16[256,1152]{1,0:T(8,128)(2,1)} %get-tuple-element.594), channel_id=1, source_target_pairs={{0,24},{8,16},{16,8},{24,0},{1,25},{9,17},{17,9},{25,1},{2,26},{10... | collective-permute-start | bytes 1769480 | tf_op jit(solution)/shard_map/ppermute | solution.py:773
  464.7 28.7 %collective-permute-start.73 = (bf16[4,64,1536]{2,1,0:T(8,128)(2,1)}, bf16[4,64,1536]{2,1,0:T(8,128)(2,1)}, u32[]{:S(2)}, u32[]{:S(2)}) collective-permute-start(bf16[4,64,1536]{2,1,0:T(8,128)(2,1)} %fusion.9), channel_id=1, source_target_pairs={{0,2},{1,3},{8,10},{9,11},{16,18},{17,19},{24,26},{25,27}} | collective-permute-start | bytes 2359304 | tf_op jit(solution)/shard_map/ppermute | solution.py:750
  471.0 22.4 %collective-permute-start.74 = (bf16[4,64,1536]{2,1,0:T(8,128)(2,1)}, bf16[4,64,1536]{2,1,0:T(8,128)(2,1)}, u32[]{:S(2)}, u32[]{:S(2)}) collective-permute-start(bf16[4,64,1536]{2,1,0:T(8,128)(2,1)} %fusion.10), channel_id=1, source_target_pairs={{6,4},{7,5},{14,12},{15,13},{22,20},{23,21},{30,28},{31,29}} | collective-permute-start | bytes 2359304 | tf_op jit(solution)/shard_map/ppermute | solution.py:754
  493.4 49.2 %collective-permute-start.75 = (bf16[4,256,1024]{2,1,0:T(8,128)(2,1)}, bf16[4,256,1024]{2,1,0:T(8,128)(2,1)}, u32[]{:S(2)}, u32[]{:S(2)}) collective-permute-start(bf16[4,256,1024]{2,1,0:T(8,128)(2,1)} %get-tuple-element.646), channel_id=1, source_target_pairs={{0,1},{1,0},{2,3},{3,2},{4,5},{5,4},{6,7},{7,6},{8,9},{9,8},{10,11... | collective-permute-start | bytes 6291464 | tf_op jit(solution)/shard_map/ppermute | solution.py:734
  493.7 50.4 %collective-permute-start.76 = (bf16[4,256,1024]{2,1,0:T(8,128)(2,1)}, bf16[4,256,1024]{2,1,0:T(8,128)(2,1)}, u32[]{:S(2)}, u32[]{:S(2)}) collective-permute-start(bf16[4,256,1024]{2,1,0:T(8,128)(2,1)} %get-tuple-element.647), channel_id=1, source_target_pairs={{0,1},{1,0},{2,3},{3,2},{4,5},{5,4},{6,7},{7,6},{8,9},{9,8},{10,11... | collective-permute-start | bytes 6291464 | tf_op jit(solution)/shard_map/ppermute | solution.py:734
  496.0 45.4 %collective-permute-start.77 = (bf16[1,1,512,512]{3,2,1,0:T(8,128)(2,1)}, bf16[1,1,512,512]{3,2,1,0:T(8,128)(2,1)}, u32[]{:S(2)}, u32[]{:S(2)}) collective-permute-start(bf16[1,1,512,512]{3,2,1,0:T(8,128)(2,1)} %add_convert_fusion.35), channel_id=1, source_target_pairs={{2,0},{4,2},{6,4},{3,1},{5,3},{7,5},{10,8},{12,10},{14,12},{11,9},... | collective-permute-start | bytes 1572872 | tf_op jit(solution)/shard_map/ppermute | solution.py:754
  497.4 44.7 %collective-permute-start.78 = (bf16[1,1,512,512]{3,2,1,0:T(8,128)(2,1)}, bf16[1,1,512,512]{3,2,1,0:T(8,128)(2,1)}, u32[]{:S(2)}, u32[]{:S(2)}) collective-permute-start(bf16[1,1,512,512]{3,2,1,0:T(8,128)(2,1)} %get-tuple-element.650), channel_id=1, source_target_pairs={{6,4},{7,5},{14,12},{15,13},{22,20},{23,21},{30,28},{31,29}} | collective-permute-start | bytes 1572872 | tf_op jit(solution)/shard_map/ppermute | solution.py:754
  501.5 54.9 %collective-permute-start.83 = (bf16[4,64,1536]{2,1,0:T(8,128)(2,1)}, bf16[4,64,1536]{2,1,0:T(8,128)(2,1)}, u32[]{:S(2)}, u32[]{:S(2)}) collective-permute-start(bf16[4,64,1536]{2,1,0:T(8,128)(2,1)} %get-tuple-element.874), channel_id=1, source_target_pairs={{0,2},{2,4},{1,3},{3,5},{8,10},{10,12},{9,11},{11,13},{16,18},{18,... | collective-permute-start | bytes 2359304 | tf_op jit(solution)/shard_map/ppermute | solution.py:750
  541.4 24.3 %collective-permute-start.84 = (bf16[4,64,1536]{2,1,0:T(8,128)(2,1)S(1)}, bf16[4,64,1536]{2,1,0:T(8,128)(2,1)S(1)}, u32[]{:S(2)}, u32[]{:S(2)}) collective-permute-start(bf16[4,64,1536]{2,1,0:T(8,128)(2,1)S(1)} %get-tuple-element.873), channel_id=1, source_target_pairs={{4,2},{6,4},{5,3},{7,5},{12,10},{14,12},{13,11},{15,13},{20,18},{2... | collective-permute-start | bytes 2359304 | tf_op jit(solution)/shard_map/ppermute | solution.py:754
  553.4 23.4 %collective-permute-start.80 = (bf16[256,1024]{1,0:T(8,128)(2,1)}, bf16[256,1024]{1,0:T(8,128)(2,1)}, u32[]{:S(2)}, u32[]{:S(2)}) collective-permute-start(bf16[256,1024]{1,0:T(8,128)(2,1)} %get-tuple-element.659), channel_id=1, source_target_pairs={{0,16},{8,24},{16,0},{24,8},{1,17},{9,25},{17,1},{25,9},{2,18},{10... | collective-permute-start | bytes 1572872 | tf_op jit(solution)/shard_map/ppermute | solution.py:773
  594.9 33.3 %collective-permute-start.91 = (bf16[1,1,512,512]{3,2,1,0:T(8,128)(2,1)S(1)}, bf16[1,1,512,512]{3,2,1,0:T(8,128)(2,1)S(1)}, u32[]{:S(2)}, u32[]{:S(2)}) collective-permute-start(bf16[1,1,512,512]{3,2,1,0:T(8,128)(2,1)S(1)} %add_convert_fusion.25), channel_id=1, source_target_pairs={{2,0},{4,2},{6,4},{3,1},{5,3},{7,5},{10,8},{12,10},{14,12},{11,9},... | collective-permute-start | bytes 1572872 | tf_op jit(solution)/shard_map/ppermute | solution.py:754
  596.2 32.0 %collective-permute-start.92 = (bf16[256,1024]{1,0:T(8,128)(2,1)}, bf16[256,1024]{1,0:T(8,128)(2,1)S(1)}, u32[]{:S(2)}, u32[]{:S(2)}) collective-permute-start(bf16[256,1024]{1,0:T(8,128)(2,1)} %get-tuple-element.692), channel_id=1, source_target_pairs={{0,8},{8,0},{16,24},{24,16},{1,9},{9,1},{17,25},{25,17},{2,10},{10... | collective-permute-start | bytes 1572872 | tf_op jit(solution)/shard_map/ppermute | solution.py:773
  596.8 31.4 %collective-permute-start.93 = (bf16[256,1024]{1,0:T(8,128)(2,1)}, bf16[256,1024]{1,0:T(8,128)(2,1)S(1)}, u32[]{:S(2)}, u32[]{:S(2)}) collective-permute-start(bf16[256,1024]{1,0:T(8,128)(2,1)} %get-tuple-element.693), channel_id=1, source_target_pairs={{0,16},{8,24},{16,0},{24,8},{1,17},{9,25},{17,1},{25,9},{2,18},{10... | collective-permute-start | bytes 1572872 | tf_op jit(solution)/shard_map/ppermute | solution.py:773
  598.2 30.1 %collective-permute-start.94 = (bf16[256,1024]{1,0:T(8,128)(2,1)S(1)}, bf16[256,1024]{1,0:T(8,128)(2,1)S(1)}, u32[]{:S(2)}, u32[]{:S(2)}) collective-permute-start(bf16[256,1024]{1,0:T(8,128)(2,1)S(1)} %copy-done.66), channel_id=1, source_target_pairs={{0,24},{8,16},{16,8},{24,0},{1,25},{9,17},{17,9},{25,1},{2,26},{10... | collective-permute-start | bytes 1572872 | tf_op jit(solution)/shard_map/ppermute | solution.py:773
  640.8 25.1 %collective-permute-start.98 = (bf16[256,1024]{1,0:T(8,128)(2,1)S(1)}, bf16[256,1024]{1,0:T(8,128)(2,1)S(1)}, u32[]{:S(2)}, u32[]{:S(2)}) collective-permute-start(bf16[256,1024]{1,0:T(8,128)(2,1)S(1)} %copy-done.63), channel_id=1, source_target_pairs={{0,16},{8,24},{16,0},{24,8},{1,17},{9,25},{17,1},{25,9},{2,18},{10... | collective-permute-start | bytes 1572872 | tf_op jit(solution)/shard_map/ppermute | solution.py:773
  641.9 24.1 %collective-permute-start.99 = (bf16[256,1024]{1,0:T(8,128)(2,1)S(1)}, bf16[256,1024]{1,0:T(8,128)(2,1)S(1)}, u32[]{:S(2)}, u32[]{:S(2)}) collective-permute-start(bf16[256,1024]{1,0:T(8,128)(2,1)S(1)} %copy-done.62), channel_id=1, source_target_pairs={{0,24},{8,16},{16,8},{24,0},{1,25},{9,17},{17,9},{25,1},{2,26},{10... | collective-permute-start | bytes 1572872 | tf_op jit(solution)/shard_map/ppermute | solution.py:773
  690.8 26.1 %collective-permute-start.103 = (bf16[256,1024]{1,0:T(8,128)(2,1)S(1)}, bf16[256,1024]{1,0:T(8,128)(2,1)}, u32[]{:S(2)}, u32[]{:S(2)}) collective-permute-start(bf16[256,1024]{1,0:T(8,128)(2,1)S(1)} %add_convert_fusion.23), channel_id=1, source_target_pairs={{0,1},{1,0},{2,3},{3,2},{4,5},{5,4},{6,7},{7,6},{8,9},{9,8},{10,11... | collective-permute-start | bytes 1572872 | tf_op jit(solution)/shard_map/ppermute | solution.py:734
  692.3 25.9 %collective-permute-start.102 = (bf16[256,1024]{1,0:T(8,128)(2,1)S(1)}, bf16[256,1024]{1,0:T(8,128)(2,1)}, u32[]{:S(2)}, u32[]{:S(2)}) collective-permute-start(bf16[256,1024]{1,0:T(8,128)(2,1)S(1)} %add_convert_fusion.24), channel_id=1, source_target_pairs={{0,1},{1,0},{2,3},{3,2},{4,5},{5,4},{6,7},{7,6},{8,9},{9,8},{10,11... | collective-permute-start | bytes 1572872 | tf_op jit(solution)/shard_map/ppermute | solution.py:734
  (177 other events, 1902.0 us)

commit v3 on v2

--- a/solution.py
+++ b/solution.py
@@ -368,16 +368,17 @@
     return grown / jnp.sum(grown, axis=1, keepdims=True)
 
 
-def experts_kernel(steps, first, count, more, joined, place_ref, router_ref, *refs):
+def experts_kernel(steps, first, count, micro, more, added, joined, place_ref, router_ref, *refs):
     refs = list(refs)
-    n = 1 if joined else refs[-5].shape[1]
+    n = 1 if joined else refs[-7].shape[1]
     xs = [refs.pop(0) for _ in range(2 * steps)]
     dys = [refs.pop(0) for _ in range(2 * steps)]
-    ws = [refs.pop(0) for _ in range(2 * n - 1)]
+    ws = [refs.pop(0) for _ in range(n)]
     before = [refs.pop(0) for _ in range(4)] if more else None
+    dws_before = [refs.pop(0) for _ in range(n)] if added else []
     outs = [refs.pop(0) for _ in range(4)]
     dws = [refs.pop(0) for _ in range(n)]
-    acc_ref, w_ref, xbuf, dybuf, sems, wsems = refs
+    acc_ref, w_ref, xbuf, dybuf, dwbuf, sems, wsems, dwsems = refs
     step = pl.program_id(0)
     base = place_ref[0]
     c = place_ref[1]
@@ -389,7 +390,7 @@
     def copies(t, slot):
         return [
             pltpu.make_async_copy(
-                src[2 * t + part],
+                src[2 * t + part].at[micro] if which else src[2 * t + part],
                 buf.at[slot, pl.ds(part * half, half)],
                 sems.at[slot, 2 * which + part],
             )
@@ -405,29 +406,25 @@
                 for copy in copies(t, slot):
                     copy.start()
 
-    def weight_copy(src, d):
-        if joined:
-            return pltpu.make_async_copy(src, w_ref, wsems.at[0])
-        return pltpu.make_async_copy(src, w_ref.at[:, (c + d) % n], wsems.at[d])
+    def weight_copy(d):
+        to = w_ref if joined else w_ref.at[:, c ^ d]
+        return pltpu.make_async_copy(ws[d], to, wsems.at[d])
+
+    def added_copy(d):
+        return pltpu.make_async_copy(dws_before[d], dwbuf.at[d], dwsems.at[d])
 
     slot = step % 2
 
     @pl.when(step == 0)
     def _():
         fetch(step, slot)
-        weight_copy(ws[0], 0).start()
-        for d in range(1, n):
-
-            @pl.when(c + d < n)
-            def _():
-                weight_copy(ws[n - 1 + d], d).start()
-
-            @pl.when(c + d >= n)
-            def _():
-                weight_copy(ws[n - d], d).start()
-
         for d in range(n):
-            weight_copy(ws[0], d).wait()
+            weight_copy(d).start()
+        for d in range(n):
+            weight_copy(d).wait()
+        if added:
+            for d in range(n):
+                added_copy(d).start()
 
     @pl.when(step + 1 < steps)
     def _():
@@ -484,36 +481,39 @@
         outs[part][0] = o.astype(BF)
         outs[2 + part][0, :, :width] = d.astype(BF)
         outs[2 + part][0, :, width:] = t.astype(BF)
-    grad_in = dot(x.T, dgu, 1, 0)
-    grad_back = dot(dy.T, gact, 1, 0)
 
     @pl.when(step == 0)
     def _():
-        acc_ref[:, :both] = grad_in
-        acc_ref[:, both:] = grad_back
-
-    @pl.when(step > 0)
-    def _():
-        acc_ref[:, :both] += grad_in
-        acc_ref[:, both:] += grad_back
+        acc_ref[...] = jnp.zeros_like(acc_ref)
+
+    acc_ref[:, :both] += dot(x.T, dgu, 1, 0)
+    acc_ref[:, both:] += dot(dy.T, gact, 1, 0)
 
     @pl.when(step == pl.num_programs(0) - 1)
     def _():
-        if joined:
-            dws[0][...] = acc_ref[...].astype(BF)
-        else:
+        for d in range(n):
+            if added:
+                added_copy(d).wait()
+            if joined:
+                total = acc_ref[...]
+                dws[0][...] = (total + dwbuf[0].astype(F32) if added else total).astype(BF)
+                continue
             planes, _, shard, _ = w_ref.shape
-            for d in range(n):
-                for plane in range(planes):
-                    row = pl.multiple_of((plane * n + (c + d) % n) * shard, shard)
-                    dws[d][plane] = acc_ref[pl.ds(row, shard)].astype(BF)
-
-
-def experts_call(xs, dys, place, router, weights, first, count, before):
+            for plane in range(planes):
+                row = pl.multiple_of((plane * n + (c ^ d)) * shard, shard)
+                total = acc_ref[pl.ds(row, shard)]
+                if added:
+                    total = total + dwbuf[d, plane].astype(F32)
+                dws[d][plane] = total.astype(BF)
+
+
+def experts_call(
+    xs, dys, micro, place, router, weights, first, count, before, dws_before
+):
     steps = len(xs) // 2
     half, width = xs[0].shape
     tile = 2 * half
-    n = (len(weights) + 1) // 2
+    n = len(weights)
     joined = n == 1
     block = weights[0].shape
     whole_shape = block if joined else block[:1] + (n,) + block[1:]
@@ -525,14 +525,17 @@
     blocks = [out_block, out_block, dx_block, dx_block]
     rows = steps * tile
     return pl.pallas_call(
-        functools.partial(experts_kernel, steps, first, count, bool(before), joined),
+        functools.partial(
+            experts_kernel, steps, first, count, micro, bool(before), bool(dws_before), joined
+        ),
         grid=(steps,),
         in_specs=[
             pl.BlockSpec(memory_space=pltpu.SMEM),
             pl.BlockSpec((width, 128), lambda i: (0, 0)),
         ]
-        + [anywhere] * (4 * steps + len(weights))
-        + (blocks if before else []),
+        + [anywhere] * (4 * steps + n)
+        + (blocks if before else [])
+        + [anywhere] * len(dws_before),
         out_specs=blocks + [whole] * n,
         out_shape=[jax.ShapeDtypeStruct((steps, half, width), BF)] * 2
         + [jax.ShapeDtypeStruct((steps, half, width + 128), BF)] * 2
@@ -542,7 +545,9 @@
             pltpu.VMEM(whole_shape, BF),
             pltpu.VMEM((2, tile, width), BF),
             pltpu.VMEM((2, tile, width + 128), BF),
+            pltpu.VMEM(((n if dws_before else 1),) + (block if dws_before else (16, 128)), BF),
             pltpu.SemaphoreType.DMA((2, 4)),
+            pltpu.SemaphoreType.DMA((n,)),
             pltpu.SemaphoreType.DMA((n,)),
         ],
         compiler_params=params("arbitrary"),
@@ -552,20 +557,32 @@
             transcendentals=rows * lanes // 3,
         ),
         name="experts",
-    )(place, router, *xs, *dys, *weights, *(before or []))
-
-
-def back_kernel(dq_ref, cos_ref, sin_ref, wq_ref, wkv_ref, *refs):
-    *terms, dkv_ref, part_ref = refs
+    )(place, router, *xs, *dys, *weights, *(before or []), *dws_before)
+
+
+def back_kernel(dq_ref, x_ref, cos_ref, sin_ref, wq_ref, wkv_ref, *refs):
+    *terms, dkv_ref, part_ref, gain_ref = refs
     total = functools.reduce(jnp.add, [t[...].astype(F32) for t in terms])
     kw = total.shape[1] // 2
     dk = turn(total[:, :kw], cos_ref[...], -sin_ref[...]).astype(BF)
     dkv = jnp.concatenate([dk, total[:, kw:].astype(BF)], axis=1)
     dkv_ref[...] = dkv
-    part_ref[...] = (dot(dq_ref[...], wq_ref[...], 1, 1) + dot(dkv, wkv_ref[...], 1, 1)).astype(BF)
-
-
-def back_call(dq, terms, cosine, sine, w_qo, w_kv):
+    part = dot(dq_ref[...], wq_ref[...], 1, 1) + dot(dkv, wkv_ref[...], 1, 1)
+    part_ref[...] = part.astype(BF)
+    x = x_ref[...].astype(F32)
+    unit = x * lax.rsqrt(jnp.mean(x * x, axis=1, keepdims=True) + EPS)
+    sums = jnp.broadcast_to(jnp.sum(part * unit, axis=0, keepdims=True), gain_ref.shape)
+
+    @pl.when(pl.program_id(0) == 0)
+    def _():
+        gain_ref[...] = sums
+
+    @pl.when(pl.program_id(0) > 0)
+    def _():
+        gain_ref[...] += sums
+
+
+def back_call(dq, terms, x, micro, cosine, sine, w_qo, w_kv):
     rows, qw = dq.shape
     lanes = terms[0].shape[1]
     d = w_qo.shape[0]
@@ -578,26 +595,28 @@
         grid=(rows // tile,),
         in_specs=[
             row(qw),
+            pl.BlockSpec((tile, d), lambda i: (i + micro * (rows // tile), 0)),
             table,
             table,
             pl.BlockSpec((d, qw), lambda i: (0, 0)),
             pl.BlockSpec((d, lanes), lambda i: (0, 0)),
         ]
         + [row(lanes)] * len(terms),
-        out_specs=[row(lanes), row(d)],
+        out_specs=[row(lanes), row(d), pl.BlockSpec((8, d), lambda i: (0, 0))],
         out_shape=[
             jax.ShapeDtypeStruct((rows, lanes), BF),
             jax.ShapeDtypeStruct((rows, d), BF),
+            jax.ShapeDtypeStruct((8, d), F32),
         ],
         compiler_params=params("arbitrary"),
         cost_estimate=pl.CostEstimate(
             flops=2 * rows * d * (qw + lanes), bytes_accessed=8 * rows * d, transcendentals=0
         ),
         name="back",
-    )(dq, cosine, sine, w_qo, w_kv, *terms)
-
-
-def grads_kernel(pairs, extra, place_ref, *refs):
+    )(dq, x, cosine, sine, w_qo, w_kv, *terms)
+
+
+def grads_kernel(pairs, starts, extra, place_ref, *refs):
     refs = list(refs)
     sides = [[(refs.pop(0), refs.pop(0)) for _ in range(count)] for count in pairs]
     more = refs.pop(0) if extra else None
@@ -606,9 +625,13 @@
     for s in range(count):
         at = pl.ds(pl.multiple_of((place_ref[0] ^ s) * block, block), block)
         column = 0
-        for side in sides:
+        for side, firsts in zip(sides, starts):
             total = functools.reduce(
-                jnp.add, [dot(left[:, at], right[...], 0, 0) for left, right in side]
+                jnp.add,
+                [
+                    dot(left[first : first + right.shape[0], at], right[...], 0, 0)
+                    for (left, right), first in zip(side, firsts)
+                ],
             )
             refs[s][:, column : column + total.shape[1]] = total.astype(BF)
             column += total.shape[1]
@@ -620,10 +643,11 @@
     d = sides[0][0][0].shape[1]
     lanes = sum(side[0][1].shape[1] for side in sides) + (0 if extra is None else extra.shape[1])
     whole = pl.BlockSpec(memory_space=pltpu.VMEM)
-    operands = [a for side in sides for pair in side for a in pair]
+    operands = [a for side in sides for term in side for a in term[:2]]
+    starts = [[term[2] for term in side] for side in sides]
     operands += [] if extra is None else [extra]
     return pl.pallas_call(
-        functools.partial(grads_kernel, [len(side) for side in sides], extra is not None),
+        functools.partial(grads_kernel, [len(side) for side in sides], starts, extra is not None),
         in_specs=[pl.BlockSpec(memory_space=pltpu.SMEM)] + [whole] * len(operands),
         out_specs=[whole] * count,
         out_shape=[jax.ShapeDtypeStruct((d // count, lanes), BF)] * count,
@@ -734,24 +758,8 @@
     return lax.ppermute(value, "mp", [(0, 1), (1, 0)])
 
 
-def pin(*values):
-    return lax.optimization_barrier(values)
-
-
 def up_hop(value, n, s):
     return lax.ppermute(value, "ctx", [(c, c + 1) for c in range(s, n - 1)])
-
-
-def down_hop(value, n, s):
-    return lax.ppermute(value, "ctx", [(c, c - 1) for c in range(1, n - s)])
-
-
-def sum_up_hop(value, n, s):
-    return lax.ppermute(value, "ctx", [(c, c + 1) for c in range(s + 1)])
-
-
-def sum_down_hop(value, n, s):
-    return lax.ppermute(value, "ctx", [(c, c - 1) for c in range(n - 1 - s, n)])
 
 
 def add(*terms):
@@ -831,8 +839,8 @@
         mine = lax.dynamic_index_in_dim(cut, me_mp, 0, keepdims=False)
         return mine, lax.dynamic_index_in_dim(cut, 1 - me_mp, 0, keepdims=False)
 
-    def far_pieces(mine):
-        return [lax.ppermute(mine, "dp", apart(dp, s)) for s in range(1, dp)]
+    def far_pieces(mine, steps=range(1, dp)):
+        return [lax.ppermute(mine, "dp", apart(dp, s)) for s in steps]
 
     def paired(mine, far, other, near):
         return [piece for pair in zip([mine] + far, [other] + near) for piece in pair]
@@ -850,6 +858,12 @@
         full = jnp.stack(lines)
         cols = by_xor([full[:, i] for i in range(n)], me_ctx)
         return jnp.stack(cols, axis=1).reshape(dp * n * shard, full.shape[3])
+
+    live = {}
+
+    def seal(**values):
+        live.update(values)
+        live.update(lax.optimization_barrier(live))
 
     small = jnp.concatenate([w_router, norm_gain[:, None], ffn_gain[:, None]], axis=1)
     small = jnp.pad(small, ((0, 0), (0, 128 - small.shape[1])))
@@ -865,26 +879,32 @@
     w3_parts = exchange(by_xor([w3[i] for i in range(dp)], me_dp), "dp")
     own3 = by_xor(w3_parts, me_dp)
     own3 = [jnp.stack([o[g] for o in own3]) for g in range(2)]
-    ups = [[], []]
-    downs = [[], []]
-
-    def weight_hop(g, s):
+    def weight_send(g, *steps):
         if hops:
-            ups[g].append(up_hop(ups[g][-1] if s else own3[g], n, s))
-            downs[g].append(down_hop(downs[g][-1] if s else own3[g], n, s))
+            for s in steps:
+                at, hop = (2, 1) if s == 3 else (0, s)
+                live["weights"][g][s] = lax.ppermute(live["weights"][g][at], "ctx", apart(n, hop))
+
+    def seal_but(under_way, **values):
+        kept = [(d, {k: d.pop(k) for k in keys if k in d}) for d, keys in under_way()]
+        seal(**values)
+        for (d, keys), (_, taken) in zip(under_way(), kept):
+            d.update(taken)
 
     if hops:
-        kv_line, qo_line, own3 = pin(kv_line, qo_line, own3)
-        kv_pieces = gather_plane(kv_line)
-        weight_hop(0, 0)
-        kv_pieces, qo_line, ups, downs, own3 = pin(kv_pieces, qo_line, ups, downs, own3)
-        kv_full = whole_rows(kv_pieces)
-        qo_pieces = gather_plane(qo_line)
+        own3 = [{0: o} for o in own3]
+        seal(kv_line=kv_line, qo_line=qo_line, weights=own3, x=tokens, dy=cotangent, routes=routes)
+        kv_pieces = gather_plane(live.pop("kv_line"))
+        weight_send(0, 1)
+        seal(kv_pieces=kv_pieces)
+        kv_full = whole_rows(live.pop("kv_pieces"))
+        qo_pieces = gather_plane(live.pop("qo_line"))
     else:
         kv_full = lax.all_gather(kv_shard, ("dp", "ctx"), axis=0, tiled=True)
         qo_full = lax.all_gather(qo_shard, ("dp", "ctx"), axis=0, tiled=True)
         own3 = [lax.all_gather(o, "ctx", axis=1, tiled=False) for o in own3]
-        own3 = [o.reshape(width, o.shape[-1]) for o in own3]
+        own3 = [{0: o.reshape(width, o.shape[-1])} for o in own3]
+        seal(weights=own3, x=tokens, dy=cotangent, routes=routes)
     small = kv_full[:, 2 * kw :]
     router = small[:, :experts]
     router_wide = jnp.pad(router, ((0, 0), (0, 128 - experts)))
@@ -897,264 +917,356 @@
     cosine = jnp.tile(jnp.cos(angles), (1, 4))
     sine = jnp.sin(angles)
     sine = jnp.concatenate([-sine, sine, -sine, sine], axis=1)
-    x = tokens.reshape(rows, width)
-    normed, kv = kv_call(x, gain_one, kv_full, 2 * kw, cosine, sine)
+    live["x"] = live["x"].reshape(rows, width)
+    live["dy"] = live["dy"].reshape(rows, width)
+    normed, kv = kv_call(live["x"], gain_one, kv_full, 2 * kw, cosine, sine)
     kv = kv.reshape(1, micro * seq_count, local, 2 * kw)
 
-    ids = routes.reshape(rows, top)
+    ids = live.pop("routes").reshape(rows, top)
     marks = jnp.sum(
         (ids[:, :, None] == jnp.arange(128, dtype=jnp.int32)[None, None, :]).astype(F32), axis=1
     ).astype(BF)
-    dy = cotangent.reshape(rows, width)
-    dyx = jnp.concatenate([dy, marks], axis=1).reshape(micro, per, width + 128)
-    dy_cut = [halves(dyx[m]) for m in micros]
-    dy_far = [None] * micro
-    dy_near = [None] * micro
+    dyx = jnp.concatenate([live["dy"], marks], axis=1)
+    dyx = dyx.reshape(micro, 2, half, width + 128)
+    dy_cut = [
+        lax.dynamic_index_in_dim(dyx, at, 1, keepdims=False) for at in (me_mp, 1 - me_mp)
+    ]
 
     if hops:
         kv_got = up_hop(kv, n, 0)
-        kv_got, qo_pieces, normed, dy_cut = pin(kv_got, qo_pieces, normed, dy_cut)
-        kv_prev = [kv_got]
-        qo_full = whole_rows(qo_pieces)
+        seal(
+            kv=kv,
+            kv_prev=[kv_got],
+            qo_pieces=qo_pieces,
+            normed=normed,
+            dy_cut=dy_cut,
+            marks=marks[:, :experts],
+            kv_full=kv_full,
+            cosine=cosine,
+            sine=sine,
+            router=router,
+            router_wide=router_wide,
+            gain_one=gain_one,
+            gain_two=gain_two,
+        )
+        qo_full = whole_rows(live.pop("qo_pieces"))
     else:
         every = lax.all_gather(kv[0], "ctx", axis=0, tiled=False)
-        kv_prev = [from_last(every, n - me_ctx, n - 1)]
-    w_out = qo_full[:, qw:]
-    q = q_call(normed, qo_full, qw, cosine, sine).reshape(micro * seq_count, local, qw)
+        seal(
+            kv=kv,
+            kv_prev=[from_last(every, n - me_ctx, n - 1)],
+            normed=normed,
+            dy_cut=dy_cut,
+            marks=marks[:, :experts],
+            kv_full=kv_full,
+            cosine=cosine,
+            sine=sine,
+            router=router,
+            router_wide=router_wide,
+            gain_one=gain_one,
+            gain_two=gain_two,
+        )
+    live.update(qo_full=qo_full, dy_far=[], dy_near=[])
+    q = q_call(live["normed"], qo_full, qw, live["cosine"], live["sine"])
+    live["q"] = q.reshape(micro * seq_count, local, qw)
+
+    def dy_send(steps):
+        for s in steps:
+            live["dy_far"].append(lax.ppermute(live["dy_cut"][0], "dp", apart(dp, s)))
+
+    def attend(first, s, done):
+        return attn_part(
+            ctx_now,
+            live["q"],
+            live["kv"] if first else None,
+            [live["kv_prev"][s - 1]],
+            s,
+            None if first else live.pop("carry"),
+            done,
+        )
+
+    def mix(attn):
+        return dot(attn.reshape(rows, qw), live["qo_full"][:, qw:], 1, 1).astype(BF)
+
     if hops:
-        carry = None
-        own = kv
-        for s in range(1, n):
-            last = s == n - 1
-            got = None if last else up_hop(kv_prev[-1], n, s)
-            if s - 1 < micro:
-                dy_far[s - 1] = far_pieces(dy_cut[s - 1][0])
-            else:
-                weight_hop(0, 1)
-            if s >= 2:
-                dy_near[s - 2] = [swap(f) for f in dy_far[s - 2]]
-            carry = attn_part(ctx_now, q, own, [kv_prev[-1]], s, carry, last)
-            if last:
-                attn, lse = carry
-                mixed = dot(attn.reshape(rows, qw), w_out, 1, 1).astype(BF)
-                mixed, dy_near, ups, downs = pin(mixed, dy_near, ups, downs)
-            else:
-                got, carry, dy_far, dy_near = pin(got, carry, dy_far, dy_near)
-                kv_prev.append(got)
-            own = None
+        dy_send((1, 2))
+        got = up_hop(live["kv_prev"][-1], n, 1)
+        carry = attend(True, 1, False)
+        live["kv_prev"].append(got)
+        seal(carry=carry)
+        dy_send((3,))
+        got = up_hop(live["kv_prev"][-1], n, 2)
+        carry = attend(False, 2, False)
+        live["kv_prev"].append(got)
+        seal(carry=carry)
+        weight_send(0, 2)
+        attn, lse = attend(False, 3, True)
     else:
-        attn, lse = attn_part(ctx_now, q, kv, kv_prev, 1, None, True)
-        mixed = dot(attn.reshape(rows, qw), w_out, 1, 1).astype(BF)
-    for m in micros:
-        if dy_far[m] is None:
-            dy_far[m] = far_pieces(dy_cut[m][0])
-        if dy_near[m] is None:
-            dy_near[m] = [swap(f) for f in dy_far[m]]
-    dys = [paired(dy_cut[m][0], dy_far[m], dy_cut[m][1], dy_near[m]) for m in micros]
-
-    mixed_got = swap(mixed)
-    hidden = x.astype(F32) + (mixed.astype(F32) + mixed_got.astype(F32))
+        attn, lse = attend(True, 1, True)
+        dy_send(range(1, dp))
+    live["dy_near"] = [swap(f) for f in live["dy_far"]]
+    late = lambda: [(live["weights"][0], [2])]
+    seal_but(late, attn=attn, lse=lse, mixed=mix(attn))
+
+    mixed_got = swap(live["mixed"])
+    hidden = live["x"].astype(F32) + (live.pop("mixed").astype(F32) + mixed_got.astype(F32))
     inv_two = lax.rsqrt(jnp.mean(hidden * hidden, axis=1, keepdims=True) + EPS)
-    ffn_low = (hidden * inv_two * gain_two).astype(BF)
+    ffn_low = (hidden * inv_two * live["gain_two"]).astype(BF)
     x_cut = [halves(ffn_low[m * per : (m + 1) * per]) for m in micros]
-    x_far = [None] * micro
-    x_near = [None] * micro
-
-    x_cut, hidden, inv_two, ffn_low = pin(x_cut, hidden, inv_two, ffn_low)
-    x_far[0] = far_pieces(x_cut[0][0])
-    weight_hop(0, 2)
-    x_far[0], ups, downs, x_cut = pin(x_far[0], ups, downs, x_cut)
-    x_near[0] = [swap(f) for f in x_far[0]]
-    x_near[0], x_cut = pin(x_near[0], x_cut)
-    sums = []
-    dws = [[], []]
-    xs = []
+
+    seal_but(late, hidden=hidden, inv_two=inv_two, ffn_low=ffn_low, x_cut=x_cut)
+    first = far_pieces(live["x_cut"][0][0], (1, 2))
+    live["x_far"] = [first] + [[]] * (micro - 1)
+    seal()
+    live["x_far"][0] = live["x_far"][0] + far_pieces(live["x_cut"][0][0], (3,))
+    weight_send(0, 3)
+    seal()
+    live["x_near"] = [[swap(f) for f in live["x_far"][0]]] + [[]] * (micro - 1)
+    seal()
+    live.update(sums=[], dws=[[], []], parts=[])
 
     def run(g, m, before):
-        whole = [own3[g]] + ups[g] + downs[g]
+        weights = [live["weights"][g][s] for s in sorted(live["weights"][g])]
+        x_cut, dy_cut = live["x_cut"][m], live["dy_cut"]
+        xs = paired(x_cut[0], live["x_far"][m], x_cut[1], live["x_near"][m])
+        dys = paired(dy_cut[0], live["dy_far"], dy_cut[1], live["dy_near"])
         part = experts_call(
-            xs[m], dys[m], place, router_wide, whole, g * group, group, before
+            xs,
+            dys,
+            m,
+            place,
+            live["router_wide"],
+            weights,
+            g * group,
+            group,
+            before,
+            live["dws"][g],
         )
-        dws[g].append(part[4:])
-        return part[:4]
-
-    for m in micros:
-        xs.append(paired(x_cut[m][0], x_far[m], x_cut[m][1], x_near[m]))
-        sums.append(run(0, m, None))
-        if m + 1 < micro:
-            x_far[m + 1] = far_pieces(x_cut[m + 1][0])
-        weight_hop(1, m)
-        sums, dws, x_far, x_cut, ups, downs = pin(sums, dws, x_far, x_cut, ups, downs)
-        if m + 1 < micro:
-            x_near[m + 1] = [swap(f) for f in x_far[m + 1]]
-            x_near, sums, x_cut, ups, downs = pin(x_near, sums, x_cut, ups, downs)
-    if hops:
-        for s in range(micro, n - 1):
-            weight_hop(1, s)
-
-    rising = [None, None]
-    falling = [None, None]
-
-    def grad_hop(g, s):
+        live["dws"][g] = part[4:]
+        return list(part[:4])
+
+    live["x_far"][1] = far_pieces(live["x_cut"][1][0])
+    weight_send(1, 1, 2)
+    live["sums"].append(run(0, 0, None))
+    seal()
+    live["x_near"][1] = [swap(f) for f in live["x_far"][1]]
+    seal()
+    weight_send(1, 3)
+    live["sums"].append(run(0, 1, None))
+    seal()
+
+    live.update(rows=[{}, {}])
+
+    def grad_send(g, *steps):
         if hops:
-            d = n - 1 - s
-            up_terms = [dw[d] for dw in dws[g]] + ([rising[g]] if s else [])
-            down_terms = [dw[n - d] for dw in dws[g]] + ([falling[g]] if s else [])
-            rising[g] = sum_up_hop(add(*up_terms), n, s)
-            falling[g] = sum_down_hop(add(*down_terms), n, s)
+            for s in steps:
+                live["rows"][g][s] = lax.ppermute(live["dws"][g][s], "ctx", apart(n, s))
 
     def grad_own(g):
         if hops:
-            own = add(*[dw[0] for dw in dws[g]], rising[g], falling[g])
+            own = add(live["dws"][g][0], *live["rows"][g].values())
         else:
-            whole = add(*[dw[0] for dw in dws[g]]).reshape(dp, n, shard, -1)
+            whole = live["dws"][g][0].reshape(dp, n, shard, -1)
             own = lax.psum_scatter(whole, "ctx", scatter_dimension=1, tiled=False)
         return exchange(by_xor([own[i] for i in range(dp)], me_dp), "dp")
 
-    parts = []
-    dx_terms = []
-    dx_back = []
-
     def terms_of(mine, got):
         return [add(mine[s], got[s]) for s in range(dp)]
 
-    for m in micros:
-        parts.append(run(1, m, sums[m]))
-        if m > 0:
-            dx_back.append(exchange(dx_terms[m - 1], "dp"))
-        grad_hop(0, m)
-        parts, dx_back, rising, falling, dws = pin(parts, dx_back, rising, falling, dws)
-        if m + 1 < micro:
-            dx_terms.append(terms_of(parts[m][2], swap(parts[m][3])))
-            dx_terms, parts, dx_back = pin(dx_terms, parts, dx_back)
+    live.update(dx_terms=[None] * micro, dx_back=[None] * micro)
+    live.update(out_terms=[None] * micro, out_back={})
+
+    def dx_terms(m):
+        part = live["parts"][m]
+        live["dx_terms"][m] = terms_of(part[2], swap(part[3]))
+
+    def dx_send(m):
+        live["dx_back"][m] = exchange(live["dx_terms"][m], "dp")
+
+    def out_terms(m):
+        part = live["parts"][m]
+        live["out_terms"][m] = terms_of(part[0], swap(part[1]))
+
+    def out_send(m):
+        live["out_back"][m] = exchange(live["out_terms"][m], "dp")
+
+    grad_send(0, 1, 2)
+    live["parts"].append(run(1, 0, live["sums"][0]))
+    seal()
+    dx_terms(0)
+    seal()
+    dx_send(0)
+    grad_send(0, 3)
+    live["parts"].append(run(1, 1, live.pop("sums")[1]))
+    seal()
 
     cut = lambda whole, m: whole[m * per : (m + 1) * per]
-    marked = dyx.reshape(rows, width + 128)[:, width : width + experts].astype(F32) > 0.5
-    gates = masked_softmax(dot(ffn_low, router, 1, 0), marked)
-    grad_sums = [0.0, 0.0]
+    live.update({name: [None] * micro for name in ("dh", "dz", "d_attn", "dq", "dkv")})
+    live.update(dkv_sum=[{} for _ in micros])
+    live.update(router_sums=[None] * micro, gain_sums=[None] * micro)
 
     def before_attention(m):
-        total = add(*dx_back[m])
+        total = add(*live["dx_back"][m])
         moe = in_order(total, swap(total)).astype(F32)
+        low = cut(live["ffn_low"], m)
+        inv = cut(live["inv_two"], m)
         dgate = moe[:, width : width + experts]
-        gate = cut(gates, m)
+        gate = masked_softmax(
+            dot(low, live["router"], 1, 0), cut(live["marks"], m).astype(F32) > 0.5
+        )
         dlogit = gate * (dgate - jnp.sum(gate * dgate, axis=1, keepdims=True))
         dlogit = dlogit.astype(BF)
-        grad_sums[0] = grad_sums[0] + dot(cut(ffn_low, m), dlogit, 0, 0)
-        d_ffn = moe[:, :width] + dot(dlogit, router, 1, 1)
-        unit = cut(hidden, m) * cut(inv_two, m)
-        grad_sums[1] = grad_sums[1] + jnp.sum(d_ffn * unit, axis=0)
-        g_two = d_ffn * gain_two
-        dh = cut(dy, m).astype(F32) + cut(inv_two, m) * (
+        live["router_sums"][m] = dot(low, dlogit, 0, 0)
+        d_ffn = moe[:, :width] + dot(dlogit, live["router"], 1, 1)
+        unit = cut(live["hidden"], m) * inv
+        live["gain_sums"][m] = jnp.sum(d_ffn * unit, axis=0)
+        g_two = d_ffn * live["gain_two"]
+        dh = cut(live["dy"], m).astype(F32) + inv * (
             g_two - unit * jnp.mean(g_two * unit, axis=1, keepdims=True)
         )
         dz = dh.astype(BF)
-        return dh, dz, dot(dz, w_out, 1, 0).astype(BF)
-
-    def attention_back(m, d_attn):
+        live["dh"][m] = dh
+        live["dz"][m] = dz
+        live["d_attn"][m] = dot(dz, live["qo_full"][:, qw:], 1, 0).astype(BF)
+
+    def attention_back(m):
         dq, *dkv = attn_bwd(
             ctx_now,
-            q,
-            d_attn.reshape(seq_count, local, qw),
-            attn,
-            lse,
-            cosine,
-            sine,
-            kv,
-            kv_prev,
+            live["q"],
+            live["d_attn"][m].reshape(seq_count, local, qw),
+            live["attn"],
+            live["lse"],
+            live["cosine"],
+            live["sine"],
+            live["kv"],
+            live["kv_prev"],
             m * seq_count,
         )
-        return dq.reshape(per, qw), dkv
-
-    dkv_sum = [None] * micro
-
-    def dkv_hop(m, s):
+        live["dq"][m] = dq.reshape(per, qw)
+        live["dkv"][m] = dkv
+
+    def dkv_send(m, *steps):
         if hops:
-            d = n - 1 - s
-            term = dkv[m][d] if s == 0 else add(dkv[m][d], dkv_sum[m])
-            dkv_sum[m] = sum_down_hop(term, n, s)
-
-    def dkv_own(m):
+            for d in steps:
+                live["dkv_sum"][m][d] = lax.ppermute(
+                    live["dkv"][m][d], "ctx", [(c, c - d) for c in range(d, n)]
+                )
+
+    def back(m):
         if hops:
-            both = [dkv[m][0], dkv_sum[m]]
+            terms = [live["dkv"][m][0], *live["dkv_sum"][m].values()]
         else:
-            every = from_last(jnp.concatenate(dkv[m]), n - 1 - me_ctx, n)
-            both = [lax.psum_scatter(every, "ctx", scatter_dimension=0, tiled=True)]
-        return [b.reshape(per, 2 * kw) for b in both]
-
-    dh, dz, d_attn, dq, dkv = ([None] * micro for _ in range(5))
-    out_terms = [None] * micro
-    out_back = [None] * micro
-    last = micro - 1
-    dh[0], dz[0], d_attn[0] = before_attention(0)
-    dx_terms.append(terms_of(parts[last][2], swap(parts[last][3])))
-    d_attn, dx_terms, dh, dz = pin(d_attn, dx_terms, dh, dz)
-    dx_back.append(exchange(dx_terms[last], "dp"))
-    dq[0], dkv[0] = attention_back(0, d_attn[0])
-    grad_hop(0, 2)
-    dx_back, dq, dkv, rising, falling = pin(dx_back, dq, dkv, rising, falling)
-    dkv_hop(0, 0)
-    dh[last], dz[last], d_attn[last] = before_attention(last)
-    d_attn, dkv_sum, dh, dz, dkv = pin(d_attn, dkv_sum, dh, dz, dkv)
-    dkv_hop(0, 1)
-    grad_hop(1, 0)
-    dq[last], dkv[last] = attention_back(last, d_attn[last])
-    dkv_sum, dq, dkv, rising, falling, parts = pin(dkv_sum, dq, dkv, rising, falling, parts)
-    dkv_hop(0, 2)
-    dkv_hop(last, 0)
+            every = from_last(jnp.concatenate(live["dkv"][m]), n - 1 - me_ctx, n)
+            terms = [lax.psum_scatter(every, "ctx", scatter_dimension=0, tiled=True)]
+        terms = [t.reshape(per, 2 * kw) for t in terms]
+        return back_call(
+            live["dq"][m],
+            terms,
+            live["x"],
+            m,
+            live["cosine"],
+            live["sine"],
+            live["qo_full"],
+            live["kv_full"],
+        )
+
+    def out_total(m):
+        total = add(*live["out_back"][m])
+        moe = in_order(total, swap(total)).astype(F32)
+        return (cut(live["hidden"], m) + moe).astype(BF)
+
+    def early_send(*steps):
+        if hops:
+            for s in steps:
+                live["early"][s] = lax.ppermute(live["early"][s], "dp", apart(dp, s))
+
+    before_attention(0)
+    dx_terms(1)
+    grad_send(1, 1, 2)
+    out_terms(0)
+    seal_but(lambda: [(live["rows"][1], [1, 2])])
+    dx_send(1)
+    attention_back(0)
+    seal()
+    dkv_send(0, 1, 2, 3)
+    out_send(0)
+    before_attention(1)
+    out_terms(1)
+    seal_but(lambda: [(live["dkv_sum"][0], [1, 2, 3]), (live["out_back"], [0])])
+    out_send(1)
+    attention_back(1)
+    seal()
+    dkv_send(1, 1, 2, 3)
     pieces_now = dp_now if hops else jnp.zeros((1,), jnp.int32)
     early = grads_call(
         pieces_now,
         [
-            [(cut(normed, m), dq[m]) for m in micros],
-            [(dz[m], attn[m * seq_count : (m + 1) * seq_count].reshape(per, qw)) for m in micros],
+            [(live["normed"], live["dq"][m], m * per) for m in micros],
+            [(jnp.concatenate(live["dz"]), live["attn"].reshape(rows, qw), 0)],
         ],
         None,
         dp,
     )
-    out_got = [swap(parts[m][1]) for m in micros]
-    early, out_got, dkv_sum, dkv, parts = pin(early, out_got, dkv_sum, dkv, parts)
-    dkv_hop(last, 1)
-    grad_hop(1, 1)
+    seal_but(lambda: [(live["dkv_sum"][1], [1, 2, 3])], early=list(early))
+    early_send(1, 2, 3)
+    owned = [grad_own(0)]
+    dkv_first, part_first, gain_first = back(0)
+    got_first = swap(part_first)
+    out_first = out_total(0)
+    out_last = out_total(1)
+    seal(
+        got=[got_first],
+        output=[out_first, out_last],
+        owned=owned,
+        dkv_final=[dkv_first],
+        part=[part_first],
+        gain_one_sums=[gain_first],
+    )
+    grad_send(1, 3)
+    dkv_last, part_last, gain_last = back(1)
+    live["dkv_final"].append(dkv_last)
+    live["part"].append(part_last)
+    small = jnp.concatenate(
+        [
+            live["router_sums"][0] + live["router_sums"][1],
+            (live["gain_one_sums"][0] + gain_last)[0][:, None],
+            (live["gain_sums"][0] + live["gain_sums"][1])[:, None],
+        ],
+        axis=1,
+    )
+    small = jnp.pad(small, ((0, 0), (0, 128 - small.shape[1]))).astype(BF)
+    late = grads_call(
+        pieces_now,
+        [[(live["normed"], live["dkv_final"][m], m * per) for m in micros]],
+        small,
+        dp,
+    )
+    got_last = swap(part_last)
+    early = live["early"]
     if hops:
-        early = exchange(early, "dp")
-    owned = [grad_own(0)]
-    out_terms = [terms_of(parts[m][0], out_got[m]) for m in micros]
-    dkv_own_m, part = [None] * micro, [None] * micro
-
-    def back(m):
-        return back_call(dq[m], dkv_own(m), cosine, sine, qo_full, kv_full)
-
-    dkv_own_m[0], part[0] = back(0)
-    early, out_terms, dkv_sum, rising, falling, owned, part, dkv, dkv_own_m = pin(
-        early, out_terms, dkv_sum, rising, falling, owned, part, dkv, dkv_own_m
+        early = line_call(ctx_now, early, n)
+    seal_but(
+        lambda: [(live["rows"][1], [3])], late=late, early=early, got=live["got"] + [got_last]
     )
-    dkv_hop(last, 2)
+    late = live["late"]
     if hops:
-        early = exchange(line_call(ctx_now, early, n), "ctx")
-    out_back[0] = exchange(out_terms[0], "dp")
-    early, dkv_sum, out_back, out_terms, part, dkv = pin(
-        early, dkv_sum, out_back, out_terms, part, dkv
+        late = exchange(late, "dp")
+    d_normed = jnp.concatenate(
+        [p.astype(F32) + g.astype(F32) for p, g in zip(live["part"], live["got"])]
     )
-    grad_hop(1, 2)
-    dkv_own_m[last], part[last] = back(last)
-    got = [swap(p) for p in part]
-    rows_late = [(cut(normed, m), dkv_own_m[m]) for m in micros]
-    d_normed = jnp.concatenate([p.astype(F32) + g.astype(F32) for p, g in zip(part, got)])
-    out_back[last] = exchange(out_terms[last], "dp")
-    got, d_normed, out_back, rising, falling = pin(got, d_normed, out_back, rising, falling)
-    x32 = x.astype(F32)
+    x32 = live["x"].astype(F32)
     inv_one = lax.rsqrt(jnp.mean(x32 * x32, axis=1, keepdims=True) + EPS)
     n_one = x32 * inv_one
-    grad_gain_one = jnp.sum(d_normed * n_one, axis=0)
-    small_grad = jnp.concatenate(
-        [grad_sums[0], grad_gain_one[:, None], grad_sums[1][:, None]], axis=1
-    )
-    small_grad = jnp.pad(small_grad, ((0, 0), (0, 128 - small_grad.shape[1]))).astype(BF)
-    late = grads_call(pieces_now, [rows_late], small_grad, dp)
+    g_one = d_normed * live["gain_one"]
+    input_grad = (
+        jnp.concatenate(live["dh"])
+        + inv_one * (g_one - n_one * jnp.mean(g_one * n_one, axis=1, keepdims=True))
+    ).astype(BF)
+    seal_but(lambda: [(live["rows"][1], [3])], late=late, input_grad=input_grad)
+    early, late = live["early"], live["late"]
     if hops:
-        late = exchange(late, "dp")
         late = exchange(line_call(ctx_now, late, n), "ctx")
+        early = exchange(early, "ctx")
     else:
         early, late = (
             [
@@ -1164,22 +1276,16 @@
             ]
             for p in (early, late)
         )
-    owned.append(grad_own(1))
-    g_one = d_normed * gain_one
-    input_grad = (
-        jnp.concatenate(dh)
-        + inv_one * (g_one - n_one * jnp.mean(g_one * n_one, axis=1, keepdims=True))
-    ).astype(BF)
-    totals = [add(*b) for b in out_back]
-    moe = jnp.concatenate([in_order(t, swap(t)) for t in totals])
-    output = (hidden + moe.astype(F32)).astype(BF)
+    owned = [live["owned"][0], grad_own(1)]
+    output = jnp.concatenate(live["output"])
     grad_q, grad_k, grad_v, grad_o, small_grad = finish_call(early, late, qw, kw)
+    gain_part = small_grad[:, experts]
     dw_gate, dw_up, dw_down = expert_rows_call(dp_now, owned[0] + owned[1], experts, units)
     shape = tokens.shape
     return (
         output.reshape(shape),
-        input_grad.reshape(shape),
-        small_grad[:, experts],
+        live["input_grad"].reshape(shape),
+        gain_part + swap(gain_part),
         grad_q,
         grad_k,
         grad_v,

time: 731 us -> 663 us (0.907)
  starting transfers between devices: 196 us -> 122 us
  waiting for transfers between devices: 180 us -> 209 us
  other arithmetic: 89.6 us -> 69.2 us
    ppermute x36 -> x30, waiting for transfers between devices: 80.1 us -> 132 us  [the longest x6 42.8 us: dkv_send(): lax.ppermute(live['dkv'][m][d], 'ctx', [(c, c - d) for c in range(d, n)])]
    ppermute x36 -> x30, starting transfers between devices: 91.8 us -> 50.2 us  [the longest x6 14.7 us: grad_send(): live['rows'][g][s] = lax.ppermute(live['dws'][g][s], 'ctx', apart(n, s))]
    convert_element_type x24 -> x10, other arithmetic: 45.5 us -> 20.6 us  [add(): return functools.reduce(jnp.add, [t.astype(F32) for t in terms]).astype(BF)]
    ppermute x33 -> x30, starting transfers between devices: 61.9 us -> 41.3 us  [exchange(): lax.ppermute(parts[s], axis, apart(count, s))]
    ppermute x33 -> x30, waiting for transfers between devices: 58.7 us -> 38.2 us  [exchange(): lax.ppermute(parts[s], axis, apart(count, s))]
    ppermute x9 -> x3, starting transfers between devices: 20.4 us -> 7.07 us  [up_hop(): return lax.ppermute(value, 'ctx', [(c, c + 1) for c in range(s, n - 1)])]
    ppermute x6, waiting for transfers between devices: 29.5 us -> 19.4 us  [gather_plane(): lax.ppermute(value, 'dp', apart(dp, s))]
    unnamed x233 -> x164, local copies, waits for them, and re-layouts: 21.7 us -> 21 us
  transfers between devices with their start and end apart: 113 -> 96, of which waited for: 36 -> 36; matrix products, arithmetic and copies ran while one was open for 14% -> 13% of each run, Pallas kernels for 27% -> 29%
where the time goes in v3:
time: 663 us; the launch traced here: 655 us
  waiting for transfers between devices  209 us (32%)
  Pallas kernels  206 us (31%)
  starting transfers between devices  122 us (18%)
  other arithmetic  69.2 us (10%)
  local copies, waits for them, and re-layouts  34.2 us (5%)
  matrix products  11.5 us (2%)
    pallas_call x4, Pallas kernels, experts_call(): pl.pallas_call(functools.partial(experts_kernel, steps, first, count, mic...  123 us
    ppermute x6, waiting for transfers between devices, dkv_send(): lax.ppermute(live['dkv'][m][d], 'ctx', [(c, c - d) for c in range(d, n)])  42.8 us
    ppermute x30, starting transfers between devices, exchange(): lax.ppermute(parts[s], axis, apart(count, s))  41.3 us
    ppermute x30, waiting for transfers between devices, exchange(): lax.ppermute(parts[s], axis, apart(count, s))  38.2 us
    ppermute x6, waiting for transfers between devices, weight_send(): lax.ppermute(live['weights'][g][at], 'ctx', apart(n, hop))  32.6 us
    ppermute x3, waiting for transfers between devices, dy_send(): live['dy_far'].append(lax.ppermute(live['dy_cut'][0], 'dp', apart(dp, s)))  24.9 us
    pallas_call x2, Pallas kernels, attn_bwd(): pl.pallas_call(functools.partial(attn_bwd_kernel, counts), grid=(seqs, pa...  21 us
    unnamed x164, local copies, waits for them, and re-layouts  21 us
  transfers between devices with their start and end apart: 96, of which 36 were waited for; matrix products, arithmetic and copies ran while one was open for 13% of the time, Pallas kernels for 29%

profile of v3, /device:TPU:0, one launch (start us, length us, event | category | flops | bytes accessed | tf_op | source)
XLA Modules:
  0.0 654.6 jit_solution(16317250519054421843)
XLA Ops:
  2.3 4.1 collective-permute-start.1
  17.4 3.8 collective-permute-start.2
  21.2 3.9 collective-permute-done.2
  28.2 3.8 collective-permute-done.4
  44.1 5.1 collective-permute-done.11
  49.2 3.8 collective-permute-done.10
  56.7 5.7 kv.1
  62.4 4.5 collective-permute-start.13
  73.2 6.7 %convert_reduce_fusion = bf16[1024,128]{1,0:T(8,128)(2,1)S(1)} fusion(s32[1024,8]{1,0:T(8,128)} %copy.134), kind=kLoop, calls=%fused_computation.14 | loop fusion | flops 3014656 | bytes 294912 | tf_op jit(solution)/shard_map/reduce_sum | solution.py:926
  82.8 8.4 %collective-permute-done.15 = bf16[4,64,1024]{2,1,0:T(8,128)(2,1)} collective-permute-done((bf16[4,64,1024]{2,1,0:T(8,128)(2,1)S(1)}, bf16[4,64,1024]{2,1,0:T(8,128)(2,1)}, u32[]{:S(2)}, u32[]{:S(2)}) %collective-permute-start.15) | collective-permute-done | bytes 524320 | tf_op jit(solution)/shard_map/ppermute | solution.py:854
  101.7 5.7 q.1
  107.4 8.1 %attn_fwd.3 = (f32[2,2,4,1024]{3,2,1,0:T(4,128)}, f32[2,2,2,128,1024]{4,3,2,1,0:T(8,128)}) custom-call(s32[1]{0:T(128)} %bitcast.ctx_ref.place_ref, bf16[2,512,512]{2,1,0:T(8,128)(2,1)} %bitcast.244, bf16[1,2,512,512]{3,2,1,0:T(8,128)(2,1)} %bitcast.281, bf16[1,2,512,512]{3,2,1,0:T(8,128)(2,1)} %collective-permute-done.13.refs_1_.refs_3_.refs_5_, ...), custom_call_target="tpu_custom_call" | custom-call | flops 8589934592 | bytes 4194304 | tf_op jit(solution)/shard_map/attn_fwd/pallas_call | solution.py:245
  115.5 4.2 collective-permute-done.18.refs_12_
  124.2 5.5 attn_fwd.4
  129.7 19.3 %collective-permute-done.20.refs_14_ = bf16[2,256,1152]{2,1,0:T(8,128)(2,1)S(1)} collective-permute-done((bf16[2,256,1152]{2,1,0:T(8,128)(2,1)}, bf16[2,256,1152]{2,1,0:T(8,128)(2,1)S(1)}, u32[]{:S(2)}, u32[]{:S(2)}) %collective-permute-start.20) | collective-permute-done | bytes 1179680 | tf_op jit(solution)/shard_map/ppermute | solution.py:975
  150.5 5.1 attn_fwd.5
  158.8 4.7 collective-permute-start.26
  171.7 26.5 %collective-permute-done.26.refs_18_ = bf16[4,64,1536]{2,1,0:T(8,128)(2,1)S(1)} collective-permute-done((bf16[4,64,1536]{2,1,0:T(8,128)(2,1)S(1)}, bf16[4,64,1536]{2,1,0:T(8,128)(2,1)S(1)}, u32[]{:S(2)}, u32[]{:S(2)}) %collective-permute-start.26) | collective-permute-done | bytes 786464 | tf_op jit(solution)/shard_map/ppermute | solution.py:886
  200.3 13.2 %collective-permute-done.30.refs_6_ = bf16[256,1024]{1,0:T(8,128)(2,1)} collective-permute-done((bf16[256,1024]{1,0:T(8,128)(2,1)S(1)}, bf16[256,1024]{1,0:T(8,128)(2,1)}, u32[]{:S(2)}, u32[]{:S(2)}) %collective-permute-start.30) | collective-permute-done | bytes 524320 | tf_op jit(solution)/shard_map/ppermute | solution.py:843
  213.5 3.7 collective-permute-done.29.refs_19_
  229.9 30.2 %experts.4 = (bf16[4,256,1024]{2,1,0:T(8,128)(2,1)}, bf16[4,256,1024]{2,1,0:T(8,128)(2,1)}, bf16[4,256,1152]{2,1,0:T(8,128)(2,1)}, bf16[4,256,1152]{2,1,0:T(8,12...) custom-call(s32[2]{0:T(128)} %pad_add_fusion.place_ref, ...), custom_call_target="tpu_custom_call" | custom-call | flops 19327352832 | bytes 23068672 | tf_op jit(solution)/shard_map/experts/pallas_call | solution.py:527
  269.4 30.1 %experts.5 = (bf16[4,256,1024]{2,1,0:T(8,128)(2,1)}, bf16[4,256,1024]{2,1,0:T(8,128)(2,1)}, bf16[4,256,1152]{2,1,0:T(8,128)(2,1)}, bf16[4,256,1152]{2,1,0:T(8,12...) custom-call(s32[2]{0:T(128)} %pad_add_fusion.place_ref, ...), custom_call_target="tpu_custom_call" | custom-call | flops 19327352832 | bytes 23068672 | tf_op jit(solution)/shard_map/experts/pallas_call | solution.py:527
  302.0 30.9 %experts.6 = (bf16[4,256,1024]{2,1,0:T(8,128)(2,1)}, bf16[4,256,1024]{2,1,0:T(8,128)(2,1)}, bf16[4,256,1152]{2,1,0:T(8,128)(2,1)}, bf16[4,256,1152]{2,1,0:T(8,12...) custom-call(s32[2]{0:T(128)} %pad_add_fusion.place_ref, ...), custom_call_target="tpu_custom_call" | custom-call | flops 19327352832 | bytes 23068672 | tf_op jit(solution)/shard_map/experts/pallas_call | solution.py:527
  333.0 3.1 collective-permute-done.43
  336.1 4.7 collective-permute-done.45
  340.8 3.2 fusion.26
  347.6 4.4 collective-permute-start.49
  352.0 31.7 %experts.7 = (bf16[4,256,1024]{2,1,0:T(8,128)(2,1)}, bf16[4,256,1024]{2,1,0:T(8,128)(2,1)}, bf16[4,256,1152]{2,1,0:T(8,128)(2,1)}, bf16[4,256,1152]{2,1,0:T(8,12...) custom-call(s32[2]{0:T(128)} %pad_add_fusion.place_ref, ...), custom_call_target="tpu_custom_call" | custom-call | flops 19327352832 | bytes 23068672 | tf_op jit(solution)/shard_map/experts/pallas_call | solution.py:527
  408.6 10.9 %attn_bwd.2 = (bf16[1,512,512]{2,1,0:T(8,128)(2,1)}, bf16[1,1,512,512]{3,2,1,0:T(8,128)(2,1)}, bf16[1,1,512,512]{3,2,1,0:T(8,128)(2,1)}, bf16[1,1,512,512]{3,2,1,0:T(8,128)(2,1)}, bf16[1,1,512,512]{3,2,1,0:T(8,128)(2,1)}) custom-call(s32[1]{0:T(128)} %bitcast.ctx_ref.place_ref, bf16[2,512,512]{2,1,0:T(8,128)(2,1)} %bitcast.247, ...), custom_call_target="tpu_custom_call" | custom-call | flops 21474836480 | bytes 8388608 | tf_op jit(solution)/shard_map/attn_bwd/pallas_call | solution.py:335
  422.3 3.8 collective-permute-done.57
  426.1 8.7 %collective-permute-done.54 = bf16[256,1152]{1,0:T(8,128)(2,1)} collective-permute-done((bf16[256,1152]{1,0:T(8,128)(2,1)}, bf16[256,1152]{1,0:T(8,128)(2,1)}, u32[]{:S(2)}, u32[]{:S(2)}) %collective-permute-start.54) | collective-permute-done | bytes 589856 | tf_op jit(solution)/shard_map/ppermute | solution.py:781
  456.9 31.2 %collective-permute-done.61 = bf16[1,1,512,512]{3,2,1,0:T(8,128)(2,1)} collective-permute-done((bf16[1,1,512,512]{3,2,1,0:T(8,128)(2,1)}, bf16[1,1,512,512]{3,2,1,0:T(8,128)(2,1)}, u32[]{:S(2)}, u32[]{:S(2)}) %collective-permute-start.61) | collective-permute-done | bytes 524320 | tf_op jit(solution)/shard_map/ppermute | solution.py:1151
  491.5 10.2 %attn_bwd.3 = (bf16[1,512,512]{2,1,0:T(8,128)(2,1)}, bf16[1,1,512,512]{3,2,1,0:T(8,128)(2,1)}, bf16[1,1,512,512]{3,2,1,0:T(8,128)(2,1)}, bf16[1,1,512,512]{3,2,1,0:T(8,128)(2,1)}, bf16[1,1,512,512]{3,2,1,0:T(8,128)(2,1)}) custom-call(s32[1]{0:T(128)} %bitcast.ctx_ref.place_ref, bf16[2,512,512]{2,1,0:T(8,128)(2,1)} %bitcast.248, ...), custom_call_target="tpu_custom_call" | custom-call | flops 21474836480 | bytes 8388608 | tf_op jit(solution)/shard_map/attn_bwd/pallas_call | solution.py:335
  503.1 9.9 %collective-permute-done.67 = bf16[256,1024]{1,0:T(8,128)(2,1)S(1)} collective-permute-done((bf16[256,1024]{1,0:T(8,128)(2,1)}, bf16[256,1024]{1,0:T(8,128)(2,1)S(1)}, u32[]{:S(2)}, u32[]{:S(2)}) %collective-permute-start.67) | collective-permute-done | bytes 524320 | tf_op jit(solution)/shard_map/ppermute | solution.py:781
  518.2 6.7 %grads.2 = (bf16[256,1024]{1,0:T(8,128)(2,1)}, bf16[256,1024]{1,0:T(8,128)(2,1)}, bf16[256,1024]{1,0:T(8,128)(2,1)}, bf16[256,1024]{1,0:T(8,128)(2,1)}) custom-call(s32[1]{0:T(128)} %bitcast.80.place_ref, bf16[1024,1024]{1,0:T(8,128)(2,1)} %get-tuple-element.1932.normed_ref.refs_0_.refs_2_, bf16[512,512]{1,0:T(8,128)(2,1)} %bitcast.234, ...), custom_call_target="tpu_custom_call" | custom-call | flops 2147483648 | bytes 4194304 | tf_op jit(solution)/shard_map/grads/pallas_call | solution.py:649
  538.0 5.2 back.2
  545.4 5.2 collective-permute-done.78.refs_1_
  557.4 11.6 %collective-permute-done.71 = bf16[1,1,512,512]{3,2,1,0:T(8,128)(2,1)S(1)} collective-permute-done((bf16[1,1,512,512]{3,2,1,0:T(8,128)(2,1)}, bf16[1,1,512,512]{3,2,1,0:T(8,128)(2,1)S(1)}, u32[]{:S(2)}, u32[]{:S(2)}) %collective-permute-start.71) | collective-permute-done | bytes 524320 | tf_op jit(solution)/shard_map/ppermute | solution.py:1151
  569.1 8.8 %collective-permute-done.73.refs_2_ = bf16[256,1024]{1,0:T(8,128)(2,1)S(1)} collective-permute-done((bf16[256,1024]{1,0:T(8,128)(2,1)}, bf16[256,1024]{1,0:T(8,128)(2,1)S(1)}, u32[]{:S(2)}, u32[]{:S(2)}) %collective-permute-start.73) | collective-permute-done | bytes 524320 | tf_op jit(solution)/shard_map/ppermute | solution.py:1181
  578.8 5.2 back.3
  584.1 5.7 collective-permute-start.92
  594.4 4.9 grads.3
  609.3 3.2 fusion.6
  612.5 4.9 collective-permute-done.83.refs_2_
  618.3 3.5 collective-permute-start.87
  624.0 6.2 collective-permute-start.89
  634.6 5.0 collective-permute-done.89.refs_6_
  650.9 3.3 expert_rows.1
  (434 shorter events, 213.7 us)
Async XLA Ops:
  13.0 20.4 %collective-permute-start.7 = (bf16[2,64,1536]{2,1,0:T(8,128)(2,1)}, bf16[2,64,1536]{2,1,0:T(8,128)(2,1)S(1)}, u32[]{:S(2)}, u32[]{:S(2)}) collective-permute-start(bf16[2,64,1536]{2,1,0:T(8,128)(2,1)} %get-tuple-element.2086), channel_id=1, source_target_pairs={{0,16},{8,24},{16,0},{24,8},{1,17},{9,25},{17,1},{25,9},{2,18},{10... | collective-permute-start | bytes 1179656 | tf_op jit(solution)/shard_map/ppermute | solution.py:781
  14.6 18.9 %collective-permute-start.8 = (bf16[2,64,1536]{2,1,0:T(8,128)(2,1)}, bf16[2,64,1536]{2,1,0:T(8,128)(2,1)S(1)}, u32[]{:S(2)}, u32[]{:S(2)}) collective-permute-start(bf16[2,64,1536]{2,1,0:T(8,128)(2,1)} %get-tuple-element.2123), channel_id=1, source_target_pairs={{0,8},{8,0},{16,24},{24,16},{1,9},{9,1},{17,25},{25,17},{2,10},{10... | collective-permute-start | bytes 1179656 | tf_op jit(solution)/shard_map/ppermute | solution.py:781
  35.9 17.9 %collective-permute-start.12 = (bf16[4,64,1536]{2,1,0:T(8,128)(2,1)S(1)}, bf16[4,64,1536]{2,1,0:T(8,128)(2,1)}, u32[]{:S(2)}, u32[]{:S(2)}) collective-permute-start(bf16[4,64,1536]{2,1,0:T(8,128)(2,1)S(1)} %pad_maximum_fusion.6.refs_16_), channel_id=1, source_target_pairs={{0,2},{2,0},{4,6},{6,4},{1,3},{3,1},{5,7},{7,5},{8,10},{10,8},{12,... | collective-permute-start | bytes 2359304 | tf_op jit(solution)/shard_map/ppermute | solution.py:886
  62.4 29.4 %collective-permute-start.13 = (bf16[1,2,512,512]{3,2,1,0:T(8,128)(2,1)}, bf16[1,2,512,512]{3,2,1,0:T(8,128)(2,1)}, u32[]{:S(2)}, u32[]{:S(2)}) collective-permute-start(bf16[1,2,512,512]{3,2,1,0:T(8,128)(2,1)} %bitcast.280), channel_id=1, source_target_pairs={{0,2},{2,4},{4,6},{1,3},{3,5},{5,7},{8,10},{10,12},{12,14},{9,11},... | collective-permute-start | bytes 3145736 | tf_op jit(solution)/shard_map/ppermute | solution.py:762
  69.4 21.8 %collective-permute-start.15 = (bf16[4,64,1024]{2,1,0:T(8,128)(2,1)S(1)}, bf16[4,64,1024]{2,1,0:T(8,128)(2,1)}, u32[]{:S(2)}, u32[]{:S(2)}) collective-permute-start(bf16[4,64,1024]{2,1,0:T(8,128)(2,1)S(1)} %pad_maximum_fusion.8), channel_id=1, source_target_pairs={{0,16},{8,24},{16,0},{24,8},{1,17},{9,25},{17,1},{25,9},{2,18},{10... | collective-permute-start | bytes 1572872 | tf_op jit(solution)/shard_map/ppermute | solution.py:854
  69.9 21.9 %collective-permute-start.14 = (bf16[4,64,1024]{2,1,0:T(8,128)(2,1)S(1)}, bf16[4,64,1024]{2,1,0:T(8,128)(2,1)}, u32[]{:S(2)}, u32[]{:S(2)}) collective-permute-start(bf16[4,64,1024]{2,1,0:T(8,128)(2,1)S(1)} %pad_maximum_fusion.8), channel_id=1, source_target_pairs={{0,8},{8,0},{16,24},{24,16},{1,9},{9,1},{17,25},{25,17},{2,10},{10... | collective-permute-start | bytes 1572872 | tf_op jit(solution)/shard_map/ppermute | solution.py:854
  91.8 27.9 %collective-permute-start.18 = (bf16[2,256,1152]{2,1,0:T(8,128)(2,1)}, bf16[2,256,1152]{2,1,0:T(8,128)(2,1)}, u32[]{:S(2)}, u32[]{:S(2)}) collective-permute-start(bf16[2,256,1152]{2,1,0:T(8,128)(2,1)} %get-tuple-element.1579.refs_8_), channel_id=1, source_target_pairs={{0,16},{8,24},{16,0},{24,8},{1,17},{9,25},{17,1},{25,9},{2,18},{10... | collective-permute-start | bytes 3538952 | tf_op jit(solution)/shard_map/ppermute | solution.py:975
  93.2 27.9 %collective-permute-start.17 = (bf16[2,256,1152]{2,1,0:T(8,128)(2,1)}, bf16[2,256,1152]{2,1,0:T(8,128)(2,1)}, u32[]{:S(2)}, u32[]{:S(2)}) collective-permute-start(bf16[2,256,1152]{2,1,0:T(8,128)(2,1)} %get-tuple-element.1579.refs_8_), channel_id=1, source_target_pairs={{0,8},{8,0},{16,24},{24,16},{1,9},{9,1},{17,25},{25,17},{2,10},{10... | collective-permute-start | bytes 3538952 | tf_op jit(solution)/shard_map/ppermute | solution.py:975
  121.1 27.8 %collective-permute-start.20 = (bf16[2,256,1152]{2,1,0:T(8,128)(2,1)}, bf16[2,256,1152]{2,1,0:T(8,128)(2,1)S(1)}, u32[]{:S(2)}, u32[]{:S(2)}) collective-permute-start(bf16[2,256,1152]{2,1,0:T(8,128)(2,1)} %get-tuple-element.1579.refs_8_), channel_id=1, source_target_pairs={{0,24},{8,16},{16,8},{24,0},{1,25},{9,17},{17,9},{25,1},{2,26},{10... | collective-permute-start | bytes 3538952 | tf_op jit(solution)/shard_map/ppermute | solution.py:975
  158.8 39.4 %collective-permute-start.26 = (bf16[4,64,1536]{2,1,0:T(8,128)(2,1)S(1)}, bf16[4,64,1536]{2,1,0:T(8,128)(2,1)S(1)}, u32[]{:S(2)}, u32[]{:S(2)}) collective-permute-start(bf16[4,64,1536]{2,1,0:T(8,128)(2,1)S(1)} %copy-done.31), channel_id=1, source_target_pairs={{0,4},{2,6},{4,0},{6,2},{1,5},{3,7},{5,1},{7,3},{8,12},{10,14},{12... | collective-permute-start | bytes 2359304 | tf_op jit(solution)/shard_map/ppermute | solution.py:886
  169.7 28.4 %collective-permute-start.28 = (bf16[256,1024]{1,0:T(8,128)(2,1)S(1)}, bf16[256,1024]{1,0:T(8,128)(2,1)}, u32[]{:S(2)}, u32[]{:S(2)}) collective-permute-start(bf16[256,1024]{1,0:T(8,128)(2,1)S(1)} %get-tuple-element.1445.refs_0_), channel_id=1, source_target_pairs={{0,16},{8,24},{16,0},{24,8},{1,17},{9,25},{17,1},{25,9},{2,18},{10... | collective-permute-start | bytes 1572872 | tf_op jit(solution)/shard_map/ppermute | solution.py:843
  171.3 26.9 %collective-permute-start.27 = (bf16[256,1024]{1,0:T(8,128)(2,1)S(1)}, bf16[256,1024]{1,0:T(8,128)(2,1)}, u32[]{:S(2)}, u32[]{:S(2)}) collective-permute-start(bf16[256,1024]{1,0:T(8,128)(2,1)S(1)} %get-tuple-element.1445.refs_0_), channel_id=1, source_target_pairs={{0,8},{8,0},{16,24},{24,16},{1,9},{9,1},{17,25},{25,17},{2,10},{10... | collective-permute-start | bytes 1572872 | tf_op jit(solution)/shard_map/ppermute | solution.py:843
  198.2 19.1 %collective-permute-start.29 = (bf16[4,64,1536]{2,1,0:T(8,128)(2,1)S(1)}, bf16[4,64,1536]{2,1,0:T(8,128)(2,1)S(1)}, u32[]{:S(2)}, u32[]{:S(2)}) collective-permute-start(bf16[4,64,1536]{2,1,0:T(8,128)(2,1)S(1)} %collective-permute-done.26.refs_18_), channel_id=1, source_target_pairs={{0,2},{2,0},{4,6},{6,4},{1,3},{3,1},{5,7},{7,5},{8,10},{10,8},{12,... | collective-permute-start | bytes 2359304 | tf_op jit(solution)/shard_map/ppermute | solution.py:886
  221.9 38.2 %collective-permute-start.38 = (bf16[256,1024]{1,0:T(8,128)(2,1)S(1)}, bf16[256,1024]{1,0:T(8,128)(2,1)S(1)}, u32[]{:S(2)}, u32[]{:S(2)}) collective-permute-start(bf16[256,1024]{1,0:T(8,128)(2,1)S(1)} %get-tuple-element.1571.refs_0_), channel_id=1, source_target_pairs={{0,24},{8,16},{16,8},{24,0},{1,25},{9,17},{17,9},{25,1},{2,26},{10... | collective-permute-start | bytes 1572872 | tf_op jit(solution)/shard_map/ppermute | solution.py:843
  223.3 36.9 %collective-permute-start.37 = (bf16[256,1024]{1,0:T(8,128)(2,1)S(1)}, bf16[256,1024]{1,0:T(8,128)(2,1)}, u32[]{:S(2)}, u32[]{:S(2)}) collective-permute-start(bf16[256,1024]{1,0:T(8,128)(2,1)S(1)} %get-tuple-element.1571.refs_0_), channel_id=1, source_target_pairs={{0,16},{8,24},{16,0},{24,8},{1,17},{9,25},{17,1},{25,9},{2,18},{10... | collective-permute-start | bytes 1572872 | tf_op jit(solution)/shard_map/ppermute | solution.py:843
  224.9 35.2 %collective-permute-start.36 = (bf16[256,1024]{1,0:T(8,128)(2,1)S(1)}, bf16[256,1024]{1,0:T(8,128)(2,1)}, u32[]{:S(2)}, u32[]{:S(2)}) collective-permute-start(bf16[256,1024]{1,0:T(8,128)(2,1)S(1)} %get-tuple-element.1571.refs_0_), channel_id=1, source_target_pairs={{0,8},{8,0},{16,24},{24,16},{1,9},{9,1},{17,25},{25,17},{2,10},{10... | collective-permute-start | bytes 1572872 | tf_op jit(solution)/shard_map/ppermute | solution.py:843
  225.4 37.1 %collective-permute-start.35 = (bf16[4,64,1536]{2,1,0:T(8,128)(2,1)}, bf16[4,64,1536]{2,1,0:T(8,128)(2,1)}, u32[]{:S(2)}, u32[]{:S(2)}) collective-permute-start(bf16[4,64,1536]{2,1,0:T(8,128)(2,1)} %pad_maximum_fusion.7.refs_16_), channel_id=1, source_target_pairs={{0,4},{2,6},{4,0},{6,2},{1,5},{3,7},{5,1},{7,3},{8,12},{10,14},{12... | collective-permute-start | bytes 2359304 | tf_op jit(solution)/shard_map/ppermute | solution.py:886
  228.2 34.4 %collective-permute-start.34 = (bf16[4,64,1536]{2,1,0:T(8,128)(2,1)}, bf16[4,64,1536]{2,1,0:T(8,128)(2,1)}, u32[]{:S(2)}, u32[]{:S(2)}) collective-permute-start(bf16[4,64,1536]{2,1,0:T(8,128)(2,1)} %pad_maximum_fusion.7.refs_16_), channel_id=1, source_target_pairs={{0,2},{2,0},{4,6},{6,4},{1,3},{3,1},{5,7},{7,5},{8,10},{10,8},{12,... | collective-permute-start | bytes 2359304 | tf_op jit(solution)/shard_map/ppermute | solution.py:886
  267.8 31.7 %collective-permute-start.42 = (bf16[4,64,1536]{2,1,0:T(8,128)(2,1)}, bf16[4,64,1536]{2,1,0:T(8,128)(2,1)}, u32[]{:S(2)}, u32[]{:S(2)}) collective-permute-start(bf16[4,64,1536]{2,1,0:T(8,128)(2,1)} %collective-permute-done.35.refs_18_), channel_id=1, source_target_pairs={{0,2},{2,0},{4,6},{6,4},{1,3},{3,1},{5,7},{7,5},{8,10},{10,8},{12,... | collective-permute-start | bytes 2359304 | tf_op jit(solution)/shard_map/ppermute | solution.py:886
  299.5 36.5 %collective-permute-start.43 = (bf16[4,64,1536]{2,1,0:T(8,128)(2,1)}, bf16[4,64,1536]{2,1,0:T(8,128)(2,1)}, u32[]{:S(2)}, u32[]{:S(2)}) collective-permute-start(bf16[4,64,1536]{2,1,0:T(8,128)(2,1)} %get-tuple-element.1441), channel_id=1, source_target_pairs={{0,2},{2,0},{4,6},{6,4},{1,3},{3,1},{5,7},{7,5},{8,10},{10,8},{12,... | collective-permute-start | bytes 2359304 | tf_op jit(solution)/shard_map/ppermute | solution.py:1063
  300.1 36.0 %collective-permute-start.44 = (bf16[4,64,1536]{2,1,0:T(8,128)(2,1)}, bf16[4,64,1536]{2,1,0:T(8,128)(2,1)}, u32[]{:S(2)}, u32[]{:S(2)}) collective-permute-start(bf16[4,64,1536]{2,1,0:T(8,128)(2,1)} %get-tuple-element.1442), channel_id=1, source_target_pairs={{0,4},{2,6},{4,0},{6,2},{1,5},{3,7},{5,1},{7,3},{8,12},{10,14},{12... | collective-permute-start | bytes 2359304 | tf_op jit(solution)/shard_map/ppermute | solution.py:1063
  344.1 39.6 %collective-permute-start.46 = (bf16[256,1152]{1,0:T(8,128)(2,1)}, bf16[256,1152]{1,0:T(8,128)(2,1)}, u32[]{:S(2)}, u32[]{:S(2)}) collective-permute-start(bf16[256,1152]{1,0:T(8,128)(2,1)} %get-tuple-element.1604), channel_id=1, source_target_pairs={{0,8},{8,0},{16,24},{24,16},{1,9},{9,1},{17,25},{25,17},{2,10},{10... | collective-permute-start | bytes 1769480 | tf_op jit(solution)/shard_map/ppermute | solution.py:781
  345.7 38.0 %collective-permute-start.47 = (bf16[256,1152]{1,0:T(8,128)(2,1)}, bf16[256,1152]{1,0:T(8,128)(2,1)}, u32[]{:S(2)}, u32[]{:S(2)}) collective-permute-start(bf16[256,1152]{1,0:T(8,128)(2,1)} %get-tuple-element.1605), channel_id=1, source_target_pairs={{0,16},{8,24},{16,0},{24,8},{1,17},{9,25},{17,1},{25,9},{2,18},{10... | collective-permute-start | bytes 1769480 | tf_op jit(solution)/shard_map/ppermute | solution.py:781
  346.0 37.7 %collective-permute-start.48 = (bf16[256,1152]{1,0:T(8,128)(2,1)}, bf16[256,1152]{1,0:T(8,128)(2,1)}, u32[]{:S(2)}, u32[]{:S(2)}) collective-permute-start(bf16[256,1152]{1,0:T(8,128)(2,1)} %get-tuple-element.1606), channel_id=1, source_target_pairs={{0,24},{8,16},{16,8},{24,0},{1,25},{9,17},{17,9},{25,1},{2,26},{10... | collective-permute-start | bytes 1769480 | tf_op jit(solution)/shard_map/ppermute | solution.py:781
  347.6 36.1 %collective-permute-start.49 = (bf16[4,64,1536]{2,1,0:T(8,128)(2,1)}, bf16[4,64,1536]{2,1,0:T(8,128)(2,1)}, u32[]{:S(2)}, u32[]{:S(2)}) collective-permute-start(bf16[4,64,1536]{2,1,0:T(8,128)(2,1)} %get-tuple-element.1569), channel_id=1, source_target_pairs={{0,6},{2,4},{4,2},{6,0},{1,7},{3,5},{5,3},{7,1},{8,14},{10,12},{12... | collective-permute-start | bytes 2359304 | tf_op jit(solution)/shard_map/ppermute | solution.py:1063
  386.3 36.0 %collective-permute-start.56 = (bf16[4,64,1536]{2,1,0:T(8,128)(2,1)}, bf16[4,64,1536]{2,1,0:T(8,128)(2,1)}, u32[]{:S(2)}, u32[]{:S(2)}) collective-permute-start(bf16[4,64,1536]{2,1,0:T(8,128)(2,1)} %get-tuple-element.1650), channel_id=1, source_target_pairs={{0,2},{2,0},{4,6},{6,4},{1,3},{3,1},{5,7},{7,5},{8,10},{10,8},{12,... | collective-permute-start | bytes 2359304 | tf_op jit(solution)/shard_map/ppermute | solution.py:1063
  388.3 37.8 %collective-permute-start.57 = (bf16[4,64,1536]{2,1,0:T(8,128)(2,1)}, bf16[4,64,1536]{2,1,0:T(8,128)(2,1)}, u32[]{:S(2)}, u32[]{:S(2)}) collective-permute-start(bf16[4,64,1536]{2,1,0:T(8,128)(2,1)} %get-tuple-element.1651), channel_id=1, source_target_pairs={{0,4},{2,6},{4,0},{6,2},{1,5},{3,7},{5,1},{7,3},{8,12},{10,14},{12... | collective-permute-start | bytes 2359304 | tf_op jit(solution)/shard_map/ppermute | solution.py:1063
  405.1 21.0 %collective-permute-start.53 = (bf16[256,1152]{1,0:T(8,128)(2,1)}, bf16[256,1152]{1,0:T(8,128)(2,1)}, u32[]{:S(2)}, u32[]{:S(2)}) collective-permute-start(bf16[256,1152]{1,0:T(8,128)(2,1)} %get-tuple-element.1693), channel_id=1, source_target_pairs={{0,8},{8,0},{16,24},{24,16},{1,9},{9,1},{17,25},{25,17},{2,10},{10... | collective-permute-start | bytes 1769480 | tf_op jit(solution)/shard_map/ppermute | solution.py:781
  406.7 28.1 %collective-permute-start.54 = (bf16[256,1152]{1,0:T(8,128)(2,1)}, bf16[256,1152]{1,0:T(8,128)(2,1)}, u32[]{:S(2)}, u32[]{:S(2)}) collective-permute-start(bf16[256,1152]{1,0:T(8,128)(2,1)} %get-tuple-element.1694), channel_id=1, source_target_pairs={{0,16},{8,24},{16,0},{24,8},{1,17},{9,25},{17,1},{25,9},{2,18},{10... | collective-permute-start | bytes 1769480 | tf_op jit(solution)/shard_map/ppermute | solution.py:781
  407.1 27.8 %collective-permute-start.55 = (bf16[256,1152]{1,0:T(8,128)(2,1)}, bf16[256,1152]{1,0:T(8,128)(2,1)}, u32[]{:S(2)}, u32[]{:S(2)}) collective-permute-start(bf16[256,1152]{1,0:T(8,128)(2,1)} %get-tuple-element.1695), channel_id=1, source_target_pairs={{0,24},{8,16},{16,8},{24,0},{1,25},{9,17},{17,9},{25,1},{2,26},{10... | collective-permute-start | bytes 1769480 | tf_op jit(solution)/shard_map/ppermute | solution.py:781
  436.9 18.5 %collective-permute-start.60 = (bf16[1,1,512,512]{3,2,1,0:T(8,128)(2,1)}, bf16[1,1,512,512]{3,2,1,0:T(8,128)(2,1)}, u32[]{:S(2)}, u32[]{:S(2)}) collective-permute-start(bf16[1,1,512,512]{3,2,1,0:T(8,128)(2,1)} %get-tuple-element.1736), channel_id=1, source_target_pairs={{2,0},{4,2},{6,4},{3,1},{5,3},{7,5},{10,8},{12,10},{14,12},{11,9},... | collective-permute-start | bytes 1572872 | tf_op jit(solution)/shard_map/ppermute | solution.py:1151
  438.3 49.8 %collective-permute-start.61 = (bf16[1,1,512,512]{3,2,1,0:T(8,128)(2,1)}, bf16[1,1,512,512]{3,2,1,0:T(8,128)(2,1)}, u32[]{:S(2)}, u32[]{:S(2)}) collective-permute-start(bf16[1,1,512,512]{3,2,1,0:T(8,128)(2,1)} %get-tuple-element.1737), channel_id=1, source_target_pairs={{4,0},{6,2},{5,1},{7,3},{12,8},{14,10},{13,9},{15,11},{20,16},{22,... | collective-permute-start | bytes 1572872 | tf_op jit(solution)/shard_map/ppermute | solution.py:1151
  439.6 48.9 %collective-permute-start.62 = (bf16[1,1,512,512]{3,2,1,0:T(8,128)(2,1)}, bf16[1,1,512,512]{3,2,1,0:T(8,128)(2,1)}, u32[]{:S(2)}, u32[]{:S(2)}) collective-permute-start(bf16[1,1,512,512]{3,2,1,0:T(8,128)(2,1)} %get-tuple-element.1738), channel_id=1, source_target_pairs={{6,0},{7,1},{14,8},{15,9},{22,16},{23,17},{30,24},{31,25}} | collective-permute-start | bytes 1572872 | tf_op jit(solution)/shard_map/ppermute | solution.py:1151
  441.1 49.0 %collective-permute-start.63 = (bf16[256,1024]{1,0:T(8,128)(2,1)}, bf16[256,1024]{1,0:T(8,128)(2,1)}, u32[]{:S(2)}, u32[]{:S(2)}) collective-permute-start(bf16[256,1024]{1,0:T(8,128)(2,1)} %get-tuple-element.1754), channel_id=1, source_target_pairs={{0,8},{8,0},{16,24},{24,16},{1,9},{9,1},{17,25},{25,17},{2,10},{10... | collective-permute-start | bytes 1572872 | tf_op jit(solution)/shard_map/ppermute | solution.py:781
  451.0 50.7 %collective-permute-start.64 = (bf16[256,1024]{1,0:T(8,128)(2,1)}, bf16[256,1024]{1,0:T(8,128)(2,1)}, u32[]{:S(2)}, u32[]{:S(2)}) collective-permute-start(bf16[256,1024]{1,0:T(8,128)(2,1)} %get-tuple-element.1755), channel_id=1, source_target_pairs={{0,16},{8,24},{16,0},{24,8},{1,17},{9,25},{17,1},{25,9},{2,18},{10... | collective-permute-start | bytes 1572872 | tf_op jit(solution)/shard_map/ppermute | solution.py:781
  455.3 46.4 %collective-permute-start.65 = (bf16[256,1024]{1,0:T(8,128)(2,1)}, bf16[256,1024]{1,0:T(8,128)(2,1)S(1)}, u32[]{:S(2)}, u32[]{:S(2)}) collective-permute-start(bf16[256,1024]{1,0:T(8,128)(2,1)} %get-tuple-element.1756), channel_id=1, source_target_pairs={{0,24},{8,16},{16,8},{24,0},{1,25},{9,17},{17,9},{25,1},{2,26},{10... | collective-permute-start | bytes 1572872 | tf_op jit(solution)/shard_map/ppermute | solution.py:781
  488.5 24.5 %collective-permute-start.67 = (bf16[256,1024]{1,0:T(8,128)(2,1)}, bf16[256,1024]{1,0:T(8,128)(2,1)S(1)}, u32[]{:S(2)}, u32[]{:S(2)}) collective-permute-start(bf16[256,1024]{1,0:T(8,128)(2,1)} %get-tuple-element.1800), channel_id=1, source_target_pairs={{0,16},{8,24},{16,0},{24,8},{1,17},{9,25},{17,1},{25,9},{2,18},{10... | collective-permute-start | bytes 1572872 | tf_op jit(solution)/shard_map/ppermute | solution.py:781
  490.0 23.0 %collective-permute-start.68 = (bf16[256,1024]{1,0:T(8,128)(2,1)}, bf16[256,1024]{1,0:T(8,128)(2,1)}, u32[]{:S(2)}, u32[]{:S(2)}) collective-permute-start(bf16[256,1024]{1,0:T(8,128)(2,1)} %get-tuple-element.1801), channel_id=1, source_target_pairs={{0,24},{8,16},{16,8},{24,0},{1,25},{9,17},{17,9},{25,1},{2,26},{10... | collective-permute-start | bytes 1572872 | tf_op jit(solution)/shard_map/ppermute | solution.py:781
  513.8 38.1 %collective-permute-start.69 = (bf16[1,1,512,512]{3,2,1,0:T(8,128)(2,1)}, bf16[1,1,512,512]{3,2,1,0:T(8,128)(2,1)S(1)}, u32[]{:S(2)}, u32[]{:S(2)}) collective-permute-start(bf16[1,1,512,512]{3,2,1,0:T(8,128)(2,1)} %get-tuple-element.1817), channel_id=1, source_target_pairs={{2,0},{4,2},{6,4},{3,1},{5,3},{7,5},{10,8},{12,10},{14,12},{11,9},... | collective-permute-start | bytes 1572872 | tf_op jit(solution)/shard_map/ppermute | solution.py:1151
  515.1 38.5 %collective-permute-start.70 = (bf16[1,1,512,512]{3,2,1,0:T(8,128)(2,1)}, bf16[1,1,512,512]{3,2,1,0:T(8,128)(2,1)S(1)}, u32[]{:S(2)}, u32[]{:S(2)}) collective-permute-start(bf16[1,1,512,512]{3,2,1,0:T(8,128)(2,1)} %get-tuple-element.1818), channel_id=1, source_target_pairs={{4,0},{6,2},{5,1},{7,3},{12,8},{14,10},{13,9},{15,11},{20,16},{22,... | collective-permute-start | bytes 1572872 | tf_op jit(solution)/shard_map/ppermute | solution.py:1151
  543.2 34.8 %collective-permute-start.75 = (bf16[512,1024]{1,0:T(8,128)(2,1)}, bf16[512,1024]{1,0:T(8,128)(2,1)}, u32[]{:S(2)}, u32[]{:S(2)}) collective-permute-start(bf16[512,1024]{1,0:T(8,128)(2,1)} %get-tuple-element.1960), channel_id=1, source_target_pairs={{0,1},{1,0},{2,3},{3,2},{4,5},{5,4},{6,7},{7,6},{8,9},{9,8},{10,11... | collective-permute-start | bytes 3145736 | tf_op jit(solution)/shard_map/ppermute | solution.py:758
  550.6 18.5 %collective-permute-start.71 = (bf16[1,1,512,512]{3,2,1,0:T(8,128)(2,1)}, bf16[1,1,512,512]{3,2,1,0:T(8,128)(2,1)S(1)}, u32[]{:S(2)}, u32[]{:S(2)}) collective-permute-start(bf16[1,1,512,512]{3,2,1,0:T(8,128)(2,1)} %get-tuple-element.1819), channel_id=1, source_target_pairs={{6,0},{7,1},{14,8},{15,9},{22,16},{23,17},{30,24},{31,25}} | collective-permute-start | bytes 1572872 | tf_op jit(solution)/shard_map/ppermute | solution.py:1151
  553.6 24.3 %collective-permute-start.73 = (bf16[256,1024]{1,0:T(8,128)(2,1)}, bf16[256,1024]{1,0:T(8,128)(2,1)S(1)}, u32[]{:S(2)}, u32[]{:S(2)}) collective-permute-start(bf16[256,1024]{1,0:T(8,128)(2,1)} %get-tuple-element.1878), channel_id=1, source_target_pairs={{0,16},{8,24},{16,0},{24,8},{1,17},{9,25},{17,1},{25,9},{2,18},{10... | collective-permute-start | bytes 1572872 | tf_op jit(solution)/shard_map/ppermute | solution.py:1181
  554.0 23.9 %collective-permute-start.74 = (bf16[256,1024]{1,0:T(8,128)(2,1)}, bf16[256,1024]{1,0:T(8,128)(2,1)}, u32[]{:S(2)}, u32[]{:S(2)}) collective-permute-start(bf16[256,1024]{1,0:T(8,128)(2,1)} %get-tuple-element.1879), channel_id=1, source_target_pairs={{0,24},{8,16},{16,8},{24,0},{1,25},{9,17},{17,9},{25,1},{2,26},{10... | collective-permute-start | bytes 1572872 | tf_op jit(solution)/shard_map/ppermute | solution.py:1181
  584.1 39.9 %collective-permute-start.92 = (bf16[4,64,1536]{2,1,0:T(8,128)(2,1)}, bf16[4,64,1536]{2,1,0:T(8,128)(2,1)}, u32[]{:S(2)}, u32[]{:S(2)}) collective-permute-start(bf16[4,64,1536]{2,1,0:T(8,128)(2,1)} %get-tuple-element.1917), channel_id=1, source_target_pairs={{0,6},{2,4},{4,2},{6,0},{1,7},{3,5},{5,3},{7,1},{8,14},{10,12},{12... | collective-permute-start | bytes 2359304 | tf_op jit(solution)/shard_map/ppermute | solution.py:1063
  617.4 24.6 %collective-permute-start.85 = (bf16[64,1024]{1,0:T(8,128)(2,1)}, bf16[64,1024]{1,0:T(8,128)(2,1)S(1)}, u32[]{:S(2)}, u32[]{:S(2)}) collective-permute-start(bf16[64,1024]{1,0:T(8,128)(2,1)} %get-tuple-element.1978), channel_id=1, source_target_pairs={{0,2},{2,0},{4,6},{6,4},{1,3},{3,1},{5,7},{7,5},{8,10},{10,8},{12,... | collective-permute-start | bytes 393224 | tf_op jit(solution)/shard_map/ppermute | solution.py:781
  617.4 26.3 %collective-permute-start.86 = (bf16[64,1024]{1,0:T(8,128)(2,1)}, bf16[64,1024]{1,0:T(8,128)(2,1)}, u32[]{:S(2)}, u32[]{:S(2)}) collective-permute-start(bf16[64,1024]{1,0:T(8,128)(2,1)} %get-tuple-element.1979), channel_id=1, source_target_pairs={{0,4},{2,6},{4,0},{6,2},{1,5},{3,7},{5,1},{7,3},{8,12},{10,14},{12... | collective-permute-start | bytes 393224 | tf_op jit(solution)/shard_map/ppermute | solution.py:781
  618.3 25.5 %collective-permute-start.87 = (bf16[64,1024]{1,0:T(8,128)(2,1)}, bf16[64,1024]{1,0:T(8,128)(2,1)}, u32[]{:S(2)}, u32[]{:S(2)}) collective-permute-start(bf16[64,1024]{1,0:T(8,128)(2,1)} %get-tuple-element.1980), channel_id=1, source_target_pairs={{0,6},{2,4},{4,2},{6,0},{1,7},{3,5},{5,3},{7,1},{8,14},{10,12},{12... | collective-permute-start | bytes 393224 | tf_op jit(solution)/shard_map/ppermute | solution.py:781
  (126 other events, 1704.8 us)

commit v4 on v3

--- a/solution.py
+++ b/solution.py
@@ -1188,11 +1188,12 @@
     dx_send(1)
     attention_back(0)
     seal()
-    dkv_send(0, 1, 2, 3)
+    dkv_send(0, 1, 3)
     out_send(0)
     before_attention(1)
     out_terms(1)
-    seal_but(lambda: [(live["dkv_sum"][0], [1, 2, 3]), (live["out_back"], [0])])
+    seal_but(lambda: [(live["out_back"], [0])])
+    dkv_send(0, 2)
     out_send(1)
     attention_back(1)
     seal()
@@ -1207,9 +1208,9 @@
         None,
         dp,
     )
-    seal_but(lambda: [(live["dkv_sum"][1], [1, 2, 3])], early=list(early))
+    owned = [grad_own(0)]
+    seal_but(lambda: [(live["dkv_sum"][1], [1, 2, 3])], early=list(early), owned=owned)
     early_send(1, 2, 3)
-    owned = [grad_own(0)]
     dkv_first, part_first, gain_first = back(0)
     got_first = swap(part_first)
     out_first = out_total(0)
@@ -1217,7 +1218,6 @@
     seal(
         got=[got_first],
         output=[out_first, out_last],
-        owned=owned,
         dkv_final=[dkv_first],
         part=[part_first],
         gain_one_sums=[gain_first],
@@ -1242,15 +1242,13 @@
         dp,
     )
     got_last = swap(part_last)
-    early = live["early"]
-    if hops:
-        early = line_call(ctx_now, early, n)
     seal_but(
-        lambda: [(live["rows"][1], [3])], late=late, early=early, got=live["got"] + [got_last]
-    )
-    late = live["late"]
+        lambda: [(live["rows"][1], [3])], late=late, got=live["got"] + [got_last]
+    )
+    early, late = live["early"], live["late"]
     if hops:
         late = exchange(late, "dp")
+        early = line_call(ctx_now, early, n)
     d_normed = jnp.concatenate(
         [p.astype(F32) + g.astype(F32) for p, g in zip(live["part"], live["got"])]
     )
@@ -1262,7 +1260,9 @@
         jnp.concatenate(live["dh"])
         + inv_one * (g_one - n_one * jnp.mean(g_one * n_one, axis=1, keepdims=True))
     ).astype(BF)
-    seal_but(lambda: [(live["rows"][1], [3])], late=late, input_grad=input_grad)
+    seal_but(
+        lambda: [(live["rows"][1], [3])], late=late, early=early, input_grad=input_grad
+    )
     early, late = live["early"], live["late"]
     if hops:
         late = exchange(line_call(ctx_now, late, n), "ctx")

time: 663 us -> 640 us (0.965)
  waiting for transfers between devices: 209 us -> 194 us
  starting transfers between devices: 122 us -> 114 us
    ppermute x30, waiting for transfers between devices: 38.2 us -> 17.4 us  [exchange(): lax.ppermute(parts[s], axis, apart(count, s))]
    ppermute x6, starting transfers between devices: 14.7 us -> 7.19 us  [grad_send(): live['rows'][g][s] = lax.ppermute(live['dws'][g][s], 'ctx', apart(n, s))]
    unnamed x164 -> x148, local copies, waits for them, and re-layouts: 21 us -> 22.2 us
  transfers between devices with their start and end apart: 96 -> 96, of which waited for: 36 -> 37; matrix products, arithmetic and copies ran while one was open for 13% -> 13% of each run, Pallas kernels for 29% -> 30%
where the time goes in v4:
time: 640 us; the launch traced here: 632 us
  Pallas kernels  206 us (32%)
  waiting for transfers between devices  194 us (30%)
  starting transfers between devices  114 us (18%)
  other arithmetic  69.5 us (11%)
  local copies, waits for them, and re-layouts  35.4 us (6%)
  matrix products  10.9 us (2%)
    pallas_call x4, Pallas kernels, experts_call(): pl.pallas_call(functools.partial(experts_kernel, steps, first, count, mic...  123 us
    ppermute x30, starting transfers between devices, exchange(): lax.ppermute(parts[s], axis, apart(count, s))  46.3 us
    ppermute x6, waiting for transfers between devices, dkv_send(): lax.ppermute(live['dkv'][m][d], 'ctx', [(c, c - d) for c in range(d, n)])  39.6 us
    ppermute x6, waiting for transfers between devices, weight_send(): lax.ppermute(live['weights'][g][at], 'ctx', apart(n, hop))  33.3 us
    ppermute x3, waiting for transfers between devices, dy_send(): live['dy_far'].append(lax.ppermute(live['dy_cut'][0], 'dp', apart(dp, s)))  26.6 us
    unnamed x148, local copies, waits for them, and re-layouts  22.2 us
    pallas_call x2, Pallas kernels, attn_bwd(): pl.pallas_call(functools.partial(attn_bwd_kernel, counts), grid=(seqs, pa...  21 us
    convert_element_type x10, other arithmetic, add(): return functools.reduce(jnp.add, [t.astype(F32) for t in terms]).astype(BF)  20.8 us
  transfers between devices with their start and end apart: 96, of which 37 were waited for; matrix products, arithmetic and copies ran while one was open for 13% of the time, Pallas kernels for 30%

profile of v4, /device:TPU:0, one launch (start us, length us, event | category | flops | bytes accessed | tf_op | source)
XLA Modules:
  0.0 631.9 jit_solution(17876826093806973892)
XLA Ops:
  2.3 4.1 collective-permute-start.1
  17.4 3.8 collective-permute-start.2
  21.2 3.9 collective-permute-done.2
  25.1 2.8 collective-permute-start.4
  28.2 3.8 collective-permute-done.4
  44.1 5.1 collective-permute-done.11
  49.2 3.8 collective-permute-done.10
  56.7 5.7 kv.1
  62.4 4.5 collective-permute-start.13
  73.2 6.7 %convert_reduce_fusion = bf16[1024,128]{1,0:T(8,128)(2,1)S(1)} fusion(s32[1024,8]{1,0:T(8,128)} %copy.134), kind=kLoop, calls=%fused_computation.14 | loop fusion | flops 3014656 | bytes 294912 | tf_op jit(solution)/shard_map/reduce_sum | solution.py:926
  82.8 8.4 %collective-permute-done.15 = bf16[4,64,1024]{2,1,0:T(8,128)(2,1)} collective-permute-done((bf16[4,64,1024]{2,1,0:T(8,128)(2,1)S(1)}, bf16[4,64,1024]{2,1,0:T(8,128)(2,1)}, u32[]{:S(2)}, u32[]{:S(2)}) %collective-permute-start.15) | collective-permute-done | bytes 524320 | tf_op jit(solution)/shard_map/ppermute | solution.py:854
  100.0 5.7 q.1
  105.7 8.1 %attn_fwd.3 = (f32[2,2,4,1024]{3,2,1,0:T(4,128)}, f32[2,2,2,128,1024]{4,3,2,1,0:T(8,128)}) custom-call(s32[1]{0:T(128)} %bitcast.ctx_ref.place_ref, bf16[2,512,512]{2,1,0:T(8,128)(2,1)} %bitcast.244, bf16[1,2,512,512]{3,2,1,0:T(8,128)(2,1)} %bitcast.280, bf16[1,2,512,512]{3,2,1,0:T(8,128)(2,1)} %collective-permute-done.13.refs_1_.refs_3_.refs_5_, ...), custom_call_target="tpu_custom_call" | custom-call | flops 8589934592 | bytes 4194304 | tf_op jit(solution)/shard_map/attn_fwd/pallas_call | solution.py:245
  113.8 5.9 collective-permute-done.18.refs_12_
  124.2 5.5 attn_fwd.4
  129.7 19.3 %collective-permute-done.20.refs_14_ = bf16[2,256,1152]{2,1,0:T(8,128)(2,1)S(1)} collective-permute-done((bf16[2,256,1152]{2,1,0:T(8,128)(2,1)}, bf16[2,256,1152]{2,1,0:T(8,128)(2,1)S(1)}, u32[]{:S(2)}, u32[]{:S(2)}) %collective-permute-start.20) | collective-permute-done | bytes 1179680 | tf_op jit(solution)/shard_map/ppermute | solution.py:975
  150.5 5.0 attn_fwd.5
  155.5 2.7 convolution_convert_fusion
  170.7 25.4 %collective-permute-done.26.refs_18_ = bf16[4,64,1536]{2,1,0:T(8,128)(2,1)S(1)} collective-permute-done((bf16[4,64,1536]{2,1,0:T(8,128)(2,1)S(1)}, bf16[4,64,1536]{2,1,0:T(8,128)(2,1)S(1)}, u32[]{:S(2)}, u32[]{:S(2)}) %collective-permute-start.26) | collective-permute-done | bytes 786464 | tf_op jit(solution)/shard_map/ppermute | solution.py:886
  197.6 12.7 %collective-permute-done.30.refs_6_ = bf16[256,1024]{1,0:T(8,128)(2,1)} collective-permute-done((bf16[256,1024]{1,0:T(8,128)(2,1)S(1)}, bf16[256,1024]{1,0:T(8,128)(2,1)}, u32[]{:S(2)}, u32[]{:S(2)}) %collective-permute-start.30) | collective-permute-done | bytes 524320 | tf_op jit(solution)/shard_map/ppermute | solution.py:843
  210.3 4.5 collective-permute-done.29.refs_19_
  226.4 30.1 %experts.4 = (bf16[4,256,1024]{2,1,0:T(8,128)(2,1)}, bf16[4,256,1024]{2,1,0:T(8,128)(2,1)}, bf16[4,256,1152]{2,1,0:T(8,128)(2,1)}, bf16[4,256,1152]{2,1,0:T(8,12...) custom-call(s32[2]{0:T(128)} %pad_add_fusion.place_ref, ...), custom_call_target="tpu_custom_call" | custom-call | flops 19327352832 | bytes 23068672 | tf_op jit(solution)/shard_map/experts/pallas_call | solution.py:527
  256.5 3.3 collective-permute-done.35.refs_18_
  265.8 30.2 %experts.5 = (bf16[4,256,1024]{2,1,0:T(8,128)(2,1)}, bf16[4,256,1024]{2,1,0:T(8,128)(2,1)}, bf16[4,256,1152]{2,1,0:T(8,128)(2,1)}, bf16[4,256,1152]{2,1,0:T(8,12...) custom-call(s32[2]{0:T(128)} %pad_add_fusion.place_ref, ...), custom_call_target="tpu_custom_call" | custom-call | flops 19327352832 | bytes 23068672 | tf_op jit(solution)/shard_map/experts/pallas_call | solution.py:527
  298.5 30.9 %experts.6 = (bf16[4,256,1024]{2,1,0:T(8,128)(2,1)}, bf16[4,256,1024]{2,1,0:T(8,128)(2,1)}, bf16[4,256,1152]{2,1,0:T(8,128)(2,1)}, bf16[4,256,1152]{2,1,0:T(8,12...) custom-call(s32[2]{0:T(128)} %pad_add_fusion.place_ref, ...), custom_call_target="tpu_custom_call" | custom-call | flops 19327352832 | bytes 23068672 | tf_op jit(solution)/shard_map/experts/pallas_call | solution.py:527
  329.4 3.0 collective-permute-done.43
  334.6 4.7 collective-permute-done.45
  339.4 3.2 fusion.26
  348.5 31.6 %experts.7 = (bf16[4,256,1024]{2,1,0:T(8,128)(2,1)}, bf16[4,256,1024]{2,1,0:T(8,128)(2,1)}, bf16[4,256,1152]{2,1,0:T(8,128)(2,1)}, bf16[4,256,1152]{2,1,0:T(8,12...) custom-call(s32[2]{0:T(128)} %pad_add_fusion.place_ref, ...), custom_call_target="tpu_custom_call" | custom-call | flops 19327352832 | bytes 23068672 | tf_op jit(solution)/shard_map/experts/pallas_call | solution.py:527
  405.3 10.9 %attn_bwd.2 = (bf16[1,512,512]{2,1,0:T(8,128)(2,1)}, bf16[1,1,512,512]{3,2,1,0:T(8,128)(2,1)}, bf16[1,1,512,512]{3,2,1,0:T(8,128)(2,1)}, bf16[1,1,512,512]{3,2,1,0:T(8,128)(2,1)}, bf16[1,1,512,512]{3,2,1,0:T(8,128)(2,1)}) custom-call(s32[1]{0:T(128)} %bitcast.ctx_ref.place_ref, bf16[2,512,512]{2,1,0:T(8,128)(2,1)} %bitcast.247, ...), custom_call_target="tpu_custom_call" | custom-call | flops 21474836480 | bytes 8388608 | tf_op jit(solution)/shard_map/attn_bwd/pallas_call | solution.py:335
  416.2 2.9 collective-permute-done.56
  419.1 3.6 collective-permute-done.57
  422.7 8.7 %collective-permute-done.54 = bf16[256,1152]{1,0:T(8,128)(2,1)} collective-permute-done((bf16[256,1152]{1,0:T(8,128)(2,1)}, bf16[256,1152]{1,0:T(8,128)(2,1)}, u32[]{:S(2)}, u32[]{:S(2)}) %collective-permute-start.54) | collective-permute-done | bytes 589856 | tf_op jit(solution)/shard_map/ppermute | solution.py:781
  451.3 12.1 %collective-permute-done.60 = bf16[1,1,512,512]{3,2,1,0:T(8,128)(2,1)} collective-permute-done((bf16[1,1,512,512]{3,2,1,0:T(8,128)(2,1)}, bf16[1,1,512,512]{3,2,1,0:T(8,128)(2,1)}, u32[]{:S(2)}, u32[]{:S(2)}) %collective-permute-start.60) | collective-permute-done | bytes 524320 | tf_op jit(solution)/shard_map/ppermute | solution.py:1151
  469.0 10.1 %attn_bwd.3 = (bf16[1,512,512]{2,1,0:T(8,128)(2,1)}, bf16[1,1,512,512]{3,2,1,0:T(8,128)(2,1)}, bf16[1,1,512,512]{3,2,1,0:T(8,128)(2,1)}, bf16[1,1,512,512]{3,2,1,0:T(8,128)(2,1)}, bf16[1,1,512,512]{3,2,1,0:T(8,128)(2,1)}) custom-call(s32[1]{0:T(128)} %bitcast.ctx_ref.place_ref, bf16[2,512,512]{2,1,0:T(8,128)(2,1)} %bitcast.248, ...), custom_call_target="tpu_custom_call" | custom-call | flops 21474836480 | bytes 8388608 | tf_op jit(solution)/shard_map/attn_bwd/pallas_call | solution.py:335
  479.2 8.9 %collective-permute-done.62 = bf16[1,1,512,512]{3,2,1,0:T(8,128)(2,1)S(1)} collective-permute-done((bf16[1,1,512,512]{3,2,1,0:T(8,128)(2,1)}, bf16[1,1,512,512]{3,2,1,0:T(8,128)(2,1)S(1)}, u32[]{:S(2)}, u32[]{:S(2)}) %collective-permute-start.62) | collective-permute-done | bytes 524320 | tf_op jit(solution)/shard_map/ppermute | solution.py:1151
  501.8 6.7 %grads.2 = (bf16[256,1024]{1,0:T(8,128)(2,1)}, bf16[256,1024]{1,0:T(8,128)(2,1)}, bf16[256,1024]{1,0:T(8,128)(2,1)}, bf16[256,1024]{1,0:T(8,128)(2,1)}) custom-call(s32[1]{0:T(128)} %bitcast.80.place_ref, bf16[1024,1024]{1,0:T(8,128)(2,1)} %get-tuple-element.1934.normed_ref.refs_0_.refs_2_, bf16[512,512]{1,0:T(8,128)(2,1)} %bitcast.234, ...), custom_call_target="tpu_custom_call" | custom-call | flops 2147483648 | bytes 4194304 | tf_op jit(solution)/shard_map/grads/pallas_call | solution.py:649
  513.8 5.1 back.2
  522.3 18.6 %collective-permute-done.73 = bf16[1,1,512,512]{3,2,1,0:T(8,128)(2,1)} collective-permute-done((bf16[1,1,512,512]{3,2,1,0:T(8,128)(2,1)}, bf16[1,1,512,512]{3,2,1,0:T(8,128)(2,1)}, u32[]{:S(2)}, u32[]{:S(2)}) %collective-permute-start.73) | collective-permute-done | bytes 524320 | tf_op jit(solution)/shard_map/ppermute | solution.py:1151
  545.0 11.0 %collective-permute-done.76.refs_2_ = bf16[256,1024]{1,0:T(8,128)(2,1)} collective-permute-done((bf16[256,1024]{1,0:T(8,128)(2,1)}, bf16[256,1024]{1,0:T(8,128)(2,1)}, u32[]{:S(2)}, u32[]{:S(2)}) %collective-permute-start.76) | collective-permute-done | bytes 524320 | tf_op jit(solution)/shard_map/ppermute | solution.py:1181
  556.9 5.1 back.3
  564.0 4.9 grads.3
  579.2 2.8 line.2
  582.0 5.0 fusion.6
  588.8 2.7 collective-permute-start.86
  594.5 11.7 %collective-permute-start.89 = (bf16[64,640]{1,0:T(8,128)(2,1)}, bf16[64,640]{1,0:T(8,128)(2,1)S(1)}, u32[]{:S(2)}, u32[]{:S(2)}) collective-permute-start(bf16[64,640]{1,0:T(8,128)(2,1)} %get-tuple-element.1993), channel_id=1, source_target_pairs={{0,4},{2,6},{4,0},{6,2},{1,5},{3,7},{5,1},{7,3},{8,12},{10,14},{12... | collective-permute-start | bytes 245768 | tf_op jit(solution)/shard_map/ppermute | solution.py:781
  610.3 5.0 collective-permute-done.89.refs_6_
  628.2 3.3 expert_rows.1
  (418 shorter events, 205.9 us)
Async XLA Ops:
  13.0 20.4 %collective-permute-start.7 = (bf16[2,64,1536]{2,1,0:T(8,128)(2,1)}, bf16[2,64,1536]{2,1,0:T(8,128)(2,1)S(1)}, u32[]{:S(2)}, u32[]{:S(2)}) collective-permute-start(bf16[2,64,1536]{2,1,0:T(8,128)(2,1)} %get-tuple-element.2092), channel_id=1, source_target_pairs={{0,16},{8,24},{16,0},{24,8},{1,17},{9,25},{17,1},{25,9},{2,18},{10... | collective-permute-start | bytes 1179656 | tf_op jit(solution)/shard_map/ppermute | solution.py:781
  14.6 18.9 %collective-permute-start.8 = (bf16[2,64,1536]{2,1,0:T(8,128)(2,1)}, bf16[2,64,1536]{2,1,0:T(8,128)(2,1)S(1)}, u32[]{:S(2)}, u32[]{:S(2)}) collective-permute-start(bf16[2,64,1536]{2,1,0:T(8,128)(2,1)} %get-tuple-element.2129), channel_id=1, source_target_pairs={{0,8},{8,0},{16,24},{24,16},{1,9},{9,1},{17,25},{25,17},{2,10},{10... | collective-permute-start | bytes 1179656 | tf_op jit(solution)/shard_map/ppermute | solution.py:781
  62.4 29.4 %collective-permute-start.13 = (bf16[1,2,512,512]{3,2,1,0:T(8,128)(2,1)}, bf16[1,2,512,512]{3,2,1,0:T(8,128)(2,1)}, u32[]{:S(2)}, u32[]{:S(2)}) collective-permute-start(bf16[1,2,512,512]{3,2,1,0:T(8,128)(2,1)} %bitcast.279), channel_id=1, source_target_pairs={{0,2},{2,4},{4,6},{1,3},{3,5},{5,7},{8,10},{10,12},{12,14},{9,11},... | collective-permute-start | bytes 3145736 | tf_op jit(solution)/shard_map/ppermute | solution.py:762
  69.4 21.8 %collective-permute-start.15 = (bf16[4,64,1024]{2,1,0:T(8,128)(2,1)S(1)}, bf16[4,64,1024]{2,1,0:T(8,128)(2,1)}, u32[]{:S(2)}, u32[]{:S(2)}) collective-permute-start(bf16[4,64,1024]{2,1,0:T(8,128)(2,1)S(1)} %pad_maximum_fusion.8), channel_id=1, source_target_pairs={{0,16},{8,24},{16,0},{24,8},{1,17},{9,25},{17,1},{25,9},{2,18},{10... | collective-permute-start | bytes 1572872 | tf_op jit(solution)/shard_map/ppermute | solution.py:854
  69.9 21.9 %collective-permute-start.14 = (bf16[4,64,1024]{2,1,0:T(8,128)(2,1)S(1)}, bf16[4,64,1024]{2,1,0:T(8,128)(2,1)}, u32[]{:S(2)}, u32[]{:S(2)}) collective-permute-start(bf16[4,64,1024]{2,1,0:T(8,128)(2,1)S(1)} %pad_maximum_fusion.8), channel_id=1, source_target_pairs={{0,8},{8,0},{16,24},{24,16},{1,9},{9,1},{17,25},{25,17},{2,10},{10... | collective-permute-start | bytes 1572872 | tf_op jit(solution)/shard_map/ppermute | solution.py:854
  91.8 27.9 %collective-permute-start.18 = (bf16[2,256,1152]{2,1,0:T(8,128)(2,1)}, bf16[2,256,1152]{2,1,0:T(8,128)(2,1)}, u32[]{:S(2)}, u32[]{:S(2)}) collective-permute-start(bf16[2,256,1152]{2,1,0:T(8,128)(2,1)} %get-tuple-element.1582.refs_8_), channel_id=1, source_target_pairs={{0,16},{8,24},{16,0},{24,8},{1,17},{9,25},{17,1},{25,9},{2,18},{10... | collective-permute-start | bytes 3538952 | tf_op jit(solution)/shard_map/ppermute | solution.py:975
  93.2 27.9 %collective-permute-start.17 = (bf16[2,256,1152]{2,1,0:T(8,128)(2,1)}, bf16[2,256,1152]{2,1,0:T(8,128)(2,1)}, u32[]{:S(2)}, u32[]{:S(2)}) collective-permute-start(bf16[2,256,1152]{2,1,0:T(8,128)(2,1)} %get-tuple-element.1582.refs_8_), channel_id=1, source_target_pairs={{0,8},{8,0},{16,24},{24,16},{1,9},{9,1},{17,25},{25,17},{2,10},{10... | collective-permute-start | bytes 3538952 | tf_op jit(solution)/shard_map/ppermute | solution.py:975
  121.1 27.8 %collective-permute-start.20 = (bf16[2,256,1152]{2,1,0:T(8,128)(2,1)}, bf16[2,256,1152]{2,1,0:T(8,128)(2,1)S(1)}, u32[]{:S(2)}, u32[]{:S(2)}) collective-permute-start(bf16[2,256,1152]{2,1,0:T(8,128)(2,1)} %get-tuple-element.1582.refs_8_), channel_id=1, source_target_pairs={{0,24},{8,16},{16,8},{24,0},{1,25},{9,17},{17,9},{25,1},{2,26},{10... | collective-permute-start | bytes 3538952 | tf_op jit(solution)/shard_map/ppermute | solution.py:975
  158.7 37.3 %collective-permute-start.26 = (bf16[4,64,1536]{2,1,0:T(8,128)(2,1)S(1)}, bf16[4,64,1536]{2,1,0:T(8,128)(2,1)S(1)}, u32[]{:S(2)}, u32[]{:S(2)}) collective-permute-start(bf16[4,64,1536]{2,1,0:T(8,128)(2,1)S(1)} %copy-done.31), channel_id=1, source_target_pairs={{0,4},{2,6},{4,0},{6,2},{1,5},{3,7},{5,1},{7,3},{8,12},{10,14},{12... | collective-permute-start | bytes 2359304 | tf_op jit(solution)/shard_map/ppermute | solution.py:886
  168.7 27.4 %collective-permute-start.28 = (bf16[256,1024]{1,0:T(8,128)(2,1)S(1)}, bf16[256,1024]{1,0:T(8,128)(2,1)}, u32[]{:S(2)}, u32[]{:S(2)}) collective-permute-start(bf16[256,1024]{1,0:T(8,128)(2,1)S(1)} %get-tuple-element.1448.refs_0_), channel_id=1, source_target_pairs={{0,16},{8,24},{16,0},{24,8},{1,17},{9,25},{17,1},{25,9},{2,18},{10... | collective-permute-start | bytes 1572872 | tf_op jit(solution)/shard_map/ppermute | solution.py:843
  169.3 26.7 %collective-permute-start.27 = (bf16[256,1024]{1,0:T(8,128)(2,1)S(1)}, bf16[256,1024]{1,0:T(8,128)(2,1)}, u32[]{:S(2)}, u32[]{:S(2)}) collective-permute-start(bf16[256,1024]{1,0:T(8,128)(2,1)S(1)} %get-tuple-element.1448.refs_0_), channel_id=1, source_target_pairs={{0,8},{8,0},{16,24},{24,16},{1,9},{9,1},{17,25},{25,17},{2,10},{10... | collective-permute-start | bytes 1572872 | tf_op jit(solution)/shard_map/ppermute | solution.py:843
  196.0 18.8 %collective-permute-start.29 = (bf16[4,64,1536]{2,1,0:T(8,128)(2,1)S(1)}, bf16[4,64,1536]{2,1,0:T(8,128)(2,1)S(1)}, u32[]{:S(2)}, u32[]{:S(2)}) collective-permute-start(bf16[4,64,1536]{2,1,0:T(8,128)(2,1)S(1)} %collective-permute-done.26.refs_18_), channel_id=1, source_target_pairs={{0,2},{2,0},{4,6},{6,4},{1,3},{3,1},{5,7},{7,5},{8,10},{10,8},{12,... | collective-permute-start | bytes 2359304 | tf_op jit(solution)/shard_map/ppermute | solution.py:886
  219.4 37.1 %collective-permute-start.38 = (bf16[256,1024]{1,0:T(8,128)(2,1)S(1)}, bf16[256,1024]{1,0:T(8,128)(2,1)S(1)}, u32[]{:S(2)}, u32[]{:S(2)}) collective-permute-start(bf16[256,1024]{1,0:T(8,128)(2,1)S(1)} %get-tuple-element.1574.refs_0_), channel_id=1, source_target_pairs={{0,24},{8,16},{16,8},{24,0},{1,25},{9,17},{17,9},{25,1},{2,26},{10... | collective-permute-start | bytes 1572872 | tf_op jit(solution)/shard_map/ppermute | solution.py:843
  220.8 35.7 %collective-permute-start.37 = (bf16[256,1024]{1,0:T(8,128)(2,1)S(1)}, bf16[256,1024]{1,0:T(8,128)(2,1)}, u32[]{:S(2)}, u32[]{:S(2)}) collective-permute-start(bf16[256,1024]{1,0:T(8,128)(2,1)S(1)} %get-tuple-element.1574.refs_0_), channel_id=1, source_target_pairs={{0,16},{8,24},{16,0},{24,8},{1,17},{9,25},{17,1},{25,9},{2,18},{10... | collective-permute-start | bytes 1572872 | tf_op jit(solution)/shard_map/ppermute | solution.py:843
  221.5 35.1 %collective-permute-start.36 = (bf16[256,1024]{1,0:T(8,128)(2,1)S(1)}, bf16[256,1024]{1,0:T(8,128)(2,1)}, u32[]{:S(2)}, u32[]{:S(2)}) collective-permute-start(bf16[256,1024]{1,0:T(8,128)(2,1)S(1)} %get-tuple-element.1574.refs_0_), channel_id=1, source_target_pairs={{0,8},{8,0},{16,24},{24,16},{1,9},{9,1},{17,25},{25,17},{2,10},{10... | collective-permute-start | bytes 1572872 | tf_op jit(solution)/shard_map/ppermute | solution.py:843
  222.9 36.9 %collective-permute-start.35 = (bf16[4,64,1536]{2,1,0:T(8,128)(2,1)}, bf16[4,64,1536]{2,1,0:T(8,128)(2,1)}, u32[]{:S(2)}, u32[]{:S(2)}) collective-permute-start(bf16[4,64,1536]{2,1,0:T(8,128)(2,1)} %pad_maximum_fusion.7.refs_16_), channel_id=1, source_target_pairs={{0,4},{2,6},{4,0},{6,2},{1,5},{3,7},{5,1},{7,3},{8,12},{10,14},{12... | collective-permute-start | bytes 2359304 | tf_op jit(solution)/shard_map/ppermute | solution.py:886
  224.6 35.3 %collective-permute-start.34 = (bf16[4,64,1536]{2,1,0:T(8,128)(2,1)}, bf16[4,64,1536]{2,1,0:T(8,128)(2,1)}, u32[]{:S(2)}, u32[]{:S(2)}) collective-permute-start(bf16[4,64,1536]{2,1,0:T(8,128)(2,1)} %pad_maximum_fusion.7.refs_16_), channel_id=1, source_target_pairs={{0,2},{2,0},{4,6},{6,4},{1,3},{3,1},{5,7},{7,5},{8,10},{10,8},{12,... | collective-permute-start | bytes 2359304 | tf_op jit(solution)/shard_map/ppermute | solution.py:886
  265.2 30.9 %collective-permute-start.42 = (bf16[4,64,1536]{2,1,0:T(8,128)(2,1)}, bf16[4,64,1536]{2,1,0:T(8,128)(2,1)}, u32[]{:S(2)}, u32[]{:S(2)}) collective-permute-start(bf16[4,64,1536]{2,1,0:T(8,128)(2,1)} %collective-permute-done.35.refs_18_), channel_id=1, source_target_pairs={{0,2},{2,0},{4,6},{6,4},{1,3},{3,1},{5,7},{7,5},{8,10},{10,8},{12,... | collective-permute-start | bytes 2359304 | tf_op jit(solution)/shard_map/ppermute | solution.py:886
  296.1 36.4 %collective-permute-start.43 = (bf16[4,64,1536]{2,1,0:T(8,128)(2,1)}, bf16[4,64,1536]{2,1,0:T(8,128)(2,1)}, u32[]{:S(2)}, u32[]{:S(2)}) collective-permute-start(bf16[4,64,1536]{2,1,0:T(8,128)(2,1)} %get-tuple-element.1444), channel_id=1, source_target_pairs={{0,2},{2,0},{4,6},{6,4},{1,3},{3,1},{5,7},{7,5},{8,10},{10,8},{12,... | collective-permute-start | bytes 2359304 | tf_op jit(solution)/shard_map/ppermute | solution.py:1063
  297.5 37.1 %collective-permute-start.44 = (bf16[4,64,1536]{2,1,0:T(8,128)(2,1)}, bf16[4,64,1536]{2,1,0:T(8,128)(2,1)}, u32[]{:S(2)}, u32[]{:S(2)}) collective-permute-start(bf16[4,64,1536]{2,1,0:T(8,128)(2,1)} %get-tuple-element.1445), channel_id=1, source_target_pairs={{0,4},{2,6},{4,0},{6,2},{1,5},{3,7},{5,1},{7,3},{8,12},{10,14},{12... | collective-permute-start | bytes 2359304 | tf_op jit(solution)/shard_map/ppermute | solution.py:1063
  342.6 37.5 %collective-permute-start.46 = (bf16[256,1152]{1,0:T(8,128)(2,1)}, bf16[256,1152]{1,0:T(8,128)(2,1)}, u32[]{:S(2)}, u32[]{:S(2)}) collective-permute-start(bf16[256,1152]{1,0:T(8,128)(2,1)} %get-tuple-element.1607), channel_id=1, source_target_pairs={{0,8},{8,0},{16,24},{24,16},{1,9},{9,1},{17,25},{25,17},{2,10},{10... | collective-permute-start | bytes 1769480 | tf_op jit(solution)/shard_map/ppermute | solution.py:781
  342.6 37.5 %collective-permute-start.47 = (bf16[256,1152]{1,0:T(8,128)(2,1)}, bf16[256,1152]{1,0:T(8,128)(2,1)}, u32[]{:S(2)}, u32[]{:S(2)}) collective-permute-start(bf16[256,1152]{1,0:T(8,128)(2,1)} %get-tuple-element.1608), channel_id=1, source_target_pairs={{0,16},{8,24},{16,0},{24,8},{1,17},{9,25},{17,1},{25,9},{2,18},{10... | collective-permute-start | bytes 1769480 | tf_op jit(solution)/shard_map/ppermute | solution.py:781
  344.6 35.6 %collective-permute-start.48 = (bf16[256,1152]{1,0:T(8,128)(2,1)}, bf16[256,1152]{1,0:T(8,128)(2,1)}, u32[]{:S(2)}, u32[]{:S(2)}) collective-permute-start(bf16[256,1152]{1,0:T(8,128)(2,1)} %get-tuple-element.1609), channel_id=1, source_target_pairs={{0,24},{8,16},{16,8},{24,0},{1,25},{9,17},{17,9},{25,1},{2,26},{10... | collective-permute-start | bytes 1769480 | tf_op jit(solution)/shard_map/ppermute | solution.py:781
  346.1 34.1 %collective-permute-start.49 = (bf16[4,64,1536]{2,1,0:T(8,128)(2,1)}, bf16[4,64,1536]{2,1,0:T(8,128)(2,1)}, u32[]{:S(2)}, u32[]{:S(2)}) collective-permute-start(bf16[4,64,1536]{2,1,0:T(8,128)(2,1)} %get-tuple-element.1572), channel_id=1, source_target_pairs={{0,6},{2,4},{4,2},{6,0},{1,7},{3,5},{5,3},{7,1},{8,14},{10,12},{12... | collective-permute-start | bytes 2359304 | tf_op jit(solution)/shard_map/ppermute | solution.py:1063
  382.7 36.4 %collective-permute-start.56 = (bf16[4,64,1536]{2,1,0:T(8,128)(2,1)}, bf16[4,64,1536]{2,1,0:T(8,128)(2,1)}, u32[]{:S(2)}, u32[]{:S(2)}) collective-permute-start(bf16[4,64,1536]{2,1,0:T(8,128)(2,1)} %get-tuple-element.1653), channel_id=1, source_target_pairs={{0,2},{2,0},{4,6},{6,4},{1,3},{3,1},{5,7},{7,5},{8,10},{10,8},{12,... | collective-permute-start | bytes 2359304 | tf_op jit(solution)/shard_map/ppermute | solution.py:1063
  384.9 37.8 %collective-permute-start.57 = (bf16[4,64,1536]{2,1,0:T(8,128)(2,1)}, bf16[4,64,1536]{2,1,0:T(8,128)(2,1)}, u32[]{:S(2)}, u32[]{:S(2)}) collective-permute-start(bf16[4,64,1536]{2,1,0:T(8,128)(2,1)} %get-tuple-element.1654), channel_id=1, source_target_pairs={{0,4},{2,6},{4,0},{6,2},{1,5},{3,7},{5,1},{7,3},{8,12},{10,14},{12... | collective-permute-start | bytes 2359304 | tf_op jit(solution)/shard_map/ppermute | solution.py:1063
  401.8 20.9 %collective-permute-start.53 = (bf16[256,1152]{1,0:T(8,128)(2,1)}, bf16[256,1152]{1,0:T(8,128)(2,1)}, u32[]{:S(2)}, u32[]{:S(2)}) collective-permute-start(bf16[256,1152]{1,0:T(8,128)(2,1)} %get-tuple-element.1696), channel_id=1, source_target_pairs={{0,8},{8,0},{16,24},{24,16},{1,9},{9,1},{17,25},{25,17},{2,10},{10... | collective-permute-start | bytes 1769480 | tf_op jit(solution)/shard_map/ppermute | solution.py:781
  403.3 28.1 %collective-permute-start.54 = (bf16[256,1152]{1,0:T(8,128)(2,1)}, bf16[256,1152]{1,0:T(8,128)(2,1)}, u32[]{:S(2)}, u32[]{:S(2)}) collective-permute-start(bf16[256,1152]{1,0:T(8,128)(2,1)} %get-tuple-element.1697), channel_id=1, source_target_pairs={{0,16},{8,24},{16,0},{24,8},{1,17},{9,25},{17,1},{25,9},{2,18},{10... | collective-permute-start | bytes 1769480 | tf_op jit(solution)/shard_map/ppermute | solution.py:781
  403.8 27.7 %collective-permute-start.55 = (bf16[256,1152]{1,0:T(8,128)(2,1)}, bf16[256,1152]{1,0:T(8,128)(2,1)}, u32[]{:S(2)}, u32[]{:S(2)}) collective-permute-start(bf16[256,1152]{1,0:T(8,128)(2,1)} %get-tuple-element.1698), channel_id=1, source_target_pairs={{0,24},{8,16},{16,8},{24,0},{1,25},{9,17},{17,9},{25,1},{2,26},{10... | collective-permute-start | bytes 1769480 | tf_op jit(solution)/shard_map/ppermute | solution.py:781
  434.9 28.5 %collective-permute-start.60 = (bf16[1,1,512,512]{3,2,1,0:T(8,128)(2,1)}, bf16[1,1,512,512]{3,2,1,0:T(8,128)(2,1)}, u32[]{:S(2)}, u32[]{:S(2)}) collective-permute-start(bf16[1,1,512,512]{3,2,1,0:T(8,128)(2,1)} %get-tuple-element.1741), channel_id=1, source_target_pairs={{6,0},{7,1},{14,8},{15,9},{22,16},{23,17},{30,24},{31,25}} | collective-permute-start | bytes 1572872 | tf_op jit(solution)/shard_map/ppermute | solution.py:1151
  436.4 29.7 %collective-permute-start.63 = (bf16[256,1024]{1,0:T(8,128)(2,1)}, bf16[256,1024]{1,0:T(8,128)(2,1)}, u32[]{:S(2)}, u32[]{:S(2)}) collective-permute-start(bf16[256,1024]{1,0:T(8,128)(2,1)} %get-tuple-element.1757), channel_id=1, source_target_pairs={{0,8},{8,0},{16,24},{24,16},{1,9},{9,1},{17,25},{25,17},{2,10},{10... | collective-permute-start | bytes 1572872 | tf_op jit(solution)/shard_map/ppermute | solution.py:781
  436.9 30.6 %collective-permute-start.64 = (bf16[256,1024]{1,0:T(8,128)(2,1)}, bf16[256,1024]{1,0:T(8,128)(2,1)}, u32[]{:S(2)}, u32[]{:S(2)}) collective-permute-start(bf16[256,1024]{1,0:T(8,128)(2,1)} %get-tuple-element.1758), channel_id=1, source_target_pairs={{0,16},{8,24},{16,0},{24,8},{1,17},{9,25},{17,1},{25,9},{2,18},{10... | collective-permute-start | bytes 1572872 | tf_op jit(solution)/shard_map/ppermute | solution.py:781
  447.7 31.4 %collective-permute-start.65 = (bf16[256,1024]{1,0:T(8,128)(2,1)S(1)}, bf16[256,1024]{1,0:T(8,128)(2,1)S(1)}, u32[]{:S(2)}, u32[]{:S(2)}) collective-permute-start(bf16[256,1024]{1,0:T(8,128)(2,1)S(1)} %copy-done.33), channel_id=1, source_target_pairs={{0,24},{8,16},{16,8},{24,0},{1,25},{9,17},{17,9},{25,1},{2,26},{10... | collective-permute-start | bytes 1572872 | tf_op jit(solution)/shard_map/ppermute | solution.py:781
  464.2 23.9 %collective-permute-start.62 = (bf16[1,1,512,512]{3,2,1,0:T(8,128)(2,1)}, bf16[1,1,512,512]{3,2,1,0:T(8,128)(2,1)S(1)}, u32[]{:S(2)}, u32[]{:S(2)}) collective-permute-start(bf16[1,1,512,512]{3,2,1,0:T(8,128)(2,1)} %get-tuple-element.1777), channel_id=1, source_target_pairs={{4,0},{6,2},{5,1},{7,3},{12,8},{14,10},{13,9},{15,11},{20,16},{22,... | collective-permute-start | bytes 1572872 | tf_op jit(solution)/shard_map/ppermute | solution.py:1151
  465.5 22.6 %collective-permute-start.66 = (bf16[256,1024]{1,0:T(8,128)(2,1)}, bf16[256,1024]{1,0:T(8,128)(2,1)S(1)}, u32[]{:S(2)}, u32[]{:S(2)}) collective-permute-start(bf16[256,1024]{1,0:T(8,128)(2,1)} %get-tuple-element.1805), channel_id=1, source_target_pairs={{0,8},{8,0},{16,24},{24,16},{1,9},{9,1},{17,25},{25,17},{2,10},{10... | collective-permute-start | bytes 1572872 | tf_op jit(solution)/shard_map/ppermute | solution.py:781
  466.0 24.5 %collective-permute-start.67 = (bf16[256,1024]{1,0:T(8,128)(2,1)}, bf16[256,1024]{1,0:T(8,128)(2,1)S(1)}, u32[]{:S(2)}, u32[]{:S(2)}) collective-permute-start(bf16[256,1024]{1,0:T(8,128)(2,1)} %get-tuple-element.1806), channel_id=1, source_target_pairs={{0,16},{8,24},{16,0},{24,8},{1,17},{9,25},{17,1},{25,9},{2,18},{10... | collective-permute-start | bytes 1572872 | tf_op jit(solution)/shard_map/ppermute | solution.py:781
  467.5 23.0 %collective-permute-start.68 = (bf16[256,1024]{1,0:T(8,128)(2,1)}, bf16[256,1024]{1,0:T(8,128)(2,1)}, u32[]{:S(2)}, u32[]{:S(2)}) collective-permute-start(bf16[256,1024]{1,0:T(8,128)(2,1)} %get-tuple-element.1807), channel_id=1, source_target_pairs={{0,24},{8,16},{16,8},{24,0},{1,25},{9,17},{17,9},{25,1},{2,26},{10... | collective-permute-start | bytes 1572872 | tf_op jit(solution)/shard_map/ppermute | solution.py:781
  490.6 30.0 %collective-permute-start.72 = (bf16[1,1,512,512]{3,2,1,0:T(8,128)(2,1)}, bf16[1,1,512,512]{3,2,1,0:T(8,128)(2,1)}, u32[]{:S(2)}, u32[]{:S(2)}) collective-permute-start(bf16[1,1,512,512]{3,2,1,0:T(8,128)(2,1)} %get-tuple-element.1823), channel_id=1, source_target_pairs={{2,0},{4,2},{6,4},{3,1},{5,3},{7,5},{10,8},{12,10},{14,12},{11,9},... | collective-permute-start | bytes 1572872 | tf_op jit(solution)/shard_map/ppermute | solution.py:1151
  492.1 48.8 %collective-permute-start.73 = (bf16[1,1,512,512]{3,2,1,0:T(8,128)(2,1)}, bf16[1,1,512,512]{3,2,1,0:T(8,128)(2,1)}, u32[]{:S(2)}, u32[]{:S(2)}) collective-permute-start(bf16[1,1,512,512]{3,2,1,0:T(8,128)(2,1)} %get-tuple-element.1824), channel_id=1, source_target_pairs={{4,0},{6,2},{5,1},{7,3},{12,8},{14,10},{13,9},{15,11},{20,16},{22,... | collective-permute-start | bytes 1572872 | tf_op jit(solution)/shard_map/ppermute | solution.py:1151
  513.2 27.7 %collective-permute-start.79 = (bf16[256,1024]{1,0:T(8,128)(2,1)S(1)}, bf16[256,1024]{1,0:T(8,128)(2,1)S(1)}, u32[]{:S(2)}, u32[]{:S(2)}) collective-permute-start(bf16[256,1024]{1,0:T(8,128)(2,1)S(1)} %add_convert_fusion.15), channel_id=1, source_target_pairs={{0,1},{1,0},{2,3},{3,2},{4,5},{5,4},{6,7},{7,6},{8,9},{9,8},{10,11... | collective-permute-start | bytes 1572872 | tf_op jit(solution)/shard_map/ppermute | solution.py:758
  518.9 37.1 %collective-permute-start.78 = (bf16[512,1024]{1,0:T(8,128)(2,1)}, bf16[512,1024]{1,0:T(8,128)(2,1)}, u32[]{:S(2)}, u32[]{:S(2)}) collective-permute-start(bf16[512,1024]{1,0:T(8,128)(2,1)} %get-tuple-element.1966), channel_id=1, source_target_pairs={{0,1},{1,0},{2,3},{3,2},{4,5},{5,4},{6,7},{7,6},{8,9},{9,8},{10,11... | collective-permute-start | bytes 3145736 | tf_op jit(solution)/shard_map/ppermute | solution.py:758
  519.0 25.2 %collective-permute-start.74 = (bf16[1,1,512,512]{3,2,1,0:T(8,128)(2,1)}, bf16[1,1,512,512]{3,2,1,0:T(8,128)(2,1)S(1)}, u32[]{:S(2)}, u32[]{:S(2)}) collective-permute-start(bf16[1,1,512,512]{3,2,1,0:T(8,128)(2,1)} %get-tuple-element.1825), channel_id=1, source_target_pairs={{6,0},{7,1},{14,8},{15,9},{22,16},{23,17},{30,24},{31,25}} | collective-permute-start | bytes 1572872 | tf_op jit(solution)/shard_map/ppermute | solution.py:1151
  520.6 23.6 %collective-permute-start.75 = (bf16[256,1024]{1,0:T(8,128)(2,1)}, bf16[256,1024]{1,0:T(8,128)(2,1)S(1)}, u32[]{:S(2)}, u32[]{:S(2)}) collective-permute-start(bf16[256,1024]{1,0:T(8,128)(2,1)} %get-tuple-element.1882), channel_id=1, source_target_pairs={{0,8},{8,0},{16,24},{24,16},{1,9},{9,1},{17,25},{25,17},{2,10},{10... | collective-permute-start | bytes 1572872 | tf_op jit(solution)/shard_map/ppermute | solution.py:1181
  562.1 32.4 %collective-permute-start.92 = (bf16[4,64,1536]{2,1,0:T(8,128)(2,1)}, bf16[4,64,1536]{2,1,0:T(8,128)(2,1)}, u32[]{:S(2)}, u32[]{:S(2)}) collective-permute-start(bf16[4,64,1536]{2,1,0:T(8,128)(2,1)} %get-tuple-element.1923), channel_id=1, source_target_pairs={{0,6},{2,4},{4,2},{6,0},{1,7},{3,5},{5,3},{7,1},{8,14},{10,12},{12... | collective-permute-start | bytes 2359304 | tf_op jit(solution)/shard_map/ppermute | solution.py:1063
  587.1 31.8 %collective-permute-start.85 = (bf16[64,1024]{1,0:T(8,128)(2,1)}, bf16[64,1024]{1,0:T(8,128)(2,1)S(1)}, u32[]{:S(2)}, u32[]{:S(2)}) collective-permute-start(bf16[64,1024]{1,0:T(8,128)(2,1)} %get-tuple-element.1984), channel_id=1, source_target_pairs={{0,2},{2,0},{4,6},{6,4},{1,3},{3,1},{5,7},{7,5},{8,10},{10,8},{12,... | collective-permute-start | bytes 393224 | tf_op jit(solution)/shard_map/ppermute | solution.py:781
  588.8 31.3 %collective-permute-start.86 = (bf16[64,1024]{1,0:T(8,128)(2,1)}, bf16[64,1024]{1,0:T(8,128)(2,1)}, u32[]{:S(2)}, u32[]{:S(2)}) collective-permute-start(bf16[64,1024]{1,0:T(8,128)(2,1)} %get-tuple-element.1985), channel_id=1, source_target_pairs={{0,4},{2,6},{4,0},{6,2},{1,5},{3,7},{5,1},{7,3},{8,12},{10,14},{12... | collective-permute-start | bytes 393224 | tf_op jit(solution)/shard_map/ppermute | solution.py:781
  591.5 28.5 %collective-permute-start.87 = (bf16[64,1024]{1,0:T(8,128)(2,1)}, bf16[64,1024]{1,0:T(8,128)(2,1)}, u32[]{:S(2)}, u32[]{:S(2)}) collective-permute-start(bf16[64,1024]{1,0:T(8,128)(2,1)} %get-tuple-element.1986), channel_id=1, source_target_pairs={{0,6},{2,4},{4,2},{6,0},{1,7},{3,5},{5,3},{7,1},{8,14},{10,12},{12... | collective-permute-start | bytes 393224 | tf_op jit(solution)/shard_map/ppermute | solution.py:781
  594.5 20.7 %collective-permute-start.89 = (bf16[64,640]{1,0:T(8,128)(2,1)}, bf16[64,640]{1,0:T(8,128)(2,1)S(1)}, u32[]{:S(2)}, u32[]{:S(2)}) collective-permute-start(bf16[64,640]{1,0:T(8,128)(2,1)} %get-tuple-element.1993), channel_id=1, source_target_pairs={{0,4},{2,6},{4,0},{6,2},{1,5},{3,7},{5,1},{7,3},{8,12},{10,14},{12... | collective-permute-start | bytes 245768 | tf_op jit(solution)/shard_map/ppermute | solution.py:781
  (118 other events, 1627.9 us)

commit v5 on v4

--- a/solution.py
+++ b/solution.py
@@ -869,16 +869,17 @@
     small = jnp.pad(small, ((0, 0), (0, 128 - small.shape[1])))
     kv_shard = jnp.concatenate([w_key, w_value, small], axis=1)
     qo_shard = jnp.concatenate([head_order(w_query), head_order(w_output)], axis=1)
-    side = lambda w: w.reshape(dp, 2, group, shard, units)
-    w3 = jnp.concatenate(
-        [side(w)[:, :, e] for w in (w_gate, w_up, w_down) for e in range(group)], axis=3
-    )
     if hops:
         kv_line = gather_line(kv_shard)
         qo_line = gather_line(qo_shard)
-    w3_parts = exchange(by_xor([w3[i] for i in range(dp)], me_dp), "dp")
-    own3 = by_xor(w3_parts, me_dp)
-    own3 = [jnp.stack([o[g] for o in own3]) for g in range(2)]
+
+    def own_experts(gate_up_down):
+        cut = [w.reshape(dp, 2, group, shard, units) for w in gate_up_down]
+        side = jnp.concatenate([w[:, :, e] for w in cut for e in range(group)], axis=3)
+        parts = exchange(by_xor([side[i] for i in range(dp)], me_dp), "dp")
+        parts = by_xor(parts, me_dp)
+        return [jnp.stack([p[g] for p in parts]) for g in range(2)]
+
     def weight_send(g, *steps):
         if hops:
             for s in steps:
@@ -892,16 +893,23 @@
             d.update(taken)
 
     if hops:
-        own3 = [{0: o} for o in own3]
-        seal(kv_line=kv_line, qo_line=qo_line, weights=own3, x=tokens, dy=cotangent, routes=routes)
+        seal_but(
+            lambda: [(live, ["qo_line"])],
+            kv_line=kv_line,
+            qo_line=qo_line,
+            raw=[w_gate, w_up, w_down],
+            x=tokens,
+            dy=cotangent,
+            routes=routes,
+        )
         kv_pieces = gather_plane(live.pop("kv_line"))
-        weight_send(0, 1)
         seal(kv_pieces=kv_pieces)
         kv_full = whole_rows(live.pop("kv_pieces"))
         qo_pieces = gather_plane(live.pop("qo_line"))
     else:
         kv_full = lax.all_gather(kv_shard, ("dp", "ctx"), axis=0, tiled=True)
         qo_full = lax.all_gather(qo_shard, ("dp", "ctx"), axis=0, tiled=True)
+        own3 = own_experts([w_gate, w_up, w_down])
         own3 = [lax.all_gather(o, "ctx", axis=1, tiled=False) for o in own3]
         own3 = [{0: o.reshape(width, o.shape[-1])} for o in own3]
         seal(weights=own3, x=tokens, dy=cotangent, routes=routes)
@@ -966,13 +974,13 @@
             gain_one=gain_one,
             gain_two=gain_two,
         )
-    live.update(qo_full=qo_full, dy_far=[], dy_near=[])
+    live.update(qo_full=qo_full, dy_far={}, dy_near={})
     q = q_call(live["normed"], qo_full, qw, live["cosine"], live["sine"])
     live["q"] = q.reshape(micro * seq_count, local, qw)
 
     def dy_send(steps):
         for s in steps:
-            live["dy_far"].append(lax.ppermute(live["dy_cut"][0], "dp", apart(dp, s)))
+            live["dy_far"][s] = lax.ppermute(live["dy_cut"][0], "dp", apart(dp, s))
 
     def attend(first, s, done):
         return attn_part(
@@ -994,18 +1002,19 @@
         carry = attend(True, 1, False)
         live["kv_prev"].append(got)
         seal(carry=carry)
-        dy_send((3,))
+        weights = [{0: own} for own in own_experts(live.pop("raw"))]
         got = up_hop(live["kv_prev"][-1], n, 2)
         carry = attend(False, 2, False)
         live["kv_prev"].append(got)
-        seal(carry=carry)
-        weight_send(0, 2)
+        seal(carry=carry, weights=weights)
+        weight_send(0, 1, 2)
+        dy_send((3,))
         attn, lse = attend(False, 3, True)
     else:
         attn, lse = attend(True, 1, True)
         dy_send(range(1, dp))
-    live["dy_near"] = [swap(f) for f in live["dy_far"]]
-    late = lambda: [(live["weights"][0], [2])]
+    live["dy_near"] = {s: swap(live["dy_far"][s]) for s in (1, 2)}
+    late = lambda: [(live["weights"][0], [1, 2]), (live["dy_far"], [3])]
     seal_but(late, attn=attn, lse=lse, mixed=mix(attn))
 
     mixed_got = swap(live["mixed"])
@@ -1014,12 +1023,14 @@
     ffn_low = (hidden * inv_two * live["gain_two"]).astype(BF)
     x_cut = [halves(ffn_low[m * per : (m + 1) * per]) for m in micros]
 
+    late = lambda: [(live["weights"][0], [1, 2]), (live["dy_far"], [3])]
     seal_but(late, hidden=hidden, inv_two=inv_two, ffn_low=ffn_low, x_cut=x_cut)
     first = far_pieces(live["x_cut"][0][0], (1, 2))
     live["x_far"] = [first] + [[]] * (micro - 1)
     seal()
     live["x_far"][0] = live["x_far"][0] + far_pieces(live["x_cut"][0][0], (3,))
     weight_send(0, 3)
+    live["dy_near"][3] = swap(live["dy_far"][3])
     seal()
     live["x_near"] = [[swap(f) for f in live["x_far"][0]]] + [[]] * (micro - 1)
     seal()
@@ -1029,7 +1040,12 @@
         weights = [live["weights"][g][s] for s in sorted(live["weights"][g])]
         x_cut, dy_cut = live["x_cut"][m], live["dy_cut"]
         xs = paired(x_cut[0], live["x_far"][m], x_cut[1], live["x_near"][m])
-        dys = paired(dy_cut[0], live["dy_far"], dy_cut[1], live["dy_near"])
+        dys = paired(
+            dy_cut[0],
+            [live["dy_far"][s] for s in range(1, dp)],
+            dy_cut[1],
+            [live["dy_near"][s] for s in range(1, dp)],
+        )
         part = experts_call(
             xs,
             dys,

time: 640 us -> 636 us (level)
    ppermute x3, waiting for transfers between devices: 26.6 us -> 9.12 us  [dy_send(): live['dy_far'][s] = lax.ppermute(live['dy_cut'][0], 'dp', apart(dp, s))]
    ppermute x30, waiting for transfers between devices: 17.4 us -> 30.9 us  [exchange(): lax.ppermute(parts[s], axis, apart(count, s))]
    ppermute x6, waiting for transfers between devices: 12.7 us -> 24.3 us  [far_pieces(): return [lax.ppermute(mine, 'dp', apart(dp, s)) for s in steps]]
    unnamed x148 -> x138, local copies, waits for them, and re-layouts: 22.2 us -> 16.9 us
  transfers between devices with their start and end apart: 96 -> 96, of which waited for: 37 -> 39; matrix products, arithmetic and copies ran while one was open for 13% -> 13% of each run, Pallas kernels for 30% -> 31%
where the time goes in v5:
time: 636 us; the launch traced here: 625 us
  Pallas kernels  207 us (33%)
  waiting for transfers between devices  190 us (30%)
  starting transfers between devices  117 us (18%)
  other arithmetic  68.3 us (11%)
  local copies, waits for them, and re-layouts  31.2 us (5%)
  matrix products  10.9 us (2%)
    pallas_call x4, Pallas kernels, experts_call(): pl.pallas_call(functools.partial(experts_kernel, steps, first, count, mic...  123 us
    ppermute x30, starting transfers between devices, exchange(): lax.ppermute(parts[s], axis, apart(count, s))  40 us
    ppermute x6, waiting for transfers between devices, dkv_send(): lax.ppermute(live['dkv'][m][d], 'ctx', [(c, c - d) for c in range(d, n)])  35.8 us
    ppermute x30, waiting for transfers between devices, exchange(): lax.ppermute(parts[s], axis, apart(count, s))  30.9 us
    ppermute x6, waiting for transfers between devices, weight_send(): lax.ppermute(live['weights'][g][at], 'ctx', apart(n, hop))  29.5 us
    ppermute x6, waiting for transfers between devices, far_pieces(): return [lax.ppermute(mine, 'dp', apart(dp, s)) for s in steps]  24.3 us
    pallas_call x2, Pallas kernels, attn_bwd(): pl.pallas_call(functools.partial(attn_bwd_kernel, counts), grid=(seqs, pa...  21.1 us
    convert_element_type x10, other arithmetic, add(): return functools.reduce(jnp.add, [t.astype(F32) for t in terms]).astype(BF)  21.1 us
  transfers between devices with their start and end apart: 96, of which 39 were waited for; matrix products, arithmetic and copies ran while one was open for 13% of the time, Pallas kernels for 31%

profile of v5, /device:TPU:0, one launch (start us, length us, event | category | flops | bytes accessed | tf_op | source)
XLA Modules:
  0.0 625.5 jit_solution(6395014792557257927)
XLA Ops:
  3.1 5.1 collective-permute-start.5
  14.9 7.9 %collective-permute-done.1 = bf16[64,640]{1,0:T(8,128)(2,1)S(1)} collective-permute-done((bf16[64,640]{1,0:T(8,128)(2,1)S(1)}, bf16[64,640]{1,0:T(8,128)(2,1)S(1)}, u32[]{:S(2)}, u32[]{:S(2)}) %collective-permute-start.1) | collective-permute-done | bytes 81952 | tf_op jit(solution)/shard_map/ppermute | solution.py:850
  25.5 3.5 collective-permute-done.2
  35.7 5.1 collective-permute-done.8
  40.9 4.1 collective-permute-done.7
  46.9 5.7 kv.1
  61.3 6.7 %convert_reduce_fusion = bf16[1024,128]{1,0:T(8,128)(2,1)S(1)} fusion(s32[1024,8]{1,0:T(8,128)} %copy.128), kind=kLoop, calls=%fused_computation.14 | loop fusion | flops 3014656 | bytes 294912 | tf_op jit(solution)/shard_map/reduce_sum | solution.py:934
  70.9 10.1 %collective-permute-done.11 = bf16[4,64,1024]{2,1,0:T(8,128)(2,1)} collective-permute-done((bf16[4,64,1024]{2,1,0:T(8,128)(2,1)S(1)}, bf16[4,64,1024]{2,1,0:T(8,128)(2,1)}, u32[]{:S(2)}, u32[]{:S(2)}) %collective-permute-start.11) | collective-permute-done | bytes 524320 | tf_op jit(solution)/shard_map/ppermute | solution.py:854
  89.2 5.7 q.1
  94.9 8.2 %attn_fwd.3 = (f32[2,2,4,1024]{3,2,1,0:T(4,128)}, f32[2,2,2,128,1024]{4,3,2,1,0:T(8,128)}) custom-call(s32[1]{0:T(128)} %bitcast.ctx_ref.place_ref, bf16[2,512,512]{2,1,0:T(8,128)(2,1)} %bitcast.244, bf16[1,2,512,512]{3,2,1,0:T(8,128)(2,1)} %bitcast.280, bf16[1,2,512,512]{3,2,1,0:T(8,128)(2,1)} %collective-permute-done.9.refs_1_.refs_3_.refs_5_, ...), custom_call_target="tpu_custom_call" | custom-call | flops 8589934592 | bytes 4194304 | tf_op jit(solution)/shard_map/attn_fwd/pallas_call | solution.py:245
  103.0 6.1 collective-permute-done.14.refs_12_
  116.9 5.5 attn_fwd.4
  125.9 7.0 %collective-permute-done.17 = bf16[2,64,1536]{2,1,0:T(8,128)(2,1)S(1)} collective-permute-done((bf16[2,64,1536]{2,1,0:T(8,128)(2,1)S(1)}, bf16[2,64,1536]{2,1,0:T(8,128)(2,1)S(1)}, u32[]{:S(2)}, u32[]{:S(2)}) %collective-permute-start.17) | collective-permute-done | bytes 393248 | tf_op jit(solution)/shard_map/ppermute | solution.py:781
  135.6 5.0 attn_fwd.5
  143.5 5.3 collective-permute-start.25
  148.8 6.9 %collective-permute-start.24 = (bf16[4,64,1536]{2,1,0:T(8,128)(2,1)S(1)}, bf16[4,64,1536]{2,1,0:T(8,128)(2,1)S(1)}, u32[]{:S(2)}, u32[]{:S(2)}) collective-permute-start(bf16[4,64,1536]{2,1,0:T(8,128)(2,1)S(1)} %copy-done.29), channel_id=1, source_target_pairs={{0,2},{2,0},{4,6},{6,4},{1,3},{3,1},{5,7},{7,5},{8,10},{10,8},{12,... | collective-permute-start | bytes 2359304 | tf_op jit(solution)/shard_map/ppermute | solution.py:887
  164.7 19.1 %collective-permute-done.25.refs_18_ = bf16[4,64,1536]{2,1,0:T(8,128)(2,1)S(1)} collective-permute-done((bf16[4,64,1536]{2,1,0:T(8,128)(2,1)S(1)}, bf16[4,64,1536]{2,1,0:T(8,128)(2,1)S(1)}, u32[]{:S(2)}, u32[]{:S(2)}) %collective-permute-start.25) | collective-permute-done | bytes 786464 | tf_op jit(solution)/shard_map/ppermute | solution.py:887
  185.6 10.2 %collective-permute-done.27.refs_4_ = bf16[256,1024]{1,0:T(8,128)(2,1)} collective-permute-done((bf16[256,1024]{1,0:T(8,128)(2,1)S(1)}, bf16[256,1024]{1,0:T(8,128)(2,1)}, u32[]{:S(2)}, u32[]{:S(2)}) %collective-permute-start.27) | collective-permute-done | bytes 524320 | tf_op jit(solution)/shard_map/ppermute | solution.py:843
  198.2 13.5 %collective-permute-done.30.refs_6_ = bf16[256,1024]{1,0:T(8,128)(2,1)} collective-permute-done((bf16[256,1024]{1,0:T(8,128)(2,1)S(1)}, bf16[256,1024]{1,0:T(8,128)(2,1)}, u32[]{:S(2)}, u32[]{:S(2)}) %collective-permute-start.30) | collective-permute-done | bytes 524320 | tf_op jit(solution)/shard_map/ppermute | solution.py:843
  211.7 4.6 collective-permute-done.29.refs_19_
  225.4 30.1 %experts.4 = (bf16[4,256,1024]{2,1,0:T(8,128)(2,1)}, bf16[4,256,1024]{2,1,0:T(8,128)(2,1)}, bf16[4,256,1152]{2,1,0:T(8,128)(2,1)}, bf16[4,256,1152]{2,1,0:T(8,12...) custom-call(s32[2]{0:T(128)} %pad_add_fusion.place_ref, ...), custom_call_target="tpu_custom_call" | custom-call | flops 19327352832 | bytes 23068672 | tf_op jit(solution)/shard_map/experts/pallas_call | solution.py:527
  255.7 5.7 collective-permute-done.35.refs_18_
  266.7 30.3 %experts.5 = (bf16[4,256,1024]{2,1,0:T(8,128)(2,1)}, bf16[4,256,1024]{2,1,0:T(8,128)(2,1)}, bf16[4,256,1152]{2,1,0:T(8,128)(2,1)}, bf16[4,256,1152]{2,1,0:T(8,12...) custom-call(s32[2]{0:T(128)} %pad_add_fusion.place_ref, ...), custom_call_target="tpu_custom_call" | custom-call | flops 19327352832 | bytes 23068672 | tf_op jit(solution)/shard_map/experts/pallas_call | solution.py:527
  299.6 30.9 %experts.6 = (bf16[4,256,1024]{2,1,0:T(8,128)(2,1)}, bf16[4,256,1024]{2,1,0:T(8,128)(2,1)}, bf16[4,256,1152]{2,1,0:T(8,128)(2,1)}, bf16[4,256,1152]{2,1,0:T(8,12...) custom-call(s32[2]{0:T(128)} %pad_add_fusion.place_ref, ...), custom_call_target="tpu_custom_call" | custom-call | flops 19327352832 | bytes 23068672 | tf_op jit(solution)/shard_map/experts/pallas_call | solution.py:527
  331.8 4.4 collective-permute-done.44
  336.1 4.7 collective-permute-done.45
  340.9 3.2 fusion.26
  347.6 31.7 %experts.7 = (bf16[4,256,1024]{2,1,0:T(8,128)(2,1)}, bf16[4,256,1024]{2,1,0:T(8,128)(2,1)}, bf16[4,256,1152]{2,1,0:T(8,128)(2,1)}, bf16[4,256,1152]{2,1,0:T(8,12...) custom-call(s32[2]{0:T(128)} %pad_add_fusion.place_ref, ...), custom_call_target="tpu_custom_call" | custom-call | flops 19327352832 | bytes 23068672 | tf_op jit(solution)/shard_map/experts/pallas_call | solution.py:527
  381.9 3.2 collective-permute-start.56
  406.7 10.9 %attn_bwd.2 = (bf16[1,512,512]{2,1,0:T(8,128)(2,1)}, bf16[1,1,512,512]{3,2,1,0:T(8,128)(2,1)}, bf16[1,1,512,512]{3,2,1,0:T(8,128)(2,1)}, bf16[1,1,512,512]{3,2,1,0:T(8,128)(2,1)}, bf16[1,1,512,512]{3,2,1,0:T(8,128)(2,1)}) custom-call(s32[1]{0:T(128)} %bitcast.ctx_ref.place_ref, bf16[2,512,512]{2,1,0:T(8,128)(2,1)} %bitcast.247, ...), custom_call_target="tpu_custom_call" | custom-call | flops 21474836480 | bytes 8388608 | tf_op jit(solution)/shard_map/attn_bwd/pallas_call | solution.py:335
  417.7 2.8 collective-permute-done.56
  420.5 12.3 %collective-permute-done.54 = bf16[256,1152]{1,0:T(8,128)(2,1)} collective-permute-done((bf16[256,1152]{1,0:T(8,128)(2,1)}, bf16[256,1152]{1,0:T(8,128)(2,1)}, u32[]{:S(2)}, u32[]{:S(2)}) %collective-permute-start.54) | collective-permute-done | bytes 589856 | tf_op jit(solution)/shard_map/ppermute | solution.py:781
  452.3 11.2 %collective-permute-done.60 = bf16[1,1,512,512]{3,2,1,0:T(8,128)(2,1)} collective-permute-done((bf16[1,1,512,512]{3,2,1,0:T(8,128)(2,1)}, bf16[1,1,512,512]{3,2,1,0:T(8,128)(2,1)}, u32[]{:S(2)}, u32[]{:S(2)}) %collective-permute-start.60) | collective-permute-done | bytes 524320 | tf_op jit(solution)/shard_map/ppermute | solution.py:1167
  469.3 10.1 %attn_bwd.3 = (bf16[1,512,512]{2,1,0:T(8,128)(2,1)}, bf16[1,1,512,512]{3,2,1,0:T(8,128)(2,1)}, bf16[1,1,512,512]{3,2,1,0:T(8,128)(2,1)}, bf16[1,1,512,512]{3,2,1,0:T(8,128)(2,1)}, bf16[1,1,512,512]{3,2,1,0:T(8,128)(2,1)}) custom-call(s32[1]{0:T(128)} %bitcast.ctx_ref.place_ref, bf16[2,512,512]{2,1,0:T(8,128)(2,1)} %bitcast.248, ...), custom_call_target="tpu_custom_call" | custom-call | flops 21474836480 | bytes 8388608 | tf_op jit(solution)/shard_map/attn_bwd/pallas_call | solution.py:335
  479.4 8.8 %collective-permute-done.62 = bf16[1,1,512,512]{3,2,1,0:T(8,128)(2,1)S(1)} collective-permute-done((bf16[1,1,512,512]{3,2,1,0:T(8,128)(2,1)}, bf16[1,1,512,512]{3,2,1,0:T(8,128)(2,1)S(1)}, u32[]{:S(2)}, u32[]{:S(2)}) %collective-permute-start.62) | collective-permute-done | bytes 524320 | tf_op jit(solution)/shard_map/ppermute | solution.py:1167
  501.7 6.7 %grads.2 = (bf16[256,1024]{1,0:T(8,128)(2,1)}, bf16[256,1024]{1,0:T(8,128)(2,1)}, bf16[256,1024]{1,0:T(8,128)(2,1)}, bf16[256,1024]{1,0:T(8,128)(2,1)}) custom-call(s32[1]{0:T(128)} %bitcast.80.place_ref, bf16[1024,1024]{1,0:T(8,128)(2,1)} %get-tuple-element.1918.normed_ref.refs_0_.refs_2_, bf16[512,512]{1,0:T(8,128)(2,1)} %bitcast.234, ...), custom_call_target="tpu_custom_call" | custom-call | flops 2147483648 | bytes 4194304 | tf_op jit(solution)/shard_map/grads/pallas_call | solution.py:649
  513.4 5.1 back.2
  521.9 7.3 %collective-permute-done.73 = bf16[1,1,512,512]{3,2,1,0:T(8,128)(2,1)} collective-permute-done((bf16[1,1,512,512]{3,2,1,0:T(8,128)(2,1)}, bf16[1,1,512,512]{3,2,1,0:T(8,128)(2,1)}, u32[]{:S(2)}, u32[]{:S(2)}) %collective-permute-start.73) | collective-permute-done | bytes 524320 | tf_op jit(solution)/shard_map/ppermute | solution.py:1167
  533.9 8.4 %collective-permute-done.74 = bf16[1,1,512,512]{3,2,1,0:T(8,128)(2,1)S(1)} collective-permute-done((bf16[1,1,512,512]{3,2,1,0:T(8,128)(2,1)}, bf16[1,1,512,512]{3,2,1,0:T(8,128)(2,1)S(1)}, u32[]{:S(2)}, u32[]{:S(2)}) %collective-permute-start.74) | collective-permute-done | bytes 524320 | tf_op jit(solution)/shard_map/ppermute | solution.py:1167
  543.2 8.8 %collective-permute-done.76.refs_2_ = bf16[256,1024]{1,0:T(8,128)(2,1)} collective-permute-done((bf16[256,1024]{1,0:T(8,128)(2,1)}, bf16[256,1024]{1,0:T(8,128)(2,1)}, u32[]{:S(2)}, u32[]{:S(2)}) %collective-permute-start.76) | collective-permute-done | bytes 524320 | tf_op jit(solution)/shard_map/ppermute | solution.py:1197
  552.8 5.1 back.3
  558.1 4.0 collective-permute-start.92
  563.9 5.0 grads.3
  582.0 5.0 fusion.6
  588.6 3.5 collective-permute-start.87
  594.3 6.5 %collective-permute-start.89 = (bf16[64,640]{1,0:T(8,128)(2,1)}, bf16[64,640]{1,0:T(8,128)(2,1)S(1)}, u32[]{:S(2)}, u32[]{:S(2)}) collective-permute-start(bf16[64,640]{1,0:T(8,128)(2,1)} %get-tuple-element.1977), channel_id=1, source_target_pairs={{0,4},{2,6},{4,0},{6,2},{1,5},{3,7},{5,1},{7,3},{8,12},{10,14},{12... | collective-permute-start | bytes 245768 | tf_op jit(solution)/shard_map/ppermute | solution.py:781
  604.9 4.8 collective-permute-done.89.refs_6_
  621.8 3.3 expert_rows.1
  (409 shorter events, 203.7 us)
Async XLA Ops:
  3.1 26.0 %collective-permute-start.5 = (bf16[64,1024]{1,0:T(8,128)(2,1)S(1)}, bf16[64,1024]{1,0:T(8,128)(2,1)S(1)}, u32[]{:S(2)}, u32[]{:S(2)}) collective-permute-start(bf16[64,1024]{1,0:T(8,128)(2,1)S(1)} %constant_dynamic-update-slice_fusion), channel_id=1, source_target_pairs={{0,6},{2,4},{4,2},{6,0},{1,7},{3,5},{5,3},{7,1},{8,14},{10,12},{12... | collective-permute-start | bytes 393224 | tf_op jit(solution)/shard_map/ppermute | solution.py:850
  8.2 20.9 %collective-permute-start.3 = (bf16[64,1024]{1,0:T(8,128)(2,1)S(1)}, bf16[64,1024]{1,0:T(8,128)(2,1)S(1)}, u32[]{:S(2)}, u32[]{:S(2)}) collective-permute-start(bf16[64,1024]{1,0:T(8,128)(2,1)S(1)} %constant_dynamic-update-slice_fusion), channel_id=1, source_target_pairs={{0,2},{2,0},{4,6},{6,4},{1,3},{3,1},{5,7},{7,5},{8,10},{10,8},{12,... | collective-permute-start | bytes 393224 | tf_op jit(solution)/shard_map/ppermute | solution.py:850
  52.6 28.5 %collective-permute-start.9 = (bf16[1,2,512,512]{3,2,1,0:T(8,128)(2,1)}, bf16[1,2,512,512]{3,2,1,0:T(8,128)(2,1)}, u32[]{:S(2)}, u32[]{:S(2)}) collective-permute-start(bf16[1,2,512,512]{3,2,1,0:T(8,128)(2,1)} %bitcast.279), channel_id=1, source_target_pairs={{0,2},{2,4},{4,6},{1,3},{3,5},{5,7},{8,10},{10,12},{12,14},{9,11},... | collective-permute-start | bytes 3145736 | tf_op jit(solution)/shard_map/ppermute | solution.py:762
  56.7 24.3 %collective-permute-start.11 = (bf16[4,64,1024]{2,1,0:T(8,128)(2,1)S(1)}, bf16[4,64,1024]{2,1,0:T(8,128)(2,1)}, u32[]{:S(2)}, u32[]{:S(2)}) collective-permute-start(bf16[4,64,1024]{2,1,0:T(8,128)(2,1)S(1)} %pad_maximum_fusion.8), channel_id=1, source_target_pairs={{0,16},{8,24},{16,0},{24,8},{1,17},{9,25},{17,1},{25,9},{2,18},{10... | collective-permute-start | bytes 1572872 | tf_op jit(solution)/shard_map/ppermute | solution.py:854
  58.0 23.1 %collective-permute-start.10 = (bf16[4,64,1024]{2,1,0:T(8,128)(2,1)S(1)}, bf16[4,64,1024]{2,1,0:T(8,128)(2,1)}, u32[]{:S(2)}, u32[]{:S(2)}) collective-permute-start(bf16[4,64,1024]{2,1,0:T(8,128)(2,1)S(1)} %pad_maximum_fusion.8), channel_id=1, source_target_pairs={{0,8},{8,0},{16,24},{24,16},{1,9},{9,1},{17,25},{25,17},{2,10},{10... | collective-permute-start | bytes 1572872 | tf_op jit(solution)/shard_map/ppermute | solution.py:854
  81.1 28.0 %collective-permute-start.14 = (bf16[2,256,1152]{2,1,0:T(8,128)(2,1)}, bf16[2,256,1152]{2,1,0:T(8,128)(2,1)}, u32[]{:S(2)}, u32[]{:S(2)}) collective-permute-start(bf16[2,256,1152]{2,1,0:T(8,128)(2,1)} %get-tuple-element.1566.refs_8_), channel_id=1, source_target_pairs={{0,16},{8,24},{16,0},{24,8},{1,17},{9,25},{17,1},{25,9},{2,18},{10... | collective-permute-start | bytes 3538952 | tf_op jit(solution)/shard_map/ppermute | solution.py:983
  82.5 27.9 %collective-permute-start.13 = (bf16[2,256,1152]{2,1,0:T(8,128)(2,1)}, bf16[2,256,1152]{2,1,0:T(8,128)(2,1)}, u32[]{:S(2)}, u32[]{:S(2)}) collective-permute-start(bf16[2,256,1152]{2,1,0:T(8,128)(2,1)} %get-tuple-element.1566.refs_8_), channel_id=1, source_target_pairs={{0,8},{8,0},{16,24},{24,16},{1,9},{9,1},{17,25},{25,17},{2,10},{10... | collective-permute-start | bytes 3538952 | tf_op jit(solution)/shard_map/ppermute | solution.py:983
  110.5 24.6 %collective-permute-start.16 = (bf16[1,2,512,512]{3,2,1,0:T(8,128)(2,1)}, bf16[1,2,512,512]{3,2,1,0:T(8,128)(2,1)}, u32[]{:S(2)}, u32[]{:S(2)}) collective-permute-start(bf16[1,2,512,512]{3,2,1,0:T(8,128)(2,1)} %collective-permute-done.15.refs_0_.refs_1_.refs_2_.refs_6_), channel_id=1, source_target_pairs={{4,6},{5,7},{12,14},{13,15},{20,22},{21,23},{28,30},{29,31}} | collective-permute-start | bytes 3145736 | tf_op jit(solution)/shard_map/ppermute | solution.py:762
  143.5 40.4 %collective-permute-start.25 = (bf16[4,64,1536]{2,1,0:T(8,128)(2,1)S(1)}, bf16[4,64,1536]{2,1,0:T(8,128)(2,1)S(1)}, u32[]{:S(2)}, u32[]{:S(2)}) collective-permute-start(bf16[4,64,1536]{2,1,0:T(8,128)(2,1)S(1)} %copy-done.29), channel_id=1, source_target_pairs={{0,4},{2,6},{4,0},{6,2},{1,5},{3,7},{5,1},{7,3},{8,12},{10,14},{12... | collective-permute-start | bytes 2359304 | tf_op jit(solution)/shard_map/ppermute | solution.py:887
  148.8 35.2 %collective-permute-start.24 = (bf16[4,64,1536]{2,1,0:T(8,128)(2,1)S(1)}, bf16[4,64,1536]{2,1,0:T(8,128)(2,1)S(1)}, u32[]{:S(2)}, u32[]{:S(2)}) collective-permute-start(bf16[4,64,1536]{2,1,0:T(8,128)(2,1)S(1)} %copy-done.29), channel_id=1, source_target_pairs={{0,2},{2,0},{4,6},{6,4},{1,3},{3,1},{5,7},{7,5},{8,10},{10,8},{12,... | collective-permute-start | bytes 2359304 | tf_op jit(solution)/shard_map/ppermute | solution.py:887
  155.6 30.0 %collective-permute-start.23 = (bf16[2,256,1152]{2,1,0:T(8,128)(2,1)}, bf16[2,256,1152]{2,1,0:T(8,128)(2,1)S(1)}, u32[]{:S(2)}, u32[]{:S(2)}) collective-permute-start(bf16[2,256,1152]{2,1,0:T(8,128)(2,1)} %get-tuple-element.1566.refs_8_), channel_id=1, source_target_pairs={{0,24},{8,16},{16,8},{24,0},{1,25},{9,17},{17,9},{25,1},{2,26},{10... | collective-permute-start | bytes 3538952 | tf_op jit(solution)/shard_map/ppermute | solution.py:983
  162.8 33.1 %collective-permute-start.27 = (bf16[256,1024]{1,0:T(8,128)(2,1)S(1)}, bf16[256,1024]{1,0:T(8,128)(2,1)}, u32[]{:S(2)}, u32[]{:S(2)}) collective-permute-start(bf16[256,1024]{1,0:T(8,128)(2,1)S(1)} %get-tuple-element.1432.refs_0_), channel_id=1, source_target_pairs={{0,16},{8,24},{16,0},{24,8},{1,17},{9,25},{17,1},{25,9},{2,18},{10... | collective-permute-start | bytes 1572872 | tf_op jit(solution)/shard_map/ppermute | solution.py:843
  164.7 31.7 %collective-permute-start.26 = (bf16[256,1024]{1,0:T(8,128)(2,1)S(1)}, bf16[256,1024]{1,0:T(8,128)(2,1)}, u32[]{:S(2)}, u32[]{:S(2)}) collective-permute-start(bf16[256,1024]{1,0:T(8,128)(2,1)S(1)} %get-tuple-element.1432.refs_0_), channel_id=1, source_target_pairs={{0,8},{8,0},{16,24},{24,16},{1,9},{9,1},{17,25},{25,17},{2,10},{10... | collective-permute-start | bytes 1572872 | tf_op jit(solution)/shard_map/ppermute | solution.py:843
  221.3 34.3 %collective-permute-start.38 = (bf16[256,1024]{1,0:T(8,128)(2,1)S(1)}, bf16[256,1024]{1,0:T(8,128)(2,1)S(1)}, u32[]{:S(2)}, u32[]{:S(2)}) collective-permute-start(bf16[256,1024]{1,0:T(8,128)(2,1)S(1)} %get-tuple-element.1558.refs_0_), channel_id=1, source_target_pairs={{0,24},{8,16},{16,8},{24,0},{1,25},{9,17},{17,9},{25,1},{2,26},{10... | collective-permute-start | bytes 1572872 | tf_op jit(solution)/shard_map/ppermute | solution.py:843
  222.9 32.8 %collective-permute-start.37 = (bf16[256,1024]{1,0:T(8,128)(2,1)S(1)}, bf16[256,1024]{1,0:T(8,128)(2,1)}, u32[]{:S(2)}, u32[]{:S(2)}) collective-permute-start(bf16[256,1024]{1,0:T(8,128)(2,1)S(1)} %get-tuple-element.1558.refs_0_), channel_id=1, source_target_pairs={{0,16},{8,24},{16,0},{24,8},{1,17},{9,25},{17,1},{25,9},{2,18},{10... | collective-permute-start | bytes 1572872 | tf_op jit(solution)/shard_map/ppermute | solution.py:843
  224.3 31.4 %collective-permute-start.36 = (bf16[256,1024]{1,0:T(8,128)(2,1)S(1)}, bf16[256,1024]{1,0:T(8,128)(2,1)}, u32[]{:S(2)}, u32[]{:S(2)}) collective-permute-start(bf16[256,1024]{1,0:T(8,128)(2,1)S(1)} %get-tuple-element.1558.refs_0_), channel_id=1, source_target_pairs={{0,8},{8,0},{16,24},{24,16},{1,9},{9,1},{17,25},{25,17},{2,10},{10... | collective-permute-start | bytes 1572872 | tf_op jit(solution)/shard_map/ppermute | solution.py:843
  224.8 36.5 %collective-permute-start.35 = (bf16[4,64,1536]{2,1,0:T(8,128)(2,1)}, bf16[4,64,1536]{2,1,0:T(8,128)(2,1)}, u32[]{:S(2)}, u32[]{:S(2)}) collective-permute-start(bf16[4,64,1536]{2,1,0:T(8,128)(2,1)} %pad_maximum_fusion.7.refs_16_), channel_id=1, source_target_pairs={{0,4},{2,6},{4,0},{6,2},{1,5},{3,7},{5,1},{7,3},{8,12},{10,14},{12... | collective-permute-start | bytes 2359304 | tf_op jit(solution)/shard_map/ppermute | solution.py:887
  225.1 36.3 %collective-permute-start.34 = (bf16[4,64,1536]{2,1,0:T(8,128)(2,1)}, bf16[4,64,1536]{2,1,0:T(8,128)(2,1)}, u32[]{:S(2)}, u32[]{:S(2)}) collective-permute-start(bf16[4,64,1536]{2,1,0:T(8,128)(2,1)} %pad_maximum_fusion.7.refs_16_), channel_id=1, source_target_pairs={{0,2},{2,0},{4,6},{6,4},{1,3},{3,1},{5,7},{7,5},{8,10},{10,8},{12,... | collective-permute-start | bytes 2359304 | tf_op jit(solution)/shard_map/ppermute | solution.py:887
  266.6 30.3 %collective-permute-start.42 = (bf16[4,64,1536]{2,1,0:T(8,128)(2,1)}, bf16[4,64,1536]{2,1,0:T(8,128)(2,1)}, u32[]{:S(2)}, u32[]{:S(2)}) collective-permute-start(bf16[4,64,1536]{2,1,0:T(8,128)(2,1)} %collective-permute-done.35.refs_18_), channel_id=1, source_target_pairs={{0,2},{2,0},{4,6},{6,4},{1,3},{3,1},{5,7},{7,5},{8,10},{10,8},{12,... | collective-permute-start | bytes 2359304 | tf_op jit(solution)/shard_map/ppermute | solution.py:887
  297.0 34.8 %collective-permute-start.43 = (bf16[4,64,1536]{2,1,0:T(8,128)(2,1)}, bf16[4,64,1536]{2,1,0:T(8,128)(2,1)}, u32[]{:S(2)}, u32[]{:S(2)}) collective-permute-start(bf16[4,64,1536]{2,1,0:T(8,128)(2,1)} %get-tuple-element.1428), channel_id=1, source_target_pairs={{0,2},{2,0},{4,6},{6,4},{1,3},{3,1},{5,7},{7,5},{8,10},{10,8},{12,... | collective-permute-start | bytes 2359304 | tf_op jit(solution)/shard_map/ppermute | solution.py:1079
  299.0 37.1 %collective-permute-start.44 = (bf16[4,64,1536]{2,1,0:T(8,128)(2,1)}, bf16[4,64,1536]{2,1,0:T(8,128)(2,1)}, u32[]{:S(2)}, u32[]{:S(2)}) collective-permute-start(bf16[4,64,1536]{2,1,0:T(8,128)(2,1)} %get-tuple-element.1429), channel_id=1, source_target_pairs={{0,4},{2,6},{4,0},{6,2},{1,5},{3,7},{5,1},{7,3},{8,12},{10,14},{12... | collective-permute-start | bytes 2359304 | tf_op jit(solution)/shard_map/ppermute | solution.py:1079
  344.1 35.2 %collective-permute-start.46 = (bf16[256,1152]{1,0:T(8,128)(2,1)}, bf16[256,1152]{1,0:T(8,128)(2,1)}, u32[]{:S(2)}, u32[]{:S(2)}) collective-permute-start(bf16[256,1152]{1,0:T(8,128)(2,1)} %get-tuple-element.1591), channel_id=1, source_target_pairs={{0,8},{8,0},{16,24},{24,16},{1,9},{9,1},{17,25},{25,17},{2,10},{10... | collective-permute-start | bytes 1769480 | tf_op jit(solution)/shard_map/ppermute | solution.py:781
  345.6 33.7 %collective-permute-start.47 = (bf16[256,1152]{1,0:T(8,128)(2,1)}, bf16[256,1152]{1,0:T(8,128)(2,1)}, u32[]{:S(2)}, u32[]{:S(2)}) collective-permute-start(bf16[256,1152]{1,0:T(8,128)(2,1)} %get-tuple-element.1592), channel_id=1, source_target_pairs={{0,16},{8,24},{16,0},{24,8},{1,17},{9,25},{17,1},{25,9},{2,18},{10... | collective-permute-start | bytes 1769480 | tf_op jit(solution)/shard_map/ppermute | solution.py:781
  346.2 33.1 %collective-permute-start.48 = (bf16[256,1152]{1,0:T(8,128)(2,1)}, bf16[256,1152]{1,0:T(8,128)(2,1)}, u32[]{:S(2)}, u32[]{:S(2)}) collective-permute-start(bf16[256,1152]{1,0:T(8,128)(2,1)} %get-tuple-element.1593), channel_id=1, source_target_pairs={{0,24},{8,16},{16,8},{24,0},{1,25},{9,17},{17,9},{25,1},{2,26},{10... | collective-permute-start | bytes 1769480 | tf_op jit(solution)/shard_map/ppermute | solution.py:781
  347.6 31.7 %collective-permute-start.49 = (bf16[4,64,1536]{2,1,0:T(8,128)(2,1)}, bf16[4,64,1536]{2,1,0:T(8,128)(2,1)}, u32[]{:S(2)}, u32[]{:S(2)}) collective-permute-start(bf16[4,64,1536]{2,1,0:T(8,128)(2,1)} %get-tuple-element.1556), channel_id=1, source_target_pairs={{0,6},{2,4},{4,2},{6,0},{1,7},{3,5},{5,3},{7,1},{8,14},{10,12},{12... | collective-permute-start | bytes 2359304 | tf_op jit(solution)/shard_map/ppermute | solution.py:1079
  381.9 38.6 %collective-permute-start.56 = (bf16[4,64,1536]{2,1,0:T(8,128)(2,1)}, bf16[4,64,1536]{2,1,0:T(8,128)(2,1)}, u32[]{:S(2)}, u32[]{:S(2)}) collective-permute-start(bf16[4,64,1536]{2,1,0:T(8,128)(2,1)} %get-tuple-element.1637), channel_id=1, source_target_pairs={{0,2},{2,0},{4,6},{6,4},{1,3},{3,1},{5,7},{7,5},{8,10},{10,8},{12,... | collective-permute-start | bytes 2359304 | tf_op jit(solution)/shard_map/ppermute | solution.py:1079
  385.1 35.4 %collective-permute-start.57 = (bf16[4,64,1536]{2,1,0:T(8,128)(2,1)}, bf16[4,64,1536]{2,1,0:T(8,128)(2,1)}, u32[]{:S(2)}, u32[]{:S(2)}) collective-permute-start(bf16[4,64,1536]{2,1,0:T(8,128)(2,1)} %get-tuple-element.1638), channel_id=1, source_target_pairs={{0,4},{2,6},{4,0},{6,2},{1,5},{3,7},{5,1},{7,3},{8,12},{10,14},{12... | collective-permute-start | bytes 2359304 | tf_op jit(solution)/shard_map/ppermute | solution.py:1079
  404.7 28.1 %collective-permute-start.54 = (bf16[256,1152]{1,0:T(8,128)(2,1)}, bf16[256,1152]{1,0:T(8,128)(2,1)}, u32[]{:S(2)}, u32[]{:S(2)}) collective-permute-start(bf16[256,1152]{1,0:T(8,128)(2,1)} %get-tuple-element.1681), channel_id=1, source_target_pairs={{0,16},{8,24},{16,0},{24,8},{1,17},{9,25},{17,1},{25,9},{2,18},{10... | collective-permute-start | bytes 1769480 | tf_op jit(solution)/shard_map/ppermute | solution.py:781
  405.3 27.5 %collective-permute-start.55 = (bf16[256,1152]{1,0:T(8,128)(2,1)}, bf16[256,1152]{1,0:T(8,128)(2,1)}, u32[]{:S(2)}, u32[]{:S(2)}) collective-permute-start(bf16[256,1152]{1,0:T(8,128)(2,1)} %get-tuple-element.1682), channel_id=1, source_target_pairs={{0,24},{8,16},{16,8},{24,0},{1,25},{9,17},{17,9},{25,1},{2,26},{10... | collective-permute-start | bytes 1769480 | tf_op jit(solution)/shard_map/ppermute | solution.py:781
  436.2 27.4 %collective-permute-start.60 = (bf16[1,1,512,512]{3,2,1,0:T(8,128)(2,1)}, bf16[1,1,512,512]{3,2,1,0:T(8,128)(2,1)}, u32[]{:S(2)}, u32[]{:S(2)}) collective-permute-start(bf16[1,1,512,512]{3,2,1,0:T(8,128)(2,1)} %get-tuple-element.1725), channel_id=1, source_target_pairs={{6,0},{7,1},{14,8},{15,9},{22,16},{23,17},{30,24},{31,25}} | collective-permute-start | bytes 1572872 | tf_op jit(solution)/shard_map/ppermute | solution.py:1167
  437.7 28.6 %collective-permute-start.63 = (bf16[256,1024]{1,0:T(8,128)(2,1)}, bf16[256,1024]{1,0:T(8,128)(2,1)}, u32[]{:S(2)}, u32[]{:S(2)}) collective-permute-start(bf16[256,1024]{1,0:T(8,128)(2,1)} %get-tuple-element.1741), channel_id=1, source_target_pairs={{0,8},{8,0},{16,24},{24,16},{1,9},{9,1},{17,25},{25,17},{2,10},{10... | collective-permute-start | bytes 1572872 | tf_op jit(solution)/shard_map/ppermute | solution.py:781
  438.3 29.5 %collective-permute-start.64 = (bf16[256,1024]{1,0:T(8,128)(2,1)}, bf16[256,1024]{1,0:T(8,128)(2,1)}, u32[]{:S(2)}, u32[]{:S(2)}) collective-permute-start(bf16[256,1024]{1,0:T(8,128)(2,1)} %get-tuple-element.1742), channel_id=1, source_target_pairs={{0,16},{8,24},{16,0},{24,8},{1,17},{9,25},{17,1},{25,9},{2,18},{10... | collective-permute-start | bytes 1572872 | tf_op jit(solution)/shard_map/ppermute | solution.py:781
  449.0 30.4 %collective-permute-start.65 = (bf16[256,1024]{1,0:T(8,128)(2,1)S(1)}, bf16[256,1024]{1,0:T(8,128)(2,1)}, u32[]{:S(2)}, u32[]{:S(2)}) collective-permute-start(bf16[256,1024]{1,0:T(8,128)(2,1)S(1)} %copy-done.32), channel_id=1, source_target_pairs={{0,24},{8,16},{16,8},{24,0},{1,25},{9,17},{17,9},{25,1},{2,26},{10... | collective-permute-start | bytes 1572872 | tf_op jit(solution)/shard_map/ppermute | solution.py:781
  464.4 23.8 %collective-permute-start.62 = (bf16[1,1,512,512]{3,2,1,0:T(8,128)(2,1)}, bf16[1,1,512,512]{3,2,1,0:T(8,128)(2,1)S(1)}, u32[]{:S(2)}, u32[]{:S(2)}) collective-permute-start(bf16[1,1,512,512]{3,2,1,0:T(8,128)(2,1)} %get-tuple-element.1761), channel_id=1, source_target_pairs={{4,0},{6,2},{5,1},{7,3},{12,8},{14,10},{13,9},{15,11},{20,16},{22,... | collective-permute-start | bytes 1572872 | tf_op jit(solution)/shard_map/ppermute | solution.py:1167
  465.7 22.5 %collective-permute-start.66 = (bf16[256,1024]{1,0:T(8,128)(2,1)}, bf16[256,1024]{1,0:T(8,128)(2,1)}, u32[]{:S(2)}, u32[]{:S(2)}) collective-permute-start(bf16[256,1024]{1,0:T(8,128)(2,1)} %get-tuple-element.1789), channel_id=1, source_target_pairs={{0,8},{8,0},{16,24},{24,16},{1,9},{9,1},{17,25},{25,17},{2,10},{10... | collective-permute-start | bytes 1572872 | tf_op jit(solution)/shard_map/ppermute | solution.py:781
  466.3 24.6 %collective-permute-start.67 = (bf16[256,1024]{1,0:T(8,128)(2,1)}, bf16[256,1024]{1,0:T(8,128)(2,1)}, u32[]{:S(2)}, u32[]{:S(2)}) collective-permute-start(bf16[256,1024]{1,0:T(8,128)(2,1)} %get-tuple-element.1790), channel_id=1, source_target_pairs={{0,16},{8,24},{16,0},{24,8},{1,17},{9,25},{17,1},{25,9},{2,18},{10... | collective-permute-start | bytes 1572872 | tf_op jit(solution)/shard_map/ppermute | solution.py:781
  467.7 23.2 %collective-permute-start.68 = (bf16[256,1024]{1,0:T(8,128)(2,1)}, bf16[256,1024]{1,0:T(8,128)(2,1)}, u32[]{:S(2)}, u32[]{:S(2)}) collective-permute-start(bf16[256,1024]{1,0:T(8,128)(2,1)} %get-tuple-element.1791), channel_id=1, source_target_pairs={{0,24},{8,16},{16,8},{24,0},{1,25},{9,17},{17,9},{25,1},{2,26},{10... | collective-permute-start | bytes 1572872 | tf_op jit(solution)/shard_map/ppermute | solution.py:781
  490.9 29.4 %collective-permute-start.72 = (bf16[1,1,512,512]{3,2,1,0:T(8,128)(2,1)}, bf16[1,1,512,512]{3,2,1,0:T(8,128)(2,1)}, u32[]{:S(2)}, u32[]{:S(2)}) collective-permute-start(bf16[1,1,512,512]{3,2,1,0:T(8,128)(2,1)} %get-tuple-element.1807), channel_id=1, source_target_pairs={{2,0},{4,2},{6,4},{3,1},{5,3},{7,5},{10,8},{12,10},{14,12},{11,9},... | collective-permute-start | bytes 1572872 | tf_op jit(solution)/shard_map/ppermute | solution.py:1167
  492.3 36.9 %collective-permute-start.73 = (bf16[1,1,512,512]{3,2,1,0:T(8,128)(2,1)}, bf16[1,1,512,512]{3,2,1,0:T(8,128)(2,1)}, u32[]{:S(2)}, u32[]{:S(2)}) collective-permute-start(bf16[1,1,512,512]{3,2,1,0:T(8,128)(2,1)} %get-tuple-element.1808), channel_id=1, source_target_pairs={{4,0},{6,2},{5,1},{7,3},{12,8},{14,10},{13,9},{15,11},{20,16},{22,... | collective-permute-start | bytes 1572872 | tf_op jit(solution)/shard_map/ppermute | solution.py:1167
  518.6 33.5 %collective-permute-start.78 = (bf16[512,1024]{1,0:T(8,128)(2,1)}, bf16[512,1024]{1,0:T(8,128)(2,1)}, u32[]{:S(2)}, u32[]{:S(2)}) collective-permute-start(bf16[512,1024]{1,0:T(8,128)(2,1)} %get-tuple-element.1950), channel_id=1, source_target_pairs={{0,1},{1,0},{2,3},{3,2},{4,5},{5,4},{6,7},{7,6},{8,9},{9,8},{10,11... | collective-permute-start | bytes 3145736 | tf_op jit(solution)/shard_map/ppermute | solution.py:758
  518.7 23.7 %collective-permute-start.74 = (bf16[1,1,512,512]{3,2,1,0:T(8,128)(2,1)}, bf16[1,1,512,512]{3,2,1,0:T(8,128)(2,1)S(1)}, u32[]{:S(2)}, u32[]{:S(2)}) collective-permute-start(bf16[1,1,512,512]{3,2,1,0:T(8,128)(2,1)} %get-tuple-element.1809), channel_id=1, source_target_pairs={{6,0},{7,1},{14,8},{15,9},{22,16},{23,17},{30,24},{31,25}} | collective-permute-start | bytes 1572872 | tf_op jit(solution)/shard_map/ppermute | solution.py:1167
  520.3 22.1 %collective-permute-start.75 = (bf16[256,1024]{1,0:T(8,128)(2,1)}, bf16[256,1024]{1,0:T(8,128)(2,1)S(1)}, u32[]{:S(2)}, u32[]{:S(2)}) collective-permute-start(bf16[256,1024]{1,0:T(8,128)(2,1)} %get-tuple-element.1866), channel_id=1, source_target_pairs={{0,8},{8,0},{16,24},{24,16},{1,9},{9,1},{17,25},{25,17},{2,10},{10... | collective-permute-start | bytes 1572872 | tf_op jit(solution)/shard_map/ppermute | solution.py:1197
  529.2 22.8 %collective-permute-start.76 = (bf16[256,1024]{1,0:T(8,128)(2,1)}, bf16[256,1024]{1,0:T(8,128)(2,1)}, u32[]{:S(2)}, u32[]{:S(2)}) collective-permute-start(bf16[256,1024]{1,0:T(8,128)(2,1)} %get-tuple-element.1867), channel_id=1, source_target_pairs={{0,16},{8,24},{16,0},{24,8},{1,17},{9,25},{17,1},{25,9},{2,18},{10... | collective-permute-start | bytes 1572872 | tf_op jit(solution)/shard_map/ppermute | solution.py:1197
  530.6 21.4 %collective-permute-start.77 = (bf16[256,1024]{1,0:T(8,128)(2,1)}, bf16[256,1024]{1,0:T(8,128)(2,1)}, u32[]{:S(2)}, u32[]{:S(2)}) collective-permute-start(bf16[256,1024]{1,0:T(8,128)(2,1)} %get-tuple-element.1868), channel_id=1, source_target_pairs={{0,24},{8,16},{16,8},{24,0},{1,25},{9,17},{17,9},{25,1},{2,26},{10... | collective-permute-start | bytes 1572872 | tf_op jit(solution)/shard_map/ppermute | solution.py:1197
  558.1 36.2 %collective-permute-start.92 = (bf16[4,64,1536]{2,1,0:T(8,128)(2,1)}, bf16[4,64,1536]{2,1,0:T(8,128)(2,1)}, u32[]{:S(2)}, u32[]{:S(2)}) collective-permute-start(bf16[4,64,1536]{2,1,0:T(8,128)(2,1)} %get-tuple-element.1907), channel_id=1, source_target_pairs={{0,6},{2,4},{4,2},{6,0},{1,7},{3,5},{5,3},{7,1},{8,14},{10,12},{12... | collective-permute-start | bytes 2359304 | tf_op jit(solution)/shard_map/ppermute | solution.py:1079
  587.7 24.9 %collective-permute-start.85 = (bf16[64,1024]{1,0:T(8,128)(2,1)}, bf16[64,1024]{1,0:T(8,128)(2,1)S(1)}, u32[]{:S(2)}, u32[]{:S(2)}) collective-permute-start(bf16[64,1024]{1,0:T(8,128)(2,1)} %get-tuple-element.1968), channel_id=1, source_target_pairs={{0,2},{2,0},{4,6},{6,4},{1,3},{3,1},{5,7},{7,5},{8,10},{10,8},{12,... | collective-permute-start | bytes 393224 | tf_op jit(solution)/shard_map/ppermute | solution.py:781
  587.7 25.6 %collective-permute-start.86 = (bf16[64,1024]{1,0:T(8,128)(2,1)}, bf16[64,1024]{1,0:T(8,128)(2,1)S(1)}, u32[]{:S(2)}, u32[]{:S(2)}) collective-permute-start(bf16[64,1024]{1,0:T(8,128)(2,1)} %get-tuple-element.1969), channel_id=1, source_target_pairs={{0,4},{2,6},{4,0},{6,2},{1,5},{3,7},{5,1},{7,3},{8,12},{10,14},{12... | collective-permute-start | bytes 393224 | tf_op jit(solution)/shard_map/ppermute | solution.py:781
  588.6 25.4 %collective-permute-start.87 = (bf16[64,1024]{1,0:T(8,128)(2,1)}, bf16[64,1024]{1,0:T(8,128)(2,1)S(1)}, u32[]{:S(2)}, u32[]{:S(2)}) collective-permute-start(bf16[64,1024]{1,0:T(8,128)(2,1)} %get-tuple-element.1970), channel_id=1, source_target_pairs={{0,6},{2,4},{4,2},{6,0},{1,7},{3,5},{5,3},{7,1},{8,14},{10,12},{12... | collective-permute-start | bytes 393224 | tf_op jit(solution)/shard_map/ppermute | solution.py:781
  (113 other events, 1770.5 us)

commit v6 on v5

--- a/solution.py
+++ b/solution.py
@@ -420,12 +420,7 @@
         fetch(step, slot)
         for d in range(n):
             weight_copy(d).start()
-        for d in range(n):
-            weight_copy(d).wait()
-        if added:
-            for d in range(n):
-                added_copy(d).start()
-
+        acc_ref[...] = jnp.zeros_like(acc_ref)
     @pl.when(step + 1 < steps)
     def _():
         fetch(step + 1, 1 - slot)
@@ -439,6 +434,15 @@
     named = dybuf[slot, :, width:].astype(F32) > 0.5
     gates = masked_softmax(dot(x, router_ref[...], 1, 0), named)
     gates = pltpu.roll(gates, 128 - base, 1)
+
+    @pl.when(step == 0)
+    def _():
+        for d in range(n):
+            weight_copy(d).wait()
+        if added:
+            for d in range(n):
+                added_copy(d).start()
+
     w_in = w_ref[..., :both].reshape(width, both)
     w_back = w_ref[..., both:].reshape(width, both // 2)
     gu = dot(x, w_in, 1, 0)
@@ -481,10 +485,6 @@
         outs[part][0] = o.astype(BF)
         outs[2 + part][0, :, :width] = d.astype(BF)
         outs[2 + part][0, :, width:] = t.astype(BF)
-
-    @pl.when(step == 0)
-    def _():
-        acc_ref[...] = jnp.zeros_like(acc_ref)
 
     acc_ref[:, :both] += dot(x.T, dgu, 1, 0)
     acc_ref[:, both:] += dot(dy.T, gact, 1, 0)

time: 636 us -> 647 us (1.017)
  Pallas kernels: 207 us -> 221 us
    pallas_call x4, Pallas kernels: 123 us -> 138 us  [experts_call(): pl.pallas_call(functools.partial(experts_kernel, steps, first, count, mic...]
  transfers between devices with their start and end apart: 96 -> 96, of which waited for: 39 -> 38; matrix products, arithmetic and copies ran while one was open for 13% -> 13% of each run, Pallas kernels for 31% -> 32%
where the time goes in v6:
time: 647 us; the launch traced here: 637 us
  Pallas kernels  221 us (34%)
  waiting for transfers between devices  187 us (29%)
  starting transfers between devices  116 us (18%)
  other arithmetic  68.3 us (11%)
  local copies, waits for them, and re-layouts  31.2 us (5%)
  matrix products  10.9 us (2%)
    pallas_call x4, Pallas kernels, experts_call(): pl.pallas_call(functools.partial(experts_kernel, steps, first, count, mic...  138 us
    ppermute x30, starting transfers between devices, exchange(): lax.ppermute(parts[s], axis, apart(count, s))  45.1 us
    ppermute x6, waiting for transfers between devices, dkv_send(): lax.ppermute(live['dkv'][m][d], 'ctx', [(c, c - d) for c in range(d, n)])  39.1 us
    ppermute x30, waiting for transfers between devices, exchange(): lax.ppermute(parts[s], axis, apart(count, s))  30.1 us
    ppermute x6, waiting for transfers between devices, weight_send(): lax.ppermute(live['weights'][g][at], 'ctx', apart(n, hop))  26.1 us
    ppermute x6, waiting for transfers between devices, far_pieces(): return [lax.ppermute(mine, 'dp', apart(dp, s)) for s in steps]  24.3 us
    pallas_call x2, Pallas kernels, attn_bwd(): pl.pallas_call(functools.partial(attn_bwd_kernel, counts), grid=(seqs, pa...  21.1 us
    convert_element_type x10, other arithmetic, add(): return functools.reduce(jnp.add, [t.astype(F32) for t in terms]).astype(BF)  21.1 us
  transfers between devices with their start and end apart: 96, of which 38 were waited for; matrix products, arithmetic and copies ran while one was open for 13% of the time, Pallas kernels for 32%

profile of v6, /device:TPU:0, one launch (start us, length us, event | category | flops | bytes accessed | tf_op | source)
XLA Modules:
  0.0 637.1 jit_solution(11897051041879879349)
XLA Ops:
  3.1 5.1 collective-permute-start.5
  14.9 7.9 %collective-permute-done.1 = bf16[64,640]{1,0:T(8,128)(2,1)S(1)} collective-permute-done((bf16[64,640]{1,0:T(8,128)(2,1)S(1)}, bf16[64,640]{1,0:T(8,128)(2,1)S(1)}, u32[]{:S(2)}, u32[]{:S(2)}) %collective-permute-start.1) | collective-permute-done | bytes 81952 | tf_op jit(solution)/shard_map/ppermute | solution.py:850
  22.8 2.7 collective-permute-start.2
  25.5 3.5 collective-permute-done.2
  35.7 5.1 collective-permute-done.8
  40.9 4.1 collective-permute-done.7
  46.9 5.7 kv.1
  61.3 6.7 %convert_reduce_fusion = bf16[1024,128]{1,0:T(8,128)(2,1)S(1)} fusion(s32[1024,8]{1,0:T(8,128)} %copy.128), kind=kLoop, calls=%fused_computation.14 | loop fusion | flops 3014656 | bytes 294912 | tf_op jit(solution)/shard_map/reduce_sum | solution.py:934
  70.9 10.1 %collective-permute-done.11 = bf16[4,64,1024]{2,1,0:T(8,128)(2,1)} collective-permute-done((bf16[4,64,1024]{2,1,0:T(8,128)(2,1)S(1)}, bf16[4,64,1024]{2,1,0:T(8,128)(2,1)}, u32[]{:S(2)}, u32[]{:S(2)}) %collective-permute-start.11) | collective-permute-done | bytes 524320 | tf_op jit(solution)/shard_map/ppermute | solution.py:854
  89.2 5.7 q.1
  94.9 8.2 %attn_fwd.3 = (f32[2,2,4,1024]{3,2,1,0:T(4,128)}, f32[2,2,2,128,1024]{4,3,2,1,0:T(8,128)}) custom-call(s32[1]{0:T(128)} %bitcast.ctx_ref.place_ref, bf16[2,512,512]{2,1,0:T(8,128)(2,1)} %bitcast.244, bf16[1,2,512,512]{3,2,1,0:T(8,128)(2,1)} %bitcast.280, bf16[1,2,512,512]{3,2,1,0:T(8,128)(2,1)} %collective-permute-done.9.refs_1_.refs_3_.refs_5_, ...), custom_call_target="tpu_custom_call" | custom-call | flops 8589934592 | bytes 4194304 | tf_op jit(solution)/shard_map/attn_fwd/pallas_call | solution.py:245
  103.0 6.1 collective-permute-done.14.refs_12_
  116.9 5.5 attn_fwd.4
  125.9 7.0 %collective-permute-done.17 = bf16[2,64,1536]{2,1,0:T(8,128)(2,1)S(1)} collective-permute-done((bf16[2,64,1536]{2,1,0:T(8,128)(2,1)S(1)}, bf16[2,64,1536]{2,1,0:T(8,128)(2,1)S(1)}, u32[]{:S(2)}, u32[]{:S(2)}) %collective-permute-start.17) | collective-permute-done | bytes 393248 | tf_op jit(solution)/shard_map/ppermute | solution.py:781
  135.6 5.0 attn_fwd.5
  140.7 2.7 convolution_convert_fusion
  143.5 5.3 collective-permute-start.25
  148.8 6.9 %collective-permute-start.24 = (bf16[4,64,1536]{2,1,0:T(8,128)(2,1)S(1)}, bf16[4,64,1536]{2,1,0:T(8,128)(2,1)S(1)}, u32[]{:S(2)}, u32[]{:S(2)}) collective-permute-start(bf16[4,64,1536]{2,1,0:T(8,128)(2,1)S(1)} %copy-done.29), channel_id=1, source_target_pairs={{0,2},{2,0},{4,6},{6,4},{1,3},{3,1},{5,7},{7,5},{8,10},{10,8},{12,... | collective-permute-start | bytes 2359304 | tf_op jit(solution)/shard_map/ppermute | solution.py:887
  164.7 19.1 %collective-permute-done.25.refs_18_ = bf16[4,64,1536]{2,1,0:T(8,128)(2,1)S(1)} collective-permute-done((bf16[4,64,1536]{2,1,0:T(8,128)(2,1)S(1)}, bf16[4,64,1536]{2,1,0:T(8,128)(2,1)S(1)}, u32[]{:S(2)}, u32[]{:S(2)}) %collective-permute-start.25) | collective-permute-done | bytes 786464 | tf_op jit(solution)/shard_map/ppermute | solution.py:887
  185.6 10.2 %collective-permute-done.27.refs_4_ = bf16[256,1024]{1,0:T(8,128)(2,1)} collective-permute-done((bf16[256,1024]{1,0:T(8,128)(2,1)S(1)}, bf16[256,1024]{1,0:T(8,128)(2,1)}, u32[]{:S(2)}, u32[]{:S(2)}) %collective-permute-start.27) | collective-permute-done | bytes 524320 | tf_op jit(solution)/shard_map/ppermute | solution.py:843
  198.2 13.5 %collective-permute-done.30.refs_6_ = bf16[256,1024]{1,0:T(8,128)(2,1)} collective-permute-done((bf16[256,1024]{1,0:T(8,128)(2,1)S(1)}, bf16[256,1024]{1,0:T(8,128)(2,1)}, u32[]{:S(2)}, u32[]{:S(2)}) %collective-permute-start.30) | collective-permute-done | bytes 524320 | tf_op jit(solution)/shard_map/ppermute | solution.py:843
  211.7 4.6 collective-permute-done.29.refs_19_
  225.4 33.6 %experts.4 = (bf16[4,256,1024]{2,1,0:T(8,128)(2,1)}, bf16[4,256,1024]{2,1,0:T(8,128)(2,1)}, bf16[4,256,1152]{2,1,0:T(8,128)(2,1)}, bf16[4,256,1152]{2,1,0:T(8,12...) custom-call(s32[2]{0:T(128)} %pad_add_fusion.place_ref, ...), custom_call_target="tpu_custom_call" | custom-call | flops 19327352832 | bytes 23068672 | tf_op jit(solution)/shard_map/experts/pallas_call | solution.py:527
  266.7 34.2 %experts.5 = (bf16[4,256,1024]{2,1,0:T(8,128)(2,1)}, bf16[4,256,1024]{2,1,0:T(8,128)(2,1)}, bf16[4,256,1152]{2,1,0:T(8,128)(2,1)}, bf16[4,256,1152]{2,1,0:T(8,12...) custom-call(s32[2]{0:T(128)} %pad_add_fusion.place_ref, ...), custom_call_target="tpu_custom_call" | custom-call | flops 19327352832 | bytes 23068672 | tf_op jit(solution)/shard_map/experts/pallas_call | solution.py:527
  303.5 34.6 %experts.6 = (bf16[4,256,1024]{2,1,0:T(8,128)(2,1)}, bf16[4,256,1024]{2,1,0:T(8,128)(2,1)}, bf16[4,256,1152]{2,1,0:T(8,128)(2,1)}, bf16[4,256,1152]{2,1,0:T(8,12...) custom-call(s32[2]{0:T(128)} %pad_add_fusion.place_ref, ...), custom_call_target="tpu_custom_call" | custom-call | flops 19327352832 | bytes 23068672 | tf_op jit(solution)/shard_map/experts/pallas_call | solution.py:527
  340.0 4.7 collective-permute-done.45
  344.7 3.2 fusion.26
  353.1 35.2 %experts.7 = (bf16[4,256,1024]{2,1,0:T(8,128)(2,1)}, bf16[4,256,1024]{2,1,0:T(8,128)(2,1)}, bf16[4,256,1152]{2,1,0:T(8,128)(2,1)}, bf16[4,256,1152]{2,1,0:T(8,12...) custom-call(s32[2]{0:T(128)} %pad_add_fusion.place_ref, ...), custom_call_target="tpu_custom_call" | custom-call | flops 19327352832 | bytes 23068672 | tf_op jit(solution)/shard_map/experts/pallas_call | solution.py:527
  390.8 2.8 collective-permute-start.57
  414.0 10.9 %attn_bwd.2 = (bf16[1,512,512]{2,1,0:T(8,128)(2,1)}, bf16[1,1,512,512]{3,2,1,0:T(8,128)(2,1)}, bf16[1,1,512,512]{3,2,1,0:T(8,128)(2,1)}, bf16[1,1,512,512]{3,2,1,0:T(8,128)(2,1)}, bf16[1,1,512,512]{3,2,1,0:T(8,128)(2,1)}) custom-call(s32[1]{0:T(128)} %bitcast.ctx_ref.place_ref, bf16[2,512,512]{2,1,0:T(8,128)(2,1)} %bitcast.247, ...), custom_call_target="tpu_custom_call" | custom-call | flops 21474836480 | bytes 8388608 | tf_op jit(solution)/shard_map/attn_bwd/pallas_call | solution.py:335
  424.9 2.7 collective-permute-done.56
  428.9 11.0 %collective-permute-done.54 = bf16[256,1152]{1,0:T(8,128)(2,1)} collective-permute-done((bf16[256,1152]{1,0:T(8,128)(2,1)}, bf16[256,1152]{1,0:T(8,128)(2,1)}, u32[]{:S(2)}, u32[]{:S(2)}) %collective-permute-start.54) | collective-permute-done | bytes 589856 | tf_op jit(solution)/shard_map/ppermute | solution.py:781
  459.5 10.3 %collective-permute-done.60 = bf16[1,1,512,512]{3,2,1,0:T(8,128)(2,1)} collective-permute-done((bf16[1,1,512,512]{3,2,1,0:T(8,128)(2,1)}, bf16[1,1,512,512]{3,2,1,0:T(8,128)(2,1)}, u32[]{:S(2)}, u32[]{:S(2)}) %collective-permute-start.60) | collective-permute-done | bytes 524320 | tf_op jit(solution)/shard_map/ppermute | solution.py:1167
  475.5 10.1 %attn_bwd.3 = (bf16[1,512,512]{2,1,0:T(8,128)(2,1)}, bf16[1,1,512,512]{3,2,1,0:T(8,128)(2,1)}, bf16[1,1,512,512]{3,2,1,0:T(8,128)(2,1)}, bf16[1,1,512,512]{3,2,1,0:T(8,128)(2,1)}, bf16[1,1,512,512]{3,2,1,0:T(8,128)(2,1)}) custom-call(s32[1]{0:T(128)} %bitcast.ctx_ref.place_ref, bf16[2,512,512]{2,1,0:T(8,128)(2,1)} %bitcast.248, ...), custom_call_target="tpu_custom_call" | custom-call | flops 21474836480 | bytes 8388608 | tf_op jit(solution)/shard_map/attn_bwd/pallas_call | solution.py:335
  485.6 9.1 %collective-permute-done.62 = bf16[1,1,512,512]{3,2,1,0:T(8,128)(2,1)S(1)} collective-permute-done((bf16[1,1,512,512]{3,2,1,0:T(8,128)(2,1)}, bf16[1,1,512,512]{3,2,1,0:T(8,128)(2,1)S(1)}, u32[]{:S(2)}, u32[]{:S(2)}) %collective-permute-start.62) | collective-permute-done | bytes 524320 | tf_op jit(solution)/shard_map/ppermute | solution.py:1167
  494.7 3.6 collective-permute-done.67
  509.1 6.7 %grads.2 = (bf16[256,1024]{1,0:T(8,128)(2,1)}, bf16[256,1024]{1,0:T(8,128)(2,1)}, bf16[256,1024]{1,0:T(8,128)(2,1)}, bf16[256,1024]{1,0:T(8,128)(2,1)}) custom-call(s32[1]{0:T(128)} %bitcast.80.place_ref, bf16[1024,1024]{1,0:T(8,128)(2,1)} %get-tuple-element.1918.normed_ref.refs_0_.refs_2_, bf16[512,512]{1,0:T(8,128)(2,1)} %bitcast.234, ...), custom_call_target="tpu_custom_call" | custom-call | flops 2147483648 | bytes 4194304 | tf_op jit(solution)/shard_map/grads/pallas_call | solution.py:649
  520.8 5.1 back.2
  528.4 19.6 %collective-permute-done.73 = bf16[1,1,512,512]{3,2,1,0:T(8,128)(2,1)} collective-permute-done((bf16[1,1,512,512]{3,2,1,0:T(8,128)(2,1)}, bf16[1,1,512,512]{3,2,1,0:T(8,128)(2,1)}, u32[]{:S(2)}, u32[]{:S(2)}) %collective-permute-start.73) | collective-permute-done | bytes 524320 | tf_op jit(solution)/shard_map/ppermute | solution.py:1167
  552.9 10.3 %collective-permute-done.76.refs_2_ = bf16[256,1024]{1,0:T(8,128)(2,1)} collective-permute-done((bf16[256,1024]{1,0:T(8,128)(2,1)}, bf16[256,1024]{1,0:T(8,128)(2,1)}, u32[]{:S(2)}, u32[]{:S(2)}) %collective-permute-start.76) | collective-permute-done | bytes 524320 | tf_op jit(solution)/shard_map/ppermute | solution.py:1197
  564.0 5.1 back.3
  571.1 5.0 grads.3
  586.4 2.8 line.2
  589.2 5.0 fusion.6
  595.5 3.1 collective-permute-start.86
  601.4 11.1 %collective-permute-start.89 = (bf16[64,640]{1,0:T(8,128)(2,1)}, bf16[64,640]{1,0:T(8,128)(2,1)S(1)}, u32[]{:S(2)}, u32[]{:S(2)}) collective-permute-start(bf16[64,640]{1,0:T(8,128)(2,1)} %get-tuple-element.1977), channel_id=1, source_target_pairs={{0,4},{2,6},{4,0},{6,2},{1,5},{3,7},{5,1},{7,3},{8,12},{10,14},{12... | collective-permute-start | bytes 245768 | tf_op jit(solution)/shard_map/ppermute | solution.py:781
  616.6 4.8 collective-permute-done.89.refs_6_
  633.4 3.3 expert_rows.1
  (409 shorter events, 196.2 us)
Async XLA Ops:
  3.1 26.0 %collective-permute-start.5 = (bf16[64,1024]{1,0:T(8,128)(2,1)S(1)}, bf16[64,1024]{1,0:T(8,128)(2,1)S(1)}, u32[]{:S(2)}, u32[]{:S(2)}) collective-permute-start(bf16[64,1024]{1,0:T(8,128)(2,1)S(1)} %constant_dynamic-update-slice_fusion), channel_id=1, source_target_pairs={{0,6},{2,4},{4,2},{6,0},{1,7},{3,5},{5,3},{7,1},{8,14},{10,12},{12... | collective-permute-start | bytes 393224 | tf_op jit(solution)/shard_map/ppermute | solution.py:850
  8.2 20.9 %collective-permute-start.4 = (bf16[64,1024]{1,0:T(8,128)(2,1)S(1)}, bf16[64,1024]{1,0:T(8,128)(2,1)S(1)}, u32[]{:S(2)}, u32[]{:S(2)}) collective-permute-start(bf16[64,1024]{1,0:T(8,128)(2,1)S(1)} %constant_dynamic-update-slice_fusion), channel_id=1, source_target_pairs={{0,4},{2,6},{4,0},{6,2},{1,5},{3,7},{5,1},{7,3},{8,12},{10,14},{12... | collective-permute-start | bytes 393224 | tf_op jit(solution)/shard_map/ppermute | solution.py:850
  8.2 20.9 %collective-permute-start.3 = (bf16[64,1024]{1,0:T(8,128)(2,1)S(1)}, bf16[64,1024]{1,0:T(8,128)(2,1)S(1)}, u32[]{:S(2)}, u32[]{:S(2)}) collective-permute-start(bf16[64,1024]{1,0:T(8,128)(2,1)S(1)} %constant_dynamic-update-slice_fusion), channel_id=1, source_target_pairs={{0,2},{2,0},{4,6},{6,4},{1,3},{3,1},{5,7},{7,5},{8,10},{10,8},{12,... | collective-permute-start | bytes 393224 | tf_op jit(solution)/shard_map/ppermute | solution.py:850
  52.6 28.5 %collective-permute-start.9 = (bf16[1,2,512,512]{3,2,1,0:T(8,128)(2,1)}, bf16[1,2,512,512]{3,2,1,0:T(8,128)(2,1)}, u32[]{:S(2)}, u32[]{:S(2)}) collective-permute-start(bf16[1,2,512,512]{3,2,1,0:T(8,128)(2,1)} %bitcast.279), channel_id=1, source_target_pairs={{0,2},{2,4},{4,6},{1,3},{3,5},{5,7},{8,10},{10,12},{12,14},{9,11},... | collective-permute-start | bytes 3145736 | tf_op jit(solution)/shard_map/ppermute | solution.py:762
  56.7 24.3 %collective-permute-start.11 = (bf16[4,64,1024]{2,1,0:T(8,128)(2,1)S(1)}, bf16[4,64,1024]{2,1,0:T(8,128)(2,1)}, u32[]{:S(2)}, u32[]{:S(2)}) collective-permute-start(bf16[4,64,1024]{2,1,0:T(8,128)(2,1)S(1)} %pad_maximum_fusion.8), channel_id=1, source_target_pairs={{0,16},{8,24},{16,0},{24,8},{1,17},{9,25},{17,1},{25,9},{2,18},{10... | collective-permute-start | bytes 1572872 | tf_op jit(solution)/shard_map/ppermute | solution.py:854
  58.0 23.1 %collective-permute-start.10 = (bf16[4,64,1024]{2,1,0:T(8,128)(2,1)S(1)}, bf16[4,64,1024]{2,1,0:T(8,128)(2,1)}, u32[]{:S(2)}, u32[]{:S(2)}) collective-permute-start(bf16[4,64,1024]{2,1,0:T(8,128)(2,1)S(1)} %pad_maximum_fusion.8), channel_id=1, source_target_pairs={{0,8},{8,0},{16,24},{24,16},{1,9},{9,1},{17,25},{25,17},{2,10},{10... | collective-permute-start | bytes 1572872 | tf_op jit(solution)/shard_map/ppermute | solution.py:854
  81.1 28.0 %collective-permute-start.14 = (bf16[2,256,1152]{2,1,0:T(8,128)(2,1)}, bf16[2,256,1152]{2,1,0:T(8,128)(2,1)}, u32[]{:S(2)}, u32[]{:S(2)}) collective-permute-start(bf16[2,256,1152]{2,1,0:T(8,128)(2,1)} %get-tuple-element.1566.refs_8_), channel_id=1, source_target_pairs={{0,16},{8,24},{16,0},{24,8},{1,17},{9,25},{17,1},{25,9},{2,18},{10... | collective-permute-start | bytes 3538952 | tf_op jit(solution)/shard_map/ppermute | solution.py:983
  82.5 27.9 %collective-permute-start.13 = (bf16[2,256,1152]{2,1,0:T(8,128)(2,1)}, bf16[2,256,1152]{2,1,0:T(8,128)(2,1)}, u32[]{:S(2)}, u32[]{:S(2)}) collective-permute-start(bf16[2,256,1152]{2,1,0:T(8,128)(2,1)} %get-tuple-element.1566.refs_8_), channel_id=1, source_target_pairs={{0,8},{8,0},{16,24},{24,16},{1,9},{9,1},{17,25},{25,17},{2,10},{10... | collective-permute-start | bytes 3538952 | tf_op jit(solution)/shard_map/ppermute | solution.py:983
  110.5 24.6 %collective-permute-start.16 = (bf16[1,2,512,512]{3,2,1,0:T(8,128)(2,1)}, bf16[1,2,512,512]{3,2,1,0:T(8,128)(2,1)}, u32[]{:S(2)}, u32[]{:S(2)}) collective-permute-start(bf16[1,2,512,512]{3,2,1,0:T(8,128)(2,1)} %collective-permute-done.15.refs_0_.refs_1_.refs_2_.refs_6_), channel_id=1, source_target_pairs={{4,6},{5,7},{12,14},{13,15},{20,22},{21,23},{28,30},{29,31}} | collective-permute-start | bytes 3145736 | tf_op jit(solution)/shard_map/ppermute | solution.py:762
  143.5 40.4 %collective-permute-start.25 = (bf16[4,64,1536]{2,1,0:T(8,128)(2,1)S(1)}, bf16[4,64,1536]{2,1,0:T(8,128)(2,1)S(1)}, u32[]{:S(2)}, u32[]{:S(2)}) collective-permute-start(bf16[4,64,1536]{2,1,0:T(8,128)(2,1)S(1)} %copy-done.29), channel_id=1, source_target_pairs={{0,4},{2,6},{4,0},{6,2},{1,5},{3,7},{5,1},{7,3},{8,12},{10,14},{12... | collective-permute-start | bytes 2359304 | tf_op jit(solution)/shard_map/ppermute | solution.py:887
  148.8 35.2 %collective-permute-start.24 = (bf16[4,64,1536]{2,1,0:T(8,128)(2,1)S(1)}, bf16[4,64,1536]{2,1,0:T(8,128)(2,1)S(1)}, u32[]{:S(2)}, u32[]{:S(2)}) collective-permute-start(bf16[4,64,1536]{2,1,0:T(8,128)(2,1)S(1)} %copy-done.29), channel_id=1, source_target_pairs={{0,2},{2,0},{4,6},{6,4},{1,3},{3,1},{5,7},{7,5},{8,10},{10,8},{12,... | collective-permute-start | bytes 2359304 | tf_op jit(solution)/shard_map/ppermute | solution.py:887
  155.6 30.0 %collective-permute-start.23 = (bf16[2,256,1152]{2,1,0:T(8,128)(2,1)}, bf16[2,256,1152]{2,1,0:T(8,128)(2,1)S(1)}, u32[]{:S(2)}, u32[]{:S(2)}) collective-permute-start(bf16[2,256,1152]{2,1,0:T(8,128)(2,1)} %get-tuple-element.1566.refs_8_), channel_id=1, source_target_pairs={{0,24},{8,16},{16,8},{24,0},{1,25},{9,17},{17,9},{25,1},{2,26},{10... | collective-permute-start | bytes 3538952 | tf_op jit(solution)/shard_map/ppermute | solution.py:983
  162.8 33.1 %collective-permute-start.27 = (bf16[256,1024]{1,0:T(8,128)(2,1)S(1)}, bf16[256,1024]{1,0:T(8,128)(2,1)}, u32[]{:S(2)}, u32[]{:S(2)}) collective-permute-start(bf16[256,1024]{1,0:T(8,128)(2,1)S(1)} %get-tuple-element.1432.refs_0_), channel_id=1, source_target_pairs={{0,16},{8,24},{16,0},{24,8},{1,17},{9,25},{17,1},{25,9},{2,18},{10... | collective-permute-start | bytes 1572872 | tf_op jit(solution)/shard_map/ppermute | solution.py:843
  164.7 31.7 %collective-permute-start.26 = (bf16[256,1024]{1,0:T(8,128)(2,1)S(1)}, bf16[256,1024]{1,0:T(8,128)(2,1)}, u32[]{:S(2)}, u32[]{:S(2)}) collective-permute-start(bf16[256,1024]{1,0:T(8,128)(2,1)S(1)} %get-tuple-element.1432.refs_0_), channel_id=1, source_target_pairs={{0,8},{8,0},{16,24},{24,16},{1,9},{9,1},{17,25},{25,17},{2,10},{10... | collective-permute-start | bytes 1572872 | tf_op jit(solution)/shard_map/ppermute | solution.py:843
  221.3 37.7 %collective-permute-start.38 = (bf16[256,1024]{1,0:T(8,128)(2,1)S(1)}, bf16[256,1024]{1,0:T(8,128)(2,1)S(1)}, u32[]{:S(2)}, u32[]{:S(2)}) collective-permute-start(bf16[256,1024]{1,0:T(8,128)(2,1)S(1)} %get-tuple-element.1558.refs_0_), channel_id=1, source_target_pairs={{0,24},{8,16},{16,8},{24,0},{1,25},{9,17},{17,9},{25,1},{2,26},{10... | collective-permute-start | bytes 1572872 | tf_op jit(solution)/shard_map/ppermute | solution.py:843
  222.9 36.2 %collective-permute-start.37 = (bf16[256,1024]{1,0:T(8,128)(2,1)S(1)}, bf16[256,1024]{1,0:T(8,128)(2,1)}, u32[]{:S(2)}, u32[]{:S(2)}) collective-permute-start(bf16[256,1024]{1,0:T(8,128)(2,1)S(1)} %get-tuple-element.1558.refs_0_), channel_id=1, source_target_pairs={{0,16},{8,24},{16,0},{24,8},{1,17},{9,25},{17,1},{25,9},{2,18},{10... | collective-permute-start | bytes 1572872 | tf_op jit(solution)/shard_map/ppermute | solution.py:843
  224.3 34.8 %collective-permute-start.36 = (bf16[256,1024]{1,0:T(8,128)(2,1)S(1)}, bf16[256,1024]{1,0:T(8,128)(2,1)}, u32[]{:S(2)}, u32[]{:S(2)}) collective-permute-start(bf16[256,1024]{1,0:T(8,128)(2,1)S(1)} %get-tuple-element.1558.refs_0_), channel_id=1, source_target_pairs={{0,8},{8,0},{16,24},{24,16},{1,9},{9,1},{17,25},{25,17},{2,10},{10... | collective-permute-start | bytes 1572872 | tf_op jit(solution)/shard_map/ppermute | solution.py:843
  224.8 36.5 %collective-permute-start.35 = (bf16[4,64,1536]{2,1,0:T(8,128)(2,1)}, bf16[4,64,1536]{2,1,0:T(8,128)(2,1)}, u32[]{:S(2)}, u32[]{:S(2)}) collective-permute-start(bf16[4,64,1536]{2,1,0:T(8,128)(2,1)} %pad_maximum_fusion.7.refs_16_), channel_id=1, source_target_pairs={{0,4},{2,6},{4,0},{6,2},{1,5},{3,7},{5,1},{7,3},{8,12},{10,14},{12... | collective-permute-start | bytes 2359304 | tf_op jit(solution)/shard_map/ppermute | solution.py:887
  225.1 36.3 %collective-permute-start.34 = (bf16[4,64,1536]{2,1,0:T(8,128)(2,1)}, bf16[4,64,1536]{2,1,0:T(8,128)(2,1)}, u32[]{:S(2)}, u32[]{:S(2)}) collective-permute-start(bf16[4,64,1536]{2,1,0:T(8,128)(2,1)} %pad_maximum_fusion.7.refs_16_), channel_id=1, source_target_pairs={{0,2},{2,0},{4,6},{6,4},{1,3},{3,1},{5,7},{7,5},{8,10},{10,8},{12,... | collective-permute-start | bytes 2359304 | tf_op jit(solution)/shard_map/ppermute | solution.py:887
  266.6 34.2 %collective-permute-start.42 = (bf16[4,64,1536]{2,1,0:T(8,128)(2,1)}, bf16[4,64,1536]{2,1,0:T(8,128)(2,1)}, u32[]{:S(2)}, u32[]{:S(2)}) collective-permute-start(bf16[4,64,1536]{2,1,0:T(8,128)(2,1)} %collective-permute-done.35.refs_18_), channel_id=1, source_target_pairs={{0,2},{2,0},{4,6},{6,4},{1,3},{3,1},{5,7},{7,5},{8,10},{10,8},{12,... | collective-permute-start | bytes 2359304 | tf_op jit(solution)/shard_map/ppermute | solution.py:887
  300.8 37.2 %collective-permute-start.43 = (bf16[4,64,1536]{2,1,0:T(8,128)(2,1)}, bf16[4,64,1536]{2,1,0:T(8,128)(2,1)}, u32[]{:S(2)}, u32[]{:S(2)}) collective-permute-start(bf16[4,64,1536]{2,1,0:T(8,128)(2,1)} %get-tuple-element.1428), channel_id=1, source_target_pairs={{0,2},{2,0},{4,6},{6,4},{1,3},{3,1},{5,7},{7,5},{8,10},{10,8},{12,... | collective-permute-start | bytes 2359304 | tf_op jit(solution)/shard_map/ppermute | solution.py:1079
  302.9 37.1 %collective-permute-start.44 = (bf16[4,64,1536]{2,1,0:T(8,128)(2,1)}, bf16[4,64,1536]{2,1,0:T(8,128)(2,1)}, u32[]{:S(2)}, u32[]{:S(2)}) collective-permute-start(bf16[4,64,1536]{2,1,0:T(8,128)(2,1)} %get-tuple-element.1429), channel_id=1, source_target_pairs={{0,4},{2,6},{4,0},{6,2},{1,5},{3,7},{5,1},{7,3},{8,12},{10,14},{12... | collective-permute-start | bytes 2359304 | tf_op jit(solution)/shard_map/ppermute | solution.py:1079
  348.0 40.3 %collective-permute-start.46 = (bf16[256,1152]{1,0:T(8,128)(2,1)}, bf16[256,1152]{1,0:T(8,128)(2,1)}, u32[]{:S(2)}, u32[]{:S(2)}) collective-permute-start(bf16[256,1152]{1,0:T(8,128)(2,1)} %get-tuple-element.1591), channel_id=1, source_target_pairs={{0,8},{8,0},{16,24},{24,16},{1,9},{9,1},{17,25},{25,17},{2,10},{10... | collective-permute-start | bytes 1769480 | tf_op jit(solution)/shard_map/ppermute | solution.py:781
  349.5 38.8 %collective-permute-start.47 = (bf16[256,1152]{1,0:T(8,128)(2,1)}, bf16[256,1152]{1,0:T(8,128)(2,1)}, u32[]{:S(2)}, u32[]{:S(2)}) collective-permute-start(bf16[256,1152]{1,0:T(8,128)(2,1)} %get-tuple-element.1592), channel_id=1, source_target_pairs={{0,16},{8,24},{16,0},{24,8},{1,17},{9,25},{17,1},{25,9},{2,18},{10... | collective-permute-start | bytes 1769480 | tf_op jit(solution)/shard_map/ppermute | solution.py:781
  350.1 38.2 %collective-permute-start.48 = (bf16[256,1152]{1,0:T(8,128)(2,1)}, bf16[256,1152]{1,0:T(8,128)(2,1)}, u32[]{:S(2)}, u32[]{:S(2)}) collective-permute-start(bf16[256,1152]{1,0:T(8,128)(2,1)} %get-tuple-element.1593), channel_id=1, source_target_pairs={{0,24},{8,16},{16,8},{24,0},{1,25},{9,17},{17,9},{25,1},{2,26},{10... | collective-permute-start | bytes 1769480 | tf_op jit(solution)/shard_map/ppermute | solution.py:781
  351.5 36.8 %collective-permute-start.49 = (bf16[4,64,1536]{2,1,0:T(8,128)(2,1)}, bf16[4,64,1536]{2,1,0:T(8,128)(2,1)}, u32[]{:S(2)}, u32[]{:S(2)}) collective-permute-start(bf16[4,64,1536]{2,1,0:T(8,128)(2,1)} %get-tuple-element.1556), channel_id=1, source_target_pairs={{0,6},{2,4},{4,2},{6,0},{1,7},{3,5},{5,3},{7,1},{8,14},{10,12},{12... | collective-permute-start | bytes 2359304 | tf_op jit(solution)/shard_map/ppermute | solution.py:1079
  390.8 36.8 %collective-permute-start.56 = (bf16[4,64,1536]{2,1,0:T(8,128)(2,1)}, bf16[4,64,1536]{2,1,0:T(8,128)(2,1)}, u32[]{:S(2)}, u32[]{:S(2)}) collective-permute-start(bf16[4,64,1536]{2,1,0:T(8,128)(2,1)} %get-tuple-element.1637), channel_id=1, source_target_pairs={{0,2},{2,0},{4,6},{6,4},{1,3},{3,1},{5,7},{7,5},{8,10},{10,8},{12,... | collective-permute-start | bytes 2359304 | tf_op jit(solution)/shard_map/ppermute | solution.py:1079
  390.8 38.1 %collective-permute-start.57 = (bf16[4,64,1536]{2,1,0:T(8,128)(2,1)}, bf16[4,64,1536]{2,1,0:T(8,128)(2,1)}, u32[]{:S(2)}, u32[]{:S(2)}) collective-permute-start(bf16[4,64,1536]{2,1,0:T(8,128)(2,1)} %get-tuple-element.1638), channel_id=1, source_target_pairs={{0,4},{2,6},{4,0},{6,2},{1,5},{3,7},{5,1},{7,3},{8,12},{10,14},{12... | collective-permute-start | bytes 2359304 | tf_op jit(solution)/shard_map/ppermute | solution.py:1079
  412.0 27.9 %collective-permute-start.54 = (bf16[256,1152]{1,0:T(8,128)(2,1)}, bf16[256,1152]{1,0:T(8,128)(2,1)}, u32[]{:S(2)}, u32[]{:S(2)}) collective-permute-start(bf16[256,1152]{1,0:T(8,128)(2,1)} %get-tuple-element.1681), channel_id=1, source_target_pairs={{0,16},{8,24},{16,0},{24,8},{1,17},{9,25},{17,1},{25,9},{2,18},{10... | collective-permute-start | bytes 1769480 | tf_op jit(solution)/shard_map/ppermute | solution.py:781
  412.6 27.3 %collective-permute-start.55 = (bf16[256,1152]{1,0:T(8,128)(2,1)}, bf16[256,1152]{1,0:T(8,128)(2,1)}, u32[]{:S(2)}, u32[]{:S(2)}) collective-permute-start(bf16[256,1152]{1,0:T(8,128)(2,1)} %get-tuple-element.1682), channel_id=1, source_target_pairs={{0,24},{8,16},{16,8},{24,0},{1,25},{9,17},{17,9},{25,1},{2,26},{10... | collective-permute-start | bytes 1769480 | tf_op jit(solution)/shard_map/ppermute | solution.py:781
  443.3 26.4 %collective-permute-start.60 = (bf16[1,1,512,512]{3,2,1,0:T(8,128)(2,1)}, bf16[1,1,512,512]{3,2,1,0:T(8,128)(2,1)}, u32[]{:S(2)}, u32[]{:S(2)}) collective-permute-start(bf16[1,1,512,512]{3,2,1,0:T(8,128)(2,1)} %get-tuple-element.1725), channel_id=1, source_target_pairs={{6,0},{7,1},{14,8},{15,9},{22,16},{23,17},{30,24},{31,25}} | collective-permute-start | bytes 1572872 | tf_op jit(solution)/shard_map/ppermute | solution.py:1167
  444.8 28.6 %collective-permute-start.63 = (bf16[256,1024]{1,0:T(8,128)(2,1)}, bf16[256,1024]{1,0:T(8,128)(2,1)}, u32[]{:S(2)}, u32[]{:S(2)}) collective-permute-start(bf16[256,1024]{1,0:T(8,128)(2,1)} %get-tuple-element.1741), channel_id=1, source_target_pairs={{0,8},{8,0},{16,24},{24,16},{1,9},{9,1},{17,25},{25,17},{2,10},{10... | collective-permute-start | bytes 1572872 | tf_op jit(solution)/shard_map/ppermute | solution.py:781
  445.4 28.6 %collective-permute-start.64 = (bf16[256,1024]{1,0:T(8,128)(2,1)}, bf16[256,1024]{1,0:T(8,128)(2,1)}, u32[]{:S(2)}, u32[]{:S(2)}) collective-permute-start(bf16[256,1024]{1,0:T(8,128)(2,1)} %get-tuple-element.1742), channel_id=1, source_target_pairs={{0,16},{8,24},{16,0},{24,8},{1,17},{9,25},{17,1},{25,9},{2,18},{10... | collective-permute-start | bytes 1572872 | tf_op jit(solution)/shard_map/ppermute | solution.py:781
  456.1 29.5 %collective-permute-start.65 = (bf16[256,1024]{1,0:T(8,128)(2,1)S(1)}, bf16[256,1024]{1,0:T(8,128)(2,1)}, u32[]{:S(2)}, u32[]{:S(2)}) collective-permute-start(bf16[256,1024]{1,0:T(8,128)(2,1)S(1)} %copy-done.32), channel_id=1, source_target_pairs={{0,24},{8,16},{16,8},{24,0},{1,25},{9,17},{17,9},{25,1},{2,26},{10... | collective-permute-start | bytes 1572872 | tf_op jit(solution)/shard_map/ppermute | solution.py:781
  470.6 24.1 %collective-permute-start.62 = (bf16[1,1,512,512]{3,2,1,0:T(8,128)(2,1)}, bf16[1,1,512,512]{3,2,1,0:T(8,128)(2,1)S(1)}, u32[]{:S(2)}, u32[]{:S(2)}) collective-permute-start(bf16[1,1,512,512]{3,2,1,0:T(8,128)(2,1)} %get-tuple-element.1761), channel_id=1, source_target_pairs={{4,0},{6,2},{5,1},{7,3},{12,8},{14,10},{13,9},{15,11},{20,16},{22,... | collective-permute-start | bytes 1572872 | tf_op jit(solution)/shard_map/ppermute | solution.py:1167
  471.9 22.8 %collective-permute-start.66 = (bf16[256,1024]{1,0:T(8,128)(2,1)}, bf16[256,1024]{1,0:T(8,128)(2,1)}, u32[]{:S(2)}, u32[]{:S(2)}) collective-permute-start(bf16[256,1024]{1,0:T(8,128)(2,1)} %get-tuple-element.1789), channel_id=1, source_target_pairs={{0,8},{8,0},{16,24},{24,16},{1,9},{9,1},{17,25},{25,17},{2,10},{10... | collective-permute-start | bytes 1572872 | tf_op jit(solution)/shard_map/ppermute | solution.py:781
  473.4 24.9 %collective-permute-start.67 = (bf16[256,1024]{1,0:T(8,128)(2,1)}, bf16[256,1024]{1,0:T(8,128)(2,1)}, u32[]{:S(2)}, u32[]{:S(2)}) collective-permute-start(bf16[256,1024]{1,0:T(8,128)(2,1)} %get-tuple-element.1790), channel_id=1, source_target_pairs={{0,16},{8,24},{16,0},{24,8},{1,17},{9,25},{17,1},{25,9},{2,18},{10... | collective-permute-start | bytes 1572872 | tf_op jit(solution)/shard_map/ppermute | solution.py:781
  474.0 24.3 %collective-permute-start.68 = (bf16[256,1024]{1,0:T(8,128)(2,1)}, bf16[256,1024]{1,0:T(8,128)(2,1)}, u32[]{:S(2)}, u32[]{:S(2)}) collective-permute-start(bf16[256,1024]{1,0:T(8,128)(2,1)} %get-tuple-element.1791), channel_id=1, source_target_pairs={{0,24},{8,16},{16,8},{24,0},{1,25},{9,17},{17,9},{25,1},{2,26},{10... | collective-permute-start | bytes 1572872 | tf_op jit(solution)/shard_map/ppermute | solution.py:781
  498.3 29.4 %collective-permute-start.72 = (bf16[1,1,512,512]{3,2,1,0:T(8,128)(2,1)}, bf16[1,1,512,512]{3,2,1,0:T(8,128)(2,1)}, u32[]{:S(2)}, u32[]{:S(2)}) collective-permute-start(bf16[1,1,512,512]{3,2,1,0:T(8,128)(2,1)} %get-tuple-element.1807), channel_id=1, source_target_pairs={{2,0},{4,2},{6,4},{3,1},{5,3},{7,5},{10,8},{12,10},{14,12},{11,9},... | collective-permute-start | bytes 1572872 | tf_op jit(solution)/shard_map/ppermute | solution.py:1167
  499.7 48.3 %collective-permute-start.73 = (bf16[1,1,512,512]{3,2,1,0:T(8,128)(2,1)}, bf16[1,1,512,512]{3,2,1,0:T(8,128)(2,1)}, u32[]{:S(2)}, u32[]{:S(2)}) collective-permute-start(bf16[1,1,512,512]{3,2,1,0:T(8,128)(2,1)} %get-tuple-element.1808), channel_id=1, source_target_pairs={{4,0},{6,2},{5,1},{7,3},{12,8},{14,10},{13,9},{15,11},{20,16},{22,... | collective-permute-start | bytes 1572872 | tf_op jit(solution)/shard_map/ppermute | solution.py:1167
  520.3 28.3 %collective-permute-start.79 = (bf16[256,1024]{1,0:T(8,128)(2,1)S(1)}, bf16[256,1024]{1,0:T(8,128)(2,1)S(1)}, u32[]{:S(2)}, u32[]{:S(2)}) collective-permute-start(bf16[256,1024]{1,0:T(8,128)(2,1)S(1)} %add_convert_fusion.15), channel_id=1, source_target_pairs={{0,1},{1,0},{2,3},{3,2},{4,5},{5,4},{6,7},{7,6},{8,9},{9,8},{10,11... | collective-permute-start | bytes 1572872 | tf_op jit(solution)/shard_map/ppermute | solution.py:758
  526.0 37.1 %collective-permute-start.78 = (bf16[512,1024]{1,0:T(8,128)(2,1)}, bf16[512,1024]{1,0:T(8,128)(2,1)}, u32[]{:S(2)}, u32[]{:S(2)}) collective-permute-start(bf16[512,1024]{1,0:T(8,128)(2,1)} %get-tuple-element.1950), channel_id=1, source_target_pairs={{0,1},{1,0},{2,3},{3,2},{4,5},{5,4},{6,7},{7,6},{8,9},{9,8},{10,11... | collective-permute-start | bytes 3145736 | tf_op jit(solution)/shard_map/ppermute | solution.py:758
  526.1 26.0 %collective-permute-start.74 = (bf16[1,1,512,512]{3,2,1,0:T(8,128)(2,1)}, bf16[1,1,512,512]{3,2,1,0:T(8,128)(2,1)S(1)}, u32[]{:S(2)}, u32[]{:S(2)}) collective-permute-start(bf16[1,1,512,512]{3,2,1,0:T(8,128)(2,1)} %get-tuple-element.1809), channel_id=1, source_target_pairs={{6,0},{7,1},{14,8},{15,9},{22,16},{23,17},{30,24},{31,25}} | collective-permute-start | bytes 1572872 | tf_op jit(solution)/shard_map/ppermute | solution.py:1167
  527.7 24.3 %collective-permute-start.75 = (bf16[256,1024]{1,0:T(8,128)(2,1)}, bf16[256,1024]{1,0:T(8,128)(2,1)S(1)}, u32[]{:S(2)}, u32[]{:S(2)}) collective-permute-start(bf16[256,1024]{1,0:T(8,128)(2,1)} %get-tuple-element.1866), channel_id=1, source_target_pairs={{0,8},{8,0},{16,24},{24,16},{1,9},{9,1},{17,25},{25,17},{2,10},{10... | collective-permute-start | bytes 1572872 | tf_op jit(solution)/shard_map/ppermute | solution.py:1197
  569.2 32.2 %collective-permute-start.92 = (bf16[4,64,1536]{2,1,0:T(8,128)(2,1)}, bf16[4,64,1536]{2,1,0:T(8,128)(2,1)}, u32[]{:S(2)}, u32[]{:S(2)}) collective-permute-start(bf16[4,64,1536]{2,1,0:T(8,128)(2,1)} %get-tuple-element.1907), channel_id=1, source_target_pairs={{0,6},{2,4},{4,2},{6,0},{1,7},{3,5},{5,3},{7,1},{8,14},{10,12},{12... | collective-permute-start | bytes 2359304 | tf_op jit(solution)/shard_map/ppermute | solution.py:1079
  594.3 29.9 %collective-permute-start.85 = (bf16[64,1024]{1,0:T(8,128)(2,1)}, bf16[64,1024]{1,0:T(8,128)(2,1)S(1)}, u32[]{:S(2)}, u32[]{:S(2)}) collective-permute-start(bf16[64,1024]{1,0:T(8,128)(2,1)} %get-tuple-element.1968), channel_id=1, source_target_pairs={{0,2},{2,0},{4,6},{6,4},{1,3},{3,1},{5,7},{7,5},{8,10},{10,8},{12,... | collective-permute-start | bytes 393224 | tf_op jit(solution)/shard_map/ppermute | solution.py:781
  595.5 29.4 %collective-permute-start.86 = (bf16[64,1024]{1,0:T(8,128)(2,1)}, bf16[64,1024]{1,0:T(8,128)(2,1)S(1)}, u32[]{:S(2)}, u32[]{:S(2)}) collective-permute-start(bf16[64,1024]{1,0:T(8,128)(2,1)} %get-tuple-element.1969), channel_id=1, source_target_pairs={{0,4},{2,6},{4,0},{6,2},{1,5},{3,7},{5,1},{7,3},{8,12},{10,14},{12... | collective-permute-start | bytes 393224 | tf_op jit(solution)/shard_map/ppermute | solution.py:781
  598.6 27.0 %collective-permute-start.87 = (bf16[64,1024]{1,0:T(8,128)(2,1)}, bf16[64,1024]{1,0:T(8,128)(2,1)S(1)}, u32[]{:S(2)}, u32[]{:S(2)}) collective-permute-start(bf16[64,1024]{1,0:T(8,128)(2,1)} %get-tuple-element.1970), channel_id=1, source_target_pairs={{0,6},{2,4},{4,2},{6,0},{1,7},{3,5},{5,3},{7,1},{8,14},{10,12},{12... | collective-permute-start | bytes 393224 | tf_op jit(solution)/shard_map/ppermute | solution.py:781
  (113 other events, 1800.1 us)
